TPU v7x, 32 devices: a whole 2x2x4 slice. The times are simulated.
32 devices in a mesh: dp: 4 (over y, x), expert: 8 (over z, core).
Axes of the slice: x: 2, y: 2, z: 4, core: 2. Of those that a mesh axis runs over, the one named last changes fastest.
Arguments:
- inputs: bfloat16 [2, 4, 1536, 2048], P(None, 'dp', 'expert'), may hold values from -6 to 6
- cotangent: bfloat16 [2, 4, 1536, 2048], P(None, 'dp', 'expert'), may hold values from -6 to 6
- membership: int32 [2, 4, 1536], P(None, 'dp'), may hold values from 0 to 8, as said below
- routes: int32 [2, 4, 1536, 8], P(None, 'dp', 'expert'), may hold values from 0 to 15, all different within a row
- gate_weights: float32 [2, 4, 1536, 8], P(None, 'dp', 'expert'), may hold values from 0.06 to 0.19
- pair_order: int32 [2, 4, 8, 1536], P(None, 'dp', 'expert'), may hold values from 0 to 1535, each once within a row
- w_query: bfloat16 [2048, 4096], P(None, ('dp', 'expert')), may hold values from -0.125 to 0.125
- w_key: bfloat16 [2048, 512], P(None, ('dp', 'expert')), may hold values from -0.125 to 0.125
- w_value: bfloat16 [2048, 512], P(None, ('dp', 'expert')), may hold values from -0.125 to 0.125
- w_output: bfloat16 [4096, 2048], P(('dp', 'expert')), may hold values from -0.5 to 0.5
- norm_gains: bfloat16 [4352], P(('dp', 'expert')), may hold values from 0.5 to 1.5
- w_gate: bfloat16 [16, 2048, 768], P('expert', 'dp'), may hold values from -0.125 to 0.125
- w_up: bfloat16 [16, 2048, 768], P('expert', 'dp'), may hold values from -0.125 to 0.125
- w_down: bfloat16 [16, 768, 2048], P('expert', None, 'dp'), may hold values from -0.625 to 0.625
Outputs:
- output: bfloat16 [2, 4, 1536, 2048], P(None, 'dp', 'expert')
- input_grad: float32 [2, 4, 1536, 2048], P(None, 'dp', 'expert')
- grad_query: float32 [2048, 4096], P(None, ('dp', 'expert'))
- grad_key: float32 [2048, 512], P(None, ('dp', 'expert'))
- grad_value: float32 [2048, 512], P(None, ('dp', 'expert'))
- grad_output: float32 [4096, 2048], P(('dp', 'expert'))
- grad_gains: float32 [4352], P(('dp', 'expert'))
- grad_gate: float32 [16, 2048, 768], P('expert', 'dp')
- grad_up: float32 [16, 2048, 768], P('expert', 'dp')
- grad_down: float32 [16, 768, 2048], P('expert', None, 'dp')
Inputs may be any that keep to these rules, and one draw needn't show every extreme that they name: `membership`: the first 1024 tokens of each group are its prompt (0); then continuations 1 to 8 follow in order, each of half to three halves of 64 tokens, together 8 * 64 tokens. `routes`: each token names 8 different experts. `pair_order`: within each block of 192 tokens the 1536 pairs carry each priority once.
All inputs are finite; a program needn't handle non-finite values.
Results may differ from a plain program's by a relative error of at most 0.019.
Values may be sent and summed in bfloat16 or wider, within the bound.
A program may use at most 384 MiB of HBM per device.

v0:
```python
import jax
import jax.numpy as jnp
from jax import lax
from jax.sharding import PartitionSpec as P

H = 32
KVH = 4
HD = 128
FF = 768
TOPK = 8
PROMPT = 1024


EPSILON = 1e-06
ROPE_BASE = 1000000.0
MASKED = -1e30


def rms_scale(values):
    return lax.rsqrt(jnp.mean(values * values, axis=-1, keepdims=True) + EPSILON)


def norm_back(upstream, values, inv_rms, norm_gain):
    lifted = upstream * norm_gain
    inner_dot = jnp.mean(lifted * values, axis=-1, keepdims=True)
    back_grad = inv_rms * lifted - values * (inv_rms * inv_rms * inv_rms) * inner_dot
    gain_grad = jnp.sum((upstream * values * inv_rms).reshape(-1, values.shape[-1]), axis=0)
    return (back_grad, gain_grad)


def rotate(values, cosine, sine_part):
    half_dim = values.shape[-1] // 2
    first_half = values[..., :half_dim]
    second_half = values[..., half_dim:]
    return jnp.concatenate(
        [
            first_half * cosine - second_half * sine_part,
            second_half * cosine + first_half * sine_part,
        ],
        axis=-1,
    )


def rounded(values):
    return lax.optimization_barrier(values.astype(jnp.bfloat16)).astype(jnp.float32)


def heads_first(values, kv_heads):
    row_count = values.shape[0]
    return jnp.transpose(values.reshape(row_count, kv_heads, -1, HD), (1, 0, 2, 3)).reshape(
        kv_heads, -1, HD
    )


def heads_last(values, row_count):
    kv_heads = values.shape[0]
    return jnp.transpose(values.reshape(kv_heads, row_count, -1, HD), (1, 0, 2, 3)).reshape(
        row_count, -1, HD
    )


def assign(route_ids, gate_vals, ranking, capacity, columns):
    row_count = route_ids.shape[0]
    pair_experts = route_ids.reshape(-1)
    earlier = (pair_experts[None, :] == pair_experts[:, None]) & (
        ranking[None, :] < ranking[:, None]
    )
    slot_of = jnp.sum(earlier.astype(jnp.int32), axis=1)
    kept_pair = slot_of < capacity
    local_col = pair_experts * capacity + slot_of
    target = jnp.where(kept_pair, local_col, columns)
    column_ids = jnp.arange(columns, dtype=jnp.int32)
    slot_table = jnp.any(
        target.reshape(row_count, -1)[:, :, None] == column_ids[None, None, :], axis=1
    ).astype(jnp.bfloat16)
    pick_rows = jnp.minimum(local_col, columns - 1)
    weight = gate_vals * kept_pair.reshape(row_count, -1).astype(jnp.float32)
    return (slot_table, target, pick_rows, weight)


def body(
    inputs,
    cotangent,
    membership,
    routes,
    gate_weights,
    pair_order,
    w_query,
    w_key,
    w_value,
    w_output,
    norm_gains,
    w_gate,
    w_up,
    w_down,
):
    micro_count = inputs.shape[0]
    row_count = inputs.shape[2]
    model_width = inputs.shape[3]
    group_len = membership.shape[2]
    member = lax.axis_index("expert")
    local_experts = w_gate.shape[0]
    experts = local_experts * lax.axis_size("expert")
    capacity = row_count * TOPK // experts
    columns = experts * capacity
    per_kv = H // KVH
    score_scale = HD ** (-0.5)

    def fetch_dense():
        return (
            lax.all_gather(w_query, ("dp", "expert"), axis=1, tiled=True),
            lax.all_gather(w_key, ("dp", "expert"), axis=1, tiled=True),
            lax.all_gather(w_value, ("dp", "expert"), axis=1, tiled=True),
            lax.all_gather(w_output, ("dp", "expert"), axis=0, tiled=True),
            lax.all_gather(norm_gains, ("dp", "expert"), axis=0, tiled=True),
        )

    def fetch_experts():
        return (
            lax.all_gather(w_gate, "dp", axis=1, tiled=True),
            lax.all_gather(w_up, "dp", axis=1, tiled=True),
            lax.all_gather(w_down, "dp", axis=2, tiled=True),
        )

    key_index = jnp.arange(group_len, dtype=jnp.int32)
    frequency = ROPE_BASE ** (-(jnp.arange(HD // 2, dtype=jnp.float32) * 2.0 / HD))
    saved = []
    outputs = []
    for batch_at in range(micro_count):
        dense_now = fetch_dense()
        expert_now = fetch_experts()
        q_full, k_full, v_full, o_full, gain_full = dense_now
        wg_full, wu_full, wd_full = expert_now
        gains_f = gain_full.astype(jnp.float32)
        gain_in = gains_f[:model_width]
        gain_mid = gains_f[model_width : 2 * model_width]
        gain_q = gains_f[2 * model_width : 2 * model_width + HD]
        gain_k = gains_f[2 * model_width + HD :]
        segment = membership[batch_at, 0]
        start_row = member * row_count
        row_index = start_row + jnp.arange(row_count, dtype=jnp.int32)
        seg_rows = lax.dynamic_slice_in_dim(segment, start_row, row_count)
        before = jnp.sum((segment[None, :] < seg_rows[:, None]).astype(jnp.int32), axis=1)
        position = jnp.where(seg_rows == 0, row_index, PROMPT + row_index - before)
        allowed = (key_index[None, :] <= row_index[:, None]) & (
            (segment[None, :] == 0) | (segment[None, :] == seg_rows[:, None])
        )
        allowed_rows = jnp.repeat(allowed, per_kv, axis=0)
        angles = position.astype(jnp.float32)[:, None] * frequency[None, :]
        cosine = jnp.cos(angles)[:, None, :]
        sine_part = jnp.sin(angles)[:, None, :]
        hidden = inputs[batch_at, 0].astype(jnp.float32)
        scale_in = rms_scale(hidden)
        normed = (hidden * scale_in * gain_in).astype(jnp.bfloat16)
        queries = jnp.dot(normed, q_full, preferred_element_type=jnp.float32).reshape(
            row_count, H, HD
        )
        scale_q = rms_scale(queries)
        q_low = rotate(queries * scale_q * gain_q, cosine, sine_part).astype(jnp.bfloat16)
        key_pre = jnp.dot(normed, k_full, preferred_element_type=jnp.float32).reshape(
            row_count, KVH, HD
        )
        scale_k = rms_scale(key_pre)
        k_low = (
            rotate(key_pre * scale_k * gain_k, cosine, sine_part)
            .astype(jnp.bfloat16)
            .reshape(row_count, KVH * HD)
        )
        v_low = jnp.dot(normed, v_full, preferred_element_type=jnp.float32).astype(jnp.bfloat16)
        k_group, v_group = (
            lax.all_gather(k_low, "expert", axis=0, tiled=True),
            lax.all_gather(v_low, "expert", axis=0, tiled=True),
        )
        q_heads = heads_first(q_low.reshape(row_count, H * HD), KVH)
        k_heads = heads_first(k_group, KVH)
        v_heads = heads_first(v_group, KVH)

        def forward_head(operands):
            query_h, key_h, value_h = operands
            scores = (
                jnp.einsum("qd,kd->qk", query_h, key_h, preferred_element_type=jnp.float32)
                * score_scale
            )
            scores = jnp.where(allowed_rows, scores, MASKED)
            row_max = jnp.max(scores, axis=-1, keepdims=True)
            scaled = jnp.exp(scores - row_max)
            row_sum = jnp.sum(scaled, axis=-1, keepdims=True)
            attn_prob = (scaled / row_sum).astype(jnp.bfloat16)
            mixed_h = jnp.dot(attn_prob, value_h, preferred_element_type=jnp.float32)
            return (mixed_h, (row_max + jnp.log(row_sum))[:, 0])

        mixed_heads, log_sum = lax.map(forward_head, (q_heads, k_heads, v_heads))
        o_low = heads_last(mixed_heads, row_count).reshape(row_count, H * HD).astype(jnp.bfloat16)
        branch = jnp.dot(o_low, o_full, preferred_element_type=jnp.float32)
        middle = hidden + branch
        scale_mid = rms_scale(middle)
        routed = (middle * scale_mid * gain_mid).astype(jnp.bfloat16)
        slot_table, target, pick_rows, weight = assign(
            routes[batch_at, 0],
            gate_weights[batch_at, 0],
            pair_order[batch_at, 0, 0],
            capacity,
            columns,
        )
        sent_rows = jnp.einsum(
            "tc,td->cd", slot_table, routed, preferred_element_type=jnp.float32
        ).astype(jnp.bfloat16)
        sent_rows = sent_rows.reshape(experts, capacity, model_width)
        received = lax.all_to_all(sent_rows, "expert", split_axis=0, concat_axis=1, tiled=True)
        gate_pre = jnp.einsum("erd,edf->erf", received, wg_full, preferred_element_type=jnp.float32)
        up_pre = jnp.einsum("erd,edf->erf", received, wu_full, preferred_element_type=jnp.float32)
        hidden_low = (jax.nn.silu(gate_pre) * up_pre).astype(jnp.bfloat16)
        result = jnp.einsum(
            "erf,efd->erd", hidden_low, wd_full, preferred_element_type=jnp.float32
        ).astype(jnp.bfloat16)
        returned = lax.all_to_all(result, "expert", split_axis=1, concat_axis=0, tiled=True)
        picked = jnp.take(returned.reshape(columns, model_width), pick_rows, axis=0).reshape(
            row_count, TOPK, model_width
        )
        expert_mix = jnp.sum(picked.astype(jnp.float32) * weight[:, :, None], axis=1)
        outputs.append((middle + expert_mix).astype(jnp.bfloat16))
        saved.append(
            {
                "hidden": hidden,
                "scale_in": scale_in,
                "normed": normed,
                "queries": queries,
                "scale_q": scale_q,
                "key_pre": key_pre,
                "scale_k": scale_k,
                "q_heads": q_heads,
                "k_heads": k_heads,
                "v_heads": v_heads,
                "log_sum": log_sum,
                "allowed_rows": allowed_rows,
                "cosine": cosine,
                "sine_part": sine_part,
                "o_low": o_low,
                "middle": middle,
                "scale_mid": scale_mid,
                "slot_table": slot_table,
                "target": target,
                "weight": weight,
                "received": received,
                "gate_pre": gate_pre,
                "up_pre": up_pre,
                "hidden_low": hidden_low,
            }
        )
    acc_query = jnp.zeros((model_width, H * HD), jnp.float32)
    acc_key = jnp.zeros((model_width, KVH * HD), jnp.float32)
    acc_value = jnp.zeros((model_width, KVH * HD), jnp.float32)
    acc_output = jnp.zeros((H * HD, model_width), jnp.float32)
    acc_gate = jnp.zeros((local_experts, model_width, FF), jnp.float32)
    acc_up = jnp.zeros((local_experts, model_width, FF), jnp.float32)
    acc_down = jnp.zeros((local_experts, FF, model_width), jnp.float32)
    grad_in = jnp.zeros((model_width,), jnp.float32)
    grad_mid = jnp.zeros((model_width,), jnp.float32)
    grad_qn = jnp.zeros((HD,), jnp.float32)
    grad_kn = jnp.zeros((HD,), jnp.float32)
    input_grads = []
    for batch_at in range(micro_count):
        dense_now = fetch_dense()
        expert_now = fetch_experts()
        q_full, k_full, v_full, o_full, gain_full = dense_now
        wg_full, wu_full, wd_full = expert_now
        gains_f = gain_full.astype(jnp.float32)
        gain_in = gains_f[:model_width]
        gain_mid = gains_f[model_width : 2 * model_width]
        gain_q = gains_f[2 * model_width : 2 * model_width + HD]
        gain_k = gains_f[2 * model_width + HD :]
        kept = saved[batch_at]
        grad_rows = cotangent[batch_at, 0].astype(jnp.float32)
        spread = (kept["weight"][:, :, None] * grad_rows[:, None, :]).reshape(-1, model_width)
        d_result = (
            jnp.zeros((columns + 1, model_width), jnp.float32)
            .at[kept["target"]]
            .add(spread)[:columns]
        )
        d_result = d_result.astype(jnp.bfloat16).reshape(experts, capacity, model_width)
        d_recv = lax.all_to_all(d_result, "expert", split_axis=0, concat_axis=1, tiled=True)
        gate_pre = kept["gate_pre"]
        up_pre = kept["up_pre"]
        d_hidden = jnp.einsum("erd,efd->erf", d_recv, wd_full, preferred_element_type=jnp.float32)
        acc_down = acc_down + jnp.einsum(
            "erf,erd->efd", kept["hidden_low"], d_recv, preferred_element_type=jnp.float32
        )
        sigmoid_g = jax.nn.sigmoid(gate_pre)
        silu_g = gate_pre * sigmoid_g
        d_gate = (d_hidden * up_pre * sigmoid_g * (1.0 + gate_pre * (1.0 - sigmoid_g))).astype(
            jnp.bfloat16
        )
        d_up = (d_hidden * silu_g).astype(jnp.bfloat16)
        acc_gate = acc_gate + jnp.einsum(
            "erd,erf->edf", kept["received"], d_gate, preferred_element_type=jnp.float32
        )
        acc_up = acc_up + jnp.einsum(
            "erd,erf->edf", kept["received"], d_up, preferred_element_type=jnp.float32
        )
        d_input_rows = jnp.einsum(
            "erf,edf->erd", d_gate, wg_full, preferred_element_type=jnp.float32
        )
        d_input_rows = d_input_rows + jnp.einsum(
            "erf,edf->erd", d_up, wu_full, preferred_element_type=jnp.float32
        )
        d_sent = lax.all_to_all(
            d_input_rows.astype(jnp.bfloat16), "expert", split_axis=1, concat_axis=0, tiled=True
        )
        d_routed = jnp.dot(
            kept["slot_table"],
            d_sent.reshape(columns, model_width),
            preferred_element_type=jnp.float32,
        )
        d_mid_norm, mid_gain_grad = norm_back(d_routed, kept["middle"], kept["scale_mid"], gain_mid)
        grad_mid = grad_mid + mid_gain_grad
        d_middle = grad_rows + d_mid_norm
        d_branch = d_middle.astype(jnp.bfloat16)
        acc_output = acc_output + jnp.einsum(
            "ti,td->id", kept["o_low"], d_branch, preferred_element_type=jnp.float32
        )
        d_mixed = jnp.einsum(
            "td,id->ti", d_branch, o_full, preferred_element_type=jnp.float32
        ).astype(jnp.bfloat16)
        d_heads = heads_first(d_mixed, KVH)
        allowed_rows = kept["allowed_rows"]

        def backward_head(operands):
            query_h, key_h, value_h, grad_h, log_h = operands
            scores = (
                jnp.einsum("qd,kd->qk", query_h, key_h, preferred_element_type=jnp.float32)
                * score_scale
            )
            scores = jnp.where(allowed_rows, scores, MASKED)
            attn_prob = jnp.exp(scores - log_h[:, None])
            prob_low = attn_prob.astype(jnp.bfloat16)
            d_prob = jnp.einsum("qd,kd->qk", grad_h, value_h, preferred_element_type=jnp.float32)
            row_dot = jnp.sum(attn_prob * d_prob, axis=-1, keepdims=True)
            d_score = (attn_prob * (d_prob - row_dot)).astype(jnp.bfloat16)
            d_query_h = jnp.dot(d_score, key_h, preferred_element_type=jnp.float32) * score_scale
            d_key_h = (
                jnp.einsum("qk,qd->kd", d_score, query_h, preferred_element_type=jnp.float32)
                * score_scale
            )
            d_value_h = jnp.einsum(
                "qk,qd->kd", prob_low, grad_h, preferred_element_type=jnp.float32
            )
            return (d_query_h, d_key_h, d_value_h)

        dq_heads, dk_heads, dv_heads = lax.map(
            backward_head,
            (kept["q_heads"], kept["k_heads"], kept["v_heads"], d_heads, kept["log_sum"]),
        )
        cosine = kept["cosine"]
        sine_part = kept["sine_part"]
        d_query = rotate(rounded(heads_last(dq_heads, row_count)), cosine, -sine_part)
        d_query, q_gain_grad = norm_back(d_query, kept["queries"], kept["scale_q"], gain_q)
        grad_qn = grad_qn + q_gain_grad
        dq_proj = d_query.reshape(row_count, H * HD).astype(jnp.bfloat16)
        dk_group = heads_last(dk_heads, group_len).reshape(group_len, KVH * HD)
        dv_group = heads_last(dv_heads, group_len).reshape(group_len, KVH * HD)
        dk_own, dv_own = (
            lax.psum_scatter(
                dk_group.astype(jnp.bfloat16), "expert", scatter_dimension=0, tiled=True
            ).astype(jnp.float32),
            lax.psum_scatter(
                dv_group.astype(jnp.bfloat16), "expert", scatter_dimension=0, tiled=True
            ).astype(jnp.float32),
        )
        d_key = rotate(rounded(dk_own).reshape(row_count, KVH, HD), cosine, -sine_part)
        d_key, k_gain_grad = norm_back(d_key, kept["key_pre"], kept["scale_k"], gain_k)
        grad_kn = grad_kn + k_gain_grad
        dk_proj = d_key.reshape(row_count, KVH * HD).astype(jnp.bfloat16)
        dv_proj = dv_own.astype(jnp.bfloat16)
        normed = kept["normed"]
        acc_query = acc_query + jnp.einsum(
            "td,ti->di", normed, dq_proj, preferred_element_type=jnp.float32
        )
        acc_key = acc_key + jnp.einsum(
            "td,ti->di", normed, dk_proj, preferred_element_type=jnp.float32
        )
        acc_value = acc_value + jnp.einsum(
            "td,ti->di", normed, dv_proj, preferred_element_type=jnp.float32
        )
        d_normed = jnp.einsum("ti,di->td", dq_proj, q_full, preferred_element_type=jnp.float32)
        d_normed = d_normed + jnp.einsum(
            "ti,di->td", dk_proj, k_full, preferred_element_type=jnp.float32
        )
        d_normed = d_normed + jnp.einsum(
            "ti,di->td", dv_proj, v_full, preferred_element_type=jnp.float32
        )
        d_in_norm, in_gain_grad = norm_back(d_normed, kept["hidden"], kept["scale_in"], gain_in)
        grad_in = grad_in + in_gain_grad
        input_grads.append(d_middle + d_in_norm)
    gain_grads = jnp.concatenate([grad_in, grad_mid, grad_qn, grad_kn])
    grad_query, grad_key, grad_value, grad_output, grad_gains = (
        lax.psum_scatter(acc_query, ("dp", "expert"), scatter_dimension=1, tiled=True),
        lax.psum_scatter(acc_key, ("dp", "expert"), scatter_dimension=1, tiled=True),
        lax.psum_scatter(acc_value, ("dp", "expert"), scatter_dimension=1, tiled=True),
        lax.psum_scatter(acc_output, ("dp", "expert"), scatter_dimension=0, tiled=True),
        lax.psum_scatter(gain_grads, ("dp", "expert"), scatter_dimension=0, tiled=True),
    )
    grad_gate, grad_up, grad_down = (
        lax.psum_scatter(
            acc_gate.astype(jnp.bfloat16), "dp", scatter_dimension=1, tiled=True
        ).astype(jnp.float32),
        lax.psum_scatter(acc_up.astype(jnp.bfloat16), "dp", scatter_dimension=1, tiled=True).astype(
            jnp.float32
        ),
        lax.psum_scatter(
            acc_down.astype(jnp.bfloat16), "dp", scatter_dimension=2, tiled=True
        ).astype(jnp.float32),
    )
    output = jnp.stack(outputs)[:, None]
    input_grad = jnp.stack(input_grads)[:, None]
    return (
        output,
        input_grad,
        grad_query,
        grad_key,
        grad_value,
        grad_output,
        grad_gains,
        grad_gate,
        grad_up,
        grad_down,
    )


def solution(mesh):
    return jax.shard_map(
        body,
        mesh=mesh,
        in_specs=(
            P(None, "dp", "expert", None),
            P(None, "dp", "expert", None),
            P(None, "dp", None),
            P(None, "dp", "expert", None),
            P(None, "dp", "expert", None),
            P(None, "dp", "expert", None),
            P(None, ("dp", "expert")),
            P(None, ("dp", "expert")),
            P(None, ("dp", "expert")),
            P(("dp", "expert"), None),
            P(("dp", "expert")),
            P("expert", "dp", None),
            P("expert", "dp", None),
            P("expert", None, "dp"),
        ),
        out_specs=(
            P(None, "dp", "expert", None),
            P(None, "dp", "expert", None),
            P(None, ("dp", "expert")),
            P(None, ("dp", "expert")),
            P(None, ("dp", "expert")),
            P(("dp", "expert"), None),
            P(("dp", "expert")),
            P("expert", "dp", None),
            P("expert", "dp", None),
            P("expert", None, "dp"),
        ),
        check_vma=False,
    )
```

profile of v0, /device:TPU:8, one launch (start us, length us, event | category | flops | bytes accessed | tf_op | source)
XLA Modules:
  0.0 3306.3 jit_solution(10857320168500275876)
XLA Ops:
  9.6 40.7 %all-reduce = bf16[4352]{0:T(1024)(128)(2,1)S(1)} all-reduce(bf16[4352]{0:T(1024)(128)(2,1)S(1)} %dynamic-update-slice), channel_id=1, replica_groups=mesh['dp'=4,'expert'=8] {'dp','expert'}, use_global_device_ids=true, to_apply=%add | all-reduce | flops 4352 | bytes 17408
  74.7 51.5 %all-gather.18.cloned.1.call-done = bf16[2048,512]{0,1:T(8,128)(2,1)} async-done(((bf16[2048,16]{0,1:T(8,128)(2,1)}), bf16[2048,512]{0,1:T(8,128)(2,1)}) %all-gather.18.cloned.1.call-update) | async-done | bytes 2097168 | tf_op jit(solution)/shard_map/all_gather | solution.py:113
  152.7 26.3 scatter_custom_fusion.1
  204.2 26.3 scatter_custom_fusion
  277.9 183.4 %all-gather.12.cloned.1.call-done = bf16[2048,4096]{1,0:T(8,128)(2,1)} async-done(((bf16[2048,128]{1,0:T(8,128)(2,1)}), bf16[2048,4096]{1,0:T(8,128)(2,1)}) %all-gather.12.cloned.1.call-update) | async-done | bytes 16777232 | tf_op jit(solution)/shard_map/all_gather | solution.py:111
  521.6 48.6 %while.57 = (s32[]{:T(128)}, bf16[4,1536,128]{2,1,0:T(8,128)(2,1)}, f32[4,1536]{1,0:T(4,128)S(1)}, bf16[4,1536,128]{2,1,0:T(8,128)(2,1)}, bf16[4,1536,128]{2,1,0...) while((s32[]{:T(128)}, bf16[4,1536,128]{2,1,0:T(8,128)(2,1)}, ...), condition=%wide.region_19.21_spmd.clone, body=%wide.region_16.20_spmd.clone.sunk | while | flops 1226832384 | bytes 52672672 | solution.py:192
  573.7 53.2 %all-gather.22.cloned.1.call-done = bf16[4096,2048]{1,0:T(8,128)(2,1)} async-done(((bf16[128,2048]{1,0:T(8,128)(2,1)}), bf16[4096,2048]{1,0:T(8,128)(2,1)}) %all-gather.22.cloned.1.call-update) | async-done | bytes 16777232 | tf_op jit(solution)/shard_map/all_gather | solution.py:114
  641.7 59.0 %all-to-all-done.4 = bf16[16,96,2048]{2,1,0:T(8,128)(2,1)} async-done(((bf16[16,96,2048]{2,1,0:T(8,128)(2,1)}), bf16[16,96,2048]{2,1,0:T(8,128)(2,1)}, u32[]{:S(2)}, u32[]{:S(2)}) %all-to-all-start.4) | async-done | bytes 6291488 | tf_op jit(solution)/shard_map/all_to_all | solution.py:281
  709.3 43.7 %while.56 = (s32[]{:T(128)}, bf16[4,1536,128]{2,1,0:T(8,128)(2,1)S(1)}, f32[4,1536]{1,0:T(4,128)S(1)}, bf16[4,1536,128]{2,1,0:T(8,128)(2,1)}, bf16[4,1536,128]{2...) while((s32[]{:T(128)}, ...), condition=%wide.region_7.8_spmd.clone, body=%wide.region_4.7_spmd.clone.sunk | while | flops 1226832384 | bytes 40089704 | solution.py:192
  768.0 76.5 %all-to-all-done.2 = bf16[16,96,2048]{2,1,0:T(8,128)(2,1)} async-done(((bf16[16,96,2048]{2,1,0:T(8,128)(2,1)}), bf16[16,96,2048]{2,1,0:T(8,128)(2,1)}, u32[]{:S(2)}, u32[]{:S(2)}) %all-to-all-start.2) | async-done | bytes 6291488 | tf_op jit(solution)/shard_map/all_to_all | solution.py:209
  942.3 46.0 %all-to-all-done = bf16[16,96,2048]{2,1,0:T(8,128)(2,1)} async-done(((bf16[16,96,2048]{2,1,0:T(8,128)(2,1)}), bf16[16,96,2048]{2,1,0:T(8,128)(2,1)}, u32[]{:S(2)}, u32[]{:S(2)}) %all-to-all-start) | async-done | bytes 6291488 | tf_op jit(solution)/shard_map/all_to_all | solution.py:209
  1076.7 55.3 %all-to-all-done.7 = bf16[2,768,2048]{2,0,1:T(2,128)(2,1)} async-done(((bf16[2,768,2048]{2,0,1:T(2,128)(2,1)}), bf16[2,768,2048]{2,0,1:T(2,128)(2,1)}, u32[]{:S(2)}, u32[]{:S(2)}) %all-to-all-start.7) | async-done | bytes 6291488 | tf_op jit(solution)/shard_map/all_to_all | solution.py:306
  1167.0 108.6 %all-to-all-done.5 = bf16[2,768,2048]{2,0,1:T(2,128)(2,1)} async-done(((bf16[2,768,2048]{2,0,1:T(2,128)(2,1)}), bf16[2,768,2048]{2,0,1:T(2,128)(2,1)}, u32[]{:S(2)}, u32[]{:S(2)}) %all-to-all-start.5) | async-done | bytes 6291488 | tf_op jit(solution)/shard_map/all_to_all | solution.py:306
  1310.8 108.6 %all-to-all-done.3 = bf16[2,768,2048]{2,0,1:T(2,128)(2,1)} async-done(((bf16[2,768,2048]{2,0,1:T(2,128)(2,1)}), bf16[2,768,2048]{2,0,1:T(2,128)(2,1)}, u32[]{:S(2)}, u32[]{:S(2)}) %all-to-all-start.3) | async-done | bytes 6291488 | tf_op jit(solution)/shard_map/all_to_all | solution.py:216
  1458.5 104.6 %all-to-all-done.1 = bf16[2,768,2048]{2,0,1:T(2,128)(2,1)} async-done(((bf16[2,768,2048]{2,0,1:T(2,128)(2,1)}), bf16[2,768,2048]{2,0,1:T(2,128)(2,1)}, u32[]{:S(2)}, u32[]{:S(2)}) %all-to-all-start.1) | async-done | bytes 6291488 | tf_op jit(solution)/shard_map/all_to_all | solution.py:216
  1638.5 155.4 %while.58 = (s32[]{:T(128)}, bf16[4,1536,128]{2,1,0:T(8,128)(2,1)}, bf16[4,1536,128]{1,2,0:T(8,128)(2,1)}, bf16[4,1536,128]{1,2,0:T(8,128)(2,1)}, bf16[4,1536,12...) while((s32[]{:T(128)}, bf16[4,1536,128]{2,1,0:T(8,128)(2,1)}, ...), condition=%wide.region_28.30_spmd.clone, body=%wide.region_26.29_spmd.clone.sunk | while | flops 3041720832 | bytes 143462608 | solution.py:349
  1813.6 155.3 %while.59 = (s32[]{:T(128)}, bf16[4,1536,128]{2,1,0:T(8,128)(2,1)}, bf16[4,1536,128]{1,2,0:T(8,128)(2,1)}, bf16[4,1536,128]{1,2,0:T(8,128)(2,1)}, bf16[4,1536,12...) while((s32[]{:T(128)}, bf16[4,1536,128]{2,1,0:T(8,128)(2,1)}, ...), condition=%wide.region_38.40_spmd.clone, body=%wide.region_36.39_spmd.clone.sunk | while | flops 3041720832 | bytes 143462608 | solution.py:349
  2116.1 25.4 convolution_add_fusion
  2225.0 69.8 %reduce-scatter.32.cloned.1.call-done = bf16[2,768,512]{2,1,0:T(8,128)(2,1)} async-done(((bf16[2,768,2048]{2,1,0:T(8,128)(2,1)}), bf16[2,768,512]{2,1,0:T(8,128)(2,1)}) %reduce-scatter.32.cloned.1.call-update) | async-done | bytes 1572880 | tf_op jit(solution)/shard_map/reduce_scatter | solution.py:409
  2304.8 39.7 %all-reduce.1 = f32[4352]{0:T(1024)S(1)} all-reduce(f32[4352]{0:T(1024)S(1)} %pad_maximum_fusion.4), channel_id=10, replica_groups=mesh['dp'=4,'expert'=8] {'dp','expert'}, use_global_device_ids=true, to_apply=%region_56.58.clone | all-reduce | flops 4352 | bytes 34816
  2350.1 84.8 %reduce-scatter.22.cloned.1.call-done = f32[2048,16]{0,1:T(8,128)} async-done(((f32[2048,512]{0,1:T(8,128)}), f32[2048,16]{0,1:T(8,128)}) %reduce-scatter.22.cloned.1.call-update) | async-done | bytes 131088 | tf_op jit(solution)/shard_map/reduce_scatter | solution.py:397
  2435.0 142.5 %reduce-scatter.24.cloned.1.call-done = f32[2048,16]{0,1:T(8,128)} async-done(((f32[2048,512]{0,1:T(8,128)}), f32[2048,16]{0,1:T(8,128)}) %reduce-scatter.24.cloned.1.call-update) | async-done | bytes 131088 | tf_op jit(solution)/shard_map/reduce_scatter | solution.py:398
  2577.5 361.3 %reduce-scatter.20.cloned.1.call-done = f32[2048,128]{1,0:T(8,128)} async-done(((f32[2048,4096]{1,0:T(8,128)}), f32[2048,128]{1,0:T(8,128)}) %reduce-scatter.20.cloned.1.call-update) | async-done | bytes 1048592 | tf_op jit(solution)/shard_map/reduce_scatter | solution.py:396
  2938.8 360.5 %reduce-scatter.26.cloned.1.call-done = f32[128,2048]{1,0:T(8,128)} async-done(((f32[4096,2048]{1,0:T(8,128)}), f32[128,2048]{1,0:T(8,128)}) %reduce-scatter.26.cloned.1.call-update) | async-done | bytes 1048592 | tf_op jit(solution)/shard_map/reduce_scatter | solution.py:399
  (755 shorter events, 1264.0 us)
Async XLA Ops:
  8.7 243.8 %all-gather.16.cloned.1.call-start = ((), (), s32[]{:S(2)}) async-start(), calls=%async_computation.21 | async-start | bytes 1769472 | tf_op jit(solution)/shard_map/all_gather | solution.py:171
  74.7 181.1 %all-gather.20.cloned.1.call-start = ((), (), s32[]{:S(2)}) async-start(), calls=%async_computation.23 | async-start | bytes 1769472 | tf_op jit(solution)/shard_map/all_gather | solution.py:172
  133.7 327.6 %all-gather.12.cloned.1.call-start = ((), (), s32[]{:S(2)}) async-start(), calls=%async_computation.19 | async-start | bytes 17301504 | tf_op jit(solution)/shard_map/all_gather | solution.py:111
  134.5 492.5 %all-gather.22.cloned.1.call-start = ((), (), s32[]{:S(2)}) async-start(), calls=%async_computation.24 | async-start | bytes 17301504 | tf_op jit(solution)/shard_map/all_gather | solution.py:114
  135.2 730.6 %all-gather.24.cloned.1.call-start = ((), (), s32[]{:S(2)}) async-start(), calls=%async_computation.25 | async-start | bytes 7864320 | tf_op jit(solution)/shard_map/all_gather | solution.py:120
  136.0 740.2 %all-gather.26.cloned.1.call-start = ((), (), s32[]{:S(2)}) async-start(), calls=%async_computation.26 | async-start | bytes 7864320 | tf_op jit(solution)/shard_map/all_gather | solution.py:121
  187.2 327.3 %all-to-all-start.6 = ((bf16[16,96,2048]{2,1,0:T(8,128)(2,1)}), bf16[16,96,2048]{2,1,0:T(8,128)(2,1)}, u32[]{:S(2)}, u32[]{:S(2)}) async-start(bf16[16,96,2048]{2,1,0:T(8,128)(2,1)} %bitcast.611), calls=%async_computation.6 | async-start | bytes 12582912 | tf_op jit(solution)/shard_map/all_to_all | solution.py:281
  193.2 693.4 %all-gather.28.cloned.1.call-start = ((), (), s32[]{:S(2)}) async-start(), calls=%async_computation.27 | async-start | bytes 7864320 | tf_op jit(solution)/shard_map/all_gather | solution.py:122
  514.4 186.2 %all-to-all-start.4 = ((bf16[16,96,2048]{2,1,0:T(8,128)(2,1)}), bf16[16,96,2048]{2,1,0:T(8,128)(2,1)}, u32[]{:S(2)}, u32[]{:S(2)}) async-start(bf16[16,96,2048]{2,1,0:T(8,128)(2,1)} %bitcast.610), calls=%async_computation.4 | async-start | bytes 12582912 | tf_op jit(solution)/shard_map/all_to_all | solution.py:281
  700.7 143.8 %all-to-all-start.2 = ((bf16[16,96,2048]{2,1,0:T(8,128)(2,1)}), bf16[16,96,2048]{2,1,0:T(8,128)(2,1)}, u32[]{:S(2)}, u32[]{:S(2)}) async-start(bf16[16,96,2048]{2,1,0:T(8,128)(2,1)} %bitcast.607), calls=%async_computation.2 | async-start | bytes 12582912 | tf_op jit(solution)/shard_map/all_to_all | solution.py:209
  844.5 143.7 %all-to-all-start = ((bf16[16,96,2048]{2,1,0:T(8,128)(2,1)}), bf16[16,96,2048]{2,1,0:T(8,128)(2,1)}, u32[]{:S(2)}, u32[]{:S(2)}) async-start(bf16[16,96,2048]{2,1,0:T(8,128)(2,1)} %bitcast.608), calls=%async_computation | async-start | bytes 12582912 | tf_op jit(solution)/shard_map/all_to_all | solution.py:209
  988.2 143.7 %all-to-all-start.7 = ((bf16[2,768,2048]{2,0,1:T(2,128)(2,1)}), bf16[2,768,2048]{2,0,1:T(2,128)(2,1)}, u32[]{:S(2)}, u32[]{:S(2)}) async-start(bf16[2,768,2048]{2,0,1:T(2,128)(2,1)} %copy.333), calls=%async_computation.7 | async-start | bytes 12582912 | tf_op jit(solution)/shard_map/all_to_all | solution.py:306
  1131.9 143.7 %all-to-all-start.5 = ((bf16[2,768,2048]{2,0,1:T(2,128)(2,1)}), bf16[2,768,2048]{2,0,1:T(2,128)(2,1)}, u32[]{:S(2)}, u32[]{:S(2)}) async-start(bf16[2,768,2048]{2,0,1:T(2,128)(2,1)} %copy.319), calls=%async_computation.5 | async-start | bytes 12582912 | tf_op jit(solution)/shard_map/all_to_all | solution.py:306
  1275.6 143.8 %all-to-all-start.3 = ((bf16[2,768,2048]{2,0,1:T(2,128)(2,1)}), bf16[2,768,2048]{2,0,1:T(2,128)(2,1)}, u32[]{:S(2)}, u32[]{:S(2)}) async-start(bf16[2,768,2048]{2,0,1:T(2,128)(2,1)} %copy.315), calls=%async_computation.3 | async-start | bytes 12582912 | tf_op jit(solution)/shard_map/all_to_all | solution.py:216
  1419.4 143.7 %all-to-all-start.1 = ((bf16[2,768,2048]{2,0,1:T(2,128)(2,1)}), bf16[2,768,2048]{2,0,1:T(2,128)(2,1)}, u32[]{:S(2)}, u32[]{:S(2)}) async-start(bf16[2,768,2048]{2,0,1:T(2,128)(2,1)} %copy.304), calls=%async_computation.1 | async-start | bytes 12582912 | tf_op jit(solution)/shard_map/all_to_all | solution.py:216
  1427.7 607.8 %reduce-scatter.34.cloned.1.call-start = ((), (), s32[]{:S(2)}) async-start(), calls=%async_computation.37 | async-start | bytes 1769472
  1809.6 227.2 %reduce-scatter.38.cloned.1.call-start = ((), (), s32[]{:S(2)}) async-start(), calls=%async_computation.39 | async-start | bytes 1769472
  1975.1 238.7 %reduce-scatter.28.cloned.1.call-start = ((), (), s32[]{:S(2)}) async-start(), calls=%async_computation.34 | async-start | bytes 7864320 | tf_op jit(solution)/shard_map/reduce_scatter | solution.py:403
  1996.3 225.4 %reduce-scatter.30.cloned.1.call-start = ((), (), s32[]{:S(2)}) async-start(), calls=%async_computation.35 | async-start | bytes 7864320 | tf_op jit(solution)/shard_map/reduce_scatter | solution.py:406
  2017.5 277.3 %reduce-scatter.32.cloned.1.call-start = ((), (), s32[]{:S(2)}) async-start(), calls=%async_computation.36 | async-start | bytes 7864320 | tf_op jit(solution)/shard_map/reduce_scatter | solution.py:409
  2035.4 399.5 %reduce-scatter.22.cloned.1.call-start = ((), (), s32[]{:S(2)}) async-start(), calls=%async_computation.31 | async-start | bytes 4325376 | tf_op jit(solution)/shard_map/reduce_scatter | solution.py:397
  2045.8 531.6 %reduce-scatter.24.cloned.1.call-start = ((), (), s32[]{:S(2)}) async-start(), calls=%async_computation.32 | async-start | bytes 4325376 | tf_op jit(solution)/shard_map/reduce_scatter | solution.py:398
  2078.7 860.1 %reduce-scatter.20.cloned.1.call-start = ((), (), s32[]{:S(2)}) async-start(), calls=%async_computation.30 | async-start | bytes 34603008 | tf_op jit(solution)/shard_map/reduce_scatter | solution.py:396
  2141.5 1157.8 %reduce-scatter.26.cloned.1.call-start = ((), (), s32[]{:S(2)}) async-start(), calls=%async_computation.33 | async-start | bytes 34603008 | tf_op jit(solution)/shard_map/reduce_scatter | solution.py:399
  (171 other events, 4133.7 us)
Sparse Core Ops, SparseCore 0:
  11.0 56.7 all-gather.13
  70.8 55.3 all-gather.17
  128.4 24.7 all-gather.15
  155.2 24.5 all-gather.19
  181.9 45.2 all-gather.29
  228.7 42.9 all-gather.31
  274.5 186.7 all-gather.11
  464.3 162.6 all-gather.21
  628.8 81.5 all-gather.23
  712.1 70.1 all-gather.25
  784.2 70.0 all-gather.27
  1809.8 32.5 reduce-scatter.33
  1971.8 32.5 reduce-scatter.37
  2006.6 32.3 reduce-scatter.35
  2041.1 32.4 reduce-scatter.39
  2076.4 72.1 reduce-scatter.27
  2151.5 70.2 reduce-scatter.29
  2224.5 70.1 reduce-scatter.31
  2297.6 137.2 reduce-scatter.21
  2437.6 139.7 reduce-scatter.23
  2580.3 358.3 reduce-scatter.19
  2941.6 357.6 reduce-scatter.25
where the time goes:
time: 3320 us; the launch traced here: 3310 us
  waiting for transfers between devices  1920 us (58%)
  matrix products  619 us (19%)
  local copies, waits for them, and re-layouts  357 us (11%)
  other arithmetic  250 us (8%)
  blocking collectives  80.4 us (2%)
  starting transfers between devices  63.7 us (2%)
    reduce_scatter x1, waiting for transfers between devices, body(): lax.psum_scatter(acc_query, ('dp', 'expert'), scatter_dimension=1, tiled=...  361 us
    reduce_scatter x1, waiting for transfers between devices, body(): lax.psum_scatter(acc_output, ('dp', 'expert'), scatter_dimension=0, tiled...  361 us
    all_to_all x2, waiting for transfers between devices, body(): lax.all_to_all(result, 'expert', split_axis=1, concat_axis=0, tiled=True)  213 us
    all_gather x1, waiting for transfers between devices, fetch_dense(): lax.all_gather(w_query, ('dp', 'expert'), axis=1, tiled=True)  183 us
    all_to_all x2, waiting for transfers between devices, body(): lax.all_to_all(d_input_rows.astype(jnp.bfloat16), 'expert', split_axis=1,...  164 us
    reduce_scatter x1, waiting for transfers between devices, body(): lax.psum_scatter(acc_value, ('dp', 'expert'), scatter_dimension=1, tiled=...  143 us
    all_to_all x2, waiting for transfers between devices, body(): lax.all_to_all(sent_rows, 'expert', split_axis=0, concat_axis=1, tiled=True)  122 us
    convert_element_type x8, other arithmetic, backward_head(): d_score = (attn_prob * (d_prob - row_dot)).astype(jnp.bfloat16)  87.5 us
  transfers between devices with their start and end apart: 30, of which 19 were waited for; matrix products, arithmetic and copies ran while one was open for 29% of the time, Pallas kernels for 0%

commit v1 on v0

v1 whole, which is shorter than its diff:
```python
import functools
import math

import jax
import jax.numpy as jnp
from jax import lax
from jax.experimental import pallas as pl
from jax.experimental.pallas import tpu as pltpu
from jax.sharding import PartitionSpec as P

H = 32
KVH = 4
HD = 128
FF = 768
TOPK = 8
PROMPT = 1024
PER_KV = H // KVH

EPSILON = 1e-06
ROPE_BASE = 1000000.0
MASKED = -1e30
LOG2E = math.log2(math.e)
SCALE = HD ** (-0.5)

bf16 = jnp.bfloat16
f32 = jnp.float32
NT = (((1,), (1,)), ((), ()))
TN = (((0,), (0,)), ((), ()))
NN = (((1,), (0,)), ((), ()))
BOTH = ("dp", "expert")
VMEM_LIMIT = 56 * 1024 * 1024


def mm(a, b, dims=NN):
    return lax.dot_general(a, b, dims, preferred_element_type=f32)


def rms_scale(values):
    return lax.rsqrt(jnp.mean(values * values, axis=-1, keepdims=True) + EPSILON)


def norm_back(upstream, values, inv_rms, norm_gain):
    lifted = upstream * norm_gain
    inner_dot = jnp.mean(lifted * values, axis=-1, keepdims=True)
    back_grad = inv_rms * lifted - values * (inv_rms * inv_rms * inv_rms) * inner_dot
    gain_grad = jnp.sum((upstream * values * inv_rms).reshape(-1, values.shape[-1]), axis=0)
    return (back_grad, gain_grad)


def rotate(values, cosine, sine_part):
    half_dim = values.shape[-1] // 2
    first_half = values[..., :half_dim]
    second_half = values[..., half_dim:]
    return jnp.concatenate(
        [
            first_half * cosine - second_half * sine_part,
            second_half * cosine + first_half * sine_part,
        ],
        axis=-1,
    )


def attend_forward(step_heads, chunk, q_ref, kv_ref, bias_ref, o_ref, log_ref):
    group_len = bias_ref.shape[1]
    keys = kv_ref[:, 0, :, :HD].reshape(group_len, HD)
    values_t = kv_ref[:, 0, :, HD:].reshape(group_len, HD).T
    rows = q_ref.shape[1]
    for step in range(PER_KV // step_heads):
        heads = range(step * step_heads, (step + 1) * step_heads)
        query = jnp.concatenate([q_ref[0, :, h * HD : (h + 1) * HD] for h in heads], axis=0)
        mixed, row_sum = 0.0, 0.0
        for at in range(0, group_len, chunk):
            scores = mm(keys[at : at + chunk], query, NT)
            prob = jnp.exp2(scores + bias_ref[0, at : at + chunk, :])
            row_sum += jnp.sum(prob, axis=0, keepdims=True)
            mixed += mm(values_t[:, at : at + chunk], prob.astype(bf16))
        out = (mixed / row_sum).T.astype(bf16)
        for i, h in enumerate(heads):
            o_ref[0, :, h * HD : (h + 1) * HD] = out[i * rows : (i + 1) * rows]
        log_ref[0, 0, step : step + 1, :] = jnp.log2(row_sum)


def attend_backward(
    step_heads, chunk, q_ref, kv_ref, bias_ref, o_ref, do_ref, log_ref, dq_ref, dkv_ref, dk_acc, dv_acc
):
    group_len = bias_ref.shape[1]
    keys = kv_ref[:, 0, :, :HD].reshape(group_len, HD)
    values = kv_ref[:, 0, :, HD:].reshape(group_len, HD)
    keys_t = keys.T
    rows = q_ref.shape[1]
    dk_acc[...] = jnp.zeros_like(dk_acc)
    dv_acc[...] = jnp.zeros_like(dv_acc)
    for step in range(PER_KV // step_heads):
        heads = range(step * step_heads, (step + 1) * step_heads)
        query = jnp.concatenate([q_ref[0, :, h * HD : (h + 1) * HD] for h in heads], axis=0)
        grad = jnp.concatenate([do_ref[0, :, h * HD : (h + 1) * HD] for h in heads], axis=0)
        mixed = jnp.concatenate([o_ref[0, :, h * HD : (h + 1) * HD] for h in heads], axis=0)
        row_dot = jnp.sum((grad.astype(f32) * mixed.astype(f32)).T, axis=0, keepdims=True)
        log_sum = log_ref[0, 0, step : step + 1, :]
        dq_t = 0.0
        for at in range(0, group_len, chunk):
            part = slice(at, at + chunk)
            scores = mm(keys[part], query, NT)
            prob = jnp.exp2(scores + (bias_ref[0, part, :] - log_sum))
            d_prob = mm(values[part], grad, NT)
            d_score = (prob * (d_prob - row_dot)).astype(bf16)
            dv_acc[part] += mm(prob.astype(bf16), grad)
            dk_acc[part] += mm(d_score, query)
            dq_t += mm(keys_t[:, part], d_score)
        out = (dq_t * SCALE).T.astype(bf16)
        for i, h in enumerate(heads):
            dq_ref[0, :, h * HD : (h + 1) * HD] = out[i * rows : (i + 1) * rows]
    blocks = dkv_ref.shape[0]
    dkv_ref[:, 0, :, :HD] = (dk_acc[...] * (1.0 / LOG2E)).astype(bf16).reshape(blocks, rows, HD)
    dkv_ref[:, 0, :, HD:] = dv_acc[...].astype(bf16).reshape(blocks, rows, HD)


def attention_specs(micro, rows, group_len, blocks, step_heads):
    wide = PER_KV * HD
    q_spec = pl.BlockSpec((1, rows, wide), lambda b, g: (b, 0, g))
    kv_spec = pl.BlockSpec((blocks, 1, rows, 2 * HD), lambda b, g: (0, b, 0, g))
    bias_spec = pl.BlockSpec((1, group_len, step_heads * rows), lambda b, g: (b, 0, 0))
    log_spec = pl.BlockSpec((1, 1, PER_KV // step_heads, step_heads * rows), lambda b, g: (b, g, 0, 0))
    return q_spec, kv_spec, bias_spec, log_spec


def run_forward(query, kv_all, bias, step_heads, chunk):
    micro, rows, _ = query.shape
    blocks = kv_all.shape[0]
    group_len = bias.shape[1]
    q_spec, kv_spec, bias_spec, log_spec = attention_specs(micro, rows, group_len, blocks, step_heads)
    flops = 4 * micro * rows * H * HD * group_len
    return pl.pallas_call(
        functools.partial(attend_forward, step_heads, chunk),
        grid=(micro, KVH),
        in_specs=[q_spec, kv_spec, bias_spec],
        out_specs=[q_spec, log_spec],
        out_shape=[
            jax.ShapeDtypeStruct(query.shape, bf16),
            jax.ShapeDtypeStruct((micro, KVH, PER_KV // step_heads, step_heads * rows), f32),
        ],
        compiler_params=pltpu.CompilerParams(vmem_limit_bytes=VMEM_LIMIT),
        cost_estimate=pl.CostEstimate(
            flops=flops, bytes_accessed=20_000_000, transcendentals=flops // (4 * HD)
        ),
    )(query, kv_all, bias)


def run_backward(query, kv_all, bias, mixed, grad, logs, step_heads, chunk):
    micro, rows, _ = query.shape
    blocks = kv_all.shape[0]
    group_len = bias.shape[1]
    q_spec, kv_spec, bias_spec, log_spec = attention_specs(micro, rows, group_len, blocks, step_heads)
    flops = 10 * micro * rows * H * HD * group_len
    return pl.pallas_call(
        functools.partial(attend_backward, step_heads, chunk),
        grid=(micro, KVH),
        in_specs=[q_spec, kv_spec, bias_spec, q_spec, q_spec, log_spec],
        out_specs=[q_spec, kv_spec],
        out_shape=[
            jax.ShapeDtypeStruct(query.shape, bf16),
            jax.ShapeDtypeStruct(kv_all.shape, bf16),
        ],
        scratch_shapes=[pltpu.VMEM((group_len, HD), f32), pltpu.VMEM((group_len, HD), f32)],
        compiler_params=pltpu.CompilerParams(vmem_limit_bytes=VMEM_LIMIT),
        cost_estimate=pl.CostEstimate(
            flops=flops, bytes_accessed=30_000_000, transcendentals=flops // (10 * HD)
        ),
    )(query, kv_all, bias, mixed, grad, logs)


def slots_of(route_ids, gate_vals, ranking, capacity, experts):
    rows = route_ids.shape[0]
    pair_experts = route_ids.reshape(-1)
    earlier = (pair_experts[None, :] == pair_experts[:, None]) & (
        ranking[None, :] < ranking[:, None]
    )
    slot = jnp.sum(earlier.astype(jnp.int32), axis=1).reshape(rows, -1)
    kept = slot < capacity
    chosen = route_ids[:, :, None] == jnp.arange(experts, dtype=jnp.int32)[None, None, :]
    chosen = chosen & kept[:, :, None]
    slot_map = jnp.sum(jnp.where(chosen, slot[:, :, None] + 1, 0), axis=1).astype(f32) - 1.0
    weight_map = jnp.sum(jnp.where(chosen, gate_vals[:, :, None], 0.0), axis=1)
    return slot_map, weight_map


def body(
    inputs,
    cotangent,
    membership,
    routes,
    gate_weights,
    pair_order,
    w_query,
    w_key,
    w_value,
    w_output,
    norm_gains,
    w_gate,
    w_up,
    w_down,
):
    micro = inputs.shape[0]
    rows = inputs.shape[2]
    width = inputs.shape[3]
    group_len = membership.shape[2]
    member = lax.axis_index("expert")
    blocks = lax.axis_size("expert")
    shards = blocks * lax.axis_size("dp")
    shard_at = lax.axis_index("dp") * blocks + member
    local_experts = w_gate.shape[0]
    experts = local_experts * blocks
    capacity = rows * TOPK // experts
    step_heads = max(1, 384 // rows)
    total = micro * rows
    q_part, k_part, v_part = w_query.shape[1], w_key.shape[1], w_value.shape[1]

    gain_len = norm_gains.shape[0]
    gain_shard = jnp.zeros((2048,), bf16).at[:gain_len].set(norm_gains).reshape(16, 128)
    gain_full = lax.all_gather(gain_shard, BOTH, axis=0, tiled=True)
    gains = gain_full.reshape(shards, 2048)[:, :gain_len].reshape(-1).astype(f32)
    gain_in = gains[:width]
    gain_mid = gains[width : 2 * width]
    gain_q = gains[2 * width : 2 * width + HD]
    gain_k = gains[2 * width + HD :]

    qkv_w = lax.all_gather(
        jnp.concatenate([w_query.T, w_key.T, w_value.T], axis=0), BOTH, axis=0, tiled=True
    )
    out_w = lax.all_gather(w_output, BOTH, axis=0, tiled=True)
    wg = lax.all_gather(w_gate, "dp", axis=1, tiled=True)
    wu = lax.all_gather(w_up, "dp", axis=1, tiled=True)
    wd = lax.all_gather(w_down, "dp", axis=2, tiled=True)

    slot_map, weight_map = jax.vmap(
        lambda r, g, o: slots_of(r, g, o, capacity, experts)
    )(routes[:, 0], gate_weights[:, 0], pair_order[:, 0, 0])
    routing = jnp.concatenate([slot_map, weight_map], axis=-1)
    routing = lax.all_gather(routing, "expert", axis=0, tiled=False)
    mine = member * local_experts
    slot_mine = lax.dynamic_slice_in_dim(routing, mine, local_experts, axis=3)
    weight_mine = lax.dynamic_slice_in_dim(routing, experts + mine, local_experts, axis=3)
    slot_mine = jnp.transpose(slot_mine, (1, 3, 0, 2))
    weight_mine = jnp.transpose(weight_mine, (1, 3, 0, 2))
    slot_ids = jnp.arange(capacity, dtype=f32)
    hit = slot_mine[:, :, :, None, :] == slot_ids[None, None, None, :, None]
    pick = hit.astype(bf16)
    weighted = jnp.where(hit, weight_mine[:, :, :, None, :], 0.0)
    slot_weight = jnp.sum(weighted, axis=-1)
    weighted = weighted.astype(bf16)

    key_index = jnp.arange(group_len, dtype=jnp.int32)
    start_row = member * rows
    segment = membership[:, 0]
    row_index = start_row + jnp.arange(rows, dtype=jnp.int32)
    seg_rows = lax.dynamic_slice_in_dim(segment, start_row, rows, axis=1)
    before = jnp.sum((segment[:, None, :] < seg_rows[:, :, None]).astype(jnp.int32), axis=2)
    position = jnp.where(seg_rows == 0, row_index[None], PROMPT + row_index[None] - before)
    allowed = (key_index[None, :, None] <= row_index[None, None, :]) & (
        (segment[:, :, None] == 0) | (segment[:, :, None] == seg_rows[:, None, :])
    )
    bias = jnp.tile(jnp.where(allowed, 0.0, MASKED).astype(f32), (1, 1, step_heads))
    frequency = ROPE_BASE ** (-(jnp.arange(HD // 2, dtype=f32) * 2.0 / HD))
    angles = position.astype(f32).reshape(total)[:, None] * frequency[None, :]
    cosine = jnp.cos(angles)[:, None, :]
    sine_part = jnp.sin(angles)[:, None, :]

    hidden = inputs[:, 0].astype(f32).reshape(total, width)
    scale_in = rms_scale(hidden)
    normed = (hidden * scale_in * gain_in).astype(bf16)
    proj = mm(normed, qkv_w, NT).reshape(total, shards, q_part + k_part + v_part)
    queries = proj[:, :, :q_part].reshape(total, H, HD)
    key_pre = proj[:, :, q_part : q_part + k_part].reshape(total, KVH, HD)
    value = proj[:, :, q_part + k_part :].reshape(total, KVH, HD).astype(bf16)
    scale_q = rms_scale(queries)
    scale_k = rms_scale(key_pre)
    q_low = rotate(queries * scale_q * (gain_q * (SCALE * LOG2E)), cosine, sine_part).astype(bf16)
    q_low = q_low.reshape(micro, rows, H * HD)
    k_low = rotate(key_pre * scale_k * gain_k, cosine, sine_part).astype(bf16)
    kv_own = jnp.concatenate([k_low, value], axis=-1).reshape(micro, rows, KVH * 2 * HD)
    kv_all = lax.all_gather(kv_own, "expert", axis=0, tiled=False)
    chunk = 256
    mixed, logs = run_forward(q_low, kv_all, bias, step_heads, chunk)

    branch = mm(mixed.reshape(total, H * HD), out_w)
    middle = hidden + branch
    scale_mid = rms_scale(middle)
    routed = (middle * scale_mid * gain_mid).astype(bf16).reshape(micro, rows, width)
    middle = middle.reshape(micro, rows, width)
    scale_mid = scale_mid.reshape(micro, rows, 1)

    outputs, d_branches, d_middles = [], [], []
    acc_gate = acc_up = acc_down = 0.0
    grad_mid = 0.0
    slots = blocks * capacity
    for at in range(micro):
        d_out = lax.all_gather(cotangent[at, 0], "expert", axis=0, tiled=False)
        tokens = lax.all_gather(routed[at], "expert", axis=0, tiled=False)
        picked = jnp.einsum("ebst,btd->ebsd", pick[at], tokens, preferred_element_type=f32)
        picked = picked.astype(bf16).reshape(local_experts, slots, width)
        d_result = jnp.einsum("ebst,btd->ebsd", pick[at], d_out, preferred_element_type=f32)
        d_result = (d_result * slot_weight[at][..., None]).astype(bf16)
        d_result = d_result.reshape(local_experts, slots, width)
        gate_pre = jnp.einsum("erd,edf->erf", picked, wg, preferred_element_type=f32)
        up_pre = jnp.einsum("erd,edf->erf", picked, wu, preferred_element_type=f32)
        d_hidden = jnp.einsum("erd,efd->erf", d_result, wd, preferred_element_type=f32)
        sigmoid_g = jax.nn.sigmoid(gate_pre)
        silu_g = gate_pre * sigmoid_g
        hidden_low = (silu_g * up_pre).astype(bf16)
        d_gate = (d_hidden * up_pre * sigmoid_g * (1.0 + gate_pre * (1.0 - sigmoid_g))).astype(bf16)
        d_up = (d_hidden * silu_g).astype(bf16)
        d_rows = jnp.einsum("erf,edf->erd", d_gate, wg, preferred_element_type=f32)
        d_rows = d_rows + jnp.einsum("erf,edf->erd", d_up, wu, preferred_element_type=f32)
        d_rows = d_rows.astype(bf16).reshape(local_experts, blocks, capacity, width)
        d_part = jnp.einsum("ebst,ebsd->btd", pick[at], d_rows, preferred_element_type=f32)
        d_part = d_part.astype(bf16).reshape(group_len, width)
        d_routed = lax.psum_scatter(d_part, "expert", scatter_dimension=0, tiled=True).astype(f32)
        result = jnp.einsum("erf,efd->erd", hidden_low, wd, preferred_element_type=f32)
        result = result.astype(bf16).reshape(local_experts, blocks, capacity, width)
        part = jnp.einsum("ebst,ebsd->btd", weighted[at], result, preferred_element_type=f32)
        part = part.astype(bf16).reshape(group_len, width)
        expert_mix = lax.psum_scatter(part, "expert", scatter_dimension=0, tiled=True).astype(f32)
        outputs.append((middle[at] + expert_mix).astype(bf16))

        acc_down += jnp.einsum("erf,erd->efd", hidden_low, d_result, preferred_element_type=f32)
        acc_gate += jnp.einsum("erd,erf->edf", picked, d_gate, preferred_element_type=f32)
        acc_up += jnp.einsum("erd,erf->edf", picked, d_up, preferred_element_type=f32)

        d_mid_norm, mid_gain_grad = norm_back(d_routed, middle[at], scale_mid[at], gain_mid)
        grad_mid = grad_mid + mid_gain_grad
        d_middle = cotangent[at, 0].astype(f32) + d_mid_norm
        d_middles.append(d_middle)
        d_branches.append(d_middle.astype(bf16))

    grad_gate = lax.psum_scatter(acc_gate.astype(bf16), "dp", scatter_dimension=1, tiled=True)
    grad_up = lax.psum_scatter(acc_up.astype(bf16), "dp", scatter_dimension=1, tiled=True)
    grad_down = lax.psum_scatter(acc_down.astype(bf16), "dp", scatter_dimension=2, tiled=True)

    d_branch = jnp.concatenate(d_branches, axis=0)
    d_middle = jnp.concatenate(d_middles, axis=0)
    grad_output = mm(mixed.reshape(total, H * HD), d_branch, TN).astype(bf16)
    grad_output = lax.psum_scatter(grad_output, BOTH, scatter_dimension=0, tiled=True)
    d_mixed = mm(d_branch, out_w, NT).astype(bf16).reshape(micro, rows, H * HD)
    dq_low, dkv_all = run_backward(q_low, kv_all, bias, mixed, d_mixed, logs, step_heads, chunk)
    dkv = lax.psum_scatter(dkv_all, "expert", scatter_dimension=0, tiled=False)
    dkv = dkv.reshape(total, KVH, 2 * HD)
    d_query = rotate(dq_low.reshape(total, H, HD).astype(f32), cosine, -sine_part)
    d_query, grad_qn = norm_back(d_query, queries, scale_q, gain_q)
    d_key = rotate(dkv[:, :, :HD].astype(f32), cosine, -sine_part)
    d_key, grad_kn = norm_back(d_key, key_pre, scale_k, gain_k)
    d_proj = jnp.concatenate(
        [
            d_query.astype(bf16).reshape(total, shards, q_part),
            d_key.astype(bf16).reshape(total, shards, k_part),
            dkv[:, :, HD:].reshape(total, shards, v_part),
        ],
        axis=-1,
    ).reshape(total, -1)
    grad_qkv = mm(d_proj, normed, TN).astype(bf16)
    grad_qkv = lax.psum_scatter(grad_qkv, BOTH, scatter_dimension=0, tiled=True).astype(f32)
    d_normed = mm(d_proj, qkv_w)
    d_in_norm, grad_in = norm_back(d_normed, hidden, scale_in, gain_in)
    input_grad = d_middle + d_in_norm

    gain_grads = jnp.concatenate([grad_in, grad_mid, grad_qn, grad_kn]).reshape(shards, gain_len)
    gain_grads = jnp.pad(gain_grads, ((0, 0), (0, 256 - gain_len % 256)))
    gain_all = lax.all_gather(gain_grads, BOTH, axis=0, tiled=False)
    grad_gains = jnp.sum(lax.dynamic_index_in_dim(gain_all, shard_at, axis=1, keepdims=False), axis=0)
    return (
        jnp.stack(outputs)[:, None],
        input_grad.reshape(micro, 1, rows, width),
        grad_qkv[:q_part].T,
        grad_qkv[q_part : q_part + k_part].T,
        grad_qkv[q_part + k_part :].T,
        grad_output.astype(f32),
        grad_gains[:gain_len],
        grad_gate.astype(f32),
        grad_up.astype(f32),
        grad_down.astype(f32),
    )


def solution(mesh):
    return jax.shard_map(
        body,
        mesh=mesh,
        in_specs=(
            P(None, "dp", "expert", None),
            P(None, "dp", "expert", None),
            P(None, "dp", None),
            P(None, "dp", "expert", None),
            P(None, "dp", "expert", None),
            P(None, "dp", "expert", None),
            P(None, ("dp", "expert")),
            P(None, ("dp", "expert")),
            P(None, ("dp", "expert")),
            P(("dp", "expert"), None),
            P(("dp", "expert")),
            P("expert", "dp", None),
            P("expert", "dp", None),
            P("expert", None, "dp"),
        ),
        out_specs=(
            P(None, "dp", "expert", None),
            P(None, "dp", "expert", None),
            P(None, ("dp", "expert")),
            P(None, ("dp", "expert")),
            P(None, ("dp", "expert")),
            P(("dp", "expert"), None),
            P(("dp", "expert")),
            P("expert", "dp", None),
            P("expert", "dp", None),
            P("expert", None, "dp"),
        ),
        check_vma=False,
    )
```

time: 3320 us -> 1980 us (0.60)
  waiting for transfers between devices: 1920 us -> 1300 us
  matrix products: 619 us -> 315 us
  local copies, waits for them, and re-layouts: 357 us -> 97.4 us
  other arithmetic: 250 us -> 75.5 us
  Pallas kernels: 0 us -> 105 us
  starting transfers between devices: 63.7 us -> 1.47 us
    all_to_all x8 -> x0, waiting for transfers between devices: 559 us -> none  [the longest x2 213 us: body(): lax.all_to_all(result, 'expert', split_axis=1, concat_axis=0, tiled=True)]
    reduce_scatter x7 -> x10, waiting for transfers between devices: 1020 us -> 703 us  [the longest x1 228 us: body(): lax.psum_scatter(grad_qkv, BOTH, scatter_dimension=0, tiled=True)]
    dot_general x102 -> x32, matrix products: 619 us -> 315 us  [the longest x6 85.3 us: mm(): return lax.dot_general(a, b, dims, preferred_element_type=f32)]
    all_gather x11, waiting for transfers between devices: 307 us -> 591 us  [the longest x2 114 us: body(): tokens = lax.all_gather(routed[at], 'expert', axis=0, tiled=False)]
    pallas_call x0 -> x2, Pallas kernels: none -> 105 us  [the longest x1 61.6 us: run_backward(): pl.pallas_call(functools.partial(attend_backward, step_heads, chunk), gri...]
    unnamed x2 -> x0, blocking collectives: 80.4 us -> none
    convert_element_type x18 -> x13, other arithmetic: 102 us -> 24.2 us  [the longest x1 4.5 us: body(): d_branches.append(d_middle.astype(bf16))]
    convert_element_type x8 -> x7, local copies, waits for them, and re-layouts: 79.6 us -> 16.5 us  [the longest x2 6.47 us: body(): d_result = (d_result * slot_weight[at][..., None]).astype(bf16)]
  transfers between devices with their start and end apart: 30 -> 21, of which waited for: 19 -> 18; matrix products, arithmetic and copies ran while one was open for 29% -> 22% of each run, Pallas kernels for 0% -> 2%
where the time goes in v1:
time: 1980 us; the launch traced here: 1960 us
  waiting for transfers between devices  1300 us (66%)
  matrix products  315 us (16%)
  Pallas kernels  105 us (5%)
  local copies, waits for them, and re-layouts  97.4 us (5%)
  other arithmetic  75.5 us (4%)
  blocking collectives  54 us (3%)
    reduce_scatter x1, waiting for transfers between devices, body(): lax.psum_scatter(grad_qkv, BOTH, scatter_dimension=0, tiled=True)  228 us
    reduce_scatter x1, waiting for transfers between devices, body(): lax.psum_scatter(grad_output, BOTH, scatter_dimension=0, tiled=True)  181 us
    reduce_scatter x2, waiting for transfers between devices, body(): lax.psum_scatter(part, 'expert', scatter_dimension=0, tiled=True)  139 us
    all_gather x2, waiting for transfers between devices, body(): tokens = lax.all_gather(routed[at], 'expert', axis=0, tiled=False)  114 us
    all_gather x1, waiting for transfers between devices, body(): lax.all_gather(jnp.concatenate([w_query.T, w_key.T, w_value.T], axis=0),...  90.4 us
    dot_general x6, matrix products, mm(): return lax.dot_general(a, b, dims, preferred_element_type=f32)  85.3 us
    all_gather x1, waiting for transfers between devices, body(): out_w = lax.all_gather(w_output, BOTH, axis=0, tiled=True)  74 us
    reduce_scatter x1, waiting for transfers between devices, body(): lax.psum_scatter(acc_down.astype(bf16), 'dp', scatter_dimension=2, tiled=...  69.7 us
  transfers between devices with their start and end apart: 21, of which 18 were waited for; matrix products, arithmetic and copies ran while one was open for 22% of the time, Pallas kernels for 2%

profile of v1, /device:TPU:8, one launch (start us, length us, event | category | flops | bytes accessed | tf_op | source)
XLA Modules:
  0.0 1962.6 jit_solution(13179503972913597766)
XLA Ops:
  11.1 37.9 %all_gather.45 = bf16[512,128]{1,0:T(8,128)(2,1)S(1)} all-gather(bf16[16,128]{1,0:T(8,128)(2,1)S(1)} %pad_bitcast_fusion), channel_id=1, replica_groups=mesh['dp'=4,'expert'=8] {'dp','expert'}, dimensions={0}, use_global_device_ids=true | all-gather | bytes 135168 | tf_op jit(solution)/shard_map/all_gather | solution.py:220
  55.9 90.4 %all-gather.18.cloned.1.call-done = bf16[5120,2048]{1,0:T(8,128)(2,1)} async-done(((bf16[160,2048]{1,0:T(8,128)(2,1)}), bf16[5120,2048]{1,0:T(8,128)(2,1)}) %all-gather.18.cloned.1.call-update) | async-done | bytes 20971536 | tf_op jit(solution)/shard_map/all_gather | solution.py:227
  210.0 26.7 %all-gather.20.cloned.1.call-done.kv_ref = bf16[8,2,192,1024]{3,2,1,0:T(8,128)(2,1)} async-done(((bf16[1,2,192,1024]{3,2,1,0:T(8,128)(2,1)}), bf16[8,2,192,1024]{3,2,1,0:T(8,128)(2,1)}) %all-gather.20.cloned.1.call-update) | async-done | bytes 6291472 | tf_op jit(solution)/shard_map/all_gather | solution.py:281
  236.7 43.8 %shard_map.213 = (bf16[2,192,4096]{2,1,0:T(8,128)(2,1)}, f32[2,4,4,384]{3,2,1,0:T(4,128)}) custom-call(bf16[2,192,4096]{2,1,0:T(8,128)(2,1)} %convert_element_type.218.q_ref, bf16[8,2,192,1024]{3,2,1,0:T(8,128)(2,1)} %all-gather.20.cloned.1.call-done.kv_ref, f32[2,1536,384]{2,1,0:T(8,128)} %copy.201.bias_ref), custom_call_target="tpu_custom_call" | custom-call | flops 9663676416 | bytes 20000000 | tf_op jit(solution)/shard_map/pallas_call | solution.py:133
  280.5 74.0 %all-gather.22.cloned.1.call-done = bf16[4096,2048]{1,0:T(8,128)(2,1)} async-done(((bf16[128,2048]{1,0:T(8,128)(2,1)}), bf16[4096,2048]{1,0:T(8,128)(2,1)}) %all-gather.22.cloned.1.call-update) | async-done | bytes 16777232 | tf_op jit(solution)/shard_map/all_gather | solution.py:230
  394.6 27.3 %all-gather.34.cloned.1.call-done = bf16[8,1,192,2048]{3,2,1,0:T(8,128)(2,1)} async-done(((bf16[1,1,192,2048]{3,2,1,0:T(8,128)(2,1)}), bf16[8,1,192,2048]{3,2,1,0:T(8,128)(2,1)}) %all-gather.34.cloned.1.call-update) | async-done | bytes 6291472 | tf_op jit(solution)/shard_map/all_gather | solution.py:297
  430.1 57.3 %all-gather.30.cloned.1.call-done = bf16[1536,2048]{1,0:T(8,128)(2,1)} async-done(((bf16[192,2048]{1,0:T(8,128)(2,1)}), bf16[1536,2048]{1,0:T(8,128)(2,1)}) %all-gather.30.cloned.1.call-update) | async-done | bytes 6291472 | tf_op jit(solution)/shard_map/all_gather | solution.py:298
  495.2 65.0 %all-gather.24.cloned.1.call-done = bf16[2,2048,768]{2,1,0:T(8,128)(2,1)} async-done(((bf16[2,512,768]{2,1,0:T(8,128)(2,1)}), bf16[2,2048,768]{2,1,0:T(8,128)(2,1)}) %all-gather.24.cloned.1.call-update) | async-done | bytes 6291472 | tf_op jit(solution)/shard_map/all_gather | solution.py:231
  570.5 61.7 %all-gather.26.cloned.1.call-done = bf16[2,2048,768]{2,1,0:T(8,128)(2,1)} async-done(((bf16[2,512,768]{2,1,0:T(8,128)(2,1)}), bf16[2,2048,768]{2,1,0:T(8,128)(2,1)}) %all-gather.26.cloned.1.call-update) | async-done | bytes 6291472 | tf_op jit(solution)/shard_map/all_gather | solution.py:232
  642.7 61.3 %all-gather.28.cloned.1.call-done = bf16[2,768,2048]{2,1,0:T(8,128)(2,1)} async-done(((bf16[2,768,512]{2,1,0:T(8,128)(2,1)}), bf16[2,768,2048]{2,1,0:T(8,128)(2,1)}) %all-gather.28.cloned.1.call-update) | async-done | bytes 6291472 | tf_op jit(solution)/shard_map/all_gather | solution.py:233
  746.5 22.3 %all-gather.36.cloned.1.call-done = bf16[8,1,192,2048]{3,2,1,0:T(8,128)(2,1)} async-done(((bf16[1,1,192,2048]{3,2,1,0:T(8,128)(2,1)}), bf16[8,1,192,2048]{3,2,1,0:T(8,128)(2,1)}) %all-gather.36.cloned.1.call-update) | async-done | bytes 6291472 | tf_op jit(solution)/shard_map/all_gather | solution.py:297
  777.3 57.1 %all-gather.32.cloned.1.call-done = bf16[1536,2048]{1,0:T(8,128)(2,1)} async-done(((bf16[192,2048]{1,0:T(8,128)(2,1)}), bf16[1536,2048]{1,0:T(8,128)(2,1)}) %all-gather.32.cloned.1.call-update) | async-done | bytes 6291472 | tf_op jit(solution)/shard_map/all_gather | solution.py:298
  862.0 16.4 multiply_convert_fusion
  931.7 43.2 %reduce-scatter.17.cloned.1.call-done = bf16[192,2048]{1,0:T(8,128)(2,1)} async-done(((bf16[1536,2048]{1,0:T(8,128)(2,1)}), bf16[192,2048]{1,0:T(8,128)(2,1)}) %reduce-scatter.17.cloned.1.call-update) | async-done | bytes 786448 | tf_op jit(solution)/shard_map/reduce_scatter | solution.py:317
  977.2 68.2 %reduce-scatter.13.cloned.1.call-done = bf16[192,2048]{1,0:T(8,128)(2,1)} async-done(((bf16[1536,2048]{1,0:T(8,128)(2,1)}), bf16[192,2048]{1,0:T(8,128)(2,1)}) %reduce-scatter.13.cloned.1.call-update) | async-done | bytes 786448 | tf_op jit(solution)/shard_map/reduce_scatter | solution.py:322
  1045.4 70.3 %reduce-scatter.11.cloned.1.call-done = bf16[192,2048]{1,0:T(8,128)(2,1)} async-done(((bf16[1536,2048]{1,0:T(8,128)(2,1)}), bf16[192,2048]{1,0:T(8,128)(2,1)}) %reduce-scatter.11.cloned.1.call-update) | async-done | bytes 786448 | tf_op jit(solution)/shard_map/reduce_scatter | solution.py:322
  1132.3 61.6 %shard_map.214 = (bf16[2,192,4096]{2,1,0:T(8,128)(2,1)}, bf16[8,2,192,1024]{3,2,1,0:T(8,128)(2,1)}) custom-call(bf16[2,192,4096]{2,1,0:T(8,128)(2,1)} %convert_element_type.218.q_ref, bf16[8,2,192,1024]{3,2,1,0:T(8,128)(2,1)} %all-gather.20.cloned.1.call-done.kv_ref, f32[2,1536,384]{2,1,0:T(8,128)} %copy.201.bias_ref, ...), custom_call_target="tpu_custom_call" | custom-call | flops 24159191040 | bytes 30000000 | tf_op jit(solution)/shard_map/pallas_call | solution.py:155
  1312.9 16.6 fusion.35
  1346.3 16.5 convolution_convert_fusion
  1366.8 42.9 %reduce-scatter.27.cloned.1.call-done = bf16[2,512,768]{2,1,0:T(8,128)(2,1)} async-done(((bf16[2,2048,768]{2,1,0:T(8,128)(2,1)}), bf16[2,512,768]{2,1,0:T(8,128)(2,1)}) %reduce-scatter.27.cloned.1.call-update) | async-done | bytes 1572880 | tf_op jit(solution)/shard_map/reduce_scatter | solution.py:336
  1413.0 69.7 %reduce-scatter.29.cloned.1.call-done = bf16[2,768,512]{2,1,0:T(8,128)(2,1)} async-done(((bf16[2,768,2048]{2,1,0:T(8,128)(2,1)}), bf16[2,768,512]{2,1,0:T(8,128)(2,1)}) %reduce-scatter.29.cloned.1.call-update) | async-done | bytes 1572880 | tf_op jit(solution)/shard_map/reduce_scatter | solution.py:337
  1491.6 47.7 %all-gather.38.cloned.1.call-done = f32[1024,256]{1,0:T(8,128)} async-done(((f32[32,256]{1,0:T(8,128)}), f32[1024,256]{1,0:T(8,128)}) %all-gather.38.cloned.1.call-update) | async-done | bytes 1048592 | tf_op jit(solution)/shard_map/all_gather | solution.py:367
  1540.9 180.7 %reduce-scatter.23.cloned.1.call-done = bf16[128,2048]{1,0:T(8,128)(2,1)} async-done(((bf16[4096,2048]{1,0:T(8,128)(2,1)}), bf16[128,2048]{1,0:T(8,128)(2,1)}) %reduce-scatter.23.cloned.1.call-update) | async-done | bytes 524304 | tf_op jit(solution)/shard_map/reduce_scatter | solution.py:342
  1723.7 228.2 %reduce-scatter.21.cloned.1.call-done = bf16[160,2048]{1,0:T(8,128)(2,1)} async-done(((bf16[5120,2048]{1,0:T(8,128)(2,1)}), bf16[160,2048]{1,0:T(8,128)(2,1)}) %reduce-scatter.21.cloned.1.call-update) | async-done | bytes 655376 | tf_op jit(solution)/shard_map/reduce_scatter | solution.py:360
  (350 shorter events, 459.5 us)
Async XLA Ops:
  7.2 139.2 %all-gather.18.cloned.1.call-start = ((), (), s32[]{:S(2)}) async-start(), calls=%async_computation.10 | async-start | bytes 21626880 | tf_op jit(solution)/shard_map/all_gather | solution.py:227
  10.4 226.3 %all-gather.20.cloned.1.call-start = ((), (), s32[]{:S(2)}) async-start(), calls=%async_computation.11 | async-start | bytes 7077888 | tf_op jit(solution)/shard_map/all_gather | solution.py:281
  53.6 107.2 %copy-start.16 = (f32[384,64]{0,1:T(8,128)}, f32[384,64]{0,1:T(8,128)S(1)}, u32[]{:S(2)}) copy-start(f32[384,64]{0,1:T(8,128)S(1)} %get-tuple-element.143) | copy-start | bytes 294916
  54.5 112.0 %copy-start.14 = (f32[384,64]{1,0:T(8,128)}, f32[384,64]{1,0:T(8,128)S(1)}, u32[]{:S(2)}) copy-start(f32[384,64]{1,0:T(8,128)S(1)} %copy.196) | copy-start | bytes 294916
  55.5 310.3 %copy-start.37 = (f32[2048]{0:T(1024)}, f32[2048]{0:T(1024)S(1)}, u32[]{:S(2)}) copy-start(f32[2048]{0:T(1024)S(1)} %get-tuple-element.135) | copy-start | bytes 24580
  174.3 180.2 %all-gather.22.cloned.1.call-start = ((), (), s32[]{:S(2)}) async-start(), calls=%async_computation.12 | async-start | bytes 17301504 | tf_op jit(solution)/shard_map/all_gather | solution.py:230
  175.0 246.9 %all-gather.34.cloned.1.call-start = ((), (), s32[]{:S(2)}) async-start(), calls=%async_computation.28 | async-start | bytes 7077888 | tf_op jit(solution)/shard_map/all_gather | solution.py:297
  177.8 309.6 %all-gather.30.cloned.1.call-start = ((), (), s32[]{:S(2)}) async-start(), calls=%async_computation.26 | async-start | bytes 7077888 | tf_op jit(solution)/shard_map/all_gather | solution.py:298
  369.1 191.1 %all-gather.24.cloned.1.call-start = ((), (), s32[]{:S(2)}) async-start(), calls=%async_computation.13 | async-start | bytes 7864320 | tf_op jit(solution)/shard_map/all_gather | solution.py:231
  369.6 262.6 %all-gather.26.cloned.1.call-start = ((), (), s32[]{:S(2)}) async-start(), calls=%async_computation.14 | async-start | bytes 7864320 | tf_op jit(solution)/shard_map/all_gather | solution.py:232
  370.4 333.7 %all-gather.28.cloned.1.call-start = ((), (), s32[]{:S(2)}) async-start(), calls=%async_computation.15 | async-start | bytes 7864320 | tf_op jit(solution)/shard_map/all_gather | solution.py:233
  371.1 397.7 %all-gather.36.cloned.1.call-start = ((), (), s32[]{:S(2)}) async-start(), calls=%async_computation.29 | async-start | bytes 7077888 | tf_op jit(solution)/shard_map/all_gather | solution.py:297
  371.9 462.5 %all-gather.32.cloned.1.call-start = ((), (), s32[]{:S(2)}) async-start(), calls=%async_computation.27 | async-start | bytes 7077888 | tf_op jit(solution)/shard_map/all_gather | solution.py:298
  372.7 559.1 %reduce-scatter.15.cloned.1.call-start = ((), (), s32[]{:S(2)}) async-start(), calls=%async_computation.18 | async-start | bytes 7077888 | tf_op jit(solution)/shard_map/reduce_scatter | solution.py:317
  746.5 228.4 %reduce-scatter.17.cloned.1.call-start = ((), (), s32[]{:S(2)}) async-start(), calls=%async_computation.19 | async-start | bytes 7077888 | tf_op jit(solution)/shard_map/reduce_scatter | solution.py:317
  904.5 140.9 %reduce-scatter.13.cloned.1.call-start = ((), (), s32[]{:S(2)}) async-start(), calls=%async_computation.17 | async-start | bytes 7077888 | tf_op jit(solution)/shard_map/reduce_scatter | solution.py:322
  918.4 197.3 %reduce-scatter.11.cloned.1.call-start = ((), (), s32[]{:S(2)}) async-start(), calls=%async_computation.16 | async-start | bytes 7077888 | tf_op jit(solution)/shard_map/reduce_scatter | solution.py:322
  931.0 370.7 %reduce-scatter.19.cloned.1.call-start = ((), (), s32[]{:S(2)}) async-start(), calls=%async_computation.20 | async-start | bytes 7077888 | tf_op jit(solution)/shard_map/reduce_scatter | solution.py:345
  1193.9 169.5 %reduce-scatter.25.cloned.1.call-start = ((), (), s32[]{:S(2)}) async-start(), calls=%async_computation.23 | async-start | bytes 7864320 | tf_op jit(solution)/shard_map/reduce_scatter | solution.py:335
  1215.6 194.0 %reduce-scatter.27.cloned.1.call-start = ((), (), s32[]{:S(2)}) async-start(), calls=%async_computation.24 | async-start | bytes 7864320 | tf_op jit(solution)/shard_map/reduce_scatter | solution.py:336
  1235.3 247.4 %reduce-scatter.29.cloned.1.call-start = ((), (), s32[]{:S(2)}) async-start(), calls=%async_computation.25 | async-start | bytes 7864320 | tf_op jit(solution)/shard_map/reduce_scatter | solution.py:337
  1253.4 286.0 %all-gather.38.cloned.1.call-start = ((), (), s32[]{:S(2)}) async-start(), calls=%async_computation.30 | async-start | bytes 1081344 | tf_op jit(solution)/shard_map/all_gather | solution.py:367
  1330.3 391.3 %reduce-scatter.23.cloned.1.call-start = ((), (), s32[]{:S(2)}) async-start(), calls=%async_computation.22 | async-start | bytes 17301504 | tf_op jit(solution)/shard_map/reduce_scatter | solution.py:342
  1344.9 607.0 %reduce-scatter.21.cloned.1.call-start = ((), (), s32[]{:S(2)}) async-start(), calls=%async_computation.21 | async-start | bytes 21626880 | tf_op jit(solution)/shard_map/reduce_scatter | solution.py:360
  (68 other events, 960.2 us)
Sparse Core Ops, SparseCore 0:
  11.4 134.8 all-gather.17
  174.4 62.2 all-gather.19
  239.7 114.6 all-gather.21
  355.9 65.9 all-gather.33
  424.0 63.3 all-gather.29
  489.1 71.0 all-gather.23
  562.0 70.1 all-gather.25
  634.0 70.0 all-gather.27
  706.3 62.5 all-gather.35
  770.9 63.3 all-gather.31
  836.7 67.8 reduce-scatter.14
  906.7 68.1 reduce-scatter.16
  977.2 68.1 reduce-scatter.12
  1047.6 68.1 reduce-scatter.10
  1194.1 68.1 reduce-scatter.18
  1265.1 71.4 reduce-scatter.24
  1339.4 70.2 reduce-scatter.26
  1412.5 70.1 reduce-scatter.28
  1486.3 53.0 all-gather.37
  1541.5 180.0 reduce-scatter.22
  1723.9 227.9 reduce-scatter.20

commit v2 on v1

--- a/solution.py
+++ b/solution.py
@@ -169,6 +169,283 @@
     )(query, kv_all, bias, mixed, grad, logs)
 
 
+MESH = pl.DeviceIdType.MESH
+
+
+def gather_kernel(phases, count, *refs):
+    ins, outs, sems = refs[:count], refs[count : 2 * count], refs[2 * count :]
+    dp = lax.axis_index("dp"); member = lax.axis_index("expert")
+    blocks = lax.axis_size("expert")
+    core = member % 2; z = member // 2
+    depth = blocks // 2
+    sibling = (dp, member + 1 - 2 * core)
+    by_x = (dp + 1 - 2 * (dp % 2), member)
+    by_y = ((dp + 2) % 4, member)
+    x_at, y_at, far_at = by_x[0], by_y[0], 3 - dp
+    above, below = (dp, member + 2), (dp, member - 2)
+    barrier = pltpu.get_barrier_semaphore()
+    peers = [(sibling, None), (by_x, None), (by_y, None), (above, z < depth - 1), (below, z > 0)]
+    for peer, ok in peers:
+        if ok is None:
+            pl.semaphore_signal(barrier, inc=1, device_id=peer, device_id_type=MESH)
+        else:
+            @pl.when(ok)
+            def _(peer=peer):
+                pl.semaphore_signal(barrier, inc=1, device_id=peer, device_id_type=MESH)
+    @pl.when((z == 0) | (z == depth - 1))
+    def _(): pl.semaphore_wait(barrier, 4)
+    @pl.when((z > 0) & (z < depth - 1))
+    def _(): pl.semaphore_wait(barrier, 5)
+
+    def guarded(ok, run):
+        if ok is None: run()
+        else: pl.when(ok)(run)
+
+    class Item:
+        pass
+
+    def make(i):
+        src, out = ins[i], outs[i]
+        rows = src.shape[0]
+        half = rows // 2
+        (own_sem, sz, rz, sxy, rxy, sc, rc) = sems[i * 7 : (i + 1) * 7]
+        def at(d, s, lo=0, n=rows):
+            return out.at[pl.ds(pl.multiple_of((d * blocks + s * 2 + core) * rows + lo, 16 if half % 16 == 0 else 8), n)]
+        def copy(a, b, ss, rs, to):
+            return pltpu.make_async_remote_copy(src_ref=a, dst_ref=b, send_sem=ss, recv_sem=rs, device_id=to, device_id_type=MESH)
+        def block(d, s):
+            return at(d, s)
+        it = Item()
+        def local():
+            return pltpu.make_async_copy(src, at(dp, z), own_sem)
+        def up(s, ref): return copy(ref, at(dp, s), sz.at[0, s], rz.at[s], above)
+        def down(s, ref): return copy(ref, at(dp, s), sz.at[1, s], rz.at[s], below)
+        def to_x(s, ref): return copy(ref, at(dp, s), sxy.at[0, s], rxy.at[0, s], by_x)
+        def to_y(s, ref): return copy(ref, at(dp, s), sxy.at[1, s], rxy.at[1, s], by_y)
+        def half_y(s):
+            return copy(at(x_at, s, 0, half), at(x_at, s, 0, half), sxy.at[2, s], rxy.at[2, s], by_y)
+        def half_x(s):
+            return copy(at(y_at, s, half, half), at(y_at, s, half, half), sxy.at[3, s], rxy.at[3, s], by_x)
+        def to_core(r, d, s, ref): return copy(ref, at(d, s), sc.at[r, s], rc.at[r, s], sibling)
+        def spread(s, ref):
+            to_x(s, ref).start(); to_y(s, ref).start(); to_core(0, dp, s, ref).start()
+        def start():
+            local().start()
+            guarded(z < depth - 1, lambda: up(z, src).start())
+            guarded(z > 0, lambda: down(z, src).start())
+            spread(z, src)
+        def z_event(s, ok, rising):
+            def run():
+                up(s, at(dp, s)).wait_recv()
+                if rising: guarded(z < depth - 1, lambda: up(s, at(dp, s)).start())
+                else: guarded(z > 0, lambda: down(s, at(dp, s)).start())
+                spread(s, at(dp, s))
+            pl.when(ok)(run)
+        def near_event(s, ok):
+            def run():
+                to_x(s, at(dp, s)).wait_recv()
+                half_y(s).start()
+                to_core(1, x_at, s, at(x_at, s)).start()
+                to_y(s, at(dp, s)).wait_recv()
+                half_x(s).start()
+                to_core(2, y_at, s, at(y_at, s)).start()
+            guarded(ok, run)
+        def far_event(s, ok):
+            def run():
+                half_y(s).wait_recv(); half_x(s).wait_recv()
+                to_core(3, far_at, s, at(far_at, s)).start()
+            guarded(ok, run)
+        def core_wait(s):
+            for r, d in enumerate((dp, x_at, y_at, far_at)):
+                to_core(r, d, s, at(d, s)).wait_recv()
+        def finish():
+            local().wait()
+            for s in range(depth):
+                for c in (to_x(s, at(dp, s)), to_y(s, at(dp, s)), half_y(s), half_x(s)): c.wait_send()
+                for r, d in enumerate((dp, x_at, y_at, far_at)): to_core(r, d, s, at(d, s)).wait_send()
+                guarded((z >= s) & (z < depth - 1), lambda: up(s, at(dp, s)).wait_send())
+                guarded((z <= s) & (z > 0), lambda: down(s, at(dp, s)).wait_send())
+        it.start, it.z_event, it.near_event, it.far_event, it.core_wait, it.finish = start, z_event, near_event, far_event, core_wait, finish
+        return it
+    items = [make(i) for i in range(count)]
+    def around(d):
+        if d == 0: return [(z, None, True)]
+        return [(z - d, z >= d, True), (z + d, z + d < depth, False)]
+    for n, phase in enumerate(phases):
+        its = [items[i] for i in phase]
+        for it in its: it.start()
+        for d in range(1, depth + 2):
+            if d < depth:
+                for s, ok, rising in around(d):
+                    for it in its: it.z_event(s, ok, rising)
+            if d - 1 < depth:
+                for s, ok, _ in around(d - 1):
+                    for it in its: it.near_event(s, ok)
+            if d - 2 >= 0:
+                for s, ok, _ in around(d - 2):
+                    for it in its: it.far_event(s, ok)
+            if n + 1 < len(phases) and d == depth: pass
+    for it in items:
+        for s in range(depth): it.core_wait(s)
+    for it in items: it.finish()
+
+def gather_rows(arrays, phases, cid):
+    shards = lax.axis_size("dp") * lax.axis_size("expert")
+    depth = lax.axis_size("expert") // 2
+    D = pltpu.SemaphoreType.DMA
+    sems = []
+    for _ in arrays:
+        sems += [D, D((2, depth)), D((depth,)), D((4, depth)), D((4, depth)), D((4, depth)), D((4, depth))]
+    return pl.pallas_call(
+        functools.partial(gather_kernel, phases, len(arrays)),
+        out_shape=[jax.ShapeDtypeStruct((shards * a.shape[0],) + a.shape[1:], a.dtype) for a in arrays],
+        in_specs=[pl.BlockSpec(memory_space=pl.ANY)] * len(arrays),
+        out_specs=[pl.BlockSpec(memory_space=pl.ANY)] * len(arrays),
+        scratch_shapes=sems,
+        compiler_params=pltpu.CompilerParams(collective_id=cid, has_side_effects=True),
+        cost_estimate=pl.CostEstimate(flops=0, bytes_accessed=400_000_000, transcendentals=0),
+    )(*arrays)
+
+
+def reduce_kernel(rows, cuts, a_ref, b_ref, o_ref, sib, got, own, far, near, plane, got_z,
+                  s0, r0, s1, r1, s2, r2, s3, r3):
+    dp = lax.axis_index("dp"); member = lax.axis_index("expert")
+    core = member % 2; z = member // 2
+    sibling = (dp, member + 1 - 2 * core)
+    by_x = (dp + 1 - 2 * (dp % 2), member)
+    by_y = ((dp + 2) % 4, member)
+    x_at, y_at = by_x[0], by_y[0]
+    far_at = 3 - dp
+    half = rows // 2
+    depth = lax.axis_size("expert") // 2
+    barrier = pltpu.get_barrier_semaphore()
+    peers = [sibling, by_x, by_y] + [(dp, ((z + d) % depth) * 2 + core) for d in range(1, depth)]
+    for peer in peers:
+        pl.semaphore_signal(barrier, inc=1, device_id=peer, device_id_type=MESH)
+    pl.semaphore_wait(barrier, len(peers))
+
+    def pick(table):
+        at = table[depth-1]
+        for i in range(depth - 1):
+            at = jnp.where(z == i, table[i], at)
+        return at
+    orders = [[3, 3, 0, 0], [2, 0, 3, 1], [1, 2, 1, 2], [0, 1, 2, 3]]
+    targets = [pick(t) for t in orders]
+    wide = 4 * rows
+    cols = b_ref.shape[1] // cuts
+
+    def copy(src, dst, ssem, rsem, to):
+        return pltpu.make_async_remote_copy(src_ref=src, dst_ref=dst, send_sem=ssem, recv_sem=rsem, device_id=to, device_id_type=MESH)
+
+    def product(half_of, k, put):
+        base = (half_of * depth + targets[k]) * wide
+        def step(i, _):
+            at = (i // cuts) * rows
+            col = pl.multiple_of((i % cuts) * cols, cols)
+            part = jnp.dot(a_ref[pl.ds(pl.multiple_of(base + at, 16), rows), :], b_ref[:, pl.ds(col, cols)], preferred_element_type=f32)
+            put(pl.ds(pl.multiple_of(at, 16), rows), pl.ds(col, cols), part)
+            return 0
+        lax.fori_loop(0, 4 * cuts, step, 0)
+
+    sib_copies, far_copies, near_copies, z_copies = {}, {}, {}, {}
+    def sib_step(k):
+        slot = k % 2
+        if k >= 2:
+            sib_copies[k - 2].wait_send()
+        def put(r, c, part):
+            sib[slot, r, c] = part.astype(bf16)
+        product(1 - core, k, put)
+        sib_copies[k] = copy(sib.at[slot], got.at[k], s0.at[slot], r0.at[k], sibling)
+        sib_copies[k].start()
+    def blk(at):
+        return pl.ds(pl.multiple_of(at * rows, 16), rows)
+    def own_step(k):
+        sib_copies[k].wait_recv()
+        def put(r, c, part):
+            own[k, r, c] = (part + got[k, r, c].astype(f32)).astype(bf16)
+        product(core, k, put)
+        base = pl.multiple_of(far_at * rows, 16)
+        far_copies[k] = (
+            copy(own.at[k, pl.ds(base, half)], far.at[k, 0], s1.at[k, 0], r1.at[k, 0], by_x),
+            copy(own.at[k, pl.ds(pl.multiple_of(base + half, 16), half)], far.at[k, 1], s1.at[k, 1], r1.at[k, 1], by_y),
+        )
+        for c in far_copies[k]: c.start()
+    def near_step(k):
+        a, b = far_copies[k]
+        a.wait_recv()
+        rng = pl.ds(pl.multiple_of(y_at * rows, 16), half)
+        own[k, rng] = (own[k, rng].astype(f32) + far[k, 0].astype(f32)).astype(bf16)
+        to_y = copy(own.at[k, blk(y_at)], near.at[k, 1], s2.at[k, 1], r2.at[k, 1], by_y)
+        to_y.start()
+        b.wait_recv()
+        rng = pl.ds(pl.multiple_of(x_at * rows + half, 16), half)
+        own[k, rng] = (own[k, rng].astype(f32) + far[k, 1].astype(f32)).astype(bf16)
+        to_x = copy(own.at[k, blk(x_at)], near.at[k, 0], s2.at[k, 0], r2.at[k, 0], by_x)
+        to_x.start()
+        near_copies[k] = (to_x, to_y)
+    def plane_step(k):
+        for c in near_copies[k]: c.wait_recv()
+        total = own[k, blk(dp)].astype(f32) + near[k, 0].astype(f32) + near[k, 1].astype(f32)
+        if k < depth - 1:
+            plane[k] = total.astype(bf16)
+            to = (dp, targets[k] * 2 + core)
+            z_copies[k] = copy(plane.at[k], got_z.at[z], s3.at[k], r3.at[z], to)
+            z_copies[k].start()
+        else:
+            o_ref[...] = total
+    sib_step(0); sib_step(1)
+    own_step(0)
+    sib_step(2)
+    own_step(1)
+    near_step(0)
+    sib_step(3)
+    own_step(2)
+    near_step(1)
+    plane_step(0)
+    own_step(3)
+    near_step(2)
+    plane_step(1)
+    near_step(3)
+    plane_step(2)
+    plane_step(3)
+    for d in range(1, depth):
+        src = (z + d) % depth
+        copy(plane.at[0], got_z.at[src], s3.at[0], r3.at[src], sibling).wait_recv()
+        o_ref[...] += got_z[src].astype(f32)
+    for k in range(depth):
+        if k >= 2: sib_copies[k].wait_send()
+        for c in far_copies[k]: c.wait_send()
+        for c in near_copies[k]: c.wait_send()
+        if k < depth - 1: z_copies[k].wait_send()
+
+def reduce_rows(a, b, rows, cid, special):
+    if not special:
+        part = mm(a, b, TN).astype(bf16)
+        return lax.psum_scatter(part, BOTH, scatter_dimension=0, tiled=True).astype(f32)
+    tokens, width = b.shape
+    depth = 4
+    at = a.reshape(tokens, 4, depth, 2, rows).transpose(3, 2, 1, 4, 0).reshape(-1, tokens)
+    D = pltpu.SemaphoreType.DMA
+    return pl.pallas_call(
+        functools.partial(reduce_kernel, rows, 4),
+        out_shape=jax.ShapeDtypeStruct((rows, width), f32),
+        in_specs=[pl.BlockSpec(memory_space=pltpu.VMEM)] * 2,
+        out_specs=pl.BlockSpec(memory_space=pltpu.VMEM),
+        scratch_shapes=[
+            pltpu.VMEM((2, 4 * rows, width), bf16),
+            pltpu.VMEM((depth, 4 * rows, width), bf16),
+            pltpu.VMEM((depth, 4 * rows, width), bf16),
+            pltpu.VMEM((depth, 2, rows // 2, width), bf16),
+            pltpu.VMEM((depth, 2, rows, width), bf16),
+            pltpu.VMEM((depth - 1, rows, width), bf16),
+            pltpu.VMEM((depth, rows, width), bf16),
+            D((2,)), D((depth,)), D((depth, 2)), D((depth, 2)), D((depth, 2)), D((depth, 2)), D((depth - 1,)), D((depth,)),
+        ],
+        compiler_params=pltpu.CompilerParams(vmem_limit_bytes=60*1024*1024, collective_id=cid, has_side_effects=True),
+        cost_estimate=pl.CostEstimate(flops=2*tokens*32*rows*width, bytes_accessed=10_000_000, transcendentals=0),
+    )(at, b)
+
+
 def slots_of(route_ids, gate_vals, ranking, capacity, experts):
     rows = route_ids.shape[0]
     pair_experts = route_ids.reshape(-1)
@@ -182,6 +459,50 @@
     slot_map = jnp.sum(jnp.where(chosen, slot[:, :, None] + 1, 0), axis=1).astype(f32) - 1.0
     weight_map = jnp.sum(jnp.where(chosen, gate_vals[:, :, None], 0.0), axis=1)
     return slot_map, weight_map
+
+
+def swap(values, bit):
+    return lax.ppermute(values, "dp", [(i, i ^ bit) for i in range(lax.axis_size("dp"))])
+
+
+def gather_parts(own, axis):
+    if lax.axis_size("dp") != 4:
+        return lax.all_gather(own, "dp", axis=axis, tiled=True)
+    at = lax.axis_index("dp")
+    size = own.shape[axis]
+    by_x, by_y = swap(own, 1), swap(own, 2)
+    far_0, far_1 = swap(by_x[:1], 2), swap(by_y[1:], 1)
+    shape = list(own.shape)
+    shape[axis] *= 4
+    full = jnp.zeros(tuple(shape), own.dtype)
+    for part, expert, bits in ((own, 0, 0), (by_x, 0, 1), (by_y, 0, 2), (far_0, 0, 3), (far_1, 1, 3)):
+        start = [expert, 0, 0]
+        start[axis] = (at ^ bits) * size
+        full = lax.dynamic_update_slice(full, part, tuple(start))
+    return full
+
+
+def scatter_far(total, axis):
+    if lax.axis_size("dp") != 4:
+        low = total.astype(bf16)
+        return [lax.psum_scatter(low, "dp", scatter_dimension=axis, tiled=True)]
+    at = lax.axis_index("dp")
+    size = total.shape[axis] // 4
+
+    def part(bits):
+        return lax.dynamic_slice_in_dim(total, (at ^ bits) * size, size, axis=axis)
+
+    far = part(3).astype(bf16)
+    return [swap(far[:1], 1), swap(far[1:], 2), part(1), part(2), part(0)]
+
+
+def scatter_near(for_y, for_x=None, near_x=None, near_y=None, own=None):
+    if for_x is None:
+        return for_y.astype(f32)
+    near_y = jnp.concatenate([near_y[:1] + for_y.astype(f32), near_y[1:]], axis=0).astype(bf16)
+    near_x = jnp.concatenate([near_x[:1], near_x[1:] + for_x.astype(f32)], axis=0).astype(bf16)
+    by_x, by_y = swap(near_x, 1), swap(near_y, 2)
+    return own + by_x.astype(f32) + by_y.astype(f32)
 
 
 def body(
@@ -215,22 +536,29 @@
     total = micro * rows
     q_part, k_part, v_part = w_query.shape[1], w_key.shape[1], w_value.shape[1]
 
+    special = blocks == 8 and shards == 32
+
     gain_len = norm_gains.shape[0]
     gain_shard = jnp.zeros((2048,), bf16).at[:gain_len].set(norm_gains).reshape(16, 128)
-    gain_full = lax.all_gather(gain_shard, BOTH, axis=0, tiled=True)
+    qkv_w = jnp.concatenate([w_query.T, w_key.T, w_value.T], axis=0)
+    if special:
+        qkv_w, out_w, gain_full = gather_rows([qkv_w, w_output, gain_shard], [(2, 0, 1)], 1)
+    else:
+        qkv_w, out_w, gain_full = (
+            lax.all_gather(part, BOTH, axis=0, tiled=True) for part in (qkv_w, w_output, gain_shard)
+        )
+    d_out_all = lax.all_gather(cotangent[:, 0], "expert", axis=0, tiled=False)
+    qkv_w, d_out_all = lax.optimization_barrier((qkv_w, d_out_all))
     gains = gain_full.reshape(shards, 2048)[:, :gain_len].reshape(-1).astype(f32)
     gain_in = gains[:width]
     gain_mid = gains[width : 2 * width]
     gain_q = gains[2 * width : 2 * width + HD]
     gain_k = gains[2 * width + HD :]
 
-    qkv_w = lax.all_gather(
-        jnp.concatenate([w_query.T, w_key.T, w_value.T], axis=0), BOTH, axis=0, tiled=True
-    )
-    out_w = lax.all_gather(w_output, BOTH, axis=0, tiled=True)
-    wg = lax.all_gather(w_gate, "dp", axis=1, tiled=True)
-    wu = lax.all_gather(w_up, "dp", axis=1, tiled=True)
-    wd = lax.all_gather(w_down, "dp", axis=2, tiled=True)
+    w_gate, w_up, w_down, qkv_w = lax.optimization_barrier((w_gate, w_up, w_down, qkv_w))
+    wg = gather_parts(w_gate, 1)
+    wu = gather_parts(w_up, 1)
+    wd = gather_parts(w_down, 2)
 
     slot_map, weight_map = jax.vmap(
         lambda r, g, o: slots_of(r, g, o, capacity, experts)
@@ -289,12 +617,12 @@
     middle = middle.reshape(micro, rows, width)
     scale_mid = scale_mid.reshape(micro, rows, 1)
 
-    outputs, d_branches, d_middles = [], [], []
+    mix_parts, d_routeds, d_branches, d_middles = [], [], [], []
     acc_gate = acc_up = acc_down = 0.0
     grad_mid = 0.0
     slots = blocks * capacity
     for at in range(micro):
-        d_out = lax.all_gather(cotangent[at, 0], "expert", axis=0, tiled=False)
+        d_out = d_out_all[:, at]
         tokens = lax.all_gather(routed[at], "expert", axis=0, tiled=False)
         picked = jnp.einsum("ebst,btd->ebsd", pick[at], tokens, preferred_element_type=f32)
         picked = picked.astype(bf16).reshape(local_experts, slots, width)
@@ -318,31 +646,37 @@
         result = jnp.einsum("erf,efd->erd", hidden_low, wd, preferred_element_type=f32)
         result = result.astype(bf16).reshape(local_experts, blocks, capacity, width)
         part = jnp.einsum("ebst,ebsd->btd", weighted[at], result, preferred_element_type=f32)
-        part = part.astype(bf16).reshape(group_len, width)
-        expert_mix = lax.psum_scatter(part, "expert", scatter_dimension=0, tiled=True).astype(f32)
-        outputs.append((middle[at] + expert_mix).astype(bf16))
+        mix_parts.append(part.astype(bf16).reshape(group_len, width))
+        d_routeds.append(d_routed)
 
         acc_down += jnp.einsum("erf,erd->efd", hidden_low, d_result, preferred_element_type=f32)
         acc_gate += jnp.einsum("erd,erf->edf", picked, d_gate, preferred_element_type=f32)
         acc_up += jnp.einsum("erd,erf->edf", picked, d_up, preferred_element_type=f32)
 
-        d_mid_norm, mid_gain_grad = norm_back(d_routed, middle[at], scale_mid[at], gain_mid)
+    scattering = [scatter_far(acc, axis) for acc, axis in ((acc_gate, 1), (acc_up, 1), (acc_down, 2))]
+    d_routeds[-1], scattering = lax.optimization_barrier((d_routeds[-1], scattering))
+    expert_grads = [scatter_near(*parts) for parts in scattering]
+    for at in range(micro):
+        d_mid_norm, mid_gain_grad = norm_back(d_routeds[at], middle[at], scale_mid[at], gain_mid)
         grad_mid = grad_mid + mid_gain_grad
         d_middle = cotangent[at, 0].astype(f32) + d_mid_norm
         d_middles.append(d_middle)
         d_branches.append(d_middle.astype(bf16))
 
-    grad_gate = lax.psum_scatter(acc_gate.astype(bf16), "dp", scatter_dimension=1, tiled=True)
-    grad_up = lax.psum_scatter(acc_up.astype(bf16), "dp", scatter_dimension=1, tiled=True)
-    grad_down = lax.psum_scatter(acc_down.astype(bf16), "dp", scatter_dimension=2, tiled=True)
-
     d_branch = jnp.concatenate(d_branches, axis=0)
     d_middle = jnp.concatenate(d_middles, axis=0)
-    grad_output = mm(mixed.reshape(total, H * HD), d_branch, TN).astype(bf16)
-    grad_output = lax.psum_scatter(grad_output, BOTH, scatter_dimension=0, tiled=True)
     d_mixed = mm(d_branch, out_w, NT).astype(bf16).reshape(micro, rows, H * HD)
     dq_low, dkv_all = run_backward(q_low, kv_all, bias, mixed, d_mixed, logs, step_heads, chunk)
+    mixed_after, dq_low, dkv_all, expert_grads = lax.optimization_barrier(
+        (mixed, dq_low, dkv_all, expert_grads)
+    )
+    grad_output = reduce_rows(mixed_after.reshape(total, H * HD), d_branch, w_output.shape[0], 2, special)
     dkv = lax.psum_scatter(dkv_all, "expert", scatter_dimension=0, tiled=False)
+    mix_parts, dkv, grad_output = lax.optimization_barrier((mix_parts, dkv, grad_output))
+    outputs = []
+    for at in range(micro):
+        mix = lax.psum_scatter(mix_parts[at], "expert", scatter_dimension=0, tiled=True)
+        outputs.append((middle[at] + mix.astype(f32)).astype(bf16))
     dkv = dkv.reshape(total, KVH, 2 * HD)
     d_query = rotate(dq_low.reshape(total, H, HD).astype(f32), cosine, -sine_part)
     d_query, grad_qn = norm_back(d_query, queries, scale_q, gain_q)
@@ -356,8 +690,7 @@
         ],
         axis=-1,
     ).reshape(total, -1)
-    grad_qkv = mm(d_proj, normed, TN).astype(bf16)
-    grad_qkv = lax.psum_scatter(grad_qkv, BOTH, scatter_dimension=0, tiled=True).astype(f32)
+    grad_qkv = reduce_rows(d_proj, normed, q_part + k_part + v_part, 3, special)
     d_normed = mm(d_proj, qkv_w)
     d_in_norm, grad_in = norm_back(d_normed, hidden, scale_in, gain_in)
     input_grad = d_middle + d_in_norm
@@ -372,11 +705,9 @@
         grad_qkv[:q_part].T,
         grad_qkv[q_part : q_part + k_part].T,
         grad_qkv[q_part + k_part :].T,
-        grad_output.astype(f32),
+        grad_output,
         grad_gains[:gain_len],
-        grad_gate.astype(f32),
-        grad_up.astype(f32),
-        grad_down.astype(f32),
+        *expert_grads,
     )
 
 

time: 1980 us -> 1430 us (0.72)
  waiting for transfers between devices: 1300 us -> 235 us
  Pallas kernels: 105 us -> 555 us
  local copies, waits for them, and re-layouts: 97.4 us -> 177 us
  blocking collectives: 54 us -> 17.7 us
  matrix products: 315 us -> 284 us
  other arithmetic: 75.5 us -> 103 us
  starting transfers between devices: 1.47 us -> 27.1 us
    reduce_scatter x7 -> x2, waiting for transfers between devices: 660 us -> 73.3 us  [body(): lax.psum_scatter(mix_parts[at], 'expert', scatter_dimension=0, tiled=True)]
    pallas_call x0 -> x3, Pallas kernels: none -> 449 us  [the longest x2 242 us: reduce_rows(): pl.pallas_call(functools.partial(reduce_kernel, rows, 4), out_shape=jax.S...]
    all_gather x7 -> x1, waiting for transfers between devices: 402 us -> 0.02 us  [body(): d_out_all = lax.all_gather(cotangent[:, 0], 'expert', axis=0, tiled=False)]
    all_gather x2, waiting for transfers between devices: 114 us -> 0.01 us  [body(): tokens = lax.all_gather(routed[at], 'expert', axis=0, tiled=False)]
    ppermute x0 -> x24, waiting for transfers between devices: none -> 111 us  [swap(): lax.ppermute(values, 'dp', [(i, i ^ bit) for i in range(lax.axis_size('dp...]
    all_gather x1, waiting for transfers between devices: 47.7 us -> 0.01 us  [body(): gain_all = lax.all_gather(gain_grads, BOTH, axis=0, tiled=False)]
    reduce_scatter x2, waiting for transfers between devices: 43.2 us -> 0.02 us  [body(): lax.psum_scatter(d_part, 'expert', scatter_dimension=0, tiled=True)]
    all_gather x1 -> x0, blocking collectives: 37.9 us -> none  [body(): gain_full = lax.all_gather(gain_shard, BOTH, axis=0, tiled=True)]
  transfers between devices with their start and end apart: 21 -> 34, of which waited for: 18 -> 13; matrix products, arithmetic and copies ran while one was open for 22% -> 33% of each run, Pallas kernels for 2% -> 36%
where the time goes in v2:
time: 1430 us; the launch traced here: 1410 us
  Pallas kernels  555 us (39%)
  matrix products  284 us (20%)
  waiting for transfers between devices  235 us (16%)
  local copies, waits for them, and re-layouts  177 us (12%)
  other arithmetic  103 us (7%)
  starting transfers between devices  27.1 us (2%)
  blocking collectives  17.7 us (1%)
  between operations  16.1 us (1%)
    pallas_call x2, Pallas kernels, reduce_rows(): pl.pallas_call(functools.partial(reduce_kernel, rows, 4), out_shape=jax.S...  242 us
    pallas_call x1, Pallas kernels, gather_rows(): pl.pallas_call(functools.partial(gather_kernel, phases, len(arrays)), out...  207 us
    ppermute x24, waiting for transfers between devices, swap(): lax.ppermute(values, 'dp', [(i, i ^ bit) for i in range(lax.axis_size('dp...  111 us
    reduce_scatter x2, waiting for transfers between devices, body(): lax.psum_scatter(mix_parts[at], 'expert', scatter_dimension=0, tiled=True)  73.3 us
    pallas_call x1, Pallas kernels, run_backward(): pl.pallas_call(functools.partial(attend_backward, step_heads, chunk), gri...  62 us
    dot_general x4, matrix products, mm(): return lax.dot_general(a, b, dims, preferred_element_type=f32)  53.2 us
    all_gather x1, waiting for transfers between devices, body(): kv_all = lax.all_gather(kv_own, 'expert', axis=0, tiled=False)  48.5 us
    pallas_call x1, Pallas kernels, run_forward(): pl.pallas_call(functools.partial(attend_forward, step_heads, chunk), grid...  43.8 us
  transfers between devices with their start and end apart: 34, of which 13 were waited for; matrix products, arithmetic and copies ran while one was open for 33% of the time, Pallas kernels for 36%

profile of v2, /device:TPU:8, one launch (start us, length us, event | category | flops | bytes accessed | tf_op | source)
XLA Modules:
  0.0 1414.8 jit_solution(11784790636530918547)
XLA Ops:
  15.5 206.6 %shard_map.213 = (bf16[5120,2048]{1,0:T(8,128)(2,1)}, bf16[4096,2048]{1,0:T(8,128)(2,1)}, bf16[512,128]{1,0:T(8,128)(2,1)}) custom-call(bf16[160,2048]{1,0:T(8,128)(2,1)} %pad_maximum_fusion.13.refs_0_, bf16[128,2048]{1,0:T(8,128)(2,1)} %refs_1_.1, bf16[16,128]{1,0:T(8,128)(2,1)} %pad_bitcast_fusion.refs_2_), custom_call_target="tpu_custom_call" | custom-call | bytes 400000000 | tf_op jit(solution)/shard_map/pallas_call | solution.py:299
  225.2 14.4 %fusion.57 = f32[384,32,160]{0,2,1:T(8,128)S(1)} fusion(bf16[384,2048,1]{1,0,2:T(8,128)(2,1)S(1)} %bitcast.289, bf16[32,160,2048]{2,1,0:T(8,128)(2,1)} %bitcast.308), kind=kOutput, calls=%fused_computation.232 | convolution fusion | flops 8053063680 | bytes 30408704 | tf_op jit(solution)/shard_map/dot_general | solution.py:35
  285.2 48.5 %all-gather.11.cloned.1.call-done.kv_ref = bf16[8,2,192,1024]{3,2,1,0:T(8,128)(2,1)} async-done(((bf16[1,2,192,1024]{3,2,1,0:T(8,128)(2,1)}), bf16[8,2,192,1024]{3,2,1,0:T(8,128)(2,1)}) %all-gather.11.cloned.1.call-update) | async-done | bytes 6291472 | tf_op jit(solution)/shard_map/all_gather | solution.py:609
  333.7 43.8 %shard_map.214 = (bf16[2,192,4096]{2,1,0:T(8,128)(2,1)}, f32[2,4,4,384]{3,2,1,0:T(4,128)}) custom-call(bf16[2,192,4096]{2,1,0:T(8,128)(2,1)} %convert_element_type.238.q_ref, bf16[8,2,192,1024]{3,2,1,0:T(8,128)(2,1)} %all-gather.11.cloned.1.call-done.kv_ref, f32[2,1536,384]{2,1,0:T(8,128)} %copy.219.bias_ref), custom_call_target="tpu_custom_call" | custom-call | flops 9663676416 | bytes 20000000 | tf_op jit(solution)/shard_map/pallas_call | solution.py:133
  397.6 17.7 %all-gather.1 = f32[16,192,32]{1,2,0:T(8,128)S(1)} all-gather(f32[2,192,32]{1,2,0:T(8,128)S(1)} %pad_maximum_fusion.14), channel_id=3, replica_groups=mesh['dp'=4,'expert'=8] {'expert'}, dimensions={0}, use_global_device_ids=true | all-gather | bytes 442368 | tf_op jit(solution)/shard_map/all_gather | solution.py:567
  420.7 12.2 collective-permute-done
  472.1 14.5 %collective-permute-done.5 = bf16[2,512,768]{2,1,0:T(8,128)(2,1)} collective-permute-done((bf16[2,512,768]{2,1,0:T(8,128)(2,1)}, bf16[2,512,768]{2,1,0:T(8,128)(2,1)}, u32[]{:S(2)}, u32[]{:S(2)}) %collective-permute-start.5) | collective-permute-done | bytes 1572896 | tf_op jit(solution)/shard_map/ppermute | solution.py:465
  503.1 17.3 %collective-permute-done.9 = bf16[2,768,512]{2,1,0:T(8,128)(2,1)} collective-permute-done((bf16[2,768,512]{2,1,0:T(8,128)(2,1)}, bf16[2,768,512]{2,1,0:T(8,128)(2,1)}, u32[]{:S(2)}, u32[]{:S(2)}) %collective-permute-start.9) | collective-permute-done | bytes 1572896 | tf_op jit(solution)/shard_map/ppermute | solution.py:465
  541.9 12.0 collective-permute-done.6
  555.9 14.3 %collective-permute-done.10 = bf16[1,768,512]{2,1,0:T(8,128)(2,1)S(1)} collective-permute-done((bf16[1,768,512]{2,1,0:T(8,128)(2,1)S(1)}, bf16[1,768,512]{2,1,0:T(8,128)(2,1)S(1)}, u32[]{:S(2)}, u32[]{:S(2)}) %collective-permute-start.10) | collective-permute-done | bytes 786464 | tf_op jit(solution)/shard_map/ppermute | solution.py:465
  597.0 11.6 multiply_convert_fusion.1
  608.6 12.5 fusion.63
  678.9 13.2 fusion.61
  731.7 12.6 fusion.64
  744.3 12.8 convolution_add_fusion.2
  762.7 12.7 fusion.65
  775.4 12.5 convolution_add_fusion.1
  841.2 12.0 convolution_convert_fusion
  853.2 11.9 collective-permute-done.23
  866.5 62.0 %shard_map.215 = (bf16[2,192,4096]{2,1,0:T(8,128)(2,1)}, bf16[8,2,192,1024]{3,2,1,0:T(8,128)(2,1)}) custom-call(bf16[2,192,4096]{2,1,0:T(8,128)(2,1)} %convert_element_type.238.q_ref, bf16[8,2,192,1024]{3,2,1,0:T(8,128)(2,1)} %all-gather.11.cloned.1.call-done.kv_ref, f32[2,1536,384]{2,1,0:T(8,128)} %copy.219.bias_ref, ...), custom_call_target="tpu_custom_call" | custom-call | flops 24159191040 | bytes 30000000 | tf_op jit(solution)/shard_map/pallas_call | solution.py:155
  1026.2 90.8 %shard_map.216 = f32[128,2048]{1,0:T(8,128)} custom-call(bf16[4096,384]{1,0:T(8,128)(2,1)} %bitcast.284, bf16[384,2048]{1,0:T(8,128)(2,1)} %pad_maximum_fusion.4.b_ref), custom_call_target="tpu_custom_call" | custom-call | flops 6442450944 | bytes 10000000 | tf_op jit(solution)/shard_map/pallas_call | solution.py:429
  1141.4 15.4 %fusion.31 = (f32[2048]{0:T(1024)S(1)}, f32[384]{0:T(512)}, bf16[384,2048]{1,0:T(8,128)(2,1)}, f32[384,2048]{1,0:T(8,128)}) fusion(bf16[2,1,192,2048]{3,2,1,0:T(8,128)(2,1)S(1)} %copy-done.7, f32[384]{0:T(512)S(1)} %copy-done.77, f32[2048]{0:T(1024)S(1)} %copy-done.66, bf16[384,5120]{0,1:T(8,128)(2,1)S(1)} %bitcast.278, ...), kind=kOutput, calls=%fused_computation.69 | convolution fusion | flops 8060925440 | bytes 31214592 | tf_op jit(solution)/shard_map/dot_general | solution.py:35
  1166.3 151.6 %shard_map.217 = f32[160,2048]{1,0:T(8,128)} custom-call(bf16[5120,384]{1,0:T(8,128)(2,1)} %bitcast.279, bf16[384,2048]{1,0:T(8,128)(2,1)} %get-tuple-element.193.b_ref), custom_call_target="tpu_custom_call" | custom-call | flops 8053063680 | bytes 10000000 | tf_op jit(solution)/shard_map/pallas_call | solution.py:429
  1331.9 71.3 %reduce-scatter.14.cloned.1.call-done = bf16[192,2048]{1,0:T(8,128)(2,1)} async-done(((bf16[1536,2048]{1,0:T(8,128)(2,1)}), bf16[192,2048]{1,0:T(8,128)(2,1)}) %reduce-scatter.14.cloned.1.call-update) | async-done | bytes 786448 | tf_op jit(solution)/shard_map/reduce_scatter | solution.py:678
  (468 shorter events, 494.6 us)
Async XLA Ops:
  7.2 218.0 %all-gather.13.cloned.1.call-start = ((), (), s32[]{:S(2)}) async-start(), calls=%async_computation.11 | async-start | bytes 14155776 | tf_op jit(solution)/shard_map/all_gather | solution.py:550
  8.0 325.7 %all-gather.11.cloned.1.call-start = ((), (), s32[]{:S(2)}) async-start(), calls=%async_computation.5 | async-start | bytes 7077888 | tf_op jit(solution)/shard_map/all_gather | solution.py:609
  252.1 330.1 %all-gather.17.cloned.1.call-start = ((), (), s32[]{:S(2)}) async-start(), calls=%async_computation.13 | async-start | bytes 7077888 | tf_op jit(solution)/shard_map/all_gather | solution.py:626
  391.0 262.3 %all-gather.15.cloned.1.call-start = ((), (), s32[]{:S(2)}) async-start(), calls=%async_computation.12 | async-start | bytes 7077888 | tf_op jit(solution)/shard_map/all_gather | solution.py:626
  417.3 395.6 %reduce-scatter.8.cloned.1.call-start = ((), (), s32[]{:S(2)}) async-start(), calls=%async_computation.7 | async-start | bytes 7077888 | tf_op jit(solution)/shard_map/reduce_scatter | solution.py:645
  418.0 68.6 %collective-permute-start.5 = (bf16[2,512,768]{2,1,0:T(8,128)(2,1)}, bf16[2,512,768]{2,1,0:T(8,128)(2,1)}, u32[]{:S(2)}, u32[]{:S(2)}) collective-permute-start(bf16[2,512,768]{2,1,0:T(8,128)(2,1)} %param.28), channel_id=1, source_target_pairs={{0,16},{8,24},{16,0},{24,8},{1,17},{9,25},{17,1},{25,9},{2,18},{10... | collective-permute-start | bytes 4718600 | tf_op jit(solution)/shard_map/ppermute | solution.py:465
  418.9 101.4 %collective-permute-start.9 = (bf16[2,768,512]{2,1,0:T(8,128)(2,1)}, bf16[2,768,512]{2,1,0:T(8,128)(2,1)}, u32[]{:S(2)}, u32[]{:S(2)}) collective-permute-start(bf16[2,768,512]{2,1,0:T(8,128)(2,1)} %param.29), channel_id=1, source_target_pairs={{0,16},{8,24},{16,0},{24,8},{1,17},{9,25},{17,1},{25,9},{2,18},{10... | collective-permute-start | bytes 4718600 | tf_op jit(solution)/shard_map/ppermute | solution.py:465
  432.8 67.5 %collective-permute-start.8 = (bf16[2,768,512]{2,1,0:T(8,128)(2,1)}, bf16[2,768,512]{2,1,0:T(8,128)(2,1)}, u32[]{:S(2)}, u32[]{:S(2)}) collective-permute-start(bf16[2,768,512]{2,1,0:T(8,128)(2,1)} %param.29), channel_id=1, source_target_pairs={{0,8},{8,0},{16,24},{24,16},{1,9},{9,1},{17,25},{25,17},{2,10},{10... | collective-permute-start | bytes 4718600 | tf_op jit(solution)/shard_map/ppermute | solution.py:465
  452.9 84.2 %collective-permute-start.2 = (bf16[1,512,768]{2,1,0:T(8,128)(2,1)S(1)}, bf16[1,512,768]{2,1,0:T(8,128)(2,1)S(1)}, u32[]{:S(2)}, u32[]{:S(2)}) collective-permute-start(bf16[1,512,768]{2,1,0:T(8,128)(2,1)S(1)} %slice.316), channel_id=1, source_target_pairs={{0,16},{8,24},{16,0},{24,8},{1,17},{9,25},{17,1},{25,9},{2,18},{10... | collective-permute-start | bytes 2359304 | tf_op jit(solution)/shard_map/ppermute | solution.py:465
  466.6 74.3 %collective-permute-start.3 = (bf16[1,512,768]{2,1,0:T(8,128)(2,1)S(1)}, bf16[1,512,768]{2,1,0:T(8,128)(2,1)S(1)}, u32[]{:S(2)}, u32[]{:S(2)}) collective-permute-start(bf16[1,512,768]{2,1,0:T(8,128)(2,1)S(1)} %slice.317), channel_id=1, source_target_pairs={{0,8},{8,0},{16,24},{24,16},{1,9},{9,1},{17,25},{25,17},{2,10},{10... | collective-permute-start | bytes 2359304 | tf_op jit(solution)/shard_map/ppermute | solution.py:465
  486.6 67.3 %collective-permute-start.6 = (bf16[1,512,768]{2,1,0:T(8,128)(2,1)S(1)}, bf16[1,512,768]{2,1,0:T(8,128)(2,1)S(1)}, u32[]{:S(2)}, u32[]{:S(2)}) collective-permute-start(bf16[1,512,768]{2,1,0:T(8,128)(2,1)S(1)} %slice.318), channel_id=1, source_target_pairs={{0,16},{8,24},{16,0},{24,8},{1,17},{9,25},{17,1},{25,9},{2,18},{10... | collective-permute-start | bytes 2359304 | tf_op jit(solution)/shard_map/ppermute | solution.py:465
  635.9 179.5 %reduce-scatter.6.cloned.1.call-start = ((), (), s32[]{:S(2)}) async-start(), calls=%async_computation.6 | async-start | bytes 7077888 | tf_op jit(solution)/shard_map/reduce_scatter | solution.py:645
  707.0 415.5 %reduce-scatter.10.cloned.1.call-start = ((), (), s32[]{:S(2)}) async-start(), calls=%async_computation.8 | async-start | bytes 7077888 | tf_op jit(solution)/shard_map/reduce_scatter | solution.py:674
  729.8 62.8 %collective-permute-start.17 = (bf16[1,768,512]{2,1,0:T(8,128)(2,1)S(1)}, bf16[1,768,512]{2,1,0:T(8,128)(2,1)S(1)}, u32[]{:S(2)}, u32[]{:S(2)}) collective-permute-start(bf16[1,768,512]{2,1,0:T(8,128)(2,1)S(1)} %get-tuple-element.194), channel_id=1, source_target_pairs={{0,16},{8,24},{16,0},{24,8},{1,17},{9,25},{17,1},{25,9},{2,18},{10... | collective-permute-start | bytes 2359304 | tf_op jit(solution)/shard_map/ppermute | solution.py:465
  731.1 84.2 %collective-permute-start.16 = (bf16[1,768,512]{2,1,0:T(8,128)(2,1)}, bf16[1,768,512]{2,1,0:T(8,128)(2,1)}, u32[]{:S(2)}, u32[]{:S(2)}) collective-permute-start(bf16[1,768,512]{2,1,0:T(8,128)(2,1)} %get-tuple-element.195), channel_id=1, source_target_pairs={{0,8},{8,0},{16,24},{24,16},{1,9},{9,1},{17,25},{25,17},{2,10},{10... | collective-permute-start | bytes 2359304 | tf_op jit(solution)/shard_map/ppermute | solution.py:465
  760.6 54.7 %collective-permute-start.13 = (bf16[1,512,768]{2,1,0:T(8,128)(2,1)}, bf16[1,512,768]{2,1,0:T(8,128)(2,1)}, u32[]{:S(2)}, u32[]{:S(2)}) collective-permute-start(bf16[1,512,768]{2,1,0:T(8,128)(2,1)} %get-tuple-element.198), channel_id=1, source_target_pairs={{0,16},{8,24},{16,0},{24,8},{1,17},{9,25},{17,1},{25,9},{2,18},{10... | collective-permute-start | bytes 2359304 | tf_op jit(solution)/shard_map/ppermute | solution.py:465
  829.4 99.1 %collective-permute-start.22 = (bf16[2,768,512]{2,1,0:T(8,128)(2,1)}, bf16[2,768,512]{2,1,0:T(8,128)(2,1)}, u32[]{:S(2)}, u32[]{:S(2)}) collective-permute-start(bf16[2,768,512]{2,1,0:T(8,128)(2,1)} %pad_maximum_fusion.9), channel_id=1, source_target_pairs={{0,8},{8,0},{16,24},{24,16},{1,9},{9,1},{17,25},{25,17},{2,10},{10... | collective-permute-start | bytes 4718600 | tf_op jit(solution)/shard_map/ppermute | solution.py:465
  832.4 99.9 %collective-permute-start.21 = (bf16[2,512,768]{2,1,0:T(8,128)(2,1)}, bf16[2,512,768]{2,1,0:T(8,128)(2,1)}, u32[]{:S(2)}, u32[]{:S(2)}) collective-permute-start(bf16[2,512,768]{2,1,0:T(8,128)(2,1)} %pad_maximum_fusion.8), channel_id=1, source_target_pairs={{0,16},{8,24},{16,0},{24,8},{1,17},{9,25},{17,1},{25,9},{2,18},{10... | collective-permute-start | bytes 4718600 | tf_op jit(solution)/shard_map/ppermute | solution.py:465
  835.1 97.2 %collective-permute-start.20 = (bf16[2,512,768]{2,1,0:T(8,128)(2,1)}, bf16[2,512,768]{2,1,0:T(8,128)(2,1)}, u32[]{:S(2)}, u32[]{:S(2)}) collective-permute-start(bf16[2,512,768]{2,1,0:T(8,128)(2,1)} %pad_maximum_fusion.7), channel_id=1, source_target_pairs={{0,8},{8,0},{16,24},{24,16},{1,9},{9,1},{17,25},{25,17},{2,10},{10... | collective-permute-start | bytes 4718600 | tf_op jit(solution)/shard_map/ppermute | solution.py:465
  837.0 99.4 %collective-permute-start.19 = (bf16[2,512,768]{2,1,0:T(8,128)(2,1)}, bf16[2,512,768]{2,1,0:T(8,128)(2,1)}, u32[]{:S(2)}, u32[]{:S(2)}) collective-permute-start(bf16[2,512,768]{2,1,0:T(8,128)(2,1)} %pad_maximum_fusion.6), channel_id=1, source_target_pairs={{0,16},{8,24},{16,0},{24,8},{1,17},{9,25},{17,1},{25,9},{2,18},{10... | collective-permute-start | bytes 4718600 | tf_op jit(solution)/shard_map/ppermute | solution.py:465
  865.1 71.4 %collective-permute-start.18 = (bf16[2,512,768]{2,1,0:T(8,128)(2,1)}, bf16[2,512,768]{2,1,0:T(8,128)(2,1)S(1)}, u32[]{:S(2)}, u32[]{:S(2)}) collective-permute-start(bf16[2,512,768]{2,1,0:T(8,128)(2,1)} %pad_maximum_fusion.5), channel_id=1, source_target_pairs={{0,8},{8,0},{16,24},{24,16},{1,9},{9,1},{17,25},{25,17},{2,10},{10... | collective-permute-start | bytes 4718600 | tf_op jit(solution)/shard_map/ppermute | solution.py:465
  940.0 388.3 %all-gather.19.cloned.1.call-start = ((), (), s32[]{:S(2)}) async-start(), calls=%async_computation.14 | async-start | bytes 1081344 | tf_op jit(solution)/shard_map/all_gather | solution.py:700
  1160.8 171.1 %reduce-scatter.12.cloned.1.call-start = ((), (), s32[]{:S(2)}) async-start(), calls=%async_computation.9 | async-start | bytes 7077888 | tf_op jit(solution)/shard_map/reduce_scatter | solution.py:678
  1161.6 241.6 %reduce-scatter.14.cloned.1.call-start = ((), (), s32[]{:S(2)}) async-start(), calls=%async_computation.10 | async-start | bytes 7077888 | tf_op jit(solution)/shard_map/reduce_scatter | solution.py:678
  (105 other events, 1920.9 us)
Sparse Core Ops, SparseCore 0:
  9.7 162.7 all-gather.12
  252.2 81.3 all-gather.10
  391.1 67.4 all-gather.16
  460.6 63.0 all-gather.14
  636.0 65.9 reduce-scatter.7
  707.2 66.0 reduce-scatter.5
  940.1 65.3 reduce-scatter.9
  1161.0 54.6 all-gather.18
  1218.0 113.9 reduce-scatter.11
  1334.1 69.0 reduce-scatter.13

commit v3 on v2

--- a/solution.py
+++ b/solution.py
@@ -307,8 +307,8 @@
     )(*arrays)
 
 
-def reduce_kernel(rows, cuts, a_ref, b_ref, o_ref, sib, got, own, far, near, plane, got_z,
-                  s0, r0, s1, r1, s2, r2, s3, r3):
+def reduce_kernel(rows, cuts, a_ref, b_ref, g_ref, o_ref, go_ref, sib, got, own, far, near, plane, got_z,
+                  s0, r0, s1, r1, s2, r2, s3, r3, g_acc, g_got, g_z, gs, gr, gsz, grz):
     dp = lax.axis_index("dp"); member = lax.axis_index("expert")
     core = member % 2; z = member // 2
     sibling = (dp, member + 1 - 2 * core)
@@ -347,6 +347,42 @@
             return 0
         lax.fori_loop(0, 4 * cuts, step, 0)
 
+    def gain_hop(i, src, to):
+        return copy(src, g_got.at[i, pl.ds(0, src.shape[0])], gs.at[i], gr.at[i], to)
+    hops = {}
+    def gain_step(i):
+        rows4 = lambda at: pl.ds(pl.multiple_of(at * 8, 8), 8)
+        if i == 0:
+            hops[0] = gain_hop(0, g_ref.at[pl.ds(pl.multiple_of((1 - core) * 32, 32), 32)], sibling)
+        elif i == 1:
+            hops[0].wait_recv()
+            g_acc[...] = g_ref[pl.ds(pl.multiple_of(core * 32, 32), 32)] + g_got[0]
+            hops[1] = gain_hop(1, g_acc.at[pl.ds(pl.multiple_of((1 - dp // 2) * 16, 16), 16)], by_y)
+        elif i == 2:
+            hops[1].wait_recv()
+            mine = pl.ds(pl.multiple_of((dp // 2) * 16, 16), 16)
+            g_acc[mine] += g_got[1, :16]
+            hops[2] = gain_hop(2, g_acc.at[rows4(x_at)], by_x)
+        elif i == 3:
+            hops[2].wait_recv()
+            g_acc[rows4(dp)] += g_got[2, :8]
+            for d in range(1, depth):
+                to = (z + d) % depth
+                hops[2 + d] = copy(g_acc.at[pl.ds(dp * 8 + to, 1)], g_z.at[z], gsz.at[d - 1], grz.at[z], (dp, to * 2 + core))
+        if i < 3:
+            hops[i].start()
+        else:
+            for d in range(1, depth):
+                hops[2 + d].start()
+    def gain_end():
+        total = g_acc[pl.ds(dp * 8 + z, 1)]
+        for d in range(1, depth):
+            src = (z + d) % depth
+            copy(g_acc.at[pl.ds(dp * 8, 1)], g_z.at[src], gsz.at[0], grz.at[src], sibling).wait_recv()
+            total += g_z[src]
+        go_ref[...] = total
+        for i in hops:
+            hops[i].wait_send()
     sib_copies, far_copies, near_copies, z_copies = {}, {}, {}, {}
     def sib_step(k):
         slot = k % 2
@@ -393,13 +429,17 @@
             z_copies[k].start()
         else:
             o_ref[...] = total
+    gain_step(0)
     sib_step(0); sib_step(1)
     own_step(0)
+    gain_step(1)
     sib_step(2)
     own_step(1)
+    gain_step(2)
     near_step(0)
     sib_step(3)
     own_step(2)
+    gain_step(3)
     near_step(1)
     plane_step(0)
     own_step(3)
@@ -412,25 +452,29 @@
         src = (z + d) % depth
         copy(plane.at[0], got_z.at[src], s3.at[0], r3.at[src], sibling).wait_recv()
         o_ref[...] += got_z[src].astype(f32)
+    gain_end()
     for k in range(depth):
         if k >= 2: sib_copies[k].wait_send()
         for c in far_copies[k]: c.wait_send()
         for c in near_copies[k]: c.wait_send()
         if k < depth - 1: z_copies[k].wait_send()
 
-def reduce_rows(a, b, rows, cid, special):
-    if not special:
-        part = mm(a, b, TN).astype(bf16)
-        return lax.psum_scatter(part, BOTH, scatter_dimension=0, tiled=True).astype(f32)
+def reduce_rows(a, b, rows, cid, gains=None):
     tokens, width = b.shape
     depth = 4
     at = a.reshape(tokens, 4, depth, 2, rows).transpose(3, 2, 1, 4, 0).reshape(-1, tokens)
     D = pltpu.SemaphoreType.DMA
+    lanes = 256
+    padded = jnp.zeros((32, lanes), f32)
+    if gains is not None:
+        padded = jnp.pad(gains, ((0, 0), (0, lanes - gains.shape[1])))
+    padded = padded.reshape(4, depth, 2, lanes).transpose(2, 0, 1, 3)
+    padded = jnp.pad(padded, ((0, 0), (0, 0), (0, 8 - depth), (0, 0))).reshape(64, lanes)
     return pl.pallas_call(
         functools.partial(reduce_kernel, rows, 4),
-        out_shape=jax.ShapeDtypeStruct((rows, width), f32),
-        in_specs=[pl.BlockSpec(memory_space=pltpu.VMEM)] * 2,
-        out_specs=pl.BlockSpec(memory_space=pltpu.VMEM),
+        out_shape=[jax.ShapeDtypeStruct((rows, width), f32), jax.ShapeDtypeStruct((1, lanes), f32)],
+        in_specs=[pl.BlockSpec(memory_space=pltpu.VMEM)] * 3,
+        out_specs=[pl.BlockSpec(memory_space=pltpu.VMEM)] * 2,
         scratch_shapes=[
             pltpu.VMEM((2, 4 * rows, width), bf16),
             pltpu.VMEM((depth, 4 * rows, width), bf16),
@@ -440,10 +484,181 @@
             pltpu.VMEM((depth - 1, rows, width), bf16),
             pltpu.VMEM((depth, rows, width), bf16),
             D((2,)), D((depth,)), D((depth, 2)), D((depth, 2)), D((depth, 2)), D((depth, 2)), D((depth - 1,)), D((depth,)),
+            pltpu.VMEM((32, lanes), f32), pltpu.VMEM((3, 32, lanes), f32), pltpu.VMEM((depth, 1, lanes), f32),
+            D((3,)), D((3,)), D((depth - 1,)), D((depth,)),
         ],
         compiler_params=pltpu.CompilerParams(vmem_limit_bytes=60*1024*1024, collective_id=cid, has_side_effects=True),
         cost_estimate=pl.CostEstimate(flops=2*tokens*32*rows*width, bytes_accessed=10_000_000, transcendentals=0),
-    )(at, b)
+    )(at, b, padded)
+
+
+ROUTE_LANES = 128
+
+
+def picks_of(routing, first, local_experts, capacity):
+    rows = routing.shape[0]
+    lanes = lax.broadcasted_iota(jnp.int32, (rows, ROUTE_LANES), 1)
+    places = lax.broadcasted_iota(jnp.int32, (rows, local_experts * capacity), 1)
+    hit, weighted = None, 0.0
+    for e in range(local_experts):
+
+        def column(base):
+            return jnp.sum(jnp.where(lanes == base + first + e, routing, 0.0), axis=1, keepdims=True)
+
+        slot = column(0).astype(jnp.int32)
+        here = places == jnp.where(slot >= 0, slot + e * capacity, -1)
+        hit = here if hit is None else hit | here
+        weighted = weighted + jnp.where(here, column(32) + column(64), 0.0)
+    return jnp.where(hit, 1.0, 0.0).astype(bf16), weighted.astype(bf16)
+
+
+def pick_kernel(capacity, local_experts, n_alias, tok_ref, cot_ref, *refs):
+    x_ref, dy_ref = refs[n_alias:]
+    width = tok_ref.shape[2]
+    first = lax.axis_index("expert") * local_experts
+    routing = cot_ref[0, :, width:]
+    hit, _ = picks_of(routing.astype(f32), first, local_experts, capacity)
+    x = mm(hit, tok_ref[0], TN).astype(bf16)
+    rows = mm(hit, routing, TN)
+    lanes = lax.broadcasted_iota(jnp.int32, rows.shape, 1)
+    owner = lax.broadcasted_iota(jnp.int32, rows.shape, 0) // capacity
+    at = lanes - first - owner
+    weight = jnp.sum(jnp.where((at == 32) | (at == 64), rows, 0.0), axis=1, keepdims=True)
+    dy = (mm(hit, cot_ref[0, :, :width], TN) * weight).astype(bf16)
+    for e in range(local_experts):
+        x_ref[e, 0, 0] = x[e * capacity : (e + 1) * capacity]
+        dy_ref[e, 0, 0] = dy[e * capacity : (e + 1) * capacity]
+
+
+def expert_kernel(n_alias, *refs):
+    x_ref, dy_ref = refs[:2]
+    parts = (refs[2:7], refs[7:12], refs[12:17])
+    z_ref, dg_ref, du_ref, y_ref, dx_ref, wg, wu, wd, sems = refs[17 + n_alias :]
+    local_experts, width, _ = wg.shape
+    at = lax.axis_index("dp")
+    size = width // 4
+    places = (at, at + 1 - 2 * (at % 2), (at + 2) % 4, 3 - at, 3 - at)
+
+    def copies(e):
+        out = []
+        for m, full in enumerate((wg, wu, wd)):
+            for p in range(4):
+                part = parts[m][p] if p < 3 else parts[m][3 + e]
+                src = part.at[e] if p < 3 else part.at[0]
+                where = pl.ds(pl.multiple_of(places[p] * size, size), size)
+                dst = full.at[e, where, :] if m < 2 else full.at[e, :, where]
+                out.append(pltpu.make_async_copy(src, dst, sems.at[e, m, p]))
+        return out
+
+    expert, chunk = pl.program_id(0), pl.program_id(1)
+
+    @pl.when((expert == 0) & (chunk == 0))
+    def _():
+        for e in range(local_experts):
+            for c in copies(e):
+                c.start()
+
+    for e in range(local_experts):
+
+        @pl.when((expert == e) & (chunk == 0))
+        def _(e=e):
+            for c in copies(e):
+                c.wait()
+
+    x, dy = x_ref[0, 0], dy_ref[0, 0]
+    gate = mm(x, wg[expert])
+    up = mm(x, wu[expert])
+    d_hidden = mm(dy, wd[expert], NT)
+    sig = 1.0 / (1.0 + jnp.exp(-gate))
+    silu = gate * sig
+    z = (silu * up).astype(bf16)
+    d_gate = (d_hidden * up * sig * (1.0 + gate * (1.0 - sig))).astype(bf16)
+    d_up = (d_hidden * silu).astype(bf16)
+    z_ref[0, 0] = z
+    dg_ref[0, 0] = d_gate
+    du_ref[0, 0] = d_up
+    dx_ref[0] = (mm(d_gate, wg[expert], NT) + mm(d_up, wu[expert], NT)).astype(bf16)
+    y_ref[0] = mm(z, wd[expert]).astype(bf16)
+
+
+def sum_kernel(capacity, routing_ref, y_ref, dx_ref, mix_ref, da_ref):
+    local_experts, _, _, width = y_ref.shape
+    first = lax.axis_index("expert") * local_experts
+    hit, weighted = picks_of(routing_ref[0].astype(f32), first, local_experts, capacity)
+    da_ref[...] = mm(hit, dx_ref[...].reshape(local_experts * capacity, width)).astype(bf16)
+    mix_ref[...] = mm(weighted, y_ref[...].reshape(local_experts * capacity, width)).astype(bf16)
+
+
+def run_experts(tokens, cot, parts, capacity, batch_at, micro, earlier):
+    blocks, rows, width = tokens.shape
+    local_experts, _, hidden = parts[0][0].shape
+    flat = [p for group in parts for p in group]
+    any_spec = pl.BlockSpec(memory_space=pl.ANY)
+    params = pltpu.CompilerParams(vmem_limit_bytes=VMEM_LIMIT)
+    slots = blocks * capacity
+    picked_spec = pl.BlockSpec((local_experts, 1, 1, capacity, width), lambda b: (0, batch_at, b, 0, 0))
+    picked = jax.ShapeDtypeStruct((local_experts, micro, blocks, capacity, width), bf16)
+    x, dy = pl.pallas_call(
+        functools.partial(pick_kernel, capacity, local_experts, len(earlier[:2])),
+        grid=(blocks,),
+        in_specs=[
+            pl.BlockSpec((1, rows, width), lambda b: (b, 0, 0)),
+            pl.BlockSpec((1, rows, cot.shape[2]), lambda b: (b, 0, 0)),
+        ]
+        + [any_spec] * len(earlier[:2]),
+        out_specs=[picked_spec] * 2,
+        out_shape=[picked] * 2,
+        input_output_aliases={2 + i: i for i in range(len(earlier[:2]))},
+        compiler_params=params,
+        cost_estimate=pl.CostEstimate(
+            flops=4 * slots * local_experts * rows * width, bytes_accessed=25_000_000, transcendentals=0
+        ),
+    )(tokens, cot, *[a.reshape(picked.shape) for a in earlier[:2]])
+    x, dy = (a.reshape(local_experts, micro, slots, width) for a in (x, dy))
+    chunk = slots // 2
+    row_spec = pl.BlockSpec((1, 1, chunk, width), lambda e, i: (e, batch_at, i, 0))
+    hid_spec = pl.BlockSpec((1, 1, chunk, hidden), lambda e, i: (e, batch_at, i, 0))
+    out_spec = pl.BlockSpec((1, chunk, width), lambda e, i: (e, i, 0))
+    hid = jax.ShapeDtypeStruct((local_experts, micro, slots, hidden), bf16)
+    out = jax.ShapeDtypeStruct((local_experts, slots, width), bf16)
+    z, dg, du, y, dx = pl.pallas_call(
+        functools.partial(expert_kernel, len(earlier[2:])),
+        grid=(local_experts, 2),
+        in_specs=[row_spec, row_spec] + [any_spec] * (len(flat) + len(earlier[2:])),
+        out_specs=[hid_spec] * 3 + [out_spec] * 2,
+        out_shape=[hid] * 3 + [out] * 2,
+        input_output_aliases={2 + len(flat) + i: i for i in range(len(earlier[2:]))},
+        scratch_shapes=[
+            pltpu.VMEM((local_experts, width, hidden), bf16),
+            pltpu.VMEM((local_experts, width, hidden), bf16),
+            pltpu.VMEM((local_experts, hidden, width), bf16),
+            pltpu.SemaphoreType.DMA((local_experts, 3, 4)),
+        ],
+        compiler_params=params,
+        cost_estimate=pl.CostEstimate(
+            flops=12 * local_experts * slots * width * hidden, bytes_accessed=50_000_000, transcendentals=0
+        ),
+    )(x, dy, *flat, *earlier[2:])
+    y, dx = (a.reshape(local_experts, blocks, capacity, width) for a in (y, dx))
+    part_spec = pl.BlockSpec((local_experts, 1, capacity, width), lambda b: (0, b, 0, 0))
+    sums = jax.ShapeDtypeStruct((blocks * rows, width), bf16)
+    sums_spec = pl.BlockSpec((rows, width), lambda b: (b, 0))
+    mix, da = pl.pallas_call(
+        functools.partial(sum_kernel, capacity),
+        grid=(blocks,),
+        in_specs=[
+            pl.BlockSpec((1, rows, ROUTE_LANES), lambda b: (b, 0, width // ROUTE_LANES)),
+            part_spec,
+            part_spec,
+        ],
+        out_specs=[sums_spec] * 2,
+        out_shape=[sums] * 2,
+        compiler_params=params,
+        cost_estimate=pl.CostEstimate(
+            flops=4 * slots * local_experts * rows * width, bytes_accessed=25_000_000, transcendentals=0
+        ),
+    )(cot, y, dx)
+    return [x, dy, z, dg, du], mix, da
 
 
 def slots_of(route_ids, gate_vals, ranking, capacity, experts):
@@ -465,47 +680,27 @@
     return lax.ppermute(values, "dp", [(i, i ^ bit) for i in range(lax.axis_size("dp"))])
 
 
-def gather_parts(own, axis):
-    if lax.axis_size("dp") != 4:
-        return lax.all_gather(own, "dp", axis=axis, tiled=True)
-    at = lax.axis_index("dp")
-    size = own.shape[axis]
-    by_x, by_y = swap(own, 1), swap(own, 2)
-    far_0, far_1 = swap(by_x[:1], 2), swap(by_y[1:], 1)
-    shape = list(own.shape)
-    shape[axis] *= 4
-    full = jnp.zeros(tuple(shape), own.dtype)
-    for part, expert, bits in ((own, 0, 0), (by_x, 0, 1), (by_y, 0, 2), (far_0, 0, 3), (far_1, 1, 3)):
-        start = [expert, 0, 0]
-        start[axis] = (at ^ bits) * size
-        full = lax.dynamic_update_slice(full, part, tuple(start))
-    return full
-
-
 def scatter_far(total, axis):
-    if lax.axis_size("dp") != 4:
-        low = total.astype(bf16)
-        return [lax.psum_scatter(low, "dp", scatter_dimension=axis, tiled=True)]
     at = lax.axis_index("dp")
     size = total.shape[axis] // 4
 
     def part(bits):
         return lax.dynamic_slice_in_dim(total, (at ^ bits) * size, size, axis=axis)
 
-    far = part(3).astype(bf16)
+    far = part(3)
     return [swap(far[:1], 1), swap(far[1:], 2), part(1), part(2), part(0)]
 
 
-def scatter_near(for_y, for_x=None, near_x=None, near_y=None, own=None):
-    if for_x is None:
-        return for_y.astype(f32)
-    near_y = jnp.concatenate([near_y[:1] + for_y.astype(f32), near_y[1:]], axis=0).astype(bf16)
-    near_x = jnp.concatenate([near_x[:1], near_x[1:] + for_x.astype(f32)], axis=0).astype(bf16)
+def scatter_near(for_y, for_x, near_x, near_y, own):
+    half_y = (near_y[:1].astype(f32) + for_y.astype(f32)).astype(bf16)
+    half_x = (near_x[1:].astype(f32) + for_x.astype(f32)).astype(bf16)
+    near_y = jnp.concatenate([half_y, near_y[1:]], axis=0)
+    near_x = jnp.concatenate([near_x[:1], half_x], axis=0)
     by_x, by_y = swap(near_x, 1), swap(near_y, 2)
-    return own + by_x.astype(f32) + by_y.astype(f32)
-
-
-def body(
+    return own.astype(f32) + by_x.astype(f32) + by_y.astype(f32)
+
+
+def body_plain(
     inputs,
     cotangent,
     membership,
@@ -536,29 +731,22 @@
     total = micro * rows
     q_part, k_part, v_part = w_query.shape[1], w_key.shape[1], w_value.shape[1]
 
-    special = blocks == 8 and shards == 32
-
     gain_len = norm_gains.shape[0]
     gain_shard = jnp.zeros((2048,), bf16).at[:gain_len].set(norm_gains).reshape(16, 128)
-    qkv_w = jnp.concatenate([w_query.T, w_key.T, w_value.T], axis=0)
-    if special:
-        qkv_w, out_w, gain_full = gather_rows([qkv_w, w_output, gain_shard], [(2, 0, 1)], 1)
-    else:
-        qkv_w, out_w, gain_full = (
-            lax.all_gather(part, BOTH, axis=0, tiled=True) for part in (qkv_w, w_output, gain_shard)
-        )
-    d_out_all = lax.all_gather(cotangent[:, 0], "expert", axis=0, tiled=False)
-    qkv_w, d_out_all = lax.optimization_barrier((qkv_w, d_out_all))
+    gain_full = lax.all_gather(gain_shard, BOTH, axis=0, tiled=True)
     gains = gain_full.reshape(shards, 2048)[:, :gain_len].reshape(-1).astype(f32)
     gain_in = gains[:width]
     gain_mid = gains[width : 2 * width]
     gain_q = gains[2 * width : 2 * width + HD]
     gain_k = gains[2 * width + HD :]
 
-    w_gate, w_up, w_down, qkv_w = lax.optimization_barrier((w_gate, w_up, w_down, qkv_w))
-    wg = gather_parts(w_gate, 1)
-    wu = gather_parts(w_up, 1)
-    wd = gather_parts(w_down, 2)
+    qkv_w = lax.all_gather(
+        jnp.concatenate([w_query.T, w_key.T, w_value.T], axis=0), BOTH, axis=0, tiled=True
+    )
+    out_w = lax.all_gather(w_output, BOTH, axis=0, tiled=True)
+    wg = lax.all_gather(w_gate, "dp", axis=1, tiled=True)
+    wu = lax.all_gather(w_up, "dp", axis=1, tiled=True)
+    wd = lax.all_gather(w_down, "dp", axis=2, tiled=True)
 
     slot_map, weight_map = jax.vmap(
         lambda r, g, o: slots_of(r, g, o, capacity, experts)
@@ -617,12 +805,12 @@
     middle = middle.reshape(micro, rows, width)
     scale_mid = scale_mid.reshape(micro, rows, 1)
 
-    mix_parts, d_routeds, d_branches, d_middles = [], [], [], []
+    outputs, d_branches, d_middles = [], [], []
     acc_gate = acc_up = acc_down = 0.0
     grad_mid = 0.0
     slots = blocks * capacity
     for at in range(micro):
-        d_out = d_out_all[:, at]
+        d_out = lax.all_gather(cotangent[at, 0], "expert", axis=0, tiled=False)
         tokens = lax.all_gather(routed[at], "expert", axis=0, tiled=False)
         picked = jnp.einsum("ebst,btd->ebsd", pick[at], tokens, preferred_element_type=f32)
         picked = picked.astype(bf16).reshape(local_experts, slots, width)
@@ -646,37 +834,31 @@
         result = jnp.einsum("erf,efd->erd", hidden_low, wd, preferred_element_type=f32)
         result = result.astype(bf16).reshape(local_experts, blocks, capacity, width)
         part = jnp.einsum("ebst,ebsd->btd", weighted[at], result, preferred_element_type=f32)
-        mix_parts.append(part.astype(bf16).reshape(group_len, width))
-        d_routeds.append(d_routed)
+        part = part.astype(bf16).reshape(group_len, width)
+        expert_mix = lax.psum_scatter(part, "expert", scatter_dimension=0, tiled=True).astype(f32)
+        outputs.append((middle[at] + expert_mix).astype(bf16))
 
         acc_down += jnp.einsum("erf,erd->efd", hidden_low, d_result, preferred_element_type=f32)
         acc_gate += jnp.einsum("erd,erf->edf", picked, d_gate, preferred_element_type=f32)
         acc_up += jnp.einsum("erd,erf->edf", picked, d_up, preferred_element_type=f32)
 
-    scattering = [scatter_far(acc, axis) for acc, axis in ((acc_gate, 1), (acc_up, 1), (acc_down, 2))]
-    d_routeds[-1], scattering = lax.optimization_barrier((d_routeds[-1], scattering))
-    expert_grads = [scatter_near(*parts) for parts in scattering]
-    for at in range(micro):
-        d_mid_norm, mid_gain_grad = norm_back(d_routeds[at], middle[at], scale_mid[at], gain_mid)
+        d_mid_norm, mid_gain_grad = norm_back(d_routed, middle[at], scale_mid[at], gain_mid)
         grad_mid = grad_mid + mid_gain_grad
         d_middle = cotangent[at, 0].astype(f32) + d_mid_norm
         d_middles.append(d_middle)
         d_branches.append(d_middle.astype(bf16))
 
+    grad_gate = lax.psum_scatter(acc_gate.astype(bf16), "dp", scatter_dimension=1, tiled=True)
+    grad_up = lax.psum_scatter(acc_up.astype(bf16), "dp", scatter_dimension=1, tiled=True)
+    grad_down = lax.psum_scatter(acc_down.astype(bf16), "dp", scatter_dimension=2, tiled=True)
+
     d_branch = jnp.concatenate(d_branches, axis=0)
     d_middle = jnp.concatenate(d_middles, axis=0)
+    grad_output = mm(mixed.reshape(total, H * HD), d_branch, TN).astype(bf16)
+    grad_output = lax.psum_scatter(grad_output, BOTH, scatter_dimension=0, tiled=True)
     d_mixed = mm(d_branch, out_w, NT).astype(bf16).reshape(micro, rows, H * HD)
     dq_low, dkv_all = run_backward(q_low, kv_all, bias, mixed, d_mixed, logs, step_heads, chunk)
-    mixed_after, dq_low, dkv_all, expert_grads = lax.optimization_barrier(
-        (mixed, dq_low, dkv_all, expert_grads)
-    )
-    grad_output = reduce_rows(mixed_after.reshape(total, H * HD), d_branch, w_output.shape[0], 2, special)
     dkv = lax.psum_scatter(dkv_all, "expert", scatter_dimension=0, tiled=False)
-    mix_parts, dkv, grad_output = lax.optimization_barrier((mix_parts, dkv, grad_output))
-    outputs = []
-    for at in range(micro):
-        mix = lax.psum_scatter(mix_parts[at], "expert", scatter_dimension=0, tiled=True)
-        outputs.append((middle[at] + mix.astype(f32)).astype(bf16))
     dkv = dkv.reshape(total, KVH, 2 * HD)
     d_query = rotate(dq_low.reshape(total, H, HD).astype(f32), cosine, -sine_part)
     d_query, grad_qn = norm_back(d_query, queries, scale_q, gain_q)
@@ -690,7 +872,8 @@
         ],
         axis=-1,
     ).reshape(total, -1)
-    grad_qkv = reduce_rows(d_proj, normed, q_part + k_part + v_part, 3, special)
+    grad_qkv = mm(d_proj, normed, TN).astype(bf16)
+    grad_qkv = lax.psum_scatter(grad_qkv, BOTH, scatter_dimension=0, tiled=True).astype(f32)
     d_normed = mm(d_proj, qkv_w)
     d_in_norm, grad_in = norm_back(d_normed, hidden, scale_in, gain_in)
     input_grad = d_middle + d_in_norm
@@ -705,15 +888,209 @@
         grad_qkv[:q_part].T,
         grad_qkv[q_part : q_part + k_part].T,
         grad_qkv[q_part + k_part :].T,
+        grad_output.astype(f32),
+        grad_gains[:gain_len],
+        grad_gate.astype(f32),
+        grad_up.astype(f32),
+        grad_down.astype(f32),
+    )
+
+
+def body_fast(
+    inputs,
+    cotangent,
+    membership,
+    routes,
+    gate_weights,
+    pair_order,
+    w_query,
+    w_key,
+    w_value,
+    w_output,
+    norm_gains,
+    w_gate,
+    w_up,
+    w_down,
+):
+    micro = inputs.shape[0]
+    rows = inputs.shape[2]
+    width = inputs.shape[3]
+    group_len = membership.shape[2]
+    member = lax.axis_index("expert")
+    blocks = lax.axis_size("expert")
+    shards = blocks * lax.axis_size("dp")
+    local_experts = w_gate.shape[0]
+    experts = local_experts * blocks
+    capacity = rows * TOPK // experts
+    step_heads = max(1, 384 // rows)
+    total = micro * rows
+    q_part, k_part, v_part = w_query.shape[1], w_key.shape[1], w_value.shape[1]
+    tie = lax.optimization_barrier
+
+    slot_map, weight_map = jax.vmap(
+        lambda r, g, o: slots_of(r, g, o, capacity, experts)
+    )(routes[:, 0], gate_weights[:, 0], pair_order[:, 0, 0])
+    weight_high = tie(weight_map.astype(bf16))
+    weight_low = (weight_map - weight_high.astype(f32)).astype(bf16)
+
+    def padded(values, lanes):
+        return jnp.pad(values, ((0, 0), (0, 0), (0, lanes - experts)))
+
+    cot_rows = jnp.concatenate(
+        [
+            cotangent[:, 0],
+            padded(slot_map.astype(bf16), 32),
+            padded(weight_high, 32),
+            padded(weight_low, ROUTE_LANES - 64),
+        ],
+        axis=-1,
+    )
+
+    gain_len = norm_gains.shape[0]
+    gain_shard = jnp.zeros((2048,), bf16).at[:gain_len].set(norm_gains).reshape(16, 128)
+    qkv_w = jnp.concatenate([w_query.T, w_key.T, w_value.T], axis=0)
+    qkv_w, out_w, gain_full = gather_rows([qkv_w, w_output, gain_shard], [(2, 0, 1)], 1)
+    qkv_w, cot_0, cot_1, w_gate, w_up, w_down = tie(
+        (qkv_w, cot_rows[0], cot_rows[1], w_gate, w_up, w_down)
+    )
+    gains = gain_full.reshape(shards, 2048)[:, :gain_len].reshape(-1).astype(f32)
+    gain_in = gains[:width]
+    gain_mid = gains[width : 2 * width]
+    gain_q = gains[2 * width : 2 * width + HD]
+    gain_k = gains[2 * width + HD :]
+    cot_0 = lax.all_gather(cot_0, "expert", axis=0, tiled=False)
+    cot_1 = lax.all_gather(cot_1, "expert", axis=0, tiled=False)
+    gate_near, up_near, down_near = ((swap(w, 1), swap(w, 2)) for w in (w_gate, w_up, w_down))
+
+    key_index = jnp.arange(group_len, dtype=jnp.int32)
+    start_row = member * rows
+    segment = membership[:, 0]
+    row_index = start_row + jnp.arange(rows, dtype=jnp.int32)
+    seg_rows = lax.dynamic_slice_in_dim(segment, start_row, rows, axis=1)
+    before = jnp.sum((segment[:, None, :] < seg_rows[:, :, None]).astype(jnp.int32), axis=2)
+    position = jnp.where(seg_rows == 0, row_index[None], PROMPT + row_index[None] - before)
+    allowed = (key_index[None, :, None] <= row_index[None, None, :]) & (
+        (segment[:, :, None] == 0) | (segment[:, :, None] == seg_rows[:, None, :])
+    )
+    bias = jnp.tile(jnp.where(allowed, 0.0, MASKED).astype(f32), (1, 1, step_heads))
+    frequency = ROPE_BASE ** (-(jnp.arange(HD // 2, dtype=f32) * 2.0 / HD))
+    angles = position.astype(f32).reshape(total)[:, None] * frequency[None, :]
+    cosine = jnp.cos(angles)[:, None, :]
+    sine_part = jnp.sin(angles)[:, None, :]
+
+    hidden = inputs[:, 0].astype(f32).reshape(total, width)
+    scale_in = rms_scale(hidden)
+    normed = (hidden * scale_in * gain_in).astype(bf16)
+    proj = mm(normed, qkv_w, NT).reshape(total, shards, q_part + k_part + v_part)
+    queries = proj[:, :, :q_part].reshape(total, H, HD)
+    key_pre = proj[:, :, q_part : q_part + k_part].reshape(total, KVH, HD)
+    value = proj[:, :, q_part + k_part :].reshape(total, KVH, HD).astype(bf16)
+    scale_q = rms_scale(queries)
+    scale_k = rms_scale(key_pre)
+    q_low = rotate(queries * scale_q * (gain_q * (SCALE * LOG2E)), cosine, sine_part).astype(bf16)
+    q_low = q_low.reshape(micro, rows, H * HD)
+    k_low = rotate(key_pre * scale_k * gain_k, cosine, sine_part).astype(bf16)
+    kv_own = jnp.concatenate([k_low, value], axis=-1).reshape(micro, rows, KVH * 2 * HD)
+    kv_own, cot_0, gate_near = tie((kv_own, cot_0, gate_near))
+    kv_all = lax.all_gather(kv_own, "expert", axis=0, tiled=False)
+    kv_all, up_near, down_near = tie((kv_all, up_near, down_near))
+    parts = [
+        (own, near[0], near[1], swap(near[0][:1], 2), swap(near[1][1:], 1))
+        for own, near in ((w_gate, gate_near), (w_up, up_near), (w_down, down_near))
+    ]
+    chunk = 256
+    mixed, logs = run_forward(q_low, kv_all, bias, step_heads, chunk)
+
+    branch = mm(mixed.reshape(total, H * HD), out_w)
+    middle = hidden + branch
+    scale_mid = rms_scale(middle)
+    routed = (middle * scale_mid * gain_mid).astype(bf16).reshape(micro, rows, width)
+    routed, parts, cot_1 = tie((routed, parts, cot_1))
+    middle = middle.reshape(micro, rows, width)
+    scale_mid = scale_mid.reshape(micro, rows, 1)
+
+    mix_parts, d_routeds, d_branches, d_middles = [], [], [], []
+    kept = []
+    for at, cot in enumerate((cot_0, cot_1)):
+        tokens = lax.all_gather(routed[at], "expert", axis=0, tiled=False)
+        kept, mix, d_part = run_experts(tokens, cot, parts, capacity, at, micro, kept)
+        kept, d_part, mix = tie((kept, d_part, mix))
+        mix_parts.append(mix)
+        d_routed = lax.psum_scatter(d_part, "expert", scatter_dimension=0, tiled=True)
+        d_routeds.append(d_routed)
+    picked, d_result, hidden_low, d_gate, d_up = (
+        a.reshape(local_experts, -1, a.shape[-1]) for a in kept
+    )
+
+    def weight_grad(rows_in, rows_out):
+        return jnp.einsum("era,erb->eab", rows_in, rows_out, preferred_element_type=f32).astype(bf16)
+
+    scattering = [
+        scatter_far(weight_grad(hidden_low, d_result), 2),
+        scatter_far(weight_grad(picked, d_gate), 1),
+        scatter_far(weight_grad(picked, d_up), 1),
+    ]
+    d_routeds[-1], scattering = tie((d_routeds[-1], scattering))
+    expert_grads = [scatter_near(*pieces) for pieces in scattering]
+    grad_mid = 0.0
+    for at in range(micro):
+        d_mid_norm, mid_gain_grad = norm_back(
+            d_routeds[at].astype(f32), middle[at], scale_mid[at], gain_mid
+        )
+        grad_mid = grad_mid + mid_gain_grad
+        d_middle = cotangent[at, 0].astype(f32) + d_mid_norm
+        d_middles.append(d_middle)
+        d_branches.append(d_middle.astype(bf16))
+
+    d_branch = jnp.concatenate(d_branches, axis=0)
+    d_middle = jnp.concatenate(d_middles, axis=0)
+    d_mixed = mm(d_branch, out_w, NT).astype(bf16).reshape(micro, rows, H * HD)
+    dq_low, dkv_all = run_backward(q_low, kv_all, bias, mixed, d_mixed, logs, step_heads, chunk)
+    mixed_after, dq_low, dkv_all, expert_grads = tie((mixed, dq_low, dkv_all, expert_grads))
+    grad_output, _ = reduce_rows(mixed_after.reshape(total, H * HD), d_branch, w_output.shape[0], 2)
+    dkv = lax.psum_scatter(dkv_all, "expert", scatter_dimension=0, tiled=False)
+    dkv, grad_output, dq_low = tie((dkv, grad_output, dq_low))
+    dkv = dkv.reshape(total, KVH, 2 * HD)
+    mix_parts, dkv = tie((mix_parts, dkv))
+    outputs = []
+    for at in range(micro):
+        mix = lax.psum_scatter(mix_parts[at], "expert", scatter_dimension=0, tiled=True)
+        outputs.append((middle[at] + mix.astype(f32)).astype(bf16))
+    d_query = rotate(dq_low.reshape(total, H, HD).astype(f32), cosine, -sine_part)
+    d_query, grad_qn = norm_back(d_query, queries, scale_q, gain_q)
+    d_key = rotate(dkv[:, :, :HD].astype(f32), cosine, -sine_part)
+    d_key, grad_kn = norm_back(d_key, key_pre, scale_k, gain_k)
+    d_proj = jnp.concatenate(
+        [
+            d_query.astype(bf16).reshape(total, shards, q_part),
+            d_key.astype(bf16).reshape(total, shards, k_part),
+            dkv[:, :, HD:].reshape(total, shards, v_part),
+        ],
+        axis=-1,
+    ).reshape(total, -1)
+    d_normed = mm(d_proj, qkv_w)
+    d_in_norm, grad_in = norm_back(d_normed, hidden, scale_in, gain_in)
+    input_grad = d_middle + d_in_norm
+    gain_grads = jnp.concatenate([grad_in, grad_mid, grad_qn, grad_kn]).reshape(shards, gain_len)
+    grad_qkv, grad_gains = reduce_rows(d_proj, normed, q_part + k_part + v_part, 3, gain_grads)
+    return (
+        jnp.stack(outputs)[:, None],
+        input_grad.reshape(micro, 1, rows, width),
+        grad_qkv[:q_part].T,
+        grad_qkv[q_part : q_part + k_part].T,
+        grad_qkv[q_part + k_part :].T,
         grad_output,
-        grad_gains[:gain_len],
-        *expert_grads,
+        grad_gains[0, :gain_len],
+        expert_grads[1],
+        expert_grads[2],
+        expert_grads[0],
     )
 
 
 def solution(mesh):
+    fast = mesh.shape["dp"] == 4 and mesh.shape["expert"] == 8
     return jax.shard_map(
-        body,
+        body_fast if fast else body_plain,
         mesh=mesh,
         in_specs=(
             P(None, "dp", "expert", None),

time: 1430 us -> 1200 us (0.84)
  matrix products: 284 us -> 101 us
  Pallas kernels: 555 us -> 608 us
  local copies, waits for them, and re-layouts: 177 us -> 140 us
  waiting for transfers between devices: 235 us -> 211 us
  blocking collectives: 17.7 us -> 0 us
  other arithmetic: 103 us -> 88.4 us
    dot_general x26 -> x3, matrix products: 231 us -> 48.2 us  [weight_grad(): jnp.einsum('era,erb->eab', rows_in, rows_out, preferred_element_type=f32)]
    pallas_call x2 -> x8, Pallas kernels: 242 us -> 342 us  [the longest x2 209 us: reduce_rows(): pl.pallas_call(functools.partial(reduce_kernel, rows, 4), out_shape=[jax....]
    ppermute x24, waiting for transfers between devices: 111 us -> 59.2 us  [swap(): lax.ppermute(values, 'dp', [(i, i ^ bit) for i in range(lax.axis_size('dp...]
    pallas_call x1, Pallas kernels: 207 us -> 160 us  [gather_rows(): pl.pallas_call(functools.partial(gather_kernel, phases, len(arrays)), out...]
    all_gather x5, waiting for transfers between devices: 48.5 us -> 90.2 us  [the longest x2 63 us: body_fast(): tokens = lax.all_gather(routed[at], 'expert', axis=0, tiled=False)]
    dynamic_update_slice x15 -> x0, local copies, waits for them, and re-layouts: 23.7 us -> none  [gather_parts(): full = lax.dynamic_update_slice(full, part, tuple(start))]
    all_gather x1 -> x0, blocking collectives: 17.7 us -> none  [body(): routing = lax.all_gather(routing, 'expert', axis=0, tiled=False)]
    reduce_scatter x5, waiting for transfers between devices: 73.3 us -> 58.6 us  [the longest x2 58.6 us: body_fast(): lax.psum_scatter(d_part, 'expert', scatter_dimension=0, tiled=True)]
  transfers between devices with their start and end apart: 34 -> 34, of which waited for: 13 -> 10; matrix products, arithmetic and copies ran while one was open for 33% -> 25% of each run, Pallas kernels for 36% -> 32%
where the time goes in v3:
time: 1200 us; the launch traced here: 1190 us
  Pallas kernels  608 us (51%)
  waiting for transfers between devices  211 us (18%)
  local copies, waits for them, and re-layouts  140 us (12%)
  matrix products  101 us (8%)
  other arithmetic  88.4 us (7%)
  starting transfers between devices  28.8 us (2%)
  between operations  15.7 us (1%)
    pallas_call x2, Pallas kernels, reduce_rows(): pl.pallas_call(functools.partial(reduce_kernel, rows, 4), out_shape=[jax....  209 us
    pallas_call x1, Pallas kernels, gather_rows(): pl.pallas_call(functools.partial(gather_kernel, phases, len(arrays)), out...  160 us
    pallas_call x2, Pallas kernels, run_experts(): pl.pallas_call(functools.partial(expert_kernel, len(earlier[2:])), grid=(...  80.1 us
    all_gather x2, waiting for transfers between devices, body_fast(): tokens = lax.all_gather(routed[at], 'expert', axis=0, tiled=False)  63 us
    pallas_call x1, Pallas kernels, run_backward(): pl.pallas_call(functools.partial(attend_backward, step_heads, chunk), gri...  61.8 us
    ppermute x24, waiting for transfers between devices, swap(): lax.ppermute(values, 'dp', [(i, i ^ bit) for i in range(lax.axis_size('dp...  59.2 us
    reduce_scatter x2, waiting for transfers between devices, body_fast(): lax.psum_scatter(d_part, 'expert', scatter_dimension=0, tiled=True)  58.6 us
    dot_general x4, matrix products, mm(): return lax.dot_general(a, b, dims, preferred_element_type=f32)  53.1 us
  transfers between devices with their start and end apart: 34, of which 10 were waited for; matrix products, arithmetic and copies ran while one was open for 25% of the time, Pallas kernels for 32%

profile of v3, /device:TPU:8, one launch (start us, length us, event | category | flops | bytes accessed | tf_op | source)
XLA Modules:
  0.0 1193.0 jit_solution(10930278538989520221)
XLA Ops:
  19.1 160.2 %shard_map.213 = (bf16[5120,2048]{1,0:T(8,128)(2,1)}, bf16[4096,2048]{1,0:T(8,128)(2,1)}, bf16[512,128]{1,0:T(8,128)(2,1)}) custom-call(bf16[160,2048]{1,0:T(8,128)(2,1)} %pad_maximum_fusion.13.refs_0_, bf16[128,2048]{1,0:T(8,128)(2,1)} %refs_1_.1, bf16[16,128]{1,0:T(8,128)(2,1)} %pad_bitcast_fusion.refs_2_), custom_call_target="tpu_custom_call" | custom-call | bytes 400000000 | tf_op jit(solution)/shard_map/pallas_call | solution.py:299
  184.8 14.7 %fusion.40 = f32[384,32,160]{0,2,1:T(8,128)S(1)} fusion(bf16[384,2048,1]{1,0,2:T(8,128)(2,1)S(1)} %bitcast.200, bf16[32,160,2048]{2,1,0:T(8,128)(2,1)} %bitcast.219), kind=kOutput, calls=%fused_computation.171 | convolution fusion | flops 8053063680 | bytes 30408704 | tf_op jit(solution)/shard_map/dot_general | solution.py:35
  218.2 27.1 %all-gather.13.cloned.1.call-done = bf16[1536,2176]{1,0:T(8,128)(2,1)} async-done(((bf16[192,2176]{1,0:T(8,128)(2,1)}), bf16[1536,2176]{1,0:T(8,128)(2,1)}) %all-gather.13.cloned.1.call-update) | async-done | bytes 6684688 | tf_op jit(solution)/shard_map/all_gather | solution.py:961
  287.9 29.6 %collective-permute-done.4.refs_13_ = bf16[2,768,512]{2,1,0:T(8,128)(2,1)} collective-permute-done((bf16[2,768,512]{2,1,0:T(8,128)(2,1)}, bf16[2,768,512]{2,1,0:T(8,128)(2,1)}, u32[]{:S(2)}, u32[]{:S(2)}) %collective-permute-start.4) | collective-permute-done | bytes 1572896 | tf_op jit(solution)/shard_map/ppermute | solution.py:680
  327.8 43.8 %shard_map.214 = (bf16[2,192,4096]{2,1,0:T(8,128)(2,1)}, f32[2,4,4,384]{3,2,1,0:T(4,128)}) custom-call(bf16[2,192,4096]{2,1,0:T(8,128)(2,1)} %convert_element_type.239.q_ref, bf16[8,2,192,1024]{3,2,1,0:T(8,128)(2,1)} %bitcast.220, f32[2,1536,384]{2,1,0:T(8,128)} %copy.136.bias_ref), custom_call_target="tpu_custom_call" | custom-call | flops 9663676416 | bytes 20000000 | tf_op jit(solution)/shard_map/pallas_call | solution.py:133
  371.6 11.4 multiply_reduce_fusion.3
  387.6 15.2 %collective-permute-done.9.refs_11_ = bf16[1,512,768]{2,1,0:T(8,128)(2,1)} collective-permute-done((bf16[1,512,768]{2,1,0:T(8,128)(2,1)}, bf16[1,512,768]{2,1,0:T(8,128)(2,1)}, u32[]{:S(2)}, u32[]{:S(2)}) %collective-permute-start.9) | collective-permute-done | bytes 786464 | tf_op jit(solution)/shard_map/ppermute | solution.py:680
  404.7 63.0 %all-gather.9.cloned.1.call-done.tok_ref = bf16[8,192,2048]{2,1,0:T(8,128)(2,1)} async-done(((bf16[1,192,2048]{2,1,0:T(8,128)(2,1)}), bf16[8,192,2048]{2,1,0:T(8,128)(2,1)}) %all-gather.9.cloned.1.call-update) | async-done | bytes 6291472 | tf_op jit(solution)/shard_map/all_gather | solution.py:1015
  467.7 14.2 %shard_map.215 = (bf16[2,2,8,96,2048]{4,3,2,1,0:T(8,128)(2,1)}, bf16[2,2,8,96,2048]{4,3,2,1,0:T(8,128)(2,1)}) custom-call(bf16[8,192,2048]{2,1,0:T(8,128)(2,1)} %all-gather.9.cloned.1.call-done.tok_ref, bf16[8,192,2176]{2,1,0:T(8,128)(2,1)} %bitcast.160), custom_call_target="tpu_custom_call" | custom-call | flops 2415919104 | bytes 25000000 | tf_op jit(solution)/shard_map/pallas_call | solution.py:601
  481.9 39.9 %shard_map.216 = (bf16[2,2,768,768]{3,2,1,0:T(8,128)(2,1)}, bf16[2,2,768,768]{3,2,1,0:T(8,128)(2,1)}, bf16[2,2,768,768]{3,2,1,0:T(8,128)(2,1)}, bf16[2,768,2048]{2,1,0:T(8,128)(2,1)}, bf16[2,768,2048]{2,1,0:T(8,128)(2,1)}) custom-call(bf16[2,2,768,2048]{3,2,1,0:T(8,128)(2,1)} %bitcast.163, bf16[2,2,768,2048]{3,2,1,0:T(8,128)(2,1)} %bitcast.167, ...), custom_call_target="tpu_custom_call" | custom-call | flops 28991029248 | bytes 50000000 | tf_op jit(solution)/shard_map/pallas_call | solution.py:624
  521.8 12.7 %shard_map.217 = (bf16[1536,2048]{1,0:T(8,128)(2,1)}, bf16[1536,2048]{1,0:T(8,128)(2,1)}) custom-call(bf16[8,192,2176]{2,1,0:T(8,128)(2,1)} %bitcast.161, bf16[2,8,96,2048]{3,2,1,0:T(8,128)(2,1)} %bitcast.187, bf16[2,8,96,2048]{3,2,1,0:T(8,128)(2,1)} %bitcast.188), custom_call_target="tpu_custom_call" | custom-call | flops 2415919104 | bytes 25000000 | tf_op jit(solution)/shard_map/pallas_call | solution.py:646
  534.5 14.1 %shard_map.218 = (bf16[2,2,8,96,2048]{4,3,2,1,0:T(8,128)(2,1)}, bf16[2,2,8,96,2048]{4,3,2,1,0:T(8,128)(2,1)}) custom-call(bf16[8,192,2048]{2,1,0:T(8,128)(2,1)} %all-gather.11.cloned.1.call-done.tok_ref, bf16[8,192,2176]{2,1,0:T(8,128)(2,1)} %bitcast.158, ...), custom_call_target="tpu_custom_call", output_to_operand_aliasing={{0}: (2, {}), {1}: (3, {})} | custom-call | flops 2415919104 | bytes 25000000 | tf_op jit(solution)/shard_map/pallas_call | solution.py:601
  548.6 40.2 %shard_map.219 = (bf16[2,2,768,768]{3,2,1,0:T(8,128)(2,1)}, bf16[2,2,768,768]{3,2,1,0:T(8,128)(2,1)}, bf16[2,2,768,768]{3,2,1,0:T(8,128)(2,1)}, bf16[2,768,2048]{2,1,0:T(8,128)(2,1)}, bf16[2,768,2048]{2,1,0:T(8,128)(2,1)}) custom-call(bf16[2,2,768,2048]{3,2,1,0:T(8,128)(2,1)} %bitcast.164, ...), custom_call_target="tpu_custom_call", output_to_operand_aliasing={{0}: (17, {}), {1}: (18, {}), {2}: (19, {})} | custom-call | flops 28991029248 | bytes 50000000 | tf_op jit(solution)/shard_map/pallas_call | solution.py:624
  588.8 12.7 %shard_map.220 = (bf16[1536,2048]{1,0:T(8,128)(2,1)}, bf16[1536,2048]{1,0:T(8,128)(2,1)}) custom-call(bf16[8,192,2176]{2,1,0:T(8,128)(2,1)} %bitcast.159, bf16[2,8,96,2048]{3,2,1,0:T(8,128)(2,1)} %bitcast.185, bf16[2,8,96,2048]{3,2,1,0:T(8,128)(2,1)} %bitcast.186), custom_call_target="tpu_custom_call" | custom-call | flops 2415919104 | bytes 25000000 | tf_op jit(solution)/shard_map/pallas_call | solution.py:646
  602.5 17.0 %convolution_convert_fusion.1 = bf16[2,2048,768]{2,1,0:T(8,128)(2,1)} fusion(bf16[2,1536,2048]{2,1,0:T(8,128)(2,1)} %bitcast.165, bf16[2,1536,768]{2,1,0:T(8,128)(2,1)} %bitcast.224), kind=kOutput, calls=%fused_computation.8 | convolution fusion | flops 9666822144 | bytes 23592960 | tf_op jit(solution)/shard_map/era,erb->eab/dot_general | solution.py:1026
  625.1 16.9 %convolution_convert_fusion.2 = bf16[2,2048,768]{2,1,0:T(8,128)(2,1)} fusion(bf16[2,1536,2048]{2,1,0:T(8,128)(2,1)} %bitcast.166, bf16[2,1536,768]{2,1,0:T(8,128)(2,1)} %bitcast.223), kind=kOutput, calls=%fused_computation.9 | convolution fusion | flops 9666822144 | bytes 23592960 | tf_op jit(solution)/shard_map/era,erb->eab/dot_general | solution.py:1026
  645.7 14.2 %convolution_convert_fusion.3 = bf16[2,768,2048]{2,1,0:T(8,128)(2,1)} fusion(bf16[2,1536,768]{2,1,0:T(8,128)(2,1)} %bitcast.222, bf16[2,1536,2048]{2,1,0:T(8,128)(2,1)S(1)} %bitcast.171), kind=kOutput, calls=%fused_computation.10 | convolution fusion | flops 9666822144 | bytes 23592960 | tf_op jit(solution)/shard_map/era,erb->eab/dot_general | solution.py:1026
  681.7 58.6 %reduce-scatter.6.cloned.1.call-done = bf16[192,2048]{1,0:T(8,128)(2,1)} async-done(((bf16[1536,2048]{1,0:T(8,128)(2,1)}), bf16[192,2048]{1,0:T(8,128)(2,1)}) %reduce-scatter.6.cloned.1.call-update) | async-done | bytes 786448 | tf_op jit(solution)/shard_map/reduce_scatter | solution.py:1019
  764.4 12.3 %convolution_convert_fusion = bf16[384,4096]{1,0:T(8,128)(2,1)} fusion(bf16[4096,2048]{1,0:T(8,128)(2,1)} %get-tuple-element.134, bf16[192,2048]{1,0:T(8,128)(2,1)S(1)} %get-tuple-element.305, bf16[192,2048]{1,0:T(8,128)(2,1)S(1)} %get-tuple-element.276), kind=kOutput, calls=%fused_computation.7 | convolution fusion | flops 6447169536 | bytes 21495808 | tf_op jit(solution)/shard_map/dot_general | solution.py:35
  783.3 61.8 %shard_map.221 = (bf16[2,192,4096]{2,1,0:T(8,128)(2,1)}, bf16[8,2,192,1024]{3,2,1,0:T(8,128)(2,1)}) custom-call(bf16[2,192,4096]{2,1,0:T(8,128)(2,1)} %convert_element_type.239.q_ref, bf16[8,2,192,1024]{3,2,1,0:T(8,128)(2,1)} %bitcast.221, f32[2,1536,384]{2,1,0:T(8,128)} %copy.136.bias_ref, bf16[2,192,4096]{2,1,0:T(8,128)(2,1)} %get-tuple-element.212.o_ref, ...), custom_call_target="tpu_custom_call" | custom-call | flops 24159191040 | bytes 30000000 | tf_op jit(solution)/shard_map/pallas_call | solution.py:155
  872.0 99.9 %shard_map.222 = (f32[128,2048]{1,0:T(8,128)}, f32[1,256]{1,0:T(1,128)}) custom-call(bf16[4096,384]{1,0:T(8,128)(2,1)} %bitcast.195, bf16[384,2048]{1,0:T(8,128)(2,1)} %pad_maximum_fusion.4.b_ref, f32[64,256]{1,0:T(8,128)} %pad.37.g_ref), custom_call_target="tpu_custom_call" | custom-call | flops 6442450944 | bytes 10000000 | tf_op jit(solution)/shard_map/pallas_call | solution.py:473
  993.2 6.9 fusion.34
  1037.0 14.8 %fusion.9 = (f32[2048]{0:T(1024)S(1)}, f32[384]{0:T(512)S(1)}, bf16[384,2048]{1,0:T(8,128)(2,1)}, f32[384,2048]{1,0:T(8,128)}) fusion(bf16[2,1,192,2048]{3,2,1,0:T(8,128)(2,1)S(1)} %copy-done.5, f32[384]{0:T(512)S(1)} %copy-done.63, f32[2048]{0:T(1024)S(1)} %copy-done.51, bf16[384,5120]{0,1:T(8,128)(2,1)S(1)} %bitcast.189, ...), kind=kOutput, calls=%fused_computation.31 | convolution fusion | flops 8060925440 | bytes 31214592 | tf_op jit(solution)/shard_map/dot_general | solution.py:35
  1062.0 108.7 %shard_map.223 = (f32[160,2048]{1,0:T(8,128)}, f32[1,256]{1,0:T(1,128)}) custom-call(bf16[5120,384]{1,0:T(8,128)(2,1)} %bitcast.190, bf16[384,2048]{1,0:T(8,128)(2,1)} %get-tuple-element.311.b_ref, f32[64,256]{1,0:T(8,128)} %bitcast.209), custom_call_target="tpu_custom_call" | custom-call | flops 8053063680 | bytes 10000000 | tf_op jit(solution)/shard_map/pallas_call | solution.py:473
  (416 shorter events, 267.4 us)
Async XLA Ops:
  7.2 238.1 %all-gather.13.cloned.1.call-start = ((), (), s32[]{:S(2)}) async-start(), calls=%async_computation.12 | async-start | bytes 7520256 | tf_op jit(solution)/shard_map/all_gather | solution.py:961
  179.3 139.7 %all-gather.15.cloned.1.call-start = ((), (), s32[]{:S(2)}) async-start(), calls=%async_computation.13 | async-start | bytes 7077888 | tf_op jit(solution)/shard_map/all_gather | solution.py:995
  245.4 142.2 %all-gather.17.cloned.1.call-start = ((), (), s32[]{:S(2)}) async-start(), calls=%async_computation.14 | async-start | bytes 7520256 | tf_op jit(solution)/shard_map/all_gather | solution.py:962
  246.1 221.6 %all-gather.9.cloned.1.call-start = ((), (), s32[]{:S(2)}) async-start(), calls=%async_computation.5 | async-start | bytes 7077888 | tf_op jit(solution)/shard_map/all_gather | solution.py:1015
  249.2 68.3 %collective-permute-start.4 = (bf16[2,768,512]{2,1,0:T(8,128)(2,1)}, bf16[2,768,512]{2,1,0:T(8,128)(2,1)}, u32[]{:S(2)}, u32[]{:S(2)}) collective-permute-start(bf16[2,768,512]{2,1,0:T(8,128)(2,1)} %refs_12_.1), channel_id=1, source_target_pairs={{0,8},{8,0},{16,24},{24,16},{1,9},{9,1},{17,25},{25,17},{2,10},{10... | collective-permute-start | bytes 4718600 | tf_op jit(solution)/shard_map/ppermute | solution.py:680
  249.8 69.2 %collective-permute-start.5 = (bf16[2,768,512]{2,1,0:T(8,128)(2,1)}, bf16[2,768,512]{2,1,0:T(8,128)(2,1)}, u32[]{:S(2)}, u32[]{:S(2)}) collective-permute-start(bf16[2,768,512]{2,1,0:T(8,128)(2,1)} %refs_12_.1), channel_id=1, source_target_pairs={{0,16},{8,24},{16,0},{24,8},{1,17},{9,25},{17,1},{25,9},{2,18},{10... | collective-permute-start | bytes 4718600 | tf_op jit(solution)/shard_map/ppermute | solution.py:680
  283.6 102.1 %collective-permute-start.6 = (bf16[1,512,768]{2,1,0:T(8,128)(2,1)S(1)}, bf16[1,512,768]{2,1,0:T(8,128)(2,1)}, u32[]{:S(2)}, u32[]{:S(2)}) collective-permute-start(bf16[1,512,768]{2,1,0:T(8,128)(2,1)S(1)} %slice.213), channel_id=1, source_target_pairs={{0,16},{8,24},{16,0},{24,8},{1,17},{9,25},{17,1},{25,9},{2,18},{10... | collective-permute-start | bytes 2359304 | tf_op jit(solution)/shard_map/ppermute | solution.py:680
  286.4 101.2 %collective-permute-start.7 = (bf16[1,512,768]{2,1,0:T(8,128)(2,1)S(1)}, bf16[1,512,768]{2,1,0:T(8,128)(2,1)}, u32[]{:S(2)}, u32[]{:S(2)}) collective-permute-start(bf16[1,512,768]{2,1,0:T(8,128)(2,1)S(1)} %slice.214), channel_id=1, source_target_pairs={{0,8},{8,0},{16,24},{24,16},{1,9},{9,1},{17,25},{25,17},{2,10},{10... | collective-permute-start | bytes 2359304 | tf_op jit(solution)/shard_map/ppermute | solution.py:680
  321.1 66.5 %collective-permute-start.10 = (bf16[1,768,512]{2,1,0:T(8,128)(2,1)}, bf16[1,768,512]{2,1,0:T(8,128)(2,1)}, u32[]{:S(2)}, u32[]{:S(2)}) collective-permute-start(bf16[1,768,512]{2,1,0:T(8,128)(2,1)} %slice.217), channel_id=1, source_target_pairs={{0,16},{8,24},{16,0},{24,8},{1,17},{9,25},{17,1},{25,9},{2,18},{10... | collective-permute-start | bytes 2359304 | tf_op jit(solution)/shard_map/ppermute | solution.py:680
  324.7 62.9 %collective-permute-start.11 = (bf16[1,768,512]{2,1,0:T(8,128)(2,1)}, bf16[1,768,512]{2,1,0:T(8,128)(2,1)}, u32[]{:S(2)}, u32[]{:S(2)}) collective-permute-start(bf16[1,768,512]{2,1,0:T(8,128)(2,1)} %slice.218), channel_id=1, source_target_pairs={{0,8},{8,0},{16,24},{24,16},{1,9},{9,1},{17,25},{25,17},{2,10},{10... | collective-permute-start | bytes 2359304 | tf_op jit(solution)/shard_map/ppermute | solution.py:680
  327.3 60.3 %collective-permute-start.8 = (bf16[1,512,768]{2,1,0:T(8,128)(2,1)}, bf16[1,512,768]{2,1,0:T(8,128)(2,1)}, u32[]{:S(2)}, u32[]{:S(2)}) collective-permute-start(bf16[1,512,768]{2,1,0:T(8,128)(2,1)} %slice.215), channel_id=1, source_target_pairs={{0,16},{8,24},{16,0},{24,8},{1,17},{9,25},{17,1},{25,9},{2,18},{10... | collective-permute-start | bytes 2359304 | tf_op jit(solution)/shard_map/ppermute | solution.py:680
  404.0 130.5 %all-gather.11.cloned.1.call-start = ((), (), s32[]{:S(2)}) async-start(), calls=%async_computation.6 | async-start | bytes 7077888 | tf_op jit(solution)/shard_map/all_gather | solution.py:1015
  404.6 277.0 %reduce-scatter.8.cloned.1.call-start = ((), (), s32[]{:S(2)}) async-start(), calls=%async_computation.8 | async-start | bytes 7077888 | tf_op jit(solution)/shard_map/reduce_scatter | solution.py:1019
  601.6 138.7 %reduce-scatter.6.cloned.1.call-start = ((), (), s32[]{:S(2)}) async-start(), calls=%async_computation.7 | async-start | bytes 7077888 | tf_op jit(solution)/shard_map/reduce_scatter | solution.py:1019
  602.3 369.7 %reduce-scatter.10.cloned.1.call-start = ((), (), s32[]{:S(2)}) async-start(), calls=%async_computation.9 | async-start | bytes 7077888 | tf_op jit(solution)/shard_map/reduce_scatter | solution.py:1051
  622.1 41.1 %collective-permute-start.16 = (bf16[1,512,768]{2,1,0:T(8,128)(2,1)}, bf16[1,512,768]{2,1,0:T(8,128)(2,1)}, u32[]{:S(2)}, u32[]{:S(2)}) collective-permute-start(bf16[1,512,768]{2,1,0:T(8,128)(2,1)} %get-tuple-element.294), channel_id=1, source_target_pairs={{0,8},{8,0},{16,24},{24,16},{1,9},{9,1},{17,25},{25,17},{2,10},{10... | collective-permute-start | bytes 2359304 | tf_op jit(solution)/shard_map/ppermute | solution.py:680
  623.6 50.7 %collective-permute-start.17 = (bf16[1,512,768]{2,1,0:T(8,128)(2,1)}, bf16[1,512,768]{2,1,0:T(8,128)(2,1)}, u32[]{:S(2)}, u32[]{:S(2)}) collective-permute-start(bf16[1,512,768]{2,1,0:T(8,128)(2,1)} %get-tuple-element.293), channel_id=1, source_target_pairs={{0,16},{8,24},{16,0},{24,8},{1,17},{9,25},{17,1},{25,9},{2,18},{10... | collective-permute-start | bytes 2359304 | tf_op jit(solution)/shard_map/ppermute | solution.py:680
  747.6 97.5 %collective-permute-start.23 = (bf16[2,512,768]{2,1,0:T(8,128)(2,1)S(1)}, bf16[2,512,768]{2,1,0:T(8,128)(2,1)}, u32[]{:S(2)}, u32[]{:S(2)}) collective-permute-start(bf16[2,512,768]{2,1,0:T(8,128)(2,1)S(1)} %pad_maximum_fusion.10), channel_id=1, source_target_pairs={{0,16},{8,24},{16,0},{24,8},{1,17},{9,25},{17,1},{25,9},{2,18},{10... | collective-permute-start | bytes 4718600 | tf_op jit(solution)/shard_map/ppermute | solution.py:680
  750.7 98.6 %collective-permute-start.20 = (bf16[2,512,768]{2,1,0:T(8,128)(2,1)S(1)}, bf16[2,512,768]{2,1,0:T(8,128)(2,1)}, u32[]{:S(2)}, u32[]{:S(2)}) collective-permute-start(bf16[2,512,768]{2,1,0:T(8,128)(2,1)S(1)} %pad_maximum_fusion.7), channel_id=1, source_target_pairs={{0,8},{8,0},{16,24},{24,16},{1,9},{9,1},{17,25},{25,17},{2,10},{10... | collective-permute-start | bytes 4718600 | tf_op jit(solution)/shard_map/ppermute | solution.py:680
  754.0 95.2 %collective-permute-start.21 = (bf16[2,512,768]{2,1,0:T(8,128)(2,1)}, bf16[2,512,768]{2,1,0:T(8,128)(2,1)}, u32[]{:S(2)}, u32[]{:S(2)}) collective-permute-start(bf16[2,512,768]{2,1,0:T(8,128)(2,1)} %pad_maximum_fusion.8), channel_id=1, source_target_pairs={{0,16},{8,24},{16,0},{24,8},{1,17},{9,25},{17,1},{25,9},{2,18},{10... | collective-permute-start | bytes 4718600 | tf_op jit(solution)/shard_map/ppermute | solution.py:680
  757.2 96.3 %collective-permute-start.18 = (bf16[2,768,512]{2,1,0:T(8,128)(2,1)}, bf16[2,768,512]{2,1,0:T(8,128)(2,1)}, u32[]{:S(2)}, u32[]{:S(2)}) collective-permute-start(bf16[2,768,512]{2,1,0:T(8,128)(2,1)} %pad_maximum_fusion.5), channel_id=1, source_target_pairs={{0,8},{8,0},{16,24},{24,16},{1,9},{9,1},{17,25},{25,17},{2,10},{10... | collective-permute-start | bytes 4718600 | tf_op jit(solution)/shard_map/ppermute | solution.py:680
  781.6 71.9 %collective-permute-start.19 = (bf16[2,768,512]{2,1,0:T(8,128)(2,1)S(1)}, bf16[2,768,512]{2,1,0:T(8,128)(2,1)S(1)}, u32[]{:S(2)}, u32[]{:S(2)}) collective-permute-start(bf16[2,768,512]{2,1,0:T(8,128)(2,1)S(1)} %copy-done.35), channel_id=1, source_target_pairs={{0,16},{8,24},{16,0},{24,8},{1,17},{9,25},{17,1},{25,9},{2,18},{10... | collective-permute-start | bytes 4718600 | tf_op jit(solution)/shard_map/ppermute | solution.py:680
  857.2 323.7 %reduce-scatter.12.cloned.1.call-start = ((), (), s32[]{:S(2)}) async-start(), calls=%async_computation.10 | async-start | bytes 7077888 | tf_op jit(solution)/shard_map/reduce_scatter | solution.py:1057
  974.7 206.3 %reduce-scatter.14.cloned.1.call-start = ((), (), s32[]{:S(2)}) async-start(), calls=%async_computation.11 | async-start | bytes 7077888 | tf_op jit(solution)/shard_map/reduce_scatter | solution.py:1057
  (92 other events, 1536.8 us)
Sparse Core Ops, SparseCore 0:
  179.4 65.8 all-gather.12
  247.5 63.5 all-gather.14
  313.3 66.5 all-gather.16
  404.2 63.5 all-gather.8
  469.8 63.3 all-gather.10
  601.7 68.0 reduce-scatter.7
  672.1 68.1 reduce-scatter.5
  857.4 81.5 reduce-scatter.9
  974.8 66.0 reduce-scatter.11
  1043.0 68.1 reduce-scatter.13

commit v4 on v3

--- a/solution.py
+++ b/solution.py
@@ -58,6 +58,98 @@
         ],
         axis=-1,
     )
+
+
+def turn(values, cosine, sine):
+    return values * cosine + pltpu.roll(values, HD // 2, 1) * sine
+
+
+def project(x_ref, wq_ref, wkv_ref, cos_ref, sin_ref, gq_ref, gk_ref, q_ref, qraw_ref, kv_ref, kraw_ref, wkv_out):
+    x = x_ref[...]
+    cosine, sine = cos_ref[...], sin_ref[...]
+    for at in range(0, PER_KV * HD, 2 * HD):
+        raw = mm(x, wq_ref[at : at + 2 * HD], NT)
+        qraw_ref[:, at : at + 2 * HD] = raw
+        for lane in (0, HD):
+            head = raw[:, lane : lane + HD]
+            normed = head * rms_scale(head) * gq_ref[...]
+            q_ref[:, at + lane : at + lane + HD] = turn(normed, cosine, sine).astype(bf16)
+    piece = HD // PER_KV
+    w_k = [wkv_ref[2 * piece * i : 2 * piece * i + piece] for i in range(PER_KV)]
+    w_v = [wkv_ref[2 * piece * i + piece : 2 * piece * (i + 1)] for i in range(PER_KV)]
+    w_kv = jnp.concatenate(w_k + w_v, axis=0)
+    wkv_out[...] = w_kv
+    raw = mm(x, w_kv, NT)
+    key = raw[:, :HD]
+    kraw_ref[...] = key
+    normed = key * rms_scale(key) * gk_ref[...]
+    kv_ref[:, :HD] = turn(normed, cosine, sine).astype(bf16)
+    kv_ref[:, HD:] = raw[:, HD:].astype(bf16)
+
+
+def run_project(x, wq, wkv, cosine, sine, gain_q, gain_k):
+    tokens, width = x.shape
+    wide = PER_KV * HD
+    whole = lambda a: pl.BlockSpec(a.shape, lambda g: (0, 0))
+    cols = lambda n: pl.BlockSpec((tokens, n), lambda g: (0, g))
+    rows = lambda n: pl.BlockSpec((n, width), lambda g: (g, 0))
+    return pl.pallas_call(
+        project,
+        grid=(KVH,),
+        in_specs=[whole(x), rows(wide), rows(2 * HD), whole(cosine), whole(sine), whole(gain_q), whole(gain_k)],
+        out_specs=[cols(wide), cols(wide), cols(2 * HD), cols(HD), rows(2 * HD)],
+        out_shape=[
+            jax.ShapeDtypeStruct((tokens, H * HD), bf16),
+            jax.ShapeDtypeStruct((tokens, H * HD), f32),
+            jax.ShapeDtypeStruct((tokens, KVH * 2 * HD), bf16),
+            jax.ShapeDtypeStruct((tokens, KVH * HD), f32),
+            jax.ShapeDtypeStruct((KVH * 2 * HD, width), bf16),
+        ],
+        compiler_params=pltpu.CompilerParams(vmem_limit_bytes=VMEM_LIMIT),
+        cost_estimate=pl.CostEstimate(
+            flops=2 * tokens * width * (H + 2 * KVH) * HD, bytes_accessed=40_000_000, transcendentals=0
+        ),
+    )(x, wq, wkv, cosine, sine, gain_q, gain_k)
+
+
+def norm_turn_back(grad, raw, cosine, sine, gain):
+    grad = turn(grad, cosine, -sine)
+    scale = rms_scale(raw)
+    lifted = grad * gain
+    inner = jnp.mean(lifted * raw, axis=-1, keepdims=True)
+    back = scale * lifted - raw * (scale * scale * scale) * inner
+    return back, jnp.sum(grad * raw * scale, axis=0, keepdims=True)
+
+
+def key_back(dkv_ref, kraw_ref, cos_ref, sin_ref, gk_ref, out_ref, out_t_ref, gain_ref):
+    gain_sum = 0.0
+    for g in range(KVH):
+        key = slice(2 * g * HD, (2 * g + 1) * HD)
+        value = slice((2 * g + 1) * HD, (2 * g + 2) * HD)
+        grad = dkv_ref[:, key].astype(f32)
+        back, part = norm_turn_back(
+            grad, kraw_ref[:, g * HD : (g + 1) * HD], cos_ref[...], sin_ref[...], gk_ref[...]
+        )
+        gain_sum += part
+        low = back.astype(bf16)
+        out_ref[:, key] = low
+        out_t_ref[key] = low.T
+        out_ref[:, value] = dkv_ref[:, value]
+        out_t_ref[value] = dkv_ref[:, value].T
+    gain_ref[...] = gain_sum
+
+
+def run_key_back(dkv, key_raw, cosine, sine, gain):
+    tokens, wide = dkv.shape
+    return pl.pallas_call(
+        key_back,
+        out_shape=[
+            jax.ShapeDtypeStruct((tokens, wide), bf16),
+            jax.ShapeDtypeStruct((wide, tokens), bf16),
+            jax.ShapeDtypeStruct((1, HD), f32),
+        ],
+        compiler_params=pltpu.CompilerParams(vmem_limit_bytes=VMEM_LIMIT),
+    )(dkv, key_raw, cosine, sine, gain)
 
 
 def attend_forward(step_heads, chunk, q_ref, kv_ref, bias_ref, o_ref, log_ref):
@@ -81,13 +173,21 @@
 
 
 def attend_backward(
-    step_heads, chunk, q_ref, kv_ref, bias_ref, o_ref, do_ref, log_ref, dq_ref, dkv_ref, dk_acc, dv_acc
+    step_heads, chunk, q_ref, kv_ref, bias_ref, o_ref, do_ref, log_ref, raw_ref, cos_ref, sin_ref, gain_ref,
+    dq_ref, dkv_ref, gain_out, dk_acc, dv_acc
 ):
     group_len = bias_ref.shape[1]
     keys = kv_ref[:, 0, :, :HD].reshape(group_len, HD)
     values = kv_ref[:, 0, :, HD:].reshape(group_len, HD)
     keys_t = keys.T
     rows = q_ref.shape[1]
+    cosine, sine, gain = cos_ref[0], sin_ref[0], gain_ref[...]
+
+    @pl.when((pl.program_id(0) == 0) & (pl.program_id(1) == 0))
+    def _():
+        gain_out[...] = jnp.zeros_like(gain_out)
+
+    gain_sum = 0.0
     dk_acc[...] = jnp.zeros_like(dk_acc)
     dv_acc[...] = jnp.zeros_like(dv_acc)
     for step in range(PER_KV // step_heads):
@@ -107,9 +207,15 @@
             dv_acc[part] += mm(prob.astype(bf16), grad)
             dk_acc[part] += mm(d_score, query)
             dq_t += mm(keys_t[:, part], d_score)
-        out = (dq_t * SCALE).T.astype(bf16)
+        out = (dq_t * SCALE).T.astype(bf16).astype(f32)
         for i, h in enumerate(heads):
-            dq_ref[0, :, h * HD : (h + 1) * HD] = out[i * rows : (i + 1) * rows]
+            head = slice(h * HD, (h + 1) * HD)
+            back, part = norm_turn_back(
+                out[i * rows : (i + 1) * rows], raw_ref[0, :, head], cosine, sine, gain
+            )
+            dq_ref[0, :, head] = back.astype(bf16)
+            gain_sum += part
+    gain_out[...] += gain_sum
     blocks = dkv_ref.shape[0]
     dkv_ref[:, 0, :, :HD] = (dk_acc[...] * (1.0 / LOG2E)).astype(bf16).reshape(blocks, rows, HD)
     dkv_ref[:, 0, :, HD:] = dv_acc[...].astype(bf16).reshape(blocks, rows, HD)
@@ -146,7 +252,7 @@
     )(query, kv_all, bias)
 
 
-def run_backward(query, kv_all, bias, mixed, grad, logs, step_heads, chunk):
+def run_backward(query, kv_all, bias, mixed, grad, logs, raw, cosine, sine, gain, step_heads, chunk):
     micro, rows, _ = query.shape
     blocks = kv_all.shape[0]
     group_len = bias.shape[1]
@@ -155,18 +261,21 @@
     return pl.pallas_call(
         functools.partial(attend_backward, step_heads, chunk),
         grid=(micro, KVH),
-        in_specs=[q_spec, kv_spec, bias_spec, q_spec, q_spec, log_spec],
-        out_specs=[q_spec, kv_spec],
+        in_specs=[q_spec, kv_spec, bias_spec, q_spec, q_spec, log_spec, q_spec]
+        + [pl.BlockSpec((1, rows, HD), lambda b, g: (b, 0, 0))] * 2
+        + [pl.BlockSpec((1, HD), lambda b, g: (0, 0))],
+        out_specs=[q_spec, kv_spec, pl.BlockSpec((1, HD), lambda b, g: (0, 0))],
         out_shape=[
             jax.ShapeDtypeStruct(query.shape, bf16),
             jax.ShapeDtypeStruct(kv_all.shape, bf16),
+            jax.ShapeDtypeStruct((1, HD), f32),
         ],
         scratch_shapes=[pltpu.VMEM((group_len, HD), f32), pltpu.VMEM((group_len, HD), f32)],
         compiler_params=pltpu.CompilerParams(vmem_limit_bytes=VMEM_LIMIT),
         cost_estimate=pl.CostEstimate(
             flops=flops, bytes_accessed=30_000_000, transcendentals=flops // (10 * HD)
         ),
-    )(query, kv_all, bias, mixed, grad, logs)
+    )(query, kv_all, bias, mixed, grad, logs, raw, cosine, sine, gain)
 
 
 MESH = pl.DeviceIdType.MESH
@@ -307,7 +416,7 @@
     )(*arrays)
 
 
-def reduce_kernel(rows, cuts, a_ref, b_ref, g_ref, o_ref, go_ref, sib, got, own, far, near, plane, got_z,
+def reduce_kernel(rows, cuts, a_ref, extra_ref, b_ref, g_ref, o_ref, go_ref, sib, got, own, far, near, plane, got_z,
                   s0, r0, s1, r1, s2, r2, s3, r3, g_acc, g_got, g_z, gs, gr, gsz, grz):
     dp = lax.axis_index("dp"); member = lax.axis_index("expert")
     core = member % 2; z = member // 2
@@ -331,20 +440,35 @@
         return at
     orders = [[3, 3, 0, 0], [2, 0, 3, 1], [1, 2, 1, 2], [0, 1, 2, 3]]
     targets = [pick(t) for t in orders]
-    wide = 4 * rows
     cols = b_ref.shape[1] // cuts
 
     def copy(src, dst, ssem, rsem, to):
         return pltpu.make_async_remote_copy(src_ref=src, dst_ref=dst, send_sem=ssem, recv_sem=rsem, device_id=to, device_id_type=MESH)
 
+    blocks = 2 * depth
+    piece = (rows - HD) // 2
+
     def product(half_of, k, put):
-        base = (half_of * depth + targets[k]) * wide
+        spot = targets[k] * 2 + half_of
+
         def step(i, _):
+            shard = (i // cuts) * blocks + spot
             at = (i // cuts) * rows
-            col = pl.multiple_of((i % cuts) * cols, cols)
-            part = jnp.dot(a_ref[pl.ds(pl.multiple_of(base + at, 16), rows), :], b_ref[:, pl.ds(col, cols)], preferred_element_type=f32)
-            put(pl.ds(pl.multiple_of(at, 16), rows), pl.ds(col, cols), part)
+            col = pl.ds(pl.multiple_of((i % cuts) * cols, cols), cols)
+            part = mm(a_ref[:, pl.ds(pl.multiple_of(shard * HD, HD), HD)], b_ref[:, col], TN)
+            put(pl.ds(pl.multiple_of(at, 16), HD), col, part)
+            if piece:
+                base = (shard // PER_KV) * (2 * HD) + (shard % PER_KV) * piece
+                small = jnp.concatenate(
+                    [
+                        extra_ref[pl.ds(pl.multiple_of(base, 16), piece), :],
+                        extra_ref[pl.ds(pl.multiple_of(base + HD, 16), piece), :],
+                    ],
+                    axis=0,
+                )
+                put(pl.ds(pl.multiple_of(at + HD, 16), 2 * piece), col, mm(small, b_ref[:, col]))
             return 0
+
         lax.fori_loop(0, 4 * cuts, step, 0)
 
     def gain_hop(i, src, to):
@@ -459,10 +583,12 @@
         for c in near_copies[k]: c.wait_send()
         if k < depth - 1: z_copies[k].wait_send()
 
-def reduce_rows(a, b, rows, cid, gains=None):
+def reduce_rows(a, extra, b, cid, gains=None):
     tokens, width = b.shape
     depth = 4
-    at = a.reshape(tokens, 4, depth, 2, rows).transpose(3, 2, 1, 4, 0).reshape(-1, tokens)
+    rows = HD + (0 if extra is None else extra.shape[0] // 32)
+    if extra is None:
+        extra = jnp.zeros((16, 128), bf16)
     D = pltpu.SemaphoreType.DMA
     lanes = 256
     padded = jnp.zeros((32, lanes), f32)
@@ -473,7 +599,7 @@
     return pl.pallas_call(
         functools.partial(reduce_kernel, rows, 4),
         out_shape=[jax.ShapeDtypeStruct((rows, width), f32), jax.ShapeDtypeStruct((1, lanes), f32)],
-        in_specs=[pl.BlockSpec(memory_space=pltpu.VMEM)] * 3,
+        in_specs=[pl.BlockSpec(memory_space=pltpu.VMEM)] * 4,
         out_specs=[pl.BlockSpec(memory_space=pltpu.VMEM)] * 2,
         scratch_shapes=[
             pltpu.VMEM((2, 4 * rows, width), bf16),
@@ -489,7 +615,7 @@
         ],
         compiler_params=pltpu.CompilerParams(vmem_limit_bytes=60*1024*1024, collective_id=cid, has_side_effects=True),
         cost_estimate=pl.CostEstimate(flops=2*tokens*32*rows*width, bytes_accessed=10_000_000, transcendentals=0),
-    )(at, b, padded)
+    )(a, extra, b, padded)
 
 
 ROUTE_LANES = 128
@@ -514,17 +640,17 @@
 
 def pick_kernel(capacity, local_experts, n_alias, tok_ref, cot_ref, *refs):
     x_ref, dy_ref = refs[n_alias:]
-    width = tok_ref.shape[2]
+    width = cot_ref.shape[2]
     first = lax.axis_index("expert") * local_experts
-    routing = cot_ref[0, :, width:]
+    routing = tok_ref[0, :, width:]
     hit, _ = picks_of(routing.astype(f32), first, local_experts, capacity)
-    x = mm(hit, tok_ref[0], TN).astype(bf16)
+    x = mm(hit, tok_ref[0, :, :width], TN).astype(bf16)
     rows = mm(hit, routing, TN)
     lanes = lax.broadcasted_iota(jnp.int32, rows.shape, 1)
     owner = lax.broadcasted_iota(jnp.int32, rows.shape, 0) // capacity
     at = lanes - first - owner
     weight = jnp.sum(jnp.where((at == 32) | (at == 64), rows, 0.0), axis=1, keepdims=True)
-    dy = (mm(hit, cot_ref[0, :, :width], TN) * weight).astype(bf16)
+    dy = (mm(hit, cot_ref[0], TN) * weight).astype(bf16)
     for e in range(local_experts):
         x_ref[e, 0, 0] = x[e * capacity : (e + 1) * capacity]
         dy_ref[e, 0, 0] = dy[e * capacity : (e + 1) * capacity]
@@ -590,7 +716,7 @@
 
 
 def run_experts(tokens, cot, parts, capacity, batch_at, micro, earlier):
-    blocks, rows, width = tokens.shape
+    blocks, rows, width = cot.shape
     local_experts, _, hidden = parts[0][0].shape
     flat = [p for group in parts for p in group]
     any_spec = pl.BlockSpec(memory_space=pl.ANY)
@@ -602,8 +728,8 @@
         functools.partial(pick_kernel, capacity, local_experts, len(earlier[:2])),
         grid=(blocks,),
         in_specs=[
+            pl.BlockSpec((1, rows, tokens.shape[2]), lambda b: (b, 0, 0)),
             pl.BlockSpec((1, rows, width), lambda b: (b, 0, 0)),
-            pl.BlockSpec((1, rows, cot.shape[2]), lambda b: (b, 0, 0)),
         ]
         + [any_spec] * len(earlier[:2]),
         out_specs=[picked_spec] * 2,
@@ -657,7 +783,7 @@
         cost_estimate=pl.CostEstimate(
             flops=4 * slots * local_experts * rows * width, bytes_accessed=25_000_000, transcendentals=0
         ),
-    )(cot, y, dx)
+    )(tokens, y, dx)
     return [x, dy, z, dg, du], mix, da
 
 
@@ -857,16 +983,20 @@
     grad_output = mm(mixed.reshape(total, H * HD), d_branch, TN).astype(bf16)
     grad_output = lax.psum_scatter(grad_output, BOTH, scatter_dimension=0, tiled=True)
     d_mixed = mm(d_branch, out_w, NT).astype(bf16).reshape(micro, rows, H * HD)
-    dq_low, dkv_all = run_backward(q_low, kv_all, bias, mixed, d_mixed, logs, step_heads, chunk)
+    cos_rows = jnp.concatenate([cosine, cosine], axis=-1).reshape(micro, rows, HD)
+    sine_rows = jnp.concatenate([-sine_part, sine_part], axis=-1).reshape(micro, rows, HD)
+    q_raw = queries.reshape(micro, rows, H * HD)
+    d_query, dkv_all, grad_qn = run_backward(
+        q_low, kv_all, bias, mixed, d_mixed, logs, q_raw, cos_rows, sine_rows, gain_q[None, :], step_heads, chunk
+    )
+    grad_qn = grad_qn[0]
     dkv = lax.psum_scatter(dkv_all, "expert", scatter_dimension=0, tiled=False)
     dkv = dkv.reshape(total, KVH, 2 * HD)
-    d_query = rotate(dq_low.reshape(total, H, HD).astype(f32), cosine, -sine_part)
-    d_query, grad_qn = norm_back(d_query, queries, scale_q, gain_q)
     d_key = rotate(dkv[:, :, :HD].astype(f32), cosine, -sine_part)
     d_key, grad_kn = norm_back(d_key, key_pre, scale_k, gain_k)
     d_proj = jnp.concatenate(
         [
-            d_query.astype(bf16).reshape(total, shards, q_part),
+            d_query.reshape(total, shards, q_part),
             d_key.astype(bf16).reshape(total, shards, k_part),
             dkv[:, :, HD:].reshape(total, shards, v_part),
         ],
@@ -936,9 +1066,8 @@
     def padded(values, lanes):
         return jnp.pad(values, ((0, 0), (0, 0), (0, lanes - experts)))
 
-    cot_rows = jnp.concatenate(
+    routing = jnp.concatenate(
         [
-            cotangent[:, 0],
             padded(slot_map.astype(bf16), 32),
             padded(weight_high, 32),
             padded(weight_low, ROUTE_LANES - 64),
@@ -948,17 +1077,19 @@
 
     gain_len = norm_gains.shape[0]
     gain_shard = jnp.zeros((2048,), bf16).at[:gain_len].set(norm_gains).reshape(16, 128)
-    qkv_w = jnp.concatenate([w_query.T, w_key.T, w_value.T], axis=0)
-    qkv_w, out_w, gain_full = gather_rows([qkv_w, w_output, gain_shard], [(2, 0, 1)], 1)
-    qkv_w, cot_0, cot_1, w_gate, w_up, w_down = tie(
-        (qkv_w, cot_rows[0], cot_rows[1], w_gate, w_up, w_down)
+    kv_w = jnp.concatenate([w_key.T, w_value.T], axis=0)
+    q_w, kv_w, out_w, gain_full = gather_rows(
+        [w_query.T, kv_w, w_output, gain_shard], [(3, 0, 1, 2)], 1
+    )
+    cot_0 = lax.all_gather(cotangent[0, 0], "expert", axis=0, tiled=False)
+    q_w, cot_0, cot_1, w_gate, w_up, w_down = tie(
+        (q_w, cot_0, cotangent[1, 0], w_gate, w_up, w_down)
     )
     gains = gain_full.reshape(shards, 2048)[:, :gain_len].reshape(-1).astype(f32)
     gain_in = gains[:width]
     gain_mid = gains[width : 2 * width]
     gain_q = gains[2 * width : 2 * width + HD]
     gain_k = gains[2 * width + HD :]
-    cot_0 = lax.all_gather(cot_0, "expert", axis=0, tiled=False)
     cot_1 = lax.all_gather(cot_1, "expert", axis=0, tiled=False)
     gate_near, up_near, down_near = ((swap(w, 1), swap(w, 2)) for w in (w_gate, w_up, w_down))
 
@@ -975,37 +1106,35 @@
     bias = jnp.tile(jnp.where(allowed, 0.0, MASKED).astype(f32), (1, 1, step_heads))
     frequency = ROPE_BASE ** (-(jnp.arange(HD // 2, dtype=f32) * 2.0 / HD))
     angles = position.astype(f32).reshape(total)[:, None] * frequency[None, :]
-    cosine = jnp.cos(angles)[:, None, :]
-    sine_part = jnp.sin(angles)[:, None, :]
+    cosine, sine = jnp.cos(angles), jnp.sin(angles)
+    cosine = jnp.concatenate([cosine, cosine], axis=-1)
+    sine = jnp.concatenate([-sine, sine], axis=-1)
+    gain_q, gain_k = gain_q[None, :], gain_k[None, :]
 
     hidden = inputs[:, 0].astype(f32).reshape(total, width)
     scale_in = rms_scale(hidden)
     normed = (hidden * scale_in * gain_in).astype(bf16)
-    proj = mm(normed, qkv_w, NT).reshape(total, shards, q_part + k_part + v_part)
-    queries = proj[:, :, :q_part].reshape(total, H, HD)
-    key_pre = proj[:, :, q_part : q_part + k_part].reshape(total, KVH, HD)
-    value = proj[:, :, q_part + k_part :].reshape(total, KVH, HD).astype(bf16)
-    scale_q = rms_scale(queries)
-    scale_k = rms_scale(key_pre)
-    q_low = rotate(queries * scale_q * (gain_q * (SCALE * LOG2E)), cosine, sine_part).astype(bf16)
-    q_low = q_low.reshape(micro, rows, H * HD)
-    k_low = rotate(key_pre * scale_k * gain_k, cosine, sine_part).astype(bf16)
-    kv_own = jnp.concatenate([k_low, value], axis=-1).reshape(micro, rows, KVH * 2 * HD)
-    kv_own, cot_0, gate_near = tie((kv_own, cot_0, gate_near))
+    q_low, q_raw, kv_own, k_raw, kv_w = run_project(
+        normed, q_w, kv_w, cosine, sine, gain_q * (SCALE * LOG2E), gain_k
+    )
+    q_low, q_raw = (a.reshape(micro, rows, H * HD) for a in (q_low, q_raw))
+    kv_own = kv_own.reshape(micro, rows, KVH * 2 * HD)
     kv_all = lax.all_gather(kv_own, "expert", axis=0, tiled=False)
-    kv_all, up_near, down_near = tie((kv_all, up_near, down_near))
+    kv_all, gate_near = tie((kv_all, gate_near))
+    chunk = 256
+    mixed, logs = run_forward(q_low, kv_all, bias, step_heads, chunk)
+    mixed, up_near, down_near = tie((mixed, up_near, down_near))
     parts = [
         (own, near[0], near[1], swap(near[0][:1], 2), swap(near[1][1:], 1))
         for own, near in ((w_gate, gate_near), (w_up, up_near), (w_down, down_near))
     ]
-    chunk = 256
-    mixed, logs = run_forward(q_low, kv_all, bias, step_heads, chunk)
 
     branch = mm(mixed.reshape(total, H * HD), out_w)
     middle = hidden + branch
     scale_mid = rms_scale(middle)
     routed = (middle * scale_mid * gain_mid).astype(bf16).reshape(micro, rows, width)
-    routed, parts, cot_1 = tie((routed, parts, cot_1))
+    routed = jnp.concatenate([routed, routing], axis=-1)
+    routed, cot_1 = tie((routed, cot_1))
     middle = middle.reshape(micro, rows, width)
     scale_mid = scale_mid.reshape(micro, rows, 1)
 
@@ -1013,8 +1142,9 @@
     kept = []
     for at, cot in enumerate((cot_0, cot_1)):
         tokens = lax.all_gather(routed[at], "expert", axis=0, tiled=False)
+        tokens, parts = tie((tokens, parts))
         kept, mix, d_part = run_experts(tokens, cot, parts, capacity, at, micro, kept)
-        kept, d_part, mix = tie((kept, d_part, mix))
+        kept, d_part, mix, d_routeds = tie((kept, d_part, mix, d_routeds))
         mix_parts.append(mix)
         d_routed = lax.psum_scatter(d_part, "expert", scatter_dimension=0, tiled=True)
         d_routeds.append(d_routed)
@@ -1045,34 +1175,27 @@
     d_branch = jnp.concatenate(d_branches, axis=0)
     d_middle = jnp.concatenate(d_middles, axis=0)
     d_mixed = mm(d_branch, out_w, NT).astype(bf16).reshape(micro, rows, H * HD)
-    dq_low, dkv_all = run_backward(q_low, kv_all, bias, mixed, d_mixed, logs, step_heads, chunk)
-    mixed_after, dq_low, dkv_all, expert_grads = tie((mixed, dq_low, dkv_all, expert_grads))
-    grad_output, _ = reduce_rows(mixed_after.reshape(total, H * HD), d_branch, w_output.shape[0], 2)
+    cos_rows, sine_rows = (a.reshape(micro, rows, HD) for a in (cosine, sine))
+    d_query, dkv_all, grad_qn = run_backward(
+        q_low, kv_all, bias, mixed, d_mixed, logs, q_raw, cos_rows, sine_rows, gain_q, step_heads, chunk
+    )
+    mixed_after, d_query, dkv_all, expert_grads = tie((mixed, d_query, dkv_all, expert_grads))
+    grad_output, _ = reduce_rows(mixed_after.reshape(total, H * HD), None, d_branch, 2)
     dkv = lax.psum_scatter(dkv_all, "expert", scatter_dimension=0, tiled=False)
-    dkv, grad_output, dq_low = tie((dkv, grad_output, dq_low))
-    dkv = dkv.reshape(total, KVH, 2 * HD)
+    dkv, grad_output, d_query = tie((dkv, grad_output, d_query))
+    d_query = d_query.reshape(total, H * HD)
+    dkv = dkv.reshape(total, KVH * 2 * HD)
     mix_parts, dkv = tie((mix_parts, dkv))
     outputs = []
     for at in range(micro):
         mix = lax.psum_scatter(mix_parts[at], "expert", scatter_dimension=0, tiled=True)
         outputs.append((middle[at] + mix.astype(f32)).astype(bf16))
-    d_query = rotate(dq_low.reshape(total, H, HD).astype(f32), cosine, -sine_part)
-    d_query, grad_qn = norm_back(d_query, queries, scale_q, gain_q)
-    d_key = rotate(dkv[:, :, :HD].astype(f32), cosine, -sine_part)
-    d_key, grad_kn = norm_back(d_key, key_pre, scale_k, gain_k)
-    d_proj = jnp.concatenate(
-        [
-            d_query.astype(bf16).reshape(total, shards, q_part),
-            d_key.astype(bf16).reshape(total, shards, k_part),
-            dkv[:, :, HD:].reshape(total, shards, v_part),
-        ],
-        axis=-1,
-    ).reshape(total, -1)
-    d_normed = mm(d_proj, qkv_w)
+    dkv, dkv_t, grad_kn = run_key_back(dkv, k_raw, cosine, sine, gain_k)
+    d_normed = mm(d_query, q_w) + mm(dkv, kv_w)
     d_in_norm, grad_in = norm_back(d_normed, hidden, scale_in, gain_in)
     input_grad = d_middle + d_in_norm
-    gain_grads = jnp.concatenate([grad_in, grad_mid, grad_qn, grad_kn]).reshape(shards, gain_len)
-    grad_qkv, grad_gains = reduce_rows(d_proj, normed, q_part + k_part + v_part, 3, gain_grads)
+    gain_grads = jnp.concatenate([grad_in, grad_mid, grad_qn[0], grad_kn[0]]).reshape(shards, gain_len)
+    grad_qkv, grad_gains = reduce_rows(d_query, dkv_t, normed, 3, gain_grads)
     return (
         jnp.stack(outputs)[:, None],
         input_grad.reshape(micro, 1, rows, width),

time: 1200 us -> 1090 us (0.908)
  local copies, waits for them, and re-layouts: 140 us -> 49.1 us
  Pallas kernels: 608 us -> 694 us
  waiting for transfers between devices: 211 us -> 147 us
  other arithmetic: 88.4 us -> 56.4 us
  matrix products: 101 us -> 87.6 us
    reduce_scatter x2, waiting for transfers between devices: 58.6 us -> 3.45 us  [body_fast(): lax.psum_scatter(d_part, 'expert', scatter_dimension=0, tiled=True)]
    pallas_call x2, Pallas kernels: 209 us -> 263 us  [reduce_rows(): pl.pallas_call(functools.partial(reduce_kernel, rows, 4), out_shape=[jax....]
    all_gather x2, waiting for transfers between devices: 63 us -> 18 us  [body_fast(): tokens = lax.all_gather(routed[at], 'expert', axis=0, tiled=False)]
    ppermute x24, waiting for transfers between devices: 59.2 us -> 89.1 us  [swap(): lax.ppermute(values, 'dp', [(i, i ^ bit) for i in range(lax.axis_size('dp...]
    all_gather x1, waiting for transfers between devices: 0.01 us -> 27.9 us  [body_fast(): kv_all = lax.all_gather(kv_own, 'expert', axis=0, tiled=False)]
    all_gather x1, waiting for transfers between devices: 27.1 us -> 0.01 us  [body_fast(): cot_0 = lax.all_gather(cotangent[0, 0], 'expert', axis=0, tiled=False)]
    unnamed x179 -> x110, local copies, waits for them, and re-layouts: 28.9 us -> 8.51 us
    pallas_call x0 -> x2, Pallas kernels: none -> 20 us  [the longest x1 16.4 us: run_project(): pl.pallas_call(project, grid=(KVH,), in_specs=[whole(x), rows(wide), rows...]
  transfers between devices with their start and end apart: 34 -> 34, of which waited for: 10 -> 17; matrix products, arithmetic and copies ran while one was open for 25% -> 16% of each run, Pallas kernels for 32% -> 63%
where the time goes in v4:
time: 1090 us; the launch traced here: 1080 us
  Pallas kernels  694 us (64%)
  waiting for transfers between devices  147 us (13%)
  matrix products  87.6 us (8%)
  other arithmetic  56.4 us (5%)
  local copies, waits for them, and re-layouts  49.1 us (5%)
  starting transfers between devices  29.5 us (3%)
  between operations  15.3 us (1%)
    pallas_call x2, Pallas kernels, reduce_rows(): pl.pallas_call(functools.partial(reduce_kernel, rows, 4), out_shape=[jax....  263 us
    pallas_call x1, Pallas kernels, gather_rows(): pl.pallas_call(functools.partial(gather_kernel, phases, len(arrays)), out...  166 us
    ppermute x24, waiting for transfers between devices, swap(): lax.ppermute(values, 'dp', [(i, i ^ bit) for i in range(lax.axis_size('dp...  89.1 us
    pallas_call x2, Pallas kernels, run_experts(): pl.pallas_call(functools.partial(expert_kernel, len(earlier[2:])), grid=(...  79.9 us
    pallas_call x1, Pallas kernels, run_backward(): pl.pallas_call(functools.partial(attend_backward, step_heads, chunk), gri...  67.4 us
    dot_general x3, matrix products, weight_grad(): jnp.einsum('era,erb->eab', rows_in, rows_out, preferred_element_type=f32)  46.9 us
    pallas_call x1, Pallas kernels, run_forward(): pl.pallas_call(functools.partial(attend_forward, step_heads, chunk), grid...  43.9 us
    dot_general x4, matrix products, mm(): return lax.dot_general(a, b, dims, preferred_element_type=f32)  40.7 us
  transfers between devices with their start and end apart: 34, of which 17 were waited for; matrix products, arithmetic and copies ran while one was open for 16% of the time, Pallas kernels for 63%

profile of v4, /device:TPU:8, one launch (start us, length us, event | category | flops | bytes accessed | tf_op | source)
XLA Modules:
  0.0 1078.1 jit_solution(15705309465052463091)
XLA Ops:
  13.2 166.0 %shard_map.213 = (bf16[4096,2048]{1,0:T(8,128)(2,1)}, bf16[1024,2048]{1,0:T(8,128)(2,1)}, bf16[4096,2048]{1,0:T(8,128)(2,1)}, bf16[512,128]{1,0:T(8,128)(2,1)}) custom-call(bf16[128,2048]{1,0:T(8,128)(2,1)} %bitcast.147, bf16[32,2048]{1,0:T(8,128)(2,1)} %pad_maximum_fusion.11.refs_1_, bf16[128,2048]{1,0:T(8,128)(2,1)} %refs_2_.1, ...), custom_call_target="tpu_custom_call" | custom-call | bytes 400000000 | tf_op jit(solution)/shard_map/pallas_call | solution.py:408
  185.3 16.4 %shard_map.214 = (bf16[384,4096]{1,0:T(8,128)(2,1)}, f32[384,4096]{1,0:T(8,128)}, bf16[384,1024]{1,0:T(8,128)(2,1)}, f32[384,512]{1,0:T(8,128)}, bf16[1024,2048]{1,0:T(8,128)(2,1)}) custom-call(bf16[384,2048]{1,0:T(8,128)(2,1)} %fusion.2.x_ref.b_ref, bf16[4096,2048]{1,0:T(8,128)(2,1)} %get-tuple-element.153.wq_ref, ...), custom_call_target="tpu_custom_call" | custom-call | flops 8053063680 | bytes 40000000 | tf_op jit(solution)/shard_map/pallas_call | solution.py:96
  223.3 17.6 %collective-permute-done.refs_3_ = bf16[2,512,768]{2,1,0:T(8,128)(2,1)} collective-permute-done((bf16[2,512,768]{2,1,0:T(8,128)(2,1)}, bf16[2,512,768]{2,1,0:T(8,128)(2,1)}, u32[]{:S(2)}, u32[]{:S(2)}) %collective-permute-start) | collective-permute-done | bytes 1572896 | tf_op jit(solution)/shard_map/ppermute | solution.py:806
  242.9 13.2 %collective-permute-done.1.refs_4_ = bf16[2,512,768]{2,1,0:T(8,128)(2,1)} collective-permute-done((bf16[2,512,768]{2,1,0:T(8,128)(2,1)}, bf16[2,512,768]{2,1,0:T(8,128)(2,1)}, u32[]{:S(2)}, u32[]{:S(2)}) %collective-permute-start.1) | collective-permute-done | bytes 1572896 | tf_op jit(solution)/shard_map/ppermute | solution.py:806
  256.1 27.9 %all-gather.8.cloned.1.call-done.kv_ref = bf16[8,2,192,1024]{3,2,1,0:T(8,128)(2,1)} async-done(((bf16[1,2,192,1024]{3,2,1,0:T(8,128)(2,1)}), bf16[8,2,192,1024]{3,2,1,0:T(8,128)(2,1)}) %all-gather.8.cloned.1.call-update) | async-done | bytes 6291472 | tf_op jit(solution)/shard_map/all_gather | solution.py:1122
  284.0 43.9 %shard_map.215 = (bf16[2,192,4096]{2,1,0:T(8,128)(2,1)}, f32[2,4,4,384]{3,2,1,0:T(4,128)}) custom-call(bf16[2,192,4096]{2,1,0:T(8,128)(2,1)} %bitcast.173, bf16[8,2,192,1024]{3,2,1,0:T(8,128)(2,1)} %all-gather.8.cloned.1.call-done.kv_ref, f32[2,1536,384]{2,1,0:T(8,128)} %copy.65.bias_ref), custom_call_target="tpu_custom_call" | custom-call | flops 9663676416 | bytes 20000000 | tf_op jit(solution)/shard_map/pallas_call | solution.py:239
  327.9 11.3 %multiply_reduce_fusion = (f32[384]{0:T(512)S(1)}, f32[384,2048]{1,0:T(8,128)S(1)}) fusion(bf16[384,4096]{1,0:T(8,128)(2,1)} %bitcast.175, bf16[4096,2048]{1,0:T(8,128)(2,1)} %get-tuple-element.163, bf16[2,1,192,2048]{3,2,1,0:T(8,128)(2,1)S(1)} %copy-done.3), kind=kOutput, calls=%fused_computation.24 | convolution fusion | flops 6445596160 | bytes 24643072 | tf_op jit(solution)/shard_map/dot_general | solution.py:35
  376.3 14.0 %collective-permute-done.8.refs_10_ = bf16[1,512,768]{2,1,0:T(8,128)(2,1)S(1)} collective-permute-done((bf16[1,512,768]{2,1,0:T(8,128)(2,1)S(1)}, bf16[1,512,768]{2,1,0:T(8,128)(2,1)S(1)}, u32[]{:S(2)}, u32[]{:S(2)}) %collective-permute-start.8) | collective-permute-done | bytes 786464 | tf_op jit(solution)/shard_map/ppermute | solution.py:806
  393.1 13.4 %collective-permute-done.6.refs_5_ = bf16[1,512,768]{2,1,0:T(8,128)(2,1)S(1)} collective-permute-done((bf16[1,512,768]{2,1,0:T(8,128)(2,1)S(1)}, bf16[1,512,768]{2,1,0:T(8,128)(2,1)S(1)}, u32[]{:S(2)}, u32[]{:S(2)}) %collective-permute-start.6) | collective-permute-done | bytes 786464 | tf_op jit(solution)/shard_map/ppermute | solution.py:806
  409.0 16.2 %all-gather.10.cloned.1.call-done.tok_ref.routing_ref = bf16[8,192,2176]{2,1,0:T(8,128)(2,1)} async-done(((bf16[1,192,2176]{2,1,0:T(8,128)(2,1)}), bf16[8,192,2176]{2,1,0:T(8,128)(2,1)}) %all-gather.10.cloned.1.call-update) | async-done | bytes 6684688 | tf_op jit(solution)/shard_map/all_gather | solution.py:1144
  425.2 14.0 %shard_map.216 = (bf16[2,2,8,96,2048]{4,3,2,1,0:T(8,128)(2,1)}, bf16[2,2,8,96,2048]{4,3,2,1,0:T(8,128)(2,1)}) custom-call(bf16[8,192,2176]{2,1,0:T(8,128)(2,1)} %all-gather.10.cloned.1.call-done.tok_ref.routing_ref, bf16[8,192,2048]{2,1,0:T(8,128)(2,1)} %bitcast.138), custom_call_target="tpu_custom_call" | custom-call | flops 2415919104 | bytes 25000000 | tf_op jit(solution)/shard_map/pallas_call | solution.py:727
  439.2 40.0 %shard_map.217 = (bf16[2,2,768,768]{3,2,1,0:T(8,128)(2,1)}, bf16[2,2,768,768]{3,2,1,0:T(8,128)(2,1)}, bf16[2,2,768,768]{3,2,1,0:T(8,128)(2,1)}, bf16[2,768,2048]{2,1,0:T(8,128)(2,1)}, bf16[2,768,2048]{2,1,0:T(8,128)(2,1)}) custom-call(bf16[2,2,768,2048]{3,2,1,0:T(8,128)(2,1)} %bitcast.130, bf16[2,2,768,2048]{3,2,1,0:T(8,128)(2,1)} %bitcast.134, ...), custom_call_target="tpu_custom_call" | custom-call | flops 28991029248 | bytes 50000000 | tf_op jit(solution)/shard_map/pallas_call | solution.py:750
  479.2 12.7 %shard_map.218 = (bf16[1536,2048]{1,0:T(8,128)(2,1)}, bf16[1536,2048]{1,0:T(8,128)(2,1)}) custom-call(bf16[8,192,2176]{2,1,0:T(8,128)(2,1)} %all-gather.10.cloned.1.call-done.tok_ref.routing_ref, bf16[2,8,96,2048]{3,2,1,0:T(8,128)(2,1)} %bitcast.144, bf16[2,8,96,2048]{3,2,1,0:T(8,128)(2,1)} %bitcast.145), custom_call_target="tpu_custom_call" | custom-call | flops 2415919104 | bytes 25000000 | tf_op jit(solution)/shard_map/pallas_call | solution.py:772
  494.0 14.0 %shard_map.219 = (bf16[2,2,8,96,2048]{4,3,2,1,0:T(8,128)(2,1)}, bf16[2,2,8,96,2048]{4,3,2,1,0:T(8,128)(2,1)}) custom-call(bf16[8,192,2176]{2,1,0:T(8,128)(2,1)} %all-gather.12.cloned.1.call-done.tok_ref.routing_ref, bf16[8,192,2048]{2,1,0:T(8,128)(2,1)} %bitcast.137, ...), custom_call_target="tpu_custom_call", output_to_operand_aliasing={{0}: (2, {}), {1}: (3, {})} | custom-call | flops 2415919104 | bytes 25000000 | tf_op jit(solution)/shard_map/pallas_call | solution.py:727
  508.0 40.0 %shard_map.220 = (bf16[2,2,768,768]{3,2,1,0:T(8,128)(2,1)}, bf16[2,2,768,768]{3,2,1,0:T(8,128)(2,1)}, bf16[2,2,768,768]{3,2,1,0:T(8,128)(2,1)}, bf16[2,768,2048]{2,1,0:T(8,128)(2,1)}, bf16[2,768,2048]{2,1,0:T(8,128)(2,1)}) custom-call(bf16[2,2,768,2048]{3,2,1,0:T(8,128)(2,1)} %bitcast.131, ...), custom_call_target="tpu_custom_call", output_to_operand_aliasing={{0}: (17, {}), {1}: (18, {}), {2}: (19, {})} | custom-call | flops 28991029248 | bytes 50000000 | tf_op jit(solution)/shard_map/pallas_call | solution.py:750
  547.9 12.8 %shard_map.221 = (bf16[1536,2048]{1,0:T(8,128)(2,1)}, bf16[1536,2048]{1,0:T(8,128)(2,1)}) custom-call(bf16[8,192,2176]{2,1,0:T(8,128)(2,1)} %all-gather.12.cloned.1.call-done.tok_ref.routing_ref, bf16[2,8,96,2048]{3,2,1,0:T(8,128)(2,1)} %bitcast.142, bf16[2,8,96,2048]{3,2,1,0:T(8,128)(2,1)} %bitcast.143), custom_call_target="tpu_custom_call" | custom-call | flops 2415919104 | bytes 25000000 | tf_op jit(solution)/shard_map/pallas_call | solution.py:772
  566.7 15.4 %convolution_convert_fusion.1 = bf16[2,2048,768]{2,1,0:T(8,128)(2,1)S(1)} fusion(bf16[2,1536,2048]{2,1,0:T(8,128)(2,1)} %bitcast.132, bf16[2,1536,768]{2,1,0:T(8,128)(2,1)} %bitcast.172), kind=kOutput, calls=%fused_computation.2 | convolution fusion | flops 9666822144 | bytes 23592960 | tf_op jit(solution)/shard_map/era,erb->eab/dot_general | solution.py:1156
  585.3 16.8 %convolution_convert_fusion.2 = bf16[2,2048,768]{2,1,0:T(8,128)(2,1)} fusion(bf16[2,1536,2048]{2,1,0:T(8,128)(2,1)} %bitcast.133, bf16[2,1536,768]{2,1,0:T(8,128)(2,1)} %bitcast.171), kind=kOutput, calls=%fused_computation.3 | convolution fusion | flops 9666822144 | bytes 23592960 | tf_op jit(solution)/shard_map/era,erb->eab/dot_general | solution.py:1156
  604.7 14.7 %convolution_convert_fusion.3 = bf16[2,768,2048]{2,1,0:T(8,128)(2,1)S(1)} fusion(bf16[2,1536,768]{2,1,0:T(8,128)(2,1)} %bitcast.170, bf16[2,1536,2048]{2,1,0:T(8,128)(2,1)} %bitcast.136), kind=kOutput, calls=%fused_computation.4 | convolution fusion | flops 9666822144 | bytes 23592960 | tf_op jit(solution)/shard_map/era,erb->eab/dot_general | solution.py:1156
  664.2 12.0 %convolution_convert_fusion = bf16[384,4096]{1,0:T(8,128)(2,1)} fusion(bf16[4096,2048]{1,0:T(8,128)(2,1)} %get-tuple-element.163, bf16[192,2048]{1,0:T(8,128)(2,1)S(1)} %get-tuple-element.351, bf16[192,2048]{1,0:T(8,128)(2,1)S(1)} %get-tuple-element.330), kind=kOutput, calls=%fused_computation.1 | convolution fusion | flops 6447169536 | bytes 21495808 | tf_op jit(solution)/shard_map/dot_general | solution.py:35
  683.6 67.4 %shard_map.222 = (bf16[2,192,4096]{2,1,0:T(8,128)(2,1)}, bf16[8,2,192,1024]{3,2,1,0:T(8,128)(2,1)}, f32[1,128]{1,0:T(1,128)}) custom-call(bf16[2,192,4096]{2,1,0:T(8,128)(2,1)} %bitcast.174, bf16[8,2,192,1024]{3,2,1,0:T(8,128)(2,1)} %all-gather.8.cloned.1.call-done.kv_ref, f32[2,1536,384]{2,1,0:T(8,128)} %copy.65.bias_ref, ...), custom_call_target="tpu_custom_call" | custom-call | flops 24159191040 | bytes 30000000 | tf_op jit(solution)/shard_map/pallas_call | solution.py:261
  767.9 109.4 %shard_map.223 = (f32[128,2048]{1,0:T(8,128)}, f32[1,256]{1,0:T(1,128)}) custom-call(bf16[384,4096]{1,0:T(8,128)(2,1)} %bitcast.176, bf16[16,128]{1,0:T(8,128)(2,1)} %broadcast_in_dim.87.extra_ref, bf16[384,2048]{1,0:T(8,128)(2,1)} %pad_maximum_fusion.b_ref, f32[64,256]{1,0:T(8,128)} %pad.37.g_ref), custom_call_target="tpu_custom_call" | custom-call | flops 6442450944 | bytes 10000000 | tf_op jit(solution)/shard_map/pallas_call | solution.py:599
  886.6 12.4 %fusion.7 = (f32[2048]{0:T(1024)S(1)}, f32[384]{0:T(512)S(1)}, f32[384,2048]{1,0:T(8,128)}) fusion(bf16[2,1,192,2048]{3,2,1,0:T(8,128)(2,1)S(1)} %copy-done.4, f32[384]{0:T(512)S(1)} %copy-done.33, f32[2048]{0:T(1024)S(1)} %copy-done.28, f32[384,2048]{1,0:T(8,128)S(1)} %fusion.35, bf16[384,4096]{1,0:T(8,128)(2,1)S(1)} %bitcast.178, ...), kind=kOutput, calls=%fused_computation.19 | convolution fusion | flops 6448739840 | bytes 27806720 | tf_op jit(solution)/shard_map/dot_general | solution.py:35
  899.8 153.6 %shard_map.225 = (f32[160,2048]{1,0:T(8,128)}, f32[1,256]{1,0:T(1,128)}) custom-call(bf16[384,4096]{1,0:T(8,128)(2,1)} %bitcast.177, bf16[1024,384]{1,0:T(8,128)(2,1)} %get-tuple-element.271.extra_ref, bf16[384,2048]{1,0:T(8,128)(2,1)} %fusion.2.x_ref.b_ref, f32[64,256]{1,0:T(8,128)} %bitcast.155), custom_call_target="tpu_custom_call" | custom-call | flops 8053063680 | bytes 10000000 | tf_op jit(solution)/shard_map/pallas_call | solution.py:599
  (298 shorter events, 187.9 us)
Async XLA Ops:
  7.2 178.1 %all-gather.14.cloned.1.call-start = ((), (), s32[]{:S(2)}) async-start(), calls=%async_computation.13 | async-start | bytes 7077888 | tf_op jit(solution)/shard_map/all_gather | solution.py:1084
  10.0 273.9 %all-gather.8.cloned.1.call-start = ((), (), s32[]{:S(2)}) async-start(), calls=%async_computation.5 | async-start | bytes 7077888 | tf_op jit(solution)/shard_map/all_gather | solution.py:1122
  201.8 147.9 %all-gather.16.cloned.1.call-start = ((), (), s32[]{:S(2)}) async-start(), calls=%async_computation.14 | async-start | bytes 7077888 | tf_op jit(solution)/shard_map/all_gather | solution.py:1093
  202.5 222.7 %all-gather.10.cloned.1.call-start = ((), (), s32[]{:S(2)}) async-start(), calls=%async_computation.6 | async-start | bytes 7520256 | tf_op jit(solution)/shard_map/all_gather | solution.py:1144
  203.3 37.6 %collective-permute-start = (bf16[2,512,768]{2,1,0:T(8,128)(2,1)}, bf16[2,512,768]{2,1,0:T(8,128)(2,1)}, u32[]{:S(2)}, u32[]{:S(2)}) collective-permute-start(bf16[2,512,768]{2,1,0:T(8,128)(2,1)} %refs_2_.3), channel_id=1, source_target_pairs={{0,8},{8,0},{16,24},{24,16},{1,9},{9,1},{17,25},{25,17},{2,10},{10... | collective-permute-start | bytes 4718600 | tf_op jit(solution)/shard_map/ppermute | solution.py:806
  218.5 37.6 %collective-permute-start.1 = (bf16[2,512,768]{2,1,0:T(8,128)(2,1)}, bf16[2,512,768]{2,1,0:T(8,128)(2,1)}, u32[]{:S(2)}, u32[]{:S(2)}) collective-permute-start(bf16[2,512,768]{2,1,0:T(8,128)(2,1)} %refs_2_.3), channel_id=1, source_target_pairs={{0,16},{8,24},{16,0},{24,8},{1,17},{9,25},{17,1},{25,9},{2,18},{10... | collective-permute-start | bytes 4718600 | tf_op jit(solution)/shard_map/ppermute | solution.py:806
  219.7 108.1 %collective-permute-start.2 = (bf16[2,512,768]{2,1,0:T(8,128)(2,1)}, bf16[2,512,768]{2,1,0:T(8,128)(2,1)}, u32[]{:S(2)}, u32[]{:S(2)}) collective-permute-start(bf16[2,512,768]{2,1,0:T(8,128)(2,1)} %refs_7_.1), channel_id=1, source_target_pairs={{0,8},{8,0},{16,24},{24,16},{1,9},{9,1},{17,25},{25,17},{2,10},{10... | collective-permute-start | bytes 4718600 | tf_op jit(solution)/shard_map/ppermute | solution.py:806
  221.3 106.6 %collective-permute-start.3 = (bf16[2,512,768]{2,1,0:T(8,128)(2,1)}, bf16[2,512,768]{2,1,0:T(8,128)(2,1)}, u32[]{:S(2)}, u32[]{:S(2)}) collective-permute-start(bf16[2,512,768]{2,1,0:T(8,128)(2,1)} %refs_7_.1), channel_id=1, source_target_pairs={{0,16},{8,24},{16,0},{24,8},{1,17},{9,25},{17,1},{25,9},{2,18},{10... | collective-permute-start | bytes 4718600 | tf_op jit(solution)/shard_map/ppermute | solution.py:806
  221.8 106.0 %collective-permute-start.4 = (bf16[2,768,512]{2,1,0:T(8,128)(2,1)}, bf16[2,768,512]{2,1,0:T(8,128)(2,1)}, u32[]{:S(2)}, u32[]{:S(2)}) collective-permute-start(bf16[2,768,512]{2,1,0:T(8,128)(2,1)} %refs_12_.1), channel_id=1, source_target_pairs={{0,8},{8,0},{16,24},{24,16},{1,9},{9,1},{17,25},{25,17},{2,10},{10... | collective-permute-start | bytes 4718600 | tf_op jit(solution)/shard_map/ppermute | solution.py:806
  240.9 87.0 %collective-permute-start.5 = (bf16[2,768,512]{2,1,0:T(8,128)(2,1)}, bf16[2,768,512]{2,1,0:T(8,128)(2,1)}, u32[]{:S(2)}, u32[]{:S(2)}) collective-permute-start(bf16[2,768,512]{2,1,0:T(8,128)(2,1)} %refs_12_.1), channel_id=1, source_target_pairs={{0,16},{8,24},{16,0},{24,8},{1,17},{9,25},{17,1},{25,9},{2,18},{10... | collective-permute-start | bytes 4718600 | tf_op jit(solution)/shard_map/ppermute | solution.py:806
  351.0 143.0 %all-gather.12.cloned.1.call-start = ((), (), s32[]{:S(2)}) async-start(), calls=%async_computation.7 | async-start | bytes 7520256 | tf_op jit(solution)/shard_map/all_gather | solution.py:1144
  351.6 212.5 %reduce-scatter.6.cloned.1.call-start = ((), (), s32[]{:S(2)}) async-start(), calls=%async_computation.8 | async-start | bytes 7077888 | tf_op jit(solution)/shard_map/reduce_scatter | solution.py:1149
  362.1 44.4 %collective-permute-start.6 = (bf16[1,512,768]{2,1,0:T(8,128)(2,1)S(1)}, bf16[1,512,768]{2,1,0:T(8,128)(2,1)S(1)}, u32[]{:S(2)}, u32[]{:S(2)}) collective-permute-start(bf16[1,512,768]{2,1,0:T(8,128)(2,1)S(1)} %slice.157), channel_id=1, source_target_pairs={{0,16},{8,24},{16,0},{24,8},{1,17},{9,25},{17,1},{25,9},{2,18},{10... | collective-permute-start | bytes 2359304 | tf_op jit(solution)/shard_map/ppermute | solution.py:806
  491.9 149.0 %reduce-scatter.8.cloned.1.call-start = ((), (), s32[]{:S(2)}) async-start(), calls=%async_computation.9 | async-start | bytes 7077888 | tf_op jit(solution)/shard_map/reduce_scatter | solution.py:1149
  564.1 313.1 %reduce-scatter.10.cloned.1.call-start = ((), (), s32[]{:S(2)}) async-start(), calls=%async_computation.10 | async-start | bytes 7077888 | tf_op jit(solution)/shard_map/reduce_scatter | solution.py:1184
  582.2 38.9 %collective-permute-start.16 = (bf16[1,512,768]{2,1,0:T(8,128)(2,1)S(1)}, bf16[1,512,768]{2,1,0:T(8,128)(2,1)S(1)}, u32[]{:S(2)}, u32[]{:S(2)}) collective-permute-start(bf16[1,512,768]{2,1,0:T(8,128)(2,1)S(1)} %get-tuple-element.340), channel_id=1, source_target_pairs={{0,8},{8,0},{16,24},{24,16},{1,9},{9,1},{17,25},{25,17},{2,10},{10... | collective-permute-start | bytes 2359304 | tf_op jit(solution)/shard_map/ppermute | solution.py:806
  583.8 46.7 %collective-permute-start.17 = (bf16[1,512,768]{2,1,0:T(8,128)(2,1)S(1)}, bf16[1,512,768]{2,1,0:T(8,128)(2,1)}, u32[]{:S(2)}, u32[]{:S(2)}) collective-permute-start(bf16[1,512,768]{2,1,0:T(8,128)(2,1)S(1)} %get-tuple-element.339), channel_id=1, source_target_pairs={{0,16},{8,24},{16,0},{24,8},{1,17},{9,25},{17,1},{25,9},{2,18},{10... | collective-permute-start | bytes 2359304 | tf_op jit(solution)/shard_map/ppermute | solution.py:806
  646.9 104.1 %collective-permute-start.23 = (bf16[2,512,768]{2,1,0:T(8,128)(2,1)S(1)}, bf16[2,512,768]{2,1,0:T(8,128)(2,1)}, u32[]{:S(2)}, u32[]{:S(2)}) collective-permute-start(bf16[2,512,768]{2,1,0:T(8,128)(2,1)S(1)} %pad_maximum_fusion.6), channel_id=1, source_target_pairs={{0,16},{8,24},{16,0},{24,8},{1,17},{9,25},{17,1},{25,9},{2,18},{10... | collective-permute-start | bytes 4718600 | tf_op jit(solution)/shard_map/ppermute | solution.py:806
  649.7 105.6 %collective-permute-start.20 = (bf16[2,512,768]{2,1,0:T(8,128)(2,1)S(1)}, bf16[2,512,768]{2,1,0:T(8,128)(2,1)}, u32[]{:S(2)}, u32[]{:S(2)}) collective-permute-start(bf16[2,512,768]{2,1,0:T(8,128)(2,1)S(1)} %pad_maximum_fusion.3), channel_id=1, source_target_pairs={{0,8},{8,0},{16,24},{24,16},{1,9},{9,1},{17,25},{25,17},{2,10},{10... | collective-permute-start | bytes 4718600 | tf_op jit(solution)/shard_map/ppermute | solution.py:806
  653.4 101.8 %collective-permute-start.21 = (bf16[2,512,768]{2,1,0:T(8,128)(2,1)}, bf16[2,512,768]{2,1,0:T(8,128)(2,1)}, u32[]{:S(2)}, u32[]{:S(2)}) collective-permute-start(bf16[2,512,768]{2,1,0:T(8,128)(2,1)} %pad_maximum_fusion.4), channel_id=1, source_target_pairs={{0,16},{8,24},{16,0},{24,8},{1,17},{9,25},{17,1},{25,9},{2,18},{10... | collective-permute-start | bytes 4718600 | tf_op jit(solution)/shard_map/ppermute | solution.py:806
  657.4 102.1 %collective-permute-start.18 = (bf16[2,768,512]{2,1,0:T(8,128)(2,1)}, bf16[2,768,512]{2,1,0:T(8,128)(2,1)}, u32[]{:S(2)}, u32[]{:S(2)}) collective-permute-start(bf16[2,768,512]{2,1,0:T(8,128)(2,1)} %pad_maximum_fusion.1), channel_id=1, source_target_pairs={{0,8},{8,0},{16,24},{24,16},{1,9},{9,1},{17,25},{25,17},{2,10},{10... | collective-permute-start | bytes 4718600 | tf_op jit(solution)/shard_map/ppermute | solution.py:806
  682.4 77.1 %collective-permute-start.19 = (bf16[2,768,512]{2,1,0:T(8,128)(2,1)}, bf16[2,768,512]{2,1,0:T(8,128)(2,1)}, u32[]{:S(2)}, u32[]{:S(2)}) collective-permute-start(bf16[2,768,512]{2,1,0:T(8,128)(2,1)} %pad_maximum_fusion.2), channel_id=1, source_target_pairs={{0,16},{8,24},{16,0},{24,8},{1,17},{9,25},{17,1},{25,9},{2,18},{10... | collective-permute-start | bytes 4718600 | tf_op jit(solution)/shard_map/ppermute | solution.py:806
  763.7 302.1 %reduce-scatter.12.cloned.1.call-start = ((), (), s32[]{:S(2)}) async-start(), calls=%async_computation.11 | async-start | bytes 7077888 | tf_op jit(solution)/shard_map/reduce_scatter | solution.py:1191
  877.3 188.8 %reduce-scatter.14.cloned.1.call-start = ((), (), s32[]{:S(2)}) async-start(), calls=%async_computation.12 | async-start | bytes 7077888 | tf_op jit(solution)/shard_map/reduce_scatter | solution.py:1191
  (59 other events, 1047.8 us)
Sparse Core Ops, SparseCore 0:
  10.3 86.1 all-gather.13
  201.9 82.0 all-gather.7
  286.2 63.4 all-gather.15
  351.8 73.4 all-gather.9
  427.3 66.6 all-gather.11
  496.1 67.9 reduce-scatter.5
  566.4 68.1 reduce-scatter.7
  763.8 98.9 reduce-scatter.9
  877.4 66.0 reduce-scatter.11
  945.7 120.3 reduce-scatter.13

commit v5 on v4

--- a/solution.py
+++ b/solution.py
@@ -281,7 +281,7 @@
 MESH = pl.DeviceIdType.MESH
 
 
-def gather_kernel(phases, count, *refs):
+def gather_kernel(phases, count, late, *refs):
     ins, outs, sems = refs[:count], refs[count : 2 * count], refs[2 * count :]
     dp = lax.axis_index("dp"); member = lax.axis_index("expert")
     blocks = lax.axis_size("expert")
@@ -315,11 +315,13 @@
 
     def make(i):
         src, out = ins[i], outs[i]
+        flat = i in late
         rows = src.shape[0]
         half = rows // 2
         (own_sem, sz, rz, sxy, rxy, sc, rc) = sems[i * 7 : (i + 1) * 7]
         def at(d, s, lo=0, n=rows):
-            return out.at[pl.ds(pl.multiple_of((d * blocks + s * 2 + core) * rows + lo, 16 if half % 16 == 0 else 8), n)]
+            first = s * 2 + core if flat else d * blocks + s * 2 + core
+            return out.at[pl.ds(pl.multiple_of(first * rows + lo, 16 if half % 16 == 0 else 8), n)]
         def copy(a, b, ss, rs, to):
             return pltpu.make_async_remote_copy(src_ref=a, dst_ref=b, send_sem=ss, recv_sem=rs, device_id=to, device_id_type=MESH)
         def block(d, s):
@@ -337,7 +339,9 @@
             return copy(at(y_at, s, half, half), at(y_at, s, half, half), sxy.at[3, s], rxy.at[3, s], by_x)
         def to_core(r, d, s, ref): return copy(ref, at(d, s), sc.at[r, s], rc.at[r, s], sibling)
         def spread(s, ref):
-            to_x(s, ref).start(); to_y(s, ref).start(); to_core(0, dp, s, ref).start()
+            if not flat:
+                to_x(s, ref).start(); to_y(s, ref).start()
+            to_core(0, dp, s, ref).start()
         def start():
             local().start()
             guarded(z < depth - 1, lambda: up(z, src).start())
@@ -364,14 +368,16 @@
                 half_y(s).wait_recv(); half_x(s).wait_recv()
                 to_core(3, far_at, s, at(far_at, s)).start()
             guarded(ok, run)
+        owners = (dp,) if flat else (dp, x_at, y_at, far_at)
         def core_wait(s):
-            for r, d in enumerate((dp, x_at, y_at, far_at)):
+            for r, d in enumerate(owners):
                 to_core(r, d, s, at(d, s)).wait_recv()
         def finish():
             local().wait()
             for s in range(depth):
-                for c in (to_x(s, at(dp, s)), to_y(s, at(dp, s)), half_y(s), half_x(s)): c.wait_send()
-                for r, d in enumerate((dp, x_at, y_at, far_at)): to_core(r, d, s, at(d, s)).wait_send()
+                if not flat:
+                    for c in (to_x(s, at(dp, s)), to_y(s, at(dp, s)), half_y(s), half_x(s)): c.wait_send()
+                for r, d in enumerate(owners): to_core(r, d, s, at(d, s)).wait_send()
                 guarded((z >= s) & (z < depth - 1), lambda: up(s, at(dp, s)).wait_send())
                 guarded((z <= s) & (z > 0), lambda: down(s, at(dp, s)).wait_send())
         it.start, it.z_event, it.near_event, it.far_event, it.core_wait, it.finish = start, z_event, near_event, far_event, core_wait, finish
@@ -383,6 +389,8 @@
     for n, phase in enumerate(phases):
         its = [items[i] for i in phase]
         for it in its: it.start()
+        lates = [items[i] for i in late]
+        for it in lates: it.start()
         for d in range(1, depth + 2):
             if d < depth:
                 for s, ok, rising in around(d):
@@ -390,15 +398,17 @@
             if d - 1 < depth:
                 for s, ok, _ in around(d - 1):
                     for it in its: it.near_event(s, ok)
+            if d < depth:
+                for s, ok, rising in around(d):
+                    for it in lates: it.z_event(s, ok, rising)
             if d - 2 >= 0:
                 for s, ok, _ in around(d - 2):
                     for it in its: it.far_event(s, ok)
-            if n + 1 < len(phases) and d == depth: pass
     for it in items:
         for s in range(depth): it.core_wait(s)
     for it in items: it.finish()
 
-def gather_rows(arrays, phases, cid):
+def gather_rows(arrays, phases, cid, late=()):
     shards = lax.axis_size("dp") * lax.axis_size("expert")
     depth = lax.axis_size("expert") // 2
     D = pltpu.SemaphoreType.DMA
@@ -406,8 +416,11 @@
     for _ in arrays:
         sems += [D, D((2, depth)), D((depth,)), D((4, depth)), D((4, depth)), D((4, depth)), D((4, depth))]
     return pl.pallas_call(
-        functools.partial(gather_kernel, phases, len(arrays)),
-        out_shape=[jax.ShapeDtypeStruct((shards * a.shape[0],) + a.shape[1:], a.dtype) for a in arrays],
+        functools.partial(gather_kernel, phases, len(arrays), late),
+        out_shape=[
+            jax.ShapeDtypeStruct(((2 * depth if i in late else shards) * a.shape[0],) + a.shape[1:], a.dtype)
+            for i, a in enumerate(arrays)
+        ],
         in_specs=[pl.BlockSpec(memory_space=pl.ANY)] * len(arrays),
         out_specs=[pl.BlockSpec(memory_space=pl.ANY)] * len(arrays),
         scratch_shapes=sems,
@@ -1078,20 +1091,17 @@
     gain_len = norm_gains.shape[0]
     gain_shard = jnp.zeros((2048,), bf16).at[:gain_len].set(norm_gains).reshape(16, 128)
     kv_w = jnp.concatenate([w_key.T, w_value.T], axis=0)
-    q_w, kv_w, out_w, gain_full = gather_rows(
-        [w_query.T, kv_w, w_output, gain_shard], [(3, 0, 1, 2)], 1
-    )
-    cot_0 = lax.all_gather(cotangent[0, 0], "expert", axis=0, tiled=False)
-    q_w, cot_0, cot_1, w_gate, w_up, w_down = tie(
-        (q_w, cot_0, cotangent[1, 0], w_gate, w_up, w_down)
-    )
+    q_w, kv_w, out_w, gain_full, cot_0 = gather_rows(
+        [w_query.T, kv_w, w_output, gain_shard, cotangent[0, 0]], [(3, 0, 1, 2)], 1, (4,)
+    )
+    cot_0 = cot_0.reshape(blocks, rows, width)
+    q_w, w_gate = tie((q_w, w_gate))
     gains = gain_full.reshape(shards, 2048)[:, :gain_len].reshape(-1).astype(f32)
     gain_in = gains[:width]
     gain_mid = gains[width : 2 * width]
     gain_q = gains[2 * width : 2 * width + HD]
     gain_k = gains[2 * width + HD :]
-    cot_1 = lax.all_gather(cot_1, "expert", axis=0, tiled=False)
-    gate_near, up_near, down_near = ((swap(w, 1), swap(w, 2)) for w in (w_gate, w_up, w_down))
+    gate_near = (swap(w_gate, 1), swap(w_gate, 2))
 
     key_index = jnp.arange(group_len, dtype=jnp.int32)
     start_row = member * rows
@@ -1119,8 +1129,11 @@
     )
     q_low, q_raw = (a.reshape(micro, rows, H * HD) for a in (q_low, q_raw))
     kv_own = kv_own.reshape(micro, rows, KVH * 2 * HD)
+    kv_own, gate_near = tie((kv_own, gate_near))
     kv_all = lax.all_gather(kv_own, "expert", axis=0, tiled=False)
-    kv_all, gate_near = tie((kv_all, gate_near))
+    kv_all, w_up, w_down, cot_1 = tie((kv_all, w_up, w_down, cotangent[1, 0]))
+    cot_1 = lax.all_gather(cot_1, "expert", axis=0, tiled=False)
+    up_near, down_near = ((swap(w, 1), swap(w, 2)) for w in (w_up, w_down))
     chunk = 256
     mixed, logs = run_forward(q_low, kv_all, bias, step_heads, chunk)
     mixed, up_near, down_near = tie((mixed, up_near, down_near))
@@ -1160,7 +1173,7 @@
         scatter_far(weight_grad(picked, d_gate), 1),
         scatter_far(weight_grad(picked, d_up), 1),
     ]
-    d_routeds[-1], scattering = tie((d_routeds[-1], scattering))
+    d_routeds[-1], scattering, mix_parts[0] = tie((d_routeds[-1], scattering, mix_parts[0]))
     expert_grads = [scatter_near(*pieces) for pieces in scattering]
     grad_mid = 0.0
     for at in range(micro):
@@ -1179,17 +1192,18 @@
     d_query, dkv_all, grad_qn = run_backward(
         q_low, kv_all, bias, mixed, d_mixed, logs, q_raw, cos_rows, sine_rows, gain_q, step_heads, chunk
     )
-    mixed_after, d_query, dkv_all, expert_grads = tie((mixed, d_query, dkv_all, expert_grads))
+    mixes = [lax.psum_scatter(mix_parts[0], "expert", scatter_dimension=0, tiled=True)]
+    mixed_after, d_query, dkv_all, expert_grads, mixes = tie(
+        (mixed, d_query, dkv_all, expert_grads, mixes)
+    )
     grad_output, _ = reduce_rows(mixed_after.reshape(total, H * HD), None, d_branch, 2)
     dkv = lax.psum_scatter(dkv_all, "expert", scatter_dimension=0, tiled=False)
     dkv, grad_output, d_query = tie((dkv, grad_output, d_query))
     d_query = d_query.reshape(total, H * HD)
     dkv = dkv.reshape(total, KVH * 2 * HD)
-    mix_parts, dkv = tie((mix_parts, dkv))
-    outputs = []
-    for at in range(micro):
-        mix = lax.psum_scatter(mix_parts[at], "expert", scatter_dimension=0, tiled=True)
-        outputs.append((middle[at] + mix.astype(f32)).astype(bf16))
+    mix_part, dkv = tie((mix_parts[1], dkv))
+    mixes.append(lax.psum_scatter(mix_part, "expert", scatter_dimension=0, tiled=True))
+    outputs = [(middle[at] + mixes[at].astype(f32)).astype(bf16) for at in range(micro)]
     dkv, dkv_t, grad_kn = run_key_back(dkv, k_raw, cosine, sine, gain_k)
     d_normed = mm(d_query, q_w) + mm(dkv, kv_w)
     d_in_norm, grad_in = norm_back(d_normed, hidden, scale_in, gain_in)

time: 1090 us -> 1060 us (0.972)
  Pallas kernels: 694 us -> 645 us
  local copies, waits for them, and re-layouts: 49.1 us -> 62.9 us
  waiting for transfers between devices: 147 us -> 160 us
    pallas_call x2, Pallas kernels: 263 us -> 219 us  [reduce_rows(): pl.pallas_call(functools.partial(reduce_kernel, rows, 4), out_shape=[jax....]
    all_gather x1, waiting for transfers between devices: 27.9 us -> 62.1 us  [body_fast(): kv_all = lax.all_gather(kv_own, 'expert', axis=0, tiled=False)]
  transfers between devices with their start and end apart: 34 -> 33, of which waited for: 17 -> 17; matrix products, arithmetic and copies ran while one was open for 16% -> 18% of each run, Pallas kernels for 63% -> 46%
where the time goes in v5:
time: 1060 us
  Pallas kernels  645 us (61%)
  waiting for transfers between devices  160 us (15%)
  matrix products  86.5 us (8%)
  local copies, waits for them, and re-layouts  62.9 us (6%)
  other arithmetic  58.8 us (6%)
  starting transfers between devices  26.9 us (3%)
  between operations  15 us (1%)
    pallas_call x2, Pallas kernels, reduce_rows(): pl.pallas_call(functools.partial(reduce_kernel, rows, 4), out_shape=[jax....  219 us
    pallas_call x1, Pallas kernels, gather_rows(): pl.pallas_call(functools.partial(gather_kernel, phases, len(arrays), late...  162 us
    ppermute x24, waiting for transfers between devices, swap(): lax.ppermute(values, 'dp', [(i, i ^ bit) for i in range(lax.axis_size('dp...  82.9 us
    pallas_call x2, Pallas kernels, run_experts(): pl.pallas_call(functools.partial(expert_kernel, len(earlier[2:])), grid=(...  80 us
    pallas_call x1, Pallas kernels, run_backward(): pl.pallas_call(functools.partial(attend_backward, step_heads, chunk), gri...  67.1 us
    all_gather x1, waiting for transfers between devices, body_fast(): kv_all = lax.all_gather(kv_own, 'expert', axis=0, tiled=False)  62.1 us
    dot_general x3, matrix products, weight_grad(): jnp.einsum('era,erb->eab', rows_in, rows_out, preferred_element_type=f32)  46.1 us
    pallas_call x1, Pallas kernels, run_forward(): pl.pallas_call(functools.partial(attend_forward, step_heads, chunk), grid...  43.8 us
  transfers between devices with their start and end apart: 33, of which 17 were waited for; matrix products, arithmetic and copies ran while one was open for 18% of the time, Pallas kernels for 46%

profile of v5, /device:TPU:8, one launch (start us, length us, event | category | flops | bytes accessed | tf_op | source)
XLA Modules:
  0.0 1055.8 jit_solution(11903755929408394554)
XLA Ops:
  12.3 161.6 %shard_map.213 = (bf16[4096,2048]{1,0:T(8,128)(2,1)}, bf16[1024,2048]{1,0:T(8,128)(2,1)}, bf16[4096,2048]{1,0:T(8,128)(2,1)}, bf16[512,128]{1,0:T(8,128)(2,1)}, bf16[1536,2048]{1,0:T(8,128)(2,1)}) custom-call(bf16[128,2048]{1,0:T(8,128)(2,1)} %bitcast.153, bf16[32,2048]{1,0:T(8,128)(2,1)} %pad_maximum_fusion.11.refs_1_, bf16[128,2048]{1,0:T(8,128)(2,1)} %refs_2_.1, ...), custom_call_target="tpu_custom_call" | custom-call | bytes 400000000 | tf_op jit(solution)/shard_map/pallas_call | solution.py:418
  189.4 16.5 %shard_map.214 = (bf16[384,4096]{1,0:T(8,128)(2,1)}, f32[384,4096]{1,0:T(8,128)}, bf16[384,1024]{1,0:T(8,128)(2,1)}, f32[384,512]{1,0:T(8,128)}, bf16[1024,2048]{1,0:T(8,128)(2,1)}) custom-call(bf16[384,2048]{1,0:T(8,128)(2,1)} %fusion.2.x_ref.b_ref, bf16[4096,2048]{1,0:T(8,128)(2,1)} %get-tuple-element.155.wq_ref, ...), custom_call_target="tpu_custom_call" | custom-call | flops 8053063680 | bytes 40000000 | tf_op jit(solution)/shard_map/pallas_call | solution.py:96
  212.4 62.1 %all-gather.11.cloned.1.call-done = bf16[16,192,1024]{2,1,0:T(8,128)(2,1)} async-done(((bf16[2,192,1024]{2,1,0:T(8,128)(2,1)}), bf16[16,192,1024]{2,1,0:T(8,128)(2,1)}) %all-gather.11.cloned.1.call-update) | async-done | bytes 6291472 | tf_op jit(solution)/shard_map/all_gather | solution.py:1133
  293.9 43.8 %shard_map.215 = (bf16[2,192,4096]{2,1,0:T(8,128)(2,1)}, f32[2,4,4,384]{3,2,1,0:T(4,128)}) custom-call(bf16[2,192,4096]{2,1,0:T(8,128)(2,1)} %bitcast.181, bf16[8,2,192,1024]{3,2,1,0:T(8,128)(2,1)} %bitcast.175, f32[2,1536,384]{2,1,0:T(8,128)} %copy.65.bias_ref), custom_call_target="tpu_custom_call" | custom-call | flops 9663676416 | bytes 20000000 | tf_op jit(solution)/shard_map/pallas_call | solution.py:239
  337.7 22.2 %collective-permute-done.4.refs_13_ = bf16[2,768,512]{2,1,0:T(8,128)(2,1)} collective-permute-done((bf16[2,768,512]{2,1,0:T(8,128)(2,1)}, bf16[2,768,512]{2,1,0:T(8,128)(2,1)}, u32[]{:S(2)}, u32[]{:S(2)}) %collective-permute-start.4) | collective-permute-done | bytes 1572896 | tf_op jit(solution)/shard_map/ppermute | solution.py:819
  361.2 11.3 %multiply_reduce_fusion = (f32[384]{0:T(512)S(1)}, f32[384,2048]{1,0:T(8,128)S(1)}) fusion(bf16[384,4096]{1,0:T(8,128)(2,1)} %bitcast.183, bf16[4096,2048]{1,0:T(8,128)(2,1)} %get-tuple-element.166, bf16[2,1,192,2048]{3,2,1,0:T(8,128)(2,1)S(1)} %copy-done.2), kind=kOutput, calls=%fused_computation.24 | convolution fusion | flops 6445596160 | bytes 24643072 | tf_op jit(solution)/shard_map/dot_general | solution.py:35
  389.1 8.5 collective-permute-done.6.refs_5_
  400.3 14.1 %collective-permute-done.10.refs_15_ = bf16[1,768,512]{2,1,0:T(8,128)(2,1)S(1)} collective-permute-done((bf16[1,768,512]{2,1,0:T(8,128)(2,1)S(1)}, bf16[1,768,512]{2,1,0:T(8,128)(2,1)S(1)}, u32[]{:S(2)}, u32[]{:S(2)}) %collective-permute-start.10) | collective-permute-done | bytes 786464 | tf_op jit(solution)/shard_map/ppermute | solution.py:819
  417.1 12.2 %collective-permute-done.8.refs_10_ = bf16[1,512,768]{2,1,0:T(8,128)(2,1)S(1)} collective-permute-done((bf16[1,512,768]{2,1,0:T(8,128)(2,1)S(1)}, bf16[1,512,768]{2,1,0:T(8,128)(2,1)S(1)}, u32[]{:S(2)}, u32[]{:S(2)}) %collective-permute-start.8) | collective-permute-done | bytes 786464 | tf_op jit(solution)/shard_map/ppermute | solution.py:819
  431.9 9.9 all-gather.9.cloned.1.call-done.tok_ref.routing_ref
  441.8 14.0 %shard_map.216 = (bf16[2,2,8,96,2048]{4,3,2,1,0:T(8,128)(2,1)}, bf16[2,2,8,96,2048]{4,3,2,1,0:T(8,128)(2,1)}) custom-call(bf16[8,192,2176]{2,1,0:T(8,128)(2,1)} %all-gather.9.cloned.1.call-done.tok_ref.routing_ref, bf16[8,192,2048]{2,1,0:T(8,128)(2,1)} %bitcast.142), custom_call_target="tpu_custom_call" | custom-call | flops 2415919104 | bytes 25000000 | tf_op jit(solution)/shard_map/pallas_call | solution.py:740
  455.9 40.0 %shard_map.217 = (bf16[2,2,768,768]{3,2,1,0:T(8,128)(2,1)}, bf16[2,2,768,768]{3,2,1,0:T(8,128)(2,1)}, bf16[2,2,768,768]{3,2,1,0:T(8,128)(2,1)}, bf16[2,768,2048]{2,1,0:T(8,128)(2,1)}, bf16[2,768,2048]{2,1,0:T(8,128)(2,1)}) custom-call(bf16[2,2,768,2048]{3,2,1,0:T(8,128)(2,1)} %bitcast.132, bf16[2,2,768,2048]{3,2,1,0:T(8,128)(2,1)} %bitcast.136, ...), custom_call_target="tpu_custom_call" | custom-call | flops 28991029248 | bytes 50000000 | tf_op jit(solution)/shard_map/pallas_call | solution.py:763
  495.9 12.8 %shard_map.218 = (bf16[1536,2048]{1,0:T(8,128)(2,1)}, bf16[1536,2048]{1,0:T(8,128)(2,1)}) custom-call(bf16[8,192,2176]{2,1,0:T(8,128)(2,1)} %all-gather.9.cloned.1.call-done.tok_ref.routing_ref, bf16[2,8,96,2048]{3,2,1,0:T(8,128)(2,1)} %bitcast.150, bf16[2,8,96,2048]{3,2,1,0:T(8,128)(2,1)} %bitcast.151), custom_call_target="tpu_custom_call" | custom-call | flops 2415919104 | bytes 25000000 | tf_op jit(solution)/shard_map/pallas_call | solution.py:785
  510.5 14.0 %shard_map.219 = (bf16[2,2,8,96,2048]{4,3,2,1,0:T(8,128)(2,1)}, bf16[2,2,8,96,2048]{4,3,2,1,0:T(8,128)(2,1)}) custom-call(bf16[8,192,2176]{2,1,0:T(8,128)(2,1)} %all-gather.7.cloned.1.call-done.tok_ref.routing_ref, bf16[8,192,2048]{2,1,0:T(8,128)(2,1)} %bitcast.141, ...), custom_call_target="tpu_custom_call", output_to_operand_aliasing={{0}: (2, {}), {1}: (3, {})} | custom-call | flops 2415919104 | bytes 25000000 | tf_op jit(solution)/shard_map/pallas_call | solution.py:740
  524.5 40.0 %shard_map.220 = (bf16[2,2,768,768]{3,2,1,0:T(8,128)(2,1)}, bf16[2,2,768,768]{3,2,1,0:T(8,128)(2,1)}, bf16[2,2,768,768]{3,2,1,0:T(8,128)(2,1)}, bf16[2,768,2048]{2,1,0:T(8,128)(2,1)}, bf16[2,768,2048]{2,1,0:T(8,128)(2,1)}) custom-call(bf16[2,2,768,2048]{3,2,1,0:T(8,128)(2,1)} %bitcast.133, ...), custom_call_target="tpu_custom_call", output_to_operand_aliasing={{0}: (17, {}), {1}: (18, {}), {2}: (19, {})} | custom-call | flops 28991029248 | bytes 50000000 | tf_op jit(solution)/shard_map/pallas_call | solution.py:763
  564.5 12.8 %shard_map.221 = (bf16[1536,2048]{1,0:T(8,128)(2,1)}, bf16[1536,2048]{1,0:T(8,128)(2,1)}) custom-call(bf16[8,192,2176]{2,1,0:T(8,128)(2,1)} %all-gather.7.cloned.1.call-done.tok_ref.routing_ref, bf16[2,8,96,2048]{3,2,1,0:T(8,128)(2,1)} %bitcast.148, bf16[2,8,96,2048]{3,2,1,0:T(8,128)(2,1)} %bitcast.149), custom_call_target="tpu_custom_call" | custom-call | flops 2415919104 | bytes 25000000 | tf_op jit(solution)/shard_map/pallas_call | solution.py:785
  580.9 16.8 %convolution_convert_fusion.1 = bf16[2,2048,768]{2,1,0:T(8,128)(2,1)} fusion(bf16[2,1536,2048]{2,1,0:T(8,128)(2,1)} %bitcast.134, bf16[2,1536,768]{2,1,0:T(8,128)(2,1)} %bitcast.180), kind=kOutput, calls=%fused_computation.2 | convolution fusion | flops 9666822144 | bytes 23592960 | tf_op jit(solution)/shard_map/era,erb->eab/dot_general | solution.py:1169
  603.4 16.9 %convolution_convert_fusion.2 = bf16[2,2048,768]{2,1,0:T(8,128)(2,1)} fusion(bf16[2,1536,2048]{2,1,0:T(8,128)(2,1)} %bitcast.135, bf16[2,1536,768]{2,1,0:T(8,128)(2,1)} %bitcast.179), kind=kOutput, calls=%fused_computation.3 | convolution fusion | flops 9666822144 | bytes 23592960 | tf_op jit(solution)/shard_map/era,erb->eab/dot_general | solution.py:1169
  624.0 12.4 %convolution_convert_fusion.3 = bf16[2,768,2048]{2,1,0:T(8,128)(2,1)S(1)} fusion(bf16[2,1536,768]{2,1,0:T(8,128)(2,1)} %bitcast.178, bf16[2,1536,2048]{2,1,0:T(8,128)(2,1)S(1)} %bitcast.140), kind=kOutput, calls=%fused_computation.4 | convolution fusion | flops 9666822144 | bytes 23592960 | tf_op jit(solution)/shard_map/era,erb->eab/dot_general | solution.py:1169
  688.4 12.1 %convolution_convert_fusion = bf16[384,4096]{1,0:T(8,128)(2,1)} fusion(bf16[4096,2048]{1,0:T(8,128)(2,1)} %get-tuple-element.166, bf16[192,2048]{1,0:T(8,128)(2,1)S(1)} %get-tuple-element.355, bf16[192,2048]{1,0:T(8,128)(2,1)S(1)} %get-tuple-element.334), kind=kOutput, calls=%fused_computation.1 | convolution fusion | flops 6447169536 | bytes 21495808 | tf_op jit(solution)/shard_map/dot_general | solution.py:35
  706.4 67.1 %shard_map.222 = (bf16[2,192,4096]{2,1,0:T(8,128)(2,1)}, bf16[8,2,192,1024]{3,2,1,0:T(8,128)(2,1)}, f32[1,128]{1,0:T(1,128)}) custom-call(bf16[2,192,4096]{2,1,0:T(8,128)(2,1)} %bitcast.182, bf16[8,2,192,1024]{3,2,1,0:T(8,128)(2,1)} %bitcast.176, f32[2,1536,384]{2,1,0:T(8,128)} %copy.65.bias_ref, bf16[2,192,4096]{2,1,0:T(8,128)(2,1)} %get-tuple-element.265.o_ref, ...), custom_call_target="tpu_custom_call" | custom-call | flops 24159191040 | bytes 30000000 | tf_op jit(solution)/shard_map/pallas_call | solution.py:261
  790.4 108.2 %shard_map.223 = (f32[128,2048]{1,0:T(8,128)}, f32[1,256]{1,0:T(1,128)}) custom-call(bf16[384,4096]{1,0:T(8,128)(2,1)} %bitcast.184, bf16[16,128]{1,0:T(8,128)(2,1)} %broadcast_in_dim.87.extra_ref, bf16[384,2048]{1,0:T(8,128)(2,1)} %pad_maximum_fusion.b_ref, f32[64,256]{1,0:T(8,128)} %pad.37.g_ref), custom_call_target="tpu_custom_call" | custom-call | flops 6442450944 | bytes 10000000 | tf_op jit(solution)/shard_map/pallas_call | solution.py:612
  908.0 12.0 %fusion.7 = (f32[2048]{0:T(1024)S(1)}, f32[384]{0:T(512)S(1)}, f32[384,2048]{1,0:T(8,128)}) fusion(bf16[2,1,192,2048]{3,2,1,0:T(8,128)(2,1)S(1)} %copy-done.3, f32[384]{0:T(512)S(1)} %copy-done.34, f32[2048]{0:T(1024)S(1)} %copy-done.28, f32[384,2048]{1,0:T(8,128)S(1)} %fusion.35, bf16[384,4096]{1,0:T(8,128)(2,1)S(1)} %bitcast.186, ...), kind=kOutput, calls=%fused_computation.19 | convolution fusion | flops 6448739840 | bytes 27806720 | tf_op jit(solution)/shard_map/dot_general | solution.py:35
  920.8 110.9 %shard_map.225 = (f32[160,2048]{1,0:T(8,128)}, f32[1,256]{1,0:T(1,128)}) custom-call(bf16[384,4096]{1,0:T(8,128)(2,1)} %bitcast.185, bf16[1024,384]{1,0:T(8,128)(2,1)} %get-tuple-element.275.extra_ref, bf16[384,2048]{1,0:T(8,128)(2,1)} %fusion.2.x_ref.b_ref, f32[64,256]{1,0:T(8,128)} %bitcast.161), custom_call_target="tpu_custom_call" | custom-call | flops 8053063680 | bytes 10000000 | tf_op jit(solution)/shard_map/pallas_call | solution.py:612
  (319 shorter events, 188.6 us)
Async XLA Ops:
  7.2 267.3 %all-gather.11.cloned.1.call-start = ((), (), s32[]{:S(2)}) async-start(), calls=%async_computation.12 | async-start | bytes 7077888 | tf_op jit(solution)/shard_map/all_gather | solution.py:1133
  173.9 37.2 %collective-permute-start = (bf16[2,512,768]{2,1,0:T(8,128)(2,1)}, bf16[2,512,768]{2,1,0:T(8,128)(2,1)S(1)}, u32[]{:S(2)}, u32[]{:S(2)}) collective-permute-start(bf16[2,512,768]{2,1,0:T(8,128)(2,1)} %refs_2_.3), channel_id=1, source_target_pairs={{0,8},{8,0},{16,24},{24,16},{1,9},{9,1},{17,25},{25,17},{2,10},{10... | collective-permute-start | bytes 4718600 | tf_op jit(solution)/shard_map/ppermute | solution.py:819
  175.4 36.9 %collective-permute-start.1 = (bf16[2,512,768]{2,1,0:T(8,128)(2,1)}, bf16[2,512,768]{2,1,0:T(8,128)(2,1)}, u32[]{:S(2)}, u32[]{:S(2)}) collective-permute-start(bf16[2,512,768]{2,1,0:T(8,128)(2,1)} %refs_2_.3), channel_id=1, source_target_pairs={{0,16},{8,24},{16,0},{24,8},{1,17},{9,25},{17,1},{25,9},{2,18},{10... | collective-permute-start | bytes 4718600 | tf_op jit(solution)/shard_map/ppermute | solution.py:819
  212.4 162.4 %all-gather.13.cloned.1.call-start = ((), (), s32[]{:S(2)}) async-start(), calls=%async_computation.13 | async-start | bytes 7077888 | tf_op jit(solution)/shard_map/all_gather | solution.py:1135
  274.6 167.2 %all-gather.9.cloned.1.call-start = ((), (), s32[]{:S(2)}) async-start(), calls=%async_computation.6 | async-start | bytes 7520256 | tf_op jit(solution)/shard_map/all_gather | solution.py:1157
  289.3 48.4 %collective-permute-start.2 = (bf16[2,512,768]{2,1,0:T(8,128)(2,1)}, bf16[2,512,768]{2,1,0:T(8,128)(2,1)}, u32[]{:S(2)}, u32[]{:S(2)}) collective-permute-start(bf16[2,512,768]{2,1,0:T(8,128)(2,1)} %refs_7_.1), channel_id=1, source_target_pairs={{0,8},{8,0},{16,24},{24,16},{1,9},{9,1},{17,25},{25,17},{2,10},{10... | collective-permute-start | bytes 4718600 | tf_op jit(solution)/shard_map/ppermute | solution.py:819
  290.9 46.8 %collective-permute-start.3 = (bf16[2,512,768]{2,1,0:T(8,128)(2,1)}, bf16[2,512,768]{2,1,0:T(8,128)(2,1)}, u32[]{:S(2)}, u32[]{:S(2)}) collective-permute-start(bf16[2,512,768]{2,1,0:T(8,128)(2,1)} %refs_7_.1), channel_id=1, source_target_pairs={{0,16},{8,24},{16,0},{24,8},{1,17},{9,25},{17,1},{25,9},{2,18},{10... | collective-permute-start | bytes 4718600 | tf_op jit(solution)/shard_map/ppermute | solution.py:819
  292.3 67.6 %collective-permute-start.4 = (bf16[2,768,512]{2,1,0:T(8,128)(2,1)}, bf16[2,768,512]{2,1,0:T(8,128)(2,1)}, u32[]{:S(2)}, u32[]{:S(2)}) collective-permute-start(bf16[2,768,512]{2,1,0:T(8,128)(2,1)} %refs_12_.1), channel_id=1, source_target_pairs={{0,8},{8,0},{16,24},{24,16},{1,9},{9,1},{17,25},{25,17},{2,10},{10... | collective-permute-start | bytes 4718600 | tf_op jit(solution)/shard_map/ppermute | solution.py:819
  292.9 68.3 %collective-permute-start.5 = (bf16[2,768,512]{2,1,0:T(8,128)(2,1)}, bf16[2,768,512]{2,1,0:T(8,128)(2,1)}, u32[]{:S(2)}, u32[]{:S(2)}) collective-permute-start(bf16[2,768,512]{2,1,0:T(8,128)(2,1)} %refs_12_.1), channel_id=1, source_target_pairs={{0,16},{8,24},{16,0},{24,8},{1,17},{9,25},{17,1},{25,9},{2,18},{10... | collective-permute-start | bytes 4718600 | tf_op jit(solution)/shard_map/ppermute | solution.py:819
  376.1 134.4 %all-gather.7.cloned.1.call-start = ((), (), s32[]{:S(2)}) async-start(), calls=%async_computation.5 | async-start | bytes 7520256 | tf_op jit(solution)/shard_map/all_gather | solution.py:1157
  376.7 204.0 %reduce-scatter.6.cloned.1.call-start = ((), (), s32[]{:S(2)}) async-start(), calls=%async_computation.7 | async-start | bytes 7077888 | tf_op jit(solution)/shard_map/reduce_scatter | solution.py:1162
  386.3 43.0 %collective-permute-start.8 = (bf16[1,512,768]{2,1,0:T(8,128)(2,1)S(1)}, bf16[1,512,768]{2,1,0:T(8,128)(2,1)S(1)}, u32[]{:S(2)}, u32[]{:S(2)}) collective-permute-start(bf16[1,512,768]{2,1,0:T(8,128)(2,1)S(1)} %slice.161), channel_id=1, source_target_pairs={{0,16},{8,24},{16,0},{24,8},{1,17},{9,25},{17,1},{25,9},{2,18},{10... | collective-permute-start | bytes 2359304 | tf_op jit(solution)/shard_map/ppermute | solution.py:819
  508.6 152.8 %reduce-scatter.8.cloned.1.call-start = ((), (), s32[]{:S(2)}) async-start(), calls=%async_computation.8 | async-start | bytes 7077888 | tf_op jit(solution)/shard_map/reduce_scatter | solution.py:1162
  580.7 205.5 %reduce-scatter.10.cloned.1.call-start = ((), (), s32[]{:S(2)}) async-start(), calls=%async_computation.9 | async-start | bytes 7077888 | tf_op jit(solution)/shard_map/reduce_scatter | solution.py:1195
  600.4 41.5 %collective-permute-start.16 = (bf16[1,512,768]{2,1,0:T(8,128)(2,1)}, bf16[1,512,768]{2,1,0:T(8,128)(2,1)}, u32[]{:S(2)}, u32[]{:S(2)}) collective-permute-start(bf16[1,512,768]{2,1,0:T(8,128)(2,1)} %get-tuple-element.344), channel_id=1, source_target_pairs={{0,8},{8,0},{16,24},{24,16},{1,9},{9,1},{17,25},{25,17},{2,10},{10... | collective-permute-start | bytes 2359304 | tf_op jit(solution)/shard_map/ppermute | solution.py:819
  601.9 52.4 %collective-permute-start.17 = (bf16[1,512,768]{2,1,0:T(8,128)(2,1)}, bf16[1,512,768]{2,1,0:T(8,128)(2,1)}, u32[]{:S(2)}, u32[]{:S(2)}) collective-permute-start(bf16[1,512,768]{2,1,0:T(8,128)(2,1)} %get-tuple-element.343), channel_id=1, source_target_pairs={{0,16},{8,24},{16,0},{24,8},{1,17},{9,25},{17,1},{25,9},{2,18},{10... | collective-permute-start | bytes 2359304 | tf_op jit(solution)/shard_map/ppermute | solution.py:819
  661.5 237.2 %reduce-scatter.12.cloned.1.call-start = ((), (), s32[]{:S(2)}) async-start(), calls=%async_computation.10 | async-start | bytes 7077888 | tf_op jit(solution)/shard_map/reduce_scatter | solution.py:1200
  667.5 37.5 %collective-permute-start.22 = (bf16[2,512,768]{2,1,0:T(8,128)(2,1)S(1)}, bf16[2,512,768]{2,1,0:T(8,128)(2,1)}, u32[]{:S(2)}, u32[]{:S(2)}) collective-permute-start(bf16[2,512,768]{2,1,0:T(8,128)(2,1)S(1)} %pad_maximum_fusion.5), channel_id=1, source_target_pairs={{0,8},{8,0},{16,24},{24,16},{1,9},{9,1},{17,25},{25,17},{2,10},{10... | collective-permute-start | bytes 4718600 | tf_op jit(solution)/shard_map/ppermute | solution.py:819
  669.6 103.9 %collective-permute-start.23 = (bf16[2,512,768]{2,1,0:T(8,128)(2,1)S(1)}, bf16[2,512,768]{2,1,0:T(8,128)(2,1)}, u32[]{:S(2)}, u32[]{:S(2)}) collective-permute-start(bf16[2,512,768]{2,1,0:T(8,128)(2,1)S(1)} %pad_maximum_fusion.6), channel_id=1, source_target_pairs={{0,16},{8,24},{16,0},{24,8},{1,17},{9,25},{17,1},{25,9},{2,18},{10... | collective-permute-start | bytes 4718600 | tf_op jit(solution)/shard_map/ppermute | solution.py:819
  672.9 104.8 %collective-permute-start.20 = (bf16[2,512,768]{2,1,0:T(8,128)(2,1)S(1)}, bf16[2,512,768]{2,1,0:T(8,128)(2,1)}, u32[]{:S(2)}, u32[]{:S(2)}) collective-permute-start(bf16[2,512,768]{2,1,0:T(8,128)(2,1)S(1)} %pad_maximum_fusion.3), channel_id=1, source_target_pairs={{0,8},{8,0},{16,24},{24,16},{1,9},{9,1},{17,25},{25,17},{2,10},{10... | collective-permute-start | bytes 4718600 | tf_op jit(solution)/shard_map/ppermute | solution.py:819
  677.3 100.4 %collective-permute-start.21 = (bf16[2,512,768]{2,1,0:T(8,128)(2,1)}, bf16[2,512,768]{2,1,0:T(8,128)(2,1)}, u32[]{:S(2)}, u32[]{:S(2)}) collective-permute-start(bf16[2,512,768]{2,1,0:T(8,128)(2,1)} %pad_maximum_fusion.4), channel_id=1, source_target_pairs={{0,16},{8,24},{16,0},{24,8},{1,17},{9,25},{17,1},{25,9},{2,18},{10... | collective-permute-start | bytes 4718600 | tf_op jit(solution)/shard_map/ppermute | solution.py:819
  680.7 101.3 %collective-permute-start.18 = (bf16[2,768,512]{2,1,0:T(8,128)(2,1)}, bf16[2,768,512]{2,1,0:T(8,128)(2,1)}, u32[]{:S(2)}, u32[]{:S(2)}) collective-permute-start(bf16[2,768,512]{2,1,0:T(8,128)(2,1)} %pad_maximum_fusion.1), channel_id=1, source_target_pairs={{0,8},{8,0},{16,24},{24,16},{1,9},{9,1},{17,25},{25,17},{2,10},{10... | collective-permute-start | bytes 4718600 | tf_op jit(solution)/shard_map/ppermute | solution.py:819
  705.0 77.0 %collective-permute-start.19 = (bf16[2,768,512]{2,1,0:T(8,128)(2,1)}, bf16[2,768,512]{2,1,0:T(8,128)(2,1)}, u32[]{:S(2)}, u32[]{:S(2)}) collective-permute-start(bf16[2,768,512]{2,1,0:T(8,128)(2,1)} %pad_maximum_fusion.2), channel_id=1, source_target_pairs={{0,16},{8,24},{16,0},{24,8},{1,17},{9,25},{17,1},{25,9},{2,18},{10... | collective-permute-start | bytes 4718600 | tf_op jit(solution)/shard_map/ppermute | solution.py:819
  786.2 257.9 %reduce-scatter.14.cloned.1.call-start = ((), (), s32[]{:S(2)}) async-start(), calls=%async_computation.11 | async-start | bytes 7077888 | tf_op jit(solution)/shard_map/reduce_scatter | solution.py:1205
  (69 other events, 1694.3 us)
Sparse Core Ops, SparseCore 0:
  212.5 61.9 all-gather.10
  276.7 63.3 all-gather.12
  376.2 65.5 all-gather.8
  443.8 66.6 all-gather.6
  512.7 67.9 reduce-scatter.5
  582.8 68.1 reduce-scatter.7
  661.6 65.8 reduce-scatter.9
  786.3 94.8 reduce-scatter.11
  898.8 66.0 reduce-scatter.13

commit v6 on v5

--- a/solution.py
+++ b/solution.py
@@ -183,7 +183,7 @@
     rows = q_ref.shape[1]
     cosine, sine, gain = cos_ref[0], sin_ref[0], gain_ref[...]
 
-    @pl.when((pl.program_id(0) == 0) & (pl.program_id(1) == 0))
+    @pl.when(pl.program_id(0) == 0)
     def _():
         gain_out[...] = jnp.zeros_like(gain_out)
 
@@ -221,61 +221,123 @@
     dkv_ref[:, 0, :, HD:] = dv_acc[...].astype(bf16).reshape(blocks, rows, HD)
 
 
-def attention_specs(micro, rows, group_len, blocks, step_heads):
+def attention_specs(rows, group_len, blocks, step_heads, at):
     wide = PER_KV * HD
-    q_spec = pl.BlockSpec((1, rows, wide), lambda b, g: (b, 0, g))
-    kv_spec = pl.BlockSpec((blocks, 1, rows, 2 * HD), lambda b, g: (0, b, 0, g))
-    bias_spec = pl.BlockSpec((1, group_len, step_heads * rows), lambda b, g: (b, 0, 0))
-    log_spec = pl.BlockSpec((1, 1, PER_KV // step_heads, step_heads * rows), lambda b, g: (b, g, 0, 0))
+    q_spec = pl.BlockSpec((1, rows, wide), lambda g: (at, 0, g))
+    kv_spec = pl.BlockSpec((blocks, 1, rows, 2 * HD), lambda g: (0, 0, 0, g))
+    bias_spec = pl.BlockSpec((1, group_len, step_heads * rows), lambda g: (at, 0, 0))
+    log_spec = pl.BlockSpec((1, 1, PER_KV // step_heads, step_heads * rows), lambda g: (at, g, 0, 0))
     return q_spec, kv_spec, bias_spec, log_spec
 
 
-def run_forward(query, kv_all, bias, step_heads, chunk):
+def run_forward(query, kv_all, bias, step_heads, chunk, at, earlier):
     micro, rows, _ = query.shape
     blocks = kv_all.shape[0]
     group_len = bias.shape[1]
-    q_spec, kv_spec, bias_spec, log_spec = attention_specs(micro, rows, group_len, blocks, step_heads)
-    flops = 4 * micro * rows * H * HD * group_len
+    q_spec, kv_spec, bias_spec, log_spec = attention_specs(rows, group_len, blocks, step_heads, at)
+    flops = 4 * rows * H * HD * group_len
+
+    def kernel(*refs):
+        attend_forward(step_heads, chunk, *refs[:3], *refs[3 + len(earlier) :])
+
     return pl.pallas_call(
-        functools.partial(attend_forward, step_heads, chunk),
-        grid=(micro, KVH),
-        in_specs=[q_spec, kv_spec, bias_spec],
+        kernel,
+        grid=(KVH,),
+        in_specs=[q_spec, kv_spec, bias_spec] + [pl.BlockSpec(memory_space=pl.ANY)] * len(earlier),
         out_specs=[q_spec, log_spec],
         out_shape=[
             jax.ShapeDtypeStruct(query.shape, bf16),
             jax.ShapeDtypeStruct((micro, KVH, PER_KV // step_heads, step_heads * rows), f32),
         ],
+        input_output_aliases={3 + i: i for i in range(len(earlier))},
         compiler_params=pltpu.CompilerParams(vmem_limit_bytes=VMEM_LIMIT),
         cost_estimate=pl.CostEstimate(
             flops=flops, bytes_accessed=20_000_000, transcendentals=flops // (4 * HD)
         ),
-    )(query, kv_all, bias)
-
-
-def run_backward(query, kv_all, bias, mixed, grad, logs, raw, cosine, sine, gain, step_heads, chunk):
+    )(query, kv_all, bias, *earlier)
+
+
+def run_backward(query, kv_all, bias, mixed, grad, logs, raw, cosine, sine, gain, step_heads, chunk, at, earlier):
     micro, rows, _ = query.shape
     blocks = kv_all.shape[0]
     group_len = bias.shape[1]
-    q_spec, kv_spec, bias_spec, log_spec = attention_specs(micro, rows, group_len, blocks, step_heads)
-    flops = 10 * micro * rows * H * HD * group_len
+    q_spec, kv_spec, bias_spec, log_spec = attention_specs(rows, group_len, blocks, step_heads, at)
+    flops = 10 * rows * H * HD * group_len
+    gain_spec = pl.BlockSpec((1, HD), lambda g: (0, 0))
+
+    def kernel(*refs):
+        attend_backward(step_heads, chunk, *refs[:10], *refs[10 + len(earlier) :])
+
     return pl.pallas_call(
-        functools.partial(attend_backward, step_heads, chunk),
-        grid=(micro, KVH),
+        kernel,
+        grid=(KVH,),
         in_specs=[q_spec, kv_spec, bias_spec, q_spec, q_spec, log_spec, q_spec]
-        + [pl.BlockSpec((1, rows, HD), lambda b, g: (b, 0, 0))] * 2
-        + [pl.BlockSpec((1, HD), lambda b, g: (0, 0))],
-        out_specs=[q_spec, kv_spec, pl.BlockSpec((1, HD), lambda b, g: (0, 0))],
+        + [pl.BlockSpec((1, rows, HD), lambda g: (at, 0, 0))] * 2
+        + [gain_spec]
+        + [pl.BlockSpec(memory_space=pl.ANY)] * len(earlier),
+        out_specs=[q_spec, kv_spec, gain_spec],
         out_shape=[
             jax.ShapeDtypeStruct(query.shape, bf16),
             jax.ShapeDtypeStruct(kv_all.shape, bf16),
             jax.ShapeDtypeStruct((1, HD), f32),
         ],
+        input_output_aliases={10 + i: i for i in range(len(earlier))},
         scratch_shapes=[pltpu.VMEM((group_len, HD), f32), pltpu.VMEM((group_len, HD), f32)],
         compiler_params=pltpu.CompilerParams(vmem_limit_bytes=VMEM_LIMIT),
         cost_estimate=pl.CostEstimate(
             flops=flops, bytes_accessed=30_000_000, transcendentals=flops // (10 * HD)
         ),
-    )(query, kv_all, bias, mixed, grad, logs, raw, cosine, sine, gain)
+    )(query, kv_all, bias, mixed, grad, logs, raw, cosine, sine, gain, *earlier)
+
+
+def middle_back(r0_ref, r1_ref, mid_ref, cot_ref, gain_ref, w_ref, mix_ref, dmid_ref, low_ref, gain_out):
+    @pl.when(pl.program_id(0) == 0)
+    def _():
+        gain_sum = 0.0
+        rows = r0_ref.shape[0]
+        for b, ref in enumerate((r0_ref, r1_ref)):
+            grad = ref[...].astype(f32)
+            middle = mid_ref[b]
+            scale = rms_scale(middle)
+            lifted = grad * gain_ref[...]
+            inner = jnp.mean(lifted * middle, axis=-1, keepdims=True)
+            total = cot_ref[b].astype(f32) + scale * lifted - middle * (scale * scale * scale) * inner
+            gain_sum += jnp.sum(grad * middle * scale, axis=0, keepdims=True)
+            dmid_ref[b * rows : (b + 1) * rows] = total
+            low_ref[b * rows : (b + 1) * rows] = total.astype(bf16)
+        gain_out[...] = gain_sum
+
+    mix_ref[...] = mm(low_ref[...], w_ref[...], NT).astype(bf16)
+
+
+def run_middle_back(routed, middle, cot, gain, out_w):
+    micro, rows, width = middle.shape
+    total = micro * rows
+    piece = 512
+    whole = lambda *shape: pl.BlockSpec(shape, lambda i: (0,) * len(shape))
+    return pl.pallas_call(
+        middle_back,
+        grid=(out_w.shape[0] // piece,),
+        in_specs=[whole(rows, width)] * 2
+        + [whole(micro, rows, width)] * 2
+        + [whole(1, width), pl.BlockSpec((piece, width), lambda i: (i, 0))],
+        out_specs=[
+            pl.BlockSpec((total, piece), lambda i: (0, i)),
+            whole(total, width),
+            whole(total, width),
+            whole(1, width),
+        ],
+        out_shape=[
+            jax.ShapeDtypeStruct((total, out_w.shape[0]), bf16),
+            jax.ShapeDtypeStruct((total, width), f32),
+            jax.ShapeDtypeStruct((total, width), bf16),
+            jax.ShapeDtypeStruct((1, width), f32),
+        ],
+        compiler_params=pltpu.CompilerParams(vmem_limit_bytes=VMEM_LIMIT),
+        cost_estimate=pl.CostEstimate(
+            flops=2 * total * width * out_w.shape[0], bytes_accessed=35_000_000, transcendentals=0
+        ),
+    )(*routed, middle, cot, gain, out_w)
 
 
 MESH = pl.DeviceIdType.MESH
@@ -342,10 +404,15 @@
             if not flat:
                 to_x(s, ref).start(); to_y(s, ref).start()
             to_core(0, dp, s, ref).start()
+        def start_up():
+            up(z, src).start()
+        def start_down():
+            down(z, src).start()
         def start():
             local().start()
-            guarded(z < depth - 1, lambda: up(z, src).start())
-            guarded(z > 0, lambda: down(z, src).start())
+            if not flat:
+                guarded(z < depth - 1, start_up)
+                guarded(z > 0, start_down)
             spread(z, src)
         def z_event(s, ok, rising):
             def run():
@@ -380,6 +447,7 @@
                 for r, d in enumerate(owners): to_core(r, d, s, at(d, s)).wait_send()
                 guarded((z >= s) & (z < depth - 1), lambda: up(s, at(dp, s)).wait_send())
                 guarded((z <= s) & (z > 0), lambda: down(s, at(dp, s)).wait_send())
+        it.start_up, it.start_down = start_up, start_down
         it.start, it.z_event, it.near_event, it.far_event, it.core_wait, it.finish = start, z_event, near_event, far_event, core_wait, finish
         return it
     items = [make(i) for i in range(count)]
@@ -391,15 +459,22 @@
         for it in its: it.start()
         lates = [items[i] for i in late]
         for it in lates: it.start()
+        def late_sends(d):
+            for it in lates:
+                if d < depth - 1:
+                    pl.when(z == d)(it.start_up)
+                    pl.when(z == depth - 1 - d)(it.start_down)
+        late_sends(0)
         for d in range(1, depth + 2):
             if d < depth:
                 for s, ok, rising in around(d):
                     for it in its: it.z_event(s, ok, rising)
+                late_sends(d)
             if d - 1 < depth:
                 for s, ok, _ in around(d - 1):
                     for it in its: it.near_event(s, ok)
-            if d < depth:
-                for s, ok, rising in around(d):
+            if d > 2:
+                for s, ok, rising in around(d - 2):
                     for it in lates: it.z_event(s, ok, rising)
             if d - 2 >= 0:
                 for s, ok, _ in around(d - 2):
@@ -653,7 +728,7 @@
 
 def pick_kernel(capacity, local_experts, n_alias, tok_ref, cot_ref, *refs):
     x_ref, dy_ref = refs[n_alias:]
-    width = cot_ref.shape[2]
+    width = cot_ref.shape[3]
     first = lax.axis_index("expert") * local_experts
     routing = tok_ref[0, :, width:]
     hit, _ = picks_of(routing.astype(f32), first, local_experts, capacity)
@@ -663,7 +738,7 @@
     owner = lax.broadcasted_iota(jnp.int32, rows.shape, 0) // capacity
     at = lanes - first - owner
     weight = jnp.sum(jnp.where((at == 32) | (at == 64), rows, 0.0), axis=1, keepdims=True)
-    dy = (mm(hit, cot_ref[0], TN) * weight).astype(bf16)
+    dy = (mm(hit, cot_ref[0, 0], TN) * weight).astype(bf16)
     for e in range(local_experts):
         x_ref[e, 0, 0] = x[e * capacity : (e + 1) * capacity]
         dy_ref[e, 0, 0] = dy[e * capacity : (e + 1) * capacity]
@@ -729,7 +804,7 @@
 
 
 def run_experts(tokens, cot, parts, capacity, batch_at, micro, earlier):
-    blocks, rows, width = cot.shape
+    blocks, _, rows, width = cot.shape
     local_experts, _, hidden = parts[0][0].shape
     flat = [p for group in parts for p in group]
     any_spec = pl.BlockSpec(memory_space=pl.ANY)
@@ -742,7 +817,7 @@
         grid=(blocks,),
         in_specs=[
             pl.BlockSpec((1, rows, tokens.shape[2]), lambda b: (b, 0, 0)),
-            pl.BlockSpec((1, rows, width), lambda b: (b, 0, 0)),
+            pl.BlockSpec((1, 1, rows, width), lambda b: (b, batch_at, 0, 0)),
         ]
         + [any_spec] * len(earlier[:2]),
         out_specs=[picked_spec] * 2,
@@ -823,20 +898,34 @@
     at = lax.axis_index("dp")
     size = total.shape[axis] // 4
 
-    def part(bits):
-        return lax.dynamic_slice_in_dim(total, (at ^ bits) * size, size, axis=axis)
-
-    far = part(3)
-    return [swap(far[:1], 1), swap(far[1:], 2), part(1), part(2), part(0)]
-
-
-def scatter_near(for_y, for_x, near_x, near_y, own):
-    half_y = (near_y[:1].astype(f32) + for_y.astype(f32)).astype(bf16)
-    half_x = (near_x[1:].astype(f32) + for_x.astype(f32)).astype(bf16)
-    near_y = jnp.concatenate([half_y, near_y[1:]], axis=0)
-    near_x = jnp.concatenate([near_x[:1], half_x], axis=0)
-    by_x, by_y = swap(near_x, 1), swap(near_y, 2)
-    return own.astype(f32) + by_x.astype(f32) + by_y.astype(f32)
+    def part(bits, expert):
+        start, sizes = [expert, 0, 0], list(total.shape)
+        start[axis] = (at ^ bits) * size
+        sizes[0], sizes[axis] = 1, size
+        return lax.dynamic_slice(total, start, sizes)
+
+    return [
+        swap(part(3, 0), 1),
+        swap(part(3, 1), 2),
+        part(1, 0),
+        part(2, 1),
+        part(2, 0),
+        part(1, 1),
+        lax.dynamic_slice_in_dim(total, at * size, size, axis=axis),
+    ]
+
+
+def scatter_near(for_y, for_x, by_x, by_y, near_y, near_x, own):
+    by_x, by_y = swap(by_x, 1), swap(by_y, 2)
+    near_y = swap((near_y.astype(f32) + for_y.astype(f32)).astype(bf16), 2)
+    near_x = swap((near_x.astype(f32) + for_x.astype(f32)).astype(bf16), 1)
+    return (by_x, by_y, near_y, near_x, own)
+
+
+def scatter_sum(by_x, by_y, near_y, near_x, own):
+    by_x = jnp.concatenate([by_x, near_x], axis=0).astype(f32)
+    by_y = jnp.concatenate([near_y, by_y], axis=0).astype(f32)
+    return own.astype(f32) + by_x + by_y
 
 
 def body_plain(
@@ -935,7 +1024,10 @@
     kv_own = jnp.concatenate([k_low, value], axis=-1).reshape(micro, rows, KVH * 2 * HD)
     kv_all = lax.all_gather(kv_own, "expert", axis=0, tiled=False)
     chunk = 256
-    mixed, logs = run_forward(q_low, kv_all, bias, step_heads, chunk)
+    mixed = []
+    for at in range(micro):
+        mixed = run_forward(q_low, kv_all[:, at : at + 1], bias, step_heads, chunk, at, mixed)
+    mixed, logs = mixed
 
     branch = mm(mixed.reshape(total, H * HD), out_w)
     middle = hidden + branch
@@ -999,10 +1091,15 @@
     cos_rows = jnp.concatenate([cosine, cosine], axis=-1).reshape(micro, rows, HD)
     sine_rows = jnp.concatenate([-sine_part, sine_part], axis=-1).reshape(micro, rows, HD)
     q_raw = queries.reshape(micro, rows, H * HD)
-    d_query, dkv_all, grad_qn = run_backward(
-        q_low, kv_all, bias, mixed, d_mixed, logs, q_raw, cos_rows, sine_rows, gain_q[None, :], step_heads, chunk
-    )
-    grad_qn = grad_qn[0]
+    d_query, dkv_list, grad_qn = [], [], 0.0
+    for at in range(micro):
+        d_query, dkv_one, part = run_backward(
+            q_low, kv_all[:, at : at + 1], bias, mixed, d_mixed, logs, q_raw, cos_rows, sine_rows,
+            gain_q[None, :], step_heads, chunk, at, [d_query] if at else []
+        )
+        dkv_list.append(dkv_one)
+        grad_qn += part[0]
+    dkv_all = jnp.concatenate(dkv_list, axis=1)
     dkv = lax.psum_scatter(dkv_all, "expert", scatter_dimension=0, tiled=False)
     dkv = dkv.reshape(total, KVH, 2 * HD)
     d_key = rotate(dkv[:, :, :HD].astype(f32), cosine, -sine_part)
@@ -1091,17 +1188,17 @@
     gain_len = norm_gains.shape[0]
     gain_shard = jnp.zeros((2048,), bf16).at[:gain_len].set(norm_gains).reshape(16, 128)
     kv_w = jnp.concatenate([w_key.T, w_value.T], axis=0)
-    q_w, kv_w, out_w, gain_full, cot_0 = gather_rows(
-        [w_query.T, kv_w, w_output, gain_shard, cotangent[0, 0]], [(3, 0, 1, 2)], 1, (4,)
-    )
-    cot_0 = cot_0.reshape(blocks, rows, width)
-    q_w, w_gate = tie((q_w, w_gate))
+    q_w, kv_w, out_w, gain_full, cot_all = gather_rows(
+        [w_query.T, kv_w, w_output, gain_shard, cotangent.reshape(total, width)], [(3, 0, 1, 2)], 1, (4,)
+    )
+    cot_all = cot_all.reshape(blocks, micro, rows, width)
+    q_w, w_gate, w_up, w_down = tie((q_w, w_gate, w_up, w_down))
     gains = gain_full.reshape(shards, 2048)[:, :gain_len].reshape(-1).astype(f32)
     gain_in = gains[:width]
     gain_mid = gains[width : 2 * width]
     gain_q = gains[2 * width : 2 * width + HD]
     gain_k = gains[2 * width + HD :]
-    gate_near = (swap(w_gate, 1), swap(w_gate, 2))
+    gate_near, up_near, down_near = ((swap(w, 1), swap(w, 2)) for w in (w_gate, w_up, w_down))
 
     key_index = jnp.arange(group_len, dtype=jnp.int32)
     start_row = member * rows
@@ -1129,13 +1226,14 @@
     )
     q_low, q_raw = (a.reshape(micro, rows, H * HD) for a in (q_low, q_raw))
     kv_own = kv_own.reshape(micro, rows, KVH * 2 * HD)
-    kv_own, gate_near = tie((kv_own, gate_near))
-    kv_all = lax.all_gather(kv_own, "expert", axis=0, tiled=False)
-    kv_all, w_up, w_down, cot_1 = tie((kv_all, w_up, w_down, cotangent[1, 0]))
-    cot_1 = lax.all_gather(cot_1, "expert", axis=0, tiled=False)
-    up_near, down_near = ((swap(w, 1), swap(w, 2)) for w in (w_up, w_down))
+    kv_0 = lax.all_gather(kv_own[0], "expert", axis=0, tiled=False)
+    kv_1 = lax.all_gather(kv_own[1], "expert", axis=0, tiled=False)
+    kv_0, gate_near = tie((kv_0, gate_near))
+    kv_all = [kv_0[:, None], kv_1[:, None]]
     chunk = 256
-    mixed, logs = run_forward(q_low, kv_all, bias, step_heads, chunk)
+    mixed = run_forward(q_low, kv_all[0], bias, step_heads, chunk, 0, [])
+    mixed, kv_all = tie((mixed, kv_all))
+    mixed, logs = run_forward(q_low, kv_all[1], bias, step_heads, chunk, 1, mixed)
     mixed, up_near, down_near = tie((mixed, up_near, down_near))
     parts = [
         (own, near[0], near[1], swap(near[0][:1], 2), swap(near[1][1:], 1))
@@ -1147,16 +1245,15 @@
     scale_mid = rms_scale(middle)
     routed = (middle * scale_mid * gain_mid).astype(bf16).reshape(micro, rows, width)
     routed = jnp.concatenate([routed, routing], axis=-1)
-    routed, cot_1 = tie((routed, cot_1))
     middle = middle.reshape(micro, rows, width)
     scale_mid = scale_mid.reshape(micro, rows, 1)
 
-    mix_parts, d_routeds, d_branches, d_middles = [], [], [], []
+    mix_parts, d_routeds = [], []
     kept = []
-    for at, cot in enumerate((cot_0, cot_1)):
+    for at in range(micro):
         tokens = lax.all_gather(routed[at], "expert", axis=0, tiled=False)
         tokens, parts = tie((tokens, parts))
-        kept, mix, d_part = run_experts(tokens, cot, parts, capacity, at, micro, kept)
+        kept, mix, d_part = run_experts(tokens, cot_all, parts, capacity, at, micro, kept)
         kept, d_part, mix, d_routeds = tie((kept, d_part, mix, d_routeds))
         mix_parts.append(mix)
         d_routed = lax.psum_scatter(d_part, "expert", scatter_dimension=0, tiled=True)
@@ -1175,29 +1272,27 @@
     ]
     d_routeds[-1], scattering, mix_parts[0] = tie((d_routeds[-1], scattering, mix_parts[0]))
     expert_grads = [scatter_near(*pieces) for pieces in scattering]
-    grad_mid = 0.0
+    d_mixed, d_middle, d_branch, grad_mid = run_middle_back(
+        d_routeds, middle, cotangent[:, 0], gain_mid[None, :], out_w
+    )
+    d_mixed = d_mixed.reshape(micro, rows, H * HD)
+    cos_rows, sine_rows = (a.reshape(micro, rows, HD) for a in (cosine, sine))
+    d_query, dkv_all, grad_qn = [], [], 0.0
     for at in range(micro):
-        d_mid_norm, mid_gain_grad = norm_back(
-            d_routeds[at].astype(f32), middle[at], scale_mid[at], gain_mid
+        d_query, dkv_one, part = run_backward(
+            q_low, kv_all[at], bias, mixed, d_mixed, logs, q_raw, cos_rows, sine_rows, gain_q,
+            step_heads, chunk, at, [d_query] if at else []
         )
-        grad_mid = grad_mid + mid_gain_grad
-        d_middle = cotangent[at, 0].astype(f32) + d_mid_norm
-        d_middles.append(d_middle)
-        d_branches.append(d_middle.astype(bf16))
-
-    d_branch = jnp.concatenate(d_branches, axis=0)
-    d_middle = jnp.concatenate(d_middles, axis=0)
-    d_mixed = mm(d_branch, out_w, NT).astype(bf16).reshape(micro, rows, H * HD)
-    cos_rows, sine_rows = (a.reshape(micro, rows, HD) for a in (cosine, sine))
-    d_query, dkv_all, grad_qn = run_backward(
-        q_low, kv_all, bias, mixed, d_mixed, logs, q_raw, cos_rows, sine_rows, gain_q, step_heads, chunk
-    )
+        dkv_all.append(dkv_one[:, 0])
+        grad_qn += part
     mixes = [lax.psum_scatter(mix_parts[0], "expert", scatter_dimension=0, tiled=True)]
     mixed_after, d_query, dkv_all, expert_grads, mixes = tie(
         (mixed, d_query, dkv_all, expert_grads, mixes)
     )
     grad_output, _ = reduce_rows(mixed_after.reshape(total, H * HD), None, d_branch, 2)
-    dkv = lax.psum_scatter(dkv_all, "expert", scatter_dimension=0, tiled=False)
+    dkv = jnp.concatenate(
+        [lax.psum_scatter(part, "expert", scatter_dimension=0, tiled=False) for part in dkv_all], axis=0
+    )
     dkv, grad_output, d_query = tie((dkv, grad_output, d_query))
     d_query = d_query.reshape(total, H * HD)
     dkv = dkv.reshape(total, KVH * 2 * HD)
@@ -1208,8 +1303,9 @@
     d_normed = mm(d_query, q_w) + mm(dkv, kv_w)
     d_in_norm, grad_in = norm_back(d_normed, hidden, scale_in, gain_in)
     input_grad = d_middle + d_in_norm
-    gain_grads = jnp.concatenate([grad_in, grad_mid, grad_qn[0], grad_kn[0]]).reshape(shards, gain_len)
+    gain_grads = jnp.concatenate([grad_in, grad_mid[0], grad_qn[0], grad_kn[0]]).reshape(shards, gain_len)
     grad_qkv, grad_gains = reduce_rows(d_query, dkv_t, normed, 3, gain_grads)
+    expert_grads = [scatter_sum(*pieces) for pieces in expert_grads]
     return (
         jnp.stack(outputs)[:, None],
         input_grad.reshape(micro, 1, rows, width),

time: 1060 us -> 1070 us (level)
  Pallas kernels: 645 us -> 710 us
  waiting for transfers between devices: 160 us -> 124 us
  matrix products: 86.5 us -> 73 us
    all_gather x2, waiting for transfers between devices: 62.1 us -> 19.5 us  [the longest x1 16.2 us: body_fast(): kv_1 = lax.all_gather(kv_own[1], 'expert', axis=0, tiled=False)]
    pallas_call x1, Pallas kernels: 162 us -> 189 us  [gather_rows(): pl.pallas_call(functools.partial(gather_kernel, phases, len(arrays), late...]
    pallas_call x2 -> x5, Pallas kernels: 111 us -> 137 us  [the longest x2 71.5 us: run_backward(): pl.pallas_call(kernel, grid=(KVH,), in_specs=[q_spec, kv_spec, bias_spec,...]
    dot_general x4 -> x3, matrix products: 40.4 us -> 28.4 us  [mm(): return lax.dot_general(a, b, dims, preferred_element_type=f32)]
    pallas_call x2, Pallas kernels: 219 us -> 231 us  [reduce_rows(): pl.pallas_call(functools.partial(reduce_kernel, rows, 4), out_shape=[jax....]
    ppermute x24 -> x30, starting transfers between devices: 25.6 us -> 33.9 us  [swap(): lax.ppermute(values, 'dp', [(i, i ^ bit) for i in range(lax.axis_size('dp...]
    ppermute x24 -> x30, waiting for transfers between devices: 82.9 us -> 81.2 us  [swap(): lax.ppermute(values, 'dp', [(i, i ^ bit) for i in range(lax.axis_size('dp...]
  transfers between devices with their start and end apart: 33 -> 40, of which waited for: 17 -> 16; matrix products, arithmetic and copies ran while one was open for 18% -> 13% of each run, Pallas kernels for 46% -> 47%
where the time goes in v6:
time: 1070 us
  Pallas kernels  710 us (66%)
  waiting for transfers between devices  124 us (12%)
  matrix products  73 us (7%)
  local copies, waits for them, and re-layouts  57.7 us (5%)
  other arithmetic  50.9 us (5%)
  starting transfers between devices  34.5 us (3%)
  between operations  15.5 us (1%)
    pallas_call x2, Pallas kernels, reduce_rows(): pl.pallas_call(functools.partial(reduce_kernel, rows, 4), out_shape=[jax....  231 us
    pallas_call x1, Pallas kernels, gather_rows(): pl.pallas_call(functools.partial(gather_kernel, phases, len(arrays), late...  189 us
    ppermute x30, waiting for transfers between devices, swap(): lax.ppermute(values, 'dp', [(i, i ^ bit) for i in range(lax.axis_size('dp...  81.2 us
    pallas_call x2, Pallas kernels, run_experts(): pl.pallas_call(functools.partial(expert_kernel, len(earlier[2:])), grid=(...  80 us
    pallas_call x2, Pallas kernels, run_backward(): pl.pallas_call(kernel, grid=(KVH,), in_specs=[q_spec, kv_spec, bias_spec,...  71.5 us
    pallas_call x2, Pallas kernels, run_forward(): pl.pallas_call(kernel, grid=(KVH,), in_specs=[q_spec, kv_spec, bias_spec]...  46.4 us
    dot_general x3, matrix products, weight_grad(): jnp.einsum('era,erb->eab', rows_in, rows_out, preferred_element_type=f32)  44.6 us
    ppermute x30, starting transfers between devices, swap(): lax.ppermute(values, 'dp', [(i, i ^ bit) for i in range(lax.axis_size('dp...  33.9 us
  transfers between devices with their start and end apart: 40, of which 16 were waited for; matrix products, arithmetic and copies ran while one was open for 13% of the time, Pallas kernels for 47%

profile of v6, /device:TPU:8, one launch (start us, length us, event | category | flops | bytes accessed | tf_op | source)
XLA Modules:
  0.0 1065.0 jit_solution(1835971374364207708)
XLA Ops:
  12.2 188.6 %shard_map.213 = (bf16[4096,2048]{1,0:T(8,128)(2,1)}, bf16[1024,2048]{1,0:T(8,128)(2,1)}, bf16[4096,2048]{1,0:T(8,128)(2,1)}, bf16[512,128]{1,0:T(8,128)(2,1)}, bf16[3072,2048]{1,0:T(8,128)(2,1)}) custom-call(bf16[128,2048]{1,0:T(8,128)(2,1)} %bitcast.145, bf16[32,2048]{1,0:T(8,128)(2,1)} %pad_maximum_fusion.5.refs_1_, bf16[128,2048]{1,0:T(8,128)(2,1)} %refs_2_.1, ...), custom_call_target="tpu_custom_call" | custom-call | bytes 400000000 | tf_op jit(solution)/shard_map/pallas_call | solution.py:493
  208.3 16.4 %shard_map.214 = (bf16[384,4096]{1,0:T(8,128)(2,1)}, f32[384,4096]{1,0:T(8,128)}, bf16[384,1024]{1,0:T(8,128)(2,1)}, f32[384,512]{1,0:T(8,128)}, bf16[1024,2048]{1,0:T(8,128)(2,1)}) custom-call(bf16[384,2048]{1,0:T(8,128)(2,1)} %fusion.2.x_ref.b_ref, bf16[4096,2048]{1,0:T(8,128)(2,1)} %get-tuple-element.183.wq_ref, ...), custom_call_target="tpu_custom_call" | custom-call | flops 8053063680 | bytes 40000000 | tf_op jit(solution)/shard_map/pallas_call | solution.py:96
  248.0 17.5 %collective-permute-done.refs_3_ = bf16[2,512,768]{2,1,0:T(8,128)(2,1)} collective-permute-done((bf16[2,512,768]{2,1,0:T(8,128)(2,1)}, bf16[2,512,768]{2,1,0:T(8,128)(2,1)}, u32[]{:S(2)}, u32[]{:S(2)}) %collective-permute-start) | collective-permute-done | bytes 1572896 | tf_op jit(solution)/shard_map/ppermute | solution.py:894
  270.7 23.2 %shard_map.215 = (bf16[2,192,4096]{2,1,0:T(8,128)(2,1)}, f32[2,4,4,384]{3,2,1,0:T(4,128)}) custom-call(bf16[2,192,4096]{2,1,0:T(8,128)(2,1)} %bitcast.175, bf16[8,1,192,1024]{3,2,1,0:T(8,128)(2,1)} %bitcast.168, f32[2,1536,384]{2,1,0:T(8,128)} %copy.72.refs_2_), custom_call_target="tpu_custom_call" | custom-call | flops 4831838208 | bytes 20000000 | tf_op jit(solution)/shard_map/pallas_call | solution.py:243
  293.9 16.2 %all-gather.13.cloned.1.call-done = bf16[1536,1024]{1,0:T(8,128)(2,1)} async-done(((bf16[192,1024]{1,0:T(8,128)(2,1)}), bf16[1536,1024]{1,0:T(8,128)(2,1)}) %all-gather.13.cloned.1.call-update) | async-done | bytes 3145744 | tf_op jit(solution)/shard_map/all_gather | solution.py:1230
  310.2 23.2 %shard_map.216 = (bf16[2,192,4096]{2,1,0:T(8,128)(2,1)}, f32[2,4,4,384]{3,2,1,0:T(4,128)}) custom-call(bf16[2,192,4096]{2,1,0:T(8,128)(2,1)} %bitcast.176, bf16[8,1,192,1024]{3,2,1,0:T(8,128)(2,1)} %bitcast.166, f32[2,1536,384]{2,1,0:T(8,128)} %copy.72.refs_2_, ...), custom_call_target="tpu_custom_call", output_to_operand_aliasing={{0}: (3, {}), {1}: (4, {})} | custom-call | flops 4831838208 | bytes 20000000 | tf_op jit(solution)/shard_map/pallas_call | solution.py:243
  374.1 14.1 %collective-permute-done.8.refs_10_ = bf16[1,512,768]{2,1,0:T(8,128)(2,1)S(1)} collective-permute-done((bf16[1,512,768]{2,1,0:T(8,128)(2,1)S(1)}, bf16[1,512,768]{2,1,0:T(8,128)(2,1)S(1)}, u32[]{:S(2)}, u32[]{:S(2)}) %collective-permute-start.8) | collective-permute-done | bytes 786464 | tf_op jit(solution)/shard_map/ppermute | solution.py:894
  391.0 13.4 %collective-permute-done.6.refs_5_ = bf16[1,512,768]{2,1,0:T(8,128)(2,1)S(1)} collective-permute-done((bf16[1,512,768]{2,1,0:T(8,128)(2,1)S(1)}, bf16[1,512,768]{2,1,0:T(8,128)(2,1)S(1)}, u32[]{:S(2)}, u32[]{:S(2)}) %collective-permute-start.6) | collective-permute-done | bytes 786464 | tf_op jit(solution)/shard_map/ppermute | solution.py:894
  406.9 14.4 %all-gather.9.cloned.1.call-done.tok_ref.routing_ref = bf16[8,192,2176]{2,1,0:T(8,128)(2,1)} async-done(((bf16[1,192,2176]{2,1,0:T(8,128)(2,1)}), bf16[8,192,2176]{2,1,0:T(8,128)(2,1)}) %all-gather.9.cloned.1.call-update) | async-done | bytes 6684688 | tf_op jit(solution)/shard_map/all_gather | solution.py:1254
  421.4 14.0 %shard_map.217 = (bf16[2,2,8,96,2048]{4,3,2,1,0:T(8,128)(2,1)}, bf16[2,2,8,96,2048]{4,3,2,1,0:T(8,128)(2,1)}) custom-call(bf16[8,192,2176]{2,1,0:T(8,128)(2,1)} %all-gather.9.cloned.1.call-done.tok_ref.routing_ref, bf16[8,2,192,2048]{3,2,1,0:T(8,128)(2,1)} %bitcast.124), custom_call_target="tpu_custom_call" | custom-call | flops 2415919104 | bytes 25000000 | tf_op jit(solution)/shard_map/pallas_call | solution.py:815
  435.4 40.0 %shard_map.218 = (bf16[2,2,768,768]{3,2,1,0:T(8,128)(2,1)}, bf16[2,2,768,768]{3,2,1,0:T(8,128)(2,1)}, bf16[2,2,768,768]{3,2,1,0:T(8,128)(2,1)}, bf16[2,768,2048]{2,1,0:T(8,128)(2,1)}, bf16[2,768,2048]{2,1,0:T(8,128)(2,1)}) custom-call(bf16[2,2,768,2048]{3,2,1,0:T(8,128)(2,1)} %bitcast.128, bf16[2,2,768,2048]{3,2,1,0:T(8,128)(2,1)} %bitcast.132, ...), custom_call_target="tpu_custom_call" | custom-call | flops 28991029248 | bytes 50000000 | tf_op jit(solution)/shard_map/pallas_call | solution.py:838
  475.4 12.7 %shard_map.219 = (bf16[1536,2048]{1,0:T(8,128)(2,1)}, bf16[1536,2048]{1,0:T(8,128)(2,1)}) custom-call(bf16[8,192,2176]{2,1,0:T(8,128)(2,1)} %all-gather.9.cloned.1.call-done.tok_ref.routing_ref, bf16[2,8,96,2048]{3,2,1,0:T(8,128)(2,1)} %bitcast.140, bf16[2,8,96,2048]{3,2,1,0:T(8,128)(2,1)} %bitcast.141), custom_call_target="tpu_custom_call" | custom-call | flops 2415919104 | bytes 25000000 | tf_op jit(solution)/shard_map/pallas_call | solution.py:860
  490.1 14.1 %shard_map.220 = (bf16[2,2,8,96,2048]{4,3,2,1,0:T(8,128)(2,1)}, bf16[2,2,8,96,2048]{4,3,2,1,0:T(8,128)(2,1)}) custom-call(bf16[8,192,2176]{2,1,0:T(8,128)(2,1)} %all-gather.7.cloned.1.call-done.tok_ref.routing_ref, bf16[8,2,192,2048]{3,2,1,0:T(8,128)(2,1)} %bitcast.125, ...), custom_call_target="tpu_custom_call", output_to_operand_aliasing={{0}: (2, {}), {1}: (3, {})} | custom-call | flops 2415919104 | bytes 25000000 | tf_op jit(solution)/shard_map/pallas_call | solution.py:815
  504.2 40.0 %shard_map.221 = (bf16[2,2,768,768]{3,2,1,0:T(8,128)(2,1)}, bf16[2,2,768,768]{3,2,1,0:T(8,128)(2,1)}, bf16[2,2,768,768]{3,2,1,0:T(8,128)(2,1)}, bf16[2,768,2048]{2,1,0:T(8,128)(2,1)}, bf16[2,768,2048]{2,1,0:T(8,128)(2,1)}) custom-call(bf16[2,2,768,2048]{3,2,1,0:T(8,128)(2,1)} %bitcast.129, ...), custom_call_target="tpu_custom_call", output_to_operand_aliasing={{0}: (17, {}), {1}: (18, {}), {2}: (19, {})} | custom-call | flops 28991029248 | bytes 50000000 | tf_op jit(solution)/shard_map/pallas_call | solution.py:838
  544.3 12.8 %shard_map.222 = (bf16[1536,2048]{1,0:T(8,128)(2,1)}, bf16[1536,2048]{1,0:T(8,128)(2,1)}) custom-call(bf16[8,192,2176]{2,1,0:T(8,128)(2,1)} %all-gather.7.cloned.1.call-done.tok_ref.routing_ref, bf16[2,8,96,2048]{3,2,1,0:T(8,128)(2,1)} %bitcast.138, bf16[2,8,96,2048]{3,2,1,0:T(8,128)(2,1)} %bitcast.139), custom_call_target="tpu_custom_call" | custom-call | flops 2415919104 | bytes 25000000 | tf_op jit(solution)/shard_map/pallas_call | solution.py:860
  560.3 15.2 %convolution_convert_fusion = bf16[2,2048,768]{2,1,0:T(8,128)(2,1)S(1)} fusion(bf16[2,1536,2048]{2,1,0:T(8,128)(2,1)} %bitcast.130, bf16[2,1536,768]{2,1,0:T(8,128)(2,1)} %bitcast.174), kind=kOutput, calls=%fused_computation.1 | convolution fusion | flops 9666822144 | bytes 23592960 | tf_op jit(solution)/shard_map/era,erb->eab/dot_general | solution.py:1266
  583.7 16.9 %convolution_convert_fusion.1 = bf16[2,2048,768]{2,1,0:T(8,128)(2,1)} fusion(bf16[2,1536,2048]{2,1,0:T(8,128)(2,1)} %bitcast.131, bf16[2,1536,768]{2,1,0:T(8,128)(2,1)} %bitcast.173), kind=kOutput, calls=%fused_computation.2 | convolution fusion | flops 9666822144 | bytes 23592960 | tf_op jit(solution)/shard_map/era,erb->eab/dot_general | solution.py:1266
  606.2 12.4 %convolution_convert_fusion.2 = bf16[2,768,2048]{2,1,0:T(8,128)(2,1)S(1)} fusion(bf16[2,1536,768]{2,1,0:T(8,128)(2,1)} %bitcast.172, bf16[2,1536,2048]{2,1,0:T(8,128)(2,1)S(1)} %bitcast.136), kind=kOutput, calls=%fused_computation.3 | convolution fusion | flops 9666822144 | bytes 23592960 | tf_op jit(solution)/shard_map/era,erb->eab/dot_general | solution.py:1266
  663.4 18.7 %shard_map.223 = (bf16[384,4096]{1,0:T(8,128)(2,1)}, f32[384,2048]{1,0:T(8,128)}, bf16[384,2048]{1,0:T(8,128)(2,1)}, f32[1,2048]{1,0:T(1,128)}) custom-call(bf16[192,2048]{1,0:T(8,128)(2,1)} %reduce-scatter.7.cloned.1.call-done.r0_ref, bf16[192,2048]{1,0:T(8,128)(2,1)} %reduce-scatter.9.cloned.1.call-done.r1_ref, f32[2,192,2048]{2,1,0:T(8,128)} %bitcast.127, ...), custom_call_target="tpu_custom_call" | custom-call | flops 6442450944 | bytes 35000000 | tf_op jit(solution)/shard_map/pallas_call | solution.py:318
  685.3 35.7 %shard_map.224 = (bf16[2,192,4096]{2,1,0:T(8,128)(2,1)}, bf16[8,1,192,1024]{3,2,1,0:T(8,128)(2,1)}, f32[1,128]{1,0:T(1,128)}) custom-call(bf16[2,192,4096]{2,1,0:T(8,128)(2,1)} %bitcast.177, bf16[8,1,192,1024]{3,2,1,0:T(8,128)(2,1)} %bitcast.169, f32[2,1536,384]{2,1,0:T(8,128)} %copy.72.refs_2_, bf16[2,192,4096]{2,1,0:T(8,128)(2,1)} %get-tuple-element.305.refs_3_, ...), custom_call_target="tpu_custom_call" | custom-call | flops 12079595520 | bytes 30000000 | tf_op jit(solution)/shard_map/pallas_call | solution.py:271
  725.7 35.7 %shard_map.225 = (bf16[2,192,4096]{2,1,0:T(8,128)(2,1)}, bf16[8,1,192,1024]{3,2,1,0:T(8,128)(2,1)}, f32[1,128]{1,0:T(1,128)}) custom-call(bf16[2,192,4096]{2,1,0:T(8,128)(2,1)} %bitcast.178, bf16[8,1,192,1024]{3,2,1,0:T(8,128)(2,1)} %bitcast.167, f32[2,1536,384]{2,1,0:T(8,128)} %copy.72.refs_2_, ...), custom_call_target="tpu_custom_call", output_to_operand_aliasing={{0}: (10, {})} | custom-call | flops 12079595520 | bytes 30000000 | tf_op jit(solution)/shard_map/pallas_call | solution.py:271
  773.3 118.1 %shard_map.226 = (f32[128,2048]{1,0:T(8,128)}, f32[1,256]{1,0:T(1,128)}) custom-call(bf16[384,4096]{1,0:T(8,128)(2,1)} %bitcast.184, bf16[16,128]{1,0:T(8,128)(2,1)} %broadcast_in_dim.95.extra_ref, bf16[384,2048]{1,0:T(8,128)(2,1)} %get-tuple-element.306.b_ref, f32[64,256]{1,0:T(8,128)} %pad.37.g_ref), custom_call_target="tpu_custom_call" | custom-call | flops 6442450944 | bytes 10000000 | tf_op jit(solution)/shard_map/pallas_call | solution.py:687
  916.6 12.3 %fusion.8 = (f32[2048]{0:T(1024)S(1)}, f32[384]{0:T(512)S(1)}, f32[384,2048]{1,0:T(8,128)}) fusion(bf16[2,1,192,2048]{3,2,1,0:T(8,128)(2,1)S(1)} %copy-done.1, f32[384]{0:T(512)S(1)} %copy-done.28, f32[2048]{0:T(1024)S(1)} %copy-done.24, f32[384,2048]{1,0:T(8,128)S(1)} %fusion.20, bf16[384,4096]{1,0:T(8,128)(2,1)S(1)} %bitcast.182, ...), kind=kOutput, calls=%fused_computation.18 | convolution fusion | flops 6448739840 | bytes 27806720 | tf_op jit(solution)/shard_map/dot_general | solution.py:35
  929.7 112.6 %shard_map.228 = (f32[160,2048]{1,0:T(8,128)}, f32[1,256]{1,0:T(1,128)}) custom-call(bf16[384,4096]{1,0:T(8,128)(2,1)} %bitcast.181, bf16[1024,384]{1,0:T(8,128)(2,1)} %get-tuple-element.317.extra_ref, bf16[384,2048]{1,0:T(8,128)(2,1)} %fusion.2.x_ref.b_ref, f32[64,256]{1,0:T(8,128)} %bitcast.155), custom_call_target="tpu_custom_call" | custom-call | flops 8053063680 | bytes 10000000 | tf_op jit(solution)/shard_map/pallas_call | solution.py:687
  (291 shorter events, 211.1 us)
Async XLA Ops:
  7.2 263.5 %all-gather.11.cloned.1.call-start = ((), (), s32[]{:S(2)}) async-start(), calls=%async_computation.14 | async-start | bytes 3538944 | tf_op jit(solution)/shard_map/all_gather | solution.py:1229
  226.8 83.4 %all-gather.13.cloned.1.call-start = ((), (), s32[]{:S(2)}) async-start(), calls=%async_computation.15 | async-start | bytes 3538944 | tf_op jit(solution)/shard_map/all_gather | solution.py:1230
  227.6 193.8 %all-gather.9.cloned.1.call-start = ((), (), s32[]{:S(2)}) async-start(), calls=%async_computation.7 | async-start | bytes 7520256 | tf_op jit(solution)/shard_map/all_gather | solution.py:1254
  229.9 103.5 %collective-permute-start.2 = (bf16[2,512,768]{2,1,0:T(8,128)(2,1)}, bf16[2,512,768]{2,1,0:T(8,128)(2,1)}, u32[]{:S(2)}, u32[]{:S(2)}) collective-permute-start(bf16[2,512,768]{2,1,0:T(8,128)(2,1)} %refs_7_.1), channel_id=1, source_target_pairs={{0,8},{8,0},{16,24},{24,16},{1,9},{9,1},{17,25},{25,17},{2,10},{10... | collective-permute-start | bytes 4718600 | tf_op jit(solution)/shard_map/ppermute | solution.py:894
  231.4 102.0 %collective-permute-start.3 = (bf16[2,512,768]{2,1,0:T(8,128)(2,1)}, bf16[2,512,768]{2,1,0:T(8,128)(2,1)}, u32[]{:S(2)}, u32[]{:S(2)}) collective-permute-start(bf16[2,512,768]{2,1,0:T(8,128)(2,1)} %refs_7_.1), channel_id=1, source_target_pairs={{0,16},{8,24},{16,0},{24,8},{1,17},{9,25},{17,1},{25,9},{2,18},{10... | collective-permute-start | bytes 4718600 | tf_op jit(solution)/shard_map/ppermute | solution.py:894
  231.9 101.5 %collective-permute-start.4 = (bf16[2,768,512]{2,1,0:T(8,128)(2,1)}, bf16[2,768,512]{2,1,0:T(8,128)(2,1)}, u32[]{:S(2)}, u32[]{:S(2)}) collective-permute-start(bf16[2,768,512]{2,1,0:T(8,128)(2,1)} %refs_12_.1), channel_id=1, source_target_pairs={{0,8},{8,0},{16,24},{24,16},{1,9},{9,1},{17,25},{25,17},{2,10},{10... | collective-permute-start | bytes 4718600 | tf_op jit(solution)/shard_map/ppermute | solution.py:894
  265.5 67.9 %collective-permute-start.5 = (bf16[2,768,512]{2,1,0:T(8,128)(2,1)}, bf16[2,768,512]{2,1,0:T(8,128)(2,1)}, u32[]{:S(2)}, u32[]{:S(2)}) collective-permute-start(bf16[2,768,512]{2,1,0:T(8,128)(2,1)} %refs_12_.1), channel_id=1, source_target_pairs={{0,16},{8,24},{16,0},{24,8},{1,17},{9,25},{17,1},{25,9},{2,18},{10... | collective-permute-start | bytes 4718600 | tf_op jit(solution)/shard_map/ppermute | solution.py:894
  349.1 141.0 %all-gather.7.cloned.1.call-start = ((), (), s32[]{:S(2)}) async-start(), calls=%async_computation.6 | async-start | bytes 7520256 | tf_op jit(solution)/shard_map/all_gather | solution.py:1254
  349.7 210.5 %reduce-scatter.7.cloned.1.call-start = ((), (), s32[]{:S(2)}) async-start(), calls=%async_computation.8 | async-start | bytes 7077888 | tf_op jit(solution)/shard_map/reduce_scatter | solution.py:1259
  360.0 44.4 %collective-permute-start.6 = (bf16[1,512,768]{2,1,0:T(8,128)(2,1)S(1)}, bf16[1,512,768]{2,1,0:T(8,128)(2,1)S(1)}, u32[]{:S(2)}, u32[]{:S(2)}) collective-permute-start(bf16[1,512,768]{2,1,0:T(8,128)(2,1)S(1)} %slice.94), channel_id=1, source_target_pairs={{0,16},{8,24},{16,0},{24,8},{1,17},{9,25},{17,1},{25,9},{2,18},{10... | collective-permute-start | bytes 2359304 | tf_op jit(solution)/shard_map/ppermute | solution.py:894
  488.1 155.5 %reduce-scatter.9.cloned.1.call-start = ((), (), s32[]{:S(2)}) async-start(), calls=%async_computation.9 | async-start | bytes 7077888 | tf_op jit(solution)/shard_map/reduce_scatter | solution.py:1259
  560.2 210.8 %reduce-scatter.11.cloned.1.call-start = ((), (), s32[]{:S(2)}) async-start(), calls=%async_computation.10 | async-start | bytes 7077888 | tf_op jit(solution)/shard_map/reduce_scatter | solution.py:1288
  580.6 43.6 %collective-permute-start.16 = (bf16[1,512,768]{2,1,0:T(8,128)(2,1)}, bf16[1,512,768]{2,1,0:T(8,128)(2,1)}, u32[]{:S(2)}, u32[]{:S(2)}) collective-permute-start(bf16[1,512,768]{2,1,0:T(8,128)(2,1)} %get-tuple-element.391), channel_id=1, source_target_pairs={{0,8},{8,0},{16,24},{24,16},{1,9},{9,1},{17,25},{25,17},{2,10},{10... | collective-permute-start | bytes 2359304 | tf_op jit(solution)/shard_map/ppermute | solution.py:894
  582.2 49.2 %collective-permute-start.17 = (bf16[1,512,768]{2,1,0:T(8,128)(2,1)}, bf16[1,512,768]{2,1,0:T(8,128)(2,1)}, u32[]{:S(2)}, u32[]{:S(2)}) collective-permute-start(bf16[1,512,768]{2,1,0:T(8,128)(2,1)} %get-tuple-element.390), channel_id=1, source_target_pairs={{0,16},{8,24},{16,0},{24,8},{1,17},{9,25},{17,1},{25,9},{2,18},{10... | collective-permute-start | bytes 2359304 | tf_op jit(solution)/shard_map/ppermute | solution.py:894
  643.6 247.8 %reduce-scatter.13.cloned.1.call-start = ((), (), s32[]{:S(2)}) async-start(), calls=%async_computation.11 | async-start | bytes 3538944 | tf_op jit(solution)/shard_map/reduce_scatter | solution.py:1294
  654.1 66.9 %collective-permute-start.25 = (bf16[1,512,768]{2,1,0:T(8,128)(2,1)}, bf16[1,512,768]{2,1,0:T(8,128)(2,1)}, u32[]{:S(2)}, u32[]{:S(2)}) collective-permute-start(bf16[1,512,768]{2,1,0:T(8,128)(2,1)} %add_convert_fusion.2), channel_id=1, source_target_pairs={{0,8},{8,0},{16,24},{24,16},{1,9},{9,1},{17,25},{25,17},{2,10},{10... | collective-permute-start | bytes 2359304 | tf_op jit(solution)/shard_map/ppermute | solution.py:894
  657.8 63.8 %collective-permute-start.24 = (bf16[1,512,768]{2,1,0:T(8,128)(2,1)}, bf16[1,512,768]{2,1,0:T(8,128)(2,1)}, u32[]{:S(2)}, u32[]{:S(2)}) collective-permute-start(bf16[1,512,768]{2,1,0:T(8,128)(2,1)} %add_convert_fusion.3), channel_id=1, source_target_pairs={{0,16},{8,24},{16,0},{24,8},{1,17},{9,25},{17,1},{25,9},{2,18},{10... | collective-permute-start | bytes 2359304 | tf_op jit(solution)/shard_map/ppermute | solution.py:894
  660.5 61.8 %collective-permute-start.21 = (bf16[1,768,512]{2,1,0:T(8,128)(2,1)}, bf16[1,768,512]{2,1,0:T(8,128)(2,1)}, u32[]{:S(2)}, u32[]{:S(2)}) collective-permute-start(bf16[1,768,512]{2,1,0:T(8,128)(2,1)} %add_convert_fusion.4), channel_id=1, source_target_pairs={{0,8},{8,0},{16,24},{24,16},{1,9},{9,1},{17,25},{25,17},{2,10},{10... | collective-permute-start | bytes 2359304 | tf_op jit(solution)/shard_map/ppermute | solution.py:894
  682.1 41.8 %collective-permute-start.20 = (bf16[1,768,512]{2,1,0:T(8,128)(2,1)}, bf16[1,768,512]{2,1,0:T(8,128)(2,1)}, u32[]{:S(2)}, u32[]{:S(2)}) collective-permute-start(bf16[1,768,512]{2,1,0:T(8,128)(2,1)} %add_convert_fusion.5), channel_id=1, source_target_pairs={{0,16},{8,24},{16,0},{24,8},{1,17},{9,25},{17,1},{25,9},{2,18},{10... | collective-permute-start | bytes 2359304 | tf_op jit(solution)/shard_map/ppermute | solution.py:894
  683.6 41.5 %collective-permute-start.18 = (bf16[1,768,512]{2,1,0:T(8,128)(2,1)S(1)}, bf16[1,768,512]{2,1,0:T(8,128)(2,1)}, u32[]{:S(2)}, u32[]{:S(2)}) collective-permute-start(bf16[1,768,512]{2,1,0:T(8,128)(2,1)S(1)} %copy-done.17), channel_id=1, source_target_pairs={{0,8},{8,0},{16,24},{24,16},{1,9},{9,1},{17,25},{25,17},{2,10},{10... | collective-permute-start | bytes 2359304 | tf_op jit(solution)/shard_map/ppermute | solution.py:894
  721.0 40.4 %collective-permute-start.19 = (bf16[1,768,512]{2,1,0:T(8,128)(2,1)S(1)}, bf16[1,768,512]{2,1,0:T(8,128)(2,1)}, u32[]{:S(2)}, u32[]{:S(2)}) collective-permute-start(bf16[1,768,512]{2,1,0:T(8,128)(2,1)S(1)} %copy-done.16), channel_id=1, source_target_pairs={{0,16},{8,24},{16,0},{24,8},{1,17},{9,25},{17,1},{25,9},{2,18},{10... | collective-permute-start | bytes 2359304 | tf_op jit(solution)/shard_map/ppermute | solution.py:894
  725.2 45.9 %collective-permute-start.27 = (bf16[1,512,768]{2,1,0:T(8,128)(2,1)S(1)}, bf16[1,512,768]{2,1,0:T(8,128)(2,1)}, u32[]{:S(2)}, u32[]{:S(2)}) collective-permute-start(bf16[1,512,768]{2,1,0:T(8,128)(2,1)S(1)} %copy-done.12), channel_id=1, source_target_pairs={{0,16},{8,24},{16,0},{24,8},{1,17},{9,25},{17,1},{25,9},{2,18},{10... | collective-permute-start | bytes 2359304 | tf_op jit(solution)/shard_map/ppermute | solution.py:894
  771.1 122.0 %reduce-scatter.15.cloned.1.call-start = ((), (), s32[]{:S(2)}) async-start(), calls=%async_computation.12 | async-start | bytes 3538944 | tf_op jit(solution)/shard_map/reduce_scatter | solution.py:1294
  771.8 280.2 %reduce-scatter.17.cloned.1.call-start = ((), (), s32[]{:S(2)}) async-start(), calls=%async_computation.13 | async-start | bytes 7077888 | tf_op jit(solution)/shard_map/reduce_scatter | solution.py:1300
  (64 other events, 1894.8 us)
Sparse Core Ops, SparseCore 0:
  226.9 43.7 all-gather.10
  273.0 37.1 all-gather.12
  349.2 72.0 all-gather.8
  423.4 66.6 all-gather.6
  492.2 67.9 reduce-scatter.6
  562.3 68.1 reduce-scatter.8
  643.7 65.9 reduce-scatter.10
  771.2 36.0 reduce-scatter.12
  809.7 83.4 reduce-scatter.14
  895.3 67.1 reduce-scatter.16

commit v7 on v6

--- a/solution.py
+++ b/solution.py
@@ -817,7 +817,7 @@
         grid=(blocks,),
         in_specs=[
             pl.BlockSpec((1, rows, tokens.shape[2]), lambda b: (b, 0, 0)),
-            pl.BlockSpec((1, 1, rows, width), lambda b: (b, batch_at, 0, 0)),
+            pl.BlockSpec((1, 1, rows, width), lambda b: (b, 0, 0, 0)),
         ]
         + [any_spec] * len(earlier[:2]),
         out_specs=[picked_spec] * 2,
@@ -1188,10 +1188,10 @@
     gain_len = norm_gains.shape[0]
     gain_shard = jnp.zeros((2048,), bf16).at[:gain_len].set(norm_gains).reshape(16, 128)
     kv_w = jnp.concatenate([w_key.T, w_value.T], axis=0)
-    q_w, kv_w, out_w, gain_full, cot_all = gather_rows(
-        [w_query.T, kv_w, w_output, gain_shard, cotangent.reshape(total, width)], [(3, 0, 1, 2)], 1, (4,)
+    q_w, kv_w, out_w, gain_full, cot_0 = gather_rows(
+        [w_query.T, kv_w, w_output, gain_shard, cotangent[0, 0]], [(3, 0, 1, 2)], 1, (4,)
     )
-    cot_all = cot_all.reshape(blocks, micro, rows, width)
+    cot_0 = cot_0.reshape(blocks, 1, rows, width)
     q_w, w_gate, w_up, w_down = tie((q_w, w_gate, w_up, w_down))
     gains = gain_full.reshape(shards, 2048)[:, :gain_len].reshape(-1).astype(f32)
     gain_in = gains[:width]
@@ -1229,7 +1229,10 @@
     kv_0 = lax.all_gather(kv_own[0], "expert", axis=0, tiled=False)
     kv_1 = lax.all_gather(kv_own[1], "expert", axis=0, tiled=False)
     kv_0, gate_near = tie((kv_0, gate_near))
+    kv_1, cot_1 = tie((kv_1, cotangent[1, 0]))
+    cot_1 = lax.all_gather(cot_1, "expert", axis=0, tiled=False)
     kv_all = [kv_0[:, None], kv_1[:, None]]
+    cots = [cot_0, cot_1[:, None]]
     chunk = 256
     mixed = run_forward(q_low, kv_all[0], bias, step_heads, chunk, 0, [])
     mixed, kv_all = tie((mixed, kv_all))
@@ -1245,6 +1248,7 @@
     scale_mid = rms_scale(middle)
     routed = (middle * scale_mid * gain_mid).astype(bf16).reshape(micro, rows, width)
     routed = jnp.concatenate([routed, routing], axis=-1)
+    routed, cots[1] = tie((routed, cots[1]))
     middle = middle.reshape(micro, rows, width)
     scale_mid = scale_mid.reshape(micro, rows, 1)
 
@@ -1253,7 +1257,7 @@
     for at in range(micro):
         tokens = lax.all_gather(routed[at], "expert", axis=0, tiled=False)
         tokens, parts = tie((tokens, parts))
-        kept, mix, d_part = run_experts(tokens, cot_all, parts, capacity, at, micro, kept)
+        kept, mix, d_part = run_experts(tokens, cots[at], parts, capacity, at, micro, kept)
         kept, d_part, mix, d_routeds = tie((kept, d_part, mix, d_routeds))
         mix_parts.append(mix)
         d_routed = lax.psum_scatter(d_part, "expert", scatter_dimension=0, tiled=True)
@@ -1265,47 +1269,71 @@
     def weight_grad(rows_in, rows_out):
         return jnp.einsum("era,erb->eab", rows_in, rows_out, preferred_element_type=f32).astype(bf16)
 
-    scattering = [
-        scatter_far(weight_grad(hidden_low, d_result), 2),
-        scatter_far(weight_grad(picked, d_gate), 1),
-        scatter_far(weight_grad(picked, d_up), 1),
-    ]
-    d_routeds[-1], scattering, mix_parts[0] = tie((d_routeds[-1], scattering, mix_parts[0]))
-    expert_grads = [scatter_near(*pieces) for pieces in scattering]
+    first = scatter_far(weight_grad(picked, d_gate), 1)
+    second = scatter_far(weight_grad(picked, d_up), 1)
+    first, hidden_low = tie((first, hidden_low))
+    first = scatter_near(*first)
+    third = scatter_far(weight_grad(hidden_low, d_result), 2)
+    d_routeds[-1], second, mix_parts[0] = tie((d_routeds[-1], second, mix_parts[0]))
+    second = scatter_near(*second)
     d_mixed, d_middle, d_branch, grad_mid = run_middle_back(
         d_routeds, middle, cotangent[:, 0], gain_mid[None, :], out_w
     )
+    d_mixed, d_branch, first, third = tie((d_mixed, d_branch, first, third))
+    third = scatter_near(*third)
     d_mixed = d_mixed.reshape(micro, rows, H * HD)
     cos_rows, sine_rows = (a.reshape(micro, rows, HD) for a in (cosine, sine))
-    d_query, dkv_all, grad_qn = [], [], 0.0
-    for at in range(micro):
+    heads = mixed.reshape(total, 4, 2, 2, 2, HD)
+
+    def share(core):
+        part = lax.dynamic_index_in_dim(heads, core, axis=4, keepdims=False)
+        return part.transpose(0, 2, 1, 3, 4).reshape(total, -1)
+
+    core = member % 2
+    pairs = [(i, i ^ 1) for i in range(blocks)]
+    got = lax.ppermute(mm(share(1 - core), d_branch, TN).astype(bf16), "expert", pairs)
+    mixes = [lax.psum_scatter(mix_parts[0], "expert", scatter_dimension=0, tiled=True)]
+
+    def backward(at, earlier):
         d_query, dkv_one, part = run_backward(
             q_low, kv_all[at], bias, mixed, d_mixed, logs, q_raw, cos_rows, sine_rows, gain_q,
-            step_heads, chunk, at, [d_query] if at else []
+            step_heads, chunk, at, earlier
         )
-        dkv_all.append(dkv_one[:, 0])
-        grad_qn += part
-    mixes = [lax.psum_scatter(mix_parts[0], "expert", scatter_dimension=0, tiled=True)]
-    mixed_after, d_query, dkv_all, expert_grads, mixes = tie(
-        (mixed, d_query, dkv_all, expert_grads, mixes)
-    )
-    grad_output, _ = reduce_rows(mixed_after.reshape(total, H * HD), None, d_branch, 2)
-    dkv = jnp.concatenate(
-        [lax.psum_scatter(part, "expert", scatter_dimension=0, tiled=False) for part in dkv_all], axis=0
-    )
-    dkv, grad_output, d_query = tie((dkv, grad_output, d_query))
+        return d_query, dkv_one[:, 0], part
+
+    d_query, dkv_0, gain_0 = backward(0, [])
+    d_query, dkv_0, got, second = tie((d_query, dkv_0, got, second))
+    dkv_0 = lax.psum_scatter(dkv_0, "expert", scatter_dimension=0, tiled=False)
+    out_grad = tie(mm(share(core), d_branch, TN).astype(bf16))
+    out_grad = (out_grad.astype(f32) + got.astype(f32)).astype(bf16)
+    d_query, out_grad = tie((d_query, out_grad))
+    out_grad = scatter_far(out_grad.reshape(2, -1, width), 1)
+    d_query, dkv_1, gain_1 = backward(1, [d_query])
+    grad_qn = gain_0 + gain_1
+    d_query, dkv_1, out_grad, mixes, third = tie((d_query, dkv_1, out_grad, mixes, third))
+    dkv_1 = lax.psum_scatter(dkv_1, "expert", scatter_dimension=0, tiled=False)
+    out_grad = scatter_sum(*scatter_near(*out_grad)).astype(bf16).reshape(-1, width)
     d_query = d_query.reshape(total, H * HD)
+    dkv = jnp.concatenate([dkv_0, dkv_1], axis=0)
     dkv = dkv.reshape(total, KVH * 2 * HD)
     mix_part, dkv = tie((mix_parts[1], dkv))
     mixes.append(lax.psum_scatter(mix_part, "expert", scatter_dimension=0, tiled=True))
     outputs = [(middle[at] + mixes[at].astype(f32)).astype(bf16) for at in range(micro)]
     dkv, dkv_t, grad_kn = run_key_back(dkv, k_raw, cosine, sine, gain_k)
+    dkv, out_grad = tie((dkv, out_grad))
     d_normed = mm(d_query, q_w) + mm(dkv, kv_w)
+    grad_output = lax.psum_scatter(
+        out_grad,
+        "expert",
+        scatter_dimension=0,
+        tiled=True,
+        axis_index_groups=[list(range(c, blocks, 2)) for c in range(2)],
+    ).astype(f32)
     d_in_norm, grad_in = norm_back(d_normed, hidden, scale_in, gain_in)
     input_grad = d_middle + d_in_norm
     gain_grads = jnp.concatenate([grad_in, grad_mid[0], grad_qn[0], grad_kn[0]]).reshape(shards, gain_len)
     grad_qkv, grad_gains = reduce_rows(d_query, dkv_t, normed, 3, gain_grads)
-    expert_grads = [scatter_sum(*pieces) for pieces in expert_grads]
+    expert_grads = [scatter_sum(*pieces) for pieces in (first, second, third)]
     return (
         jnp.stack(outputs)[:, None],
         input_grad.reshape(micro, 1, rows, width),
@@ -1314,9 +1342,7 @@
         grad_qkv[q_part + k_part :].T,
         grad_output,
         grad_gains[0, :gain_len],
-        expert_grads[1],
-        expert_grads[2],
-        expert_grads[0],
+        *expert_grads,
     )
 
 

time: 1070 us -> 1100 us (1.028)
  Pallas kernels: 710 us -> 594 us
  waiting for transfers between devices: 124 us -> 211 us
  local copies, waits for them, and re-layouts: 57.7 us -> 89.5 us
  other arithmetic: 50.9 us -> 63.1 us
    pallas_call x2 -> x1, Pallas kernels: 231 us -> 140 us  [reduce_rows(): pl.pallas_call(functools.partial(reduce_kernel, rows, 4), out_shape=[jax....]
    ppermute x30 -> x36, waiting for transfers between devices: 81.2 us -> 145 us  [swap(): lax.ppermute(values, 'dp', [(i, i ^ bit) for i in range(lax.axis_size('dp...]
    all_gather x1, waiting for transfers between devices: 16.2 us -> 42 us  [body_fast(): kv_1 = lax.all_gather(kv_own[1], 'expert', axis=0, tiled=False)]
    pallas_call x1, Pallas kernels: 189 us -> 163 us  [gather_rows(): pl.pallas_call(functools.partial(gather_kernel, phases, len(arrays), late...]
    transpose x1 -> x2, local copies, waits for them, and re-layouts: 0.01 us -> 13.1 us  [share(): return part.transpose(0, 2, 1, 3, 4).reshape(total, -1)]
    dot_general x3 -> x5, matrix products: 28.4 us -> 38.2 us  [mm(): return lax.dot_general(a, b, dims, preferred_element_type=f32)]
    ppermute x30 -> x36, starting transfers between devices: 33.9 us -> 39.5 us  [swap(): lax.ppermute(values, 'dp', [(i, i ^ bit) for i in range(lax.axis_size('dp...]
  transfers between devices with their start and end apart: 40 -> 49, of which waited for: 16 -> 23; matrix products, arithmetic and copies ran while one was open for 13% -> 18% of each run, Pallas kernels for 47% -> 37%
where the time goes in v7:
time: 1100 us
  Pallas kernels  594 us (54%)
  waiting for transfers between devices  211 us (19%)
  local copies, waits for them, and re-layouts  89.5 us (8%)
  matrix products  83.2 us (8%)
  other arithmetic  63.1 us (6%)
  starting transfers between devices  40.3 us (4%)
  between operations  15.5 us (1%)
    pallas_call x1, Pallas kernels, gather_rows(): pl.pallas_call(functools.partial(gather_kernel, phases, len(arrays), late...  163 us
    ppermute x36, waiting for transfers between devices, swap(): lax.ppermute(values, 'dp', [(i, i ^ bit) for i in range(lax.axis_size('dp...  145 us
    pallas_call x1, Pallas kernels, reduce_rows(): pl.pallas_call(functools.partial(reduce_kernel, rows, 4), out_shape=[jax....  140 us
    pallas_call x2, Pallas kernels, run_experts(): pl.pallas_call(functools.partial(expert_kernel, len(earlier[2:])), grid=(...  80 us
    pallas_call x2, Pallas kernels, run_backward(): pl.pallas_call(kernel, grid=(KVH,), in_specs=[q_spec, kv_spec, bias_spec,...  71.1 us
    pallas_call x2, Pallas kernels, run_forward(): pl.pallas_call(kernel, grid=(KVH,), in_specs=[q_spec, kv_spec, bias_spec]...  46.4 us
    dot_general x3, matrix products, weight_grad(): jnp.einsum('era,erb->eab', rows_in, rows_out, preferred_element_type=f32)  45 us
    all_gather x1, waiting for transfers between devices, body_fast(): kv_1 = lax.all_gather(kv_own[1], 'expert', axis=0, tiled=False)  42 us
  transfers between devices with their start and end apart: 49, of which 23 were waited for; matrix products, arithmetic and copies ran while one was open for 18% of the time, Pallas kernels for 37%

profile of v7, /device:TPU:8, one launch (start us, length us, event | category | flops | bytes accessed | tf_op | source)
XLA Modules:
  0.0 1095.7 jit_solution(4108882142640701827)
XLA Ops:
  12.4 163.4 %shard_map.213 = (bf16[4096,2048]{1,0:T(8,128)(2,1)}, bf16[1024,2048]{1,0:T(8,128)(2,1)}, bf16[4096,2048]{1,0:T(8,128)(2,1)}, bf16[512,128]{1,0:T(8,128)(2,1)}, bf16[1536,2048]{1,0:T(8,128)(2,1)}) custom-call(bf16[128,2048]{1,0:T(8,128)(2,1)} %bitcast.169, bf16[32,2048]{1,0:T(8,128)(2,1)} %pad_maximum_fusion.5.refs_1_, bf16[128,2048]{1,0:T(8,128)(2,1)} %refs_2_.1, ...), custom_call_target="tpu_custom_call" | custom-call | bytes 400000000 | tf_op jit(solution)/shard_map/pallas_call | solution.py:493
  183.3 16.4 %shard_map.214 = (bf16[384,4096]{1,0:T(8,128)(2,1)}, f32[384,4096]{1,0:T(8,128)}, bf16[384,1024]{1,0:T(8,128)(2,1)}, f32[384,512]{1,0:T(8,128)}, bf16[1024,2048]{1,0:T(8,128)(2,1)}) custom-call(bf16[384,2048]{1,0:T(8,128)(2,1)} %fusion.2.x_ref.b_ref, bf16[4096,2048]{1,0:T(8,128)(2,1)} %get-tuple-element.198.wq_ref, ...), custom_call_target="tpu_custom_call" | custom-call | flops 8053063680 | bytes 40000000 | tf_op jit(solution)/shard_map/pallas_call | solution.py:96
  202.6 42.0 %all-gather.15.cloned.1.call-done = bf16[1536,1024]{1,0:T(8,128)(2,1)} async-done(((bf16[192,1024]{1,0:T(8,128)(2,1)}), bf16[1536,1024]{1,0:T(8,128)(2,1)}) %all-gather.15.cloned.1.call-update) | async-done | bytes 3145744 | tf_op jit(solution)/shard_map/all_gather | solution.py:1230
  265.0 17.4 %collective-permute-done.refs_3_ = bf16[2,512,768]{2,1,0:T(8,128)(2,1)} collective-permute-done((bf16[2,512,768]{2,1,0:T(8,128)(2,1)}, bf16[2,512,768]{2,1,0:T(8,128)(2,1)}, u32[]{:S(2)}, u32[]{:S(2)}) %collective-permute-start) | collective-permute-done | bytes 1572896 | tf_op jit(solution)/shard_map/ppermute | solution.py:894
  284.4 23.2 %shard_map.215 = (bf16[2,192,4096]{2,1,0:T(8,128)(2,1)}, f32[2,4,4,384]{3,2,1,0:T(4,128)}) custom-call(bf16[2,192,4096]{2,1,0:T(8,128)(2,1)} %bitcast.202, bf16[8,1,192,1024]{3,2,1,0:T(8,128)(2,1)} %bitcast.195, f32[2,1536,384]{2,1,0:T(8,128)} %copy.80.refs_2_), custom_call_target="tpu_custom_call" | custom-call | flops 4831838208 | bytes 20000000 | tf_op jit(solution)/shard_map/pallas_call | solution.py:243
  307.7 23.2 %shard_map.216 = (bf16[2,192,4096]{2,1,0:T(8,128)(2,1)}, f32[2,4,4,384]{3,2,1,0:T(4,128)}) custom-call(bf16[2,192,4096]{2,1,0:T(8,128)(2,1)} %bitcast.203, bf16[8,1,192,1024]{3,2,1,0:T(8,128)(2,1)} %bitcast.193, f32[2,1536,384]{2,1,0:T(8,128)} %copy.80.refs_2_, ...), custom_call_target="tpu_custom_call", output_to_operand_aliasing={{0}: (3, {}), {1}: (4, {})} | custom-call | flops 4831838208 | bytes 20000000 | tf_op jit(solution)/shard_map/pallas_call | solution.py:243
  330.9 18.3 %collective-permute-done.4.refs_13_ = bf16[2,768,512]{2,1,0:T(8,128)(2,1)} collective-permute-done((bf16[2,768,512]{2,1,0:T(8,128)(2,1)}, bf16[2,768,512]{2,1,0:T(8,128)(2,1)}, u32[]{:S(2)}, u32[]{:S(2)}) %collective-permute-start.4) | collective-permute-done | bytes 1572896 | tf_op jit(solution)/shard_map/ppermute | solution.py:894
  390.9 14.1 %collective-permute-done.8.refs_10_ = bf16[1,512,768]{2,1,0:T(8,128)(2,1)S(1)} collective-permute-done((bf16[1,512,768]{2,1,0:T(8,128)(2,1)S(1)}, bf16[1,512,768]{2,1,0:T(8,128)(2,1)S(1)}, u32[]{:S(2)}, u32[]{:S(2)}) %collective-permute-start.8) | collective-permute-done | bytes 786464 | tf_op jit(solution)/shard_map/ppermute | solution.py:894
  430.5 14.0 %shard_map.217 = (bf16[2,2,8,96,2048]{4,3,2,1,0:T(8,128)(2,1)}, bf16[2,2,8,96,2048]{4,3,2,1,0:T(8,128)(2,1)}) custom-call(bf16[8,192,2176]{2,1,0:T(8,128)(2,1)} %all-gather.11.cloned.1.call-done.tok_ref.routing_ref, bf16[8,1,192,2048]{3,2,1,0:T(8,128)(2,1)} %bitcast.159), custom_call_target="tpu_custom_call" | custom-call | flops 2415919104 | bytes 25000000 | tf_op jit(solution)/shard_map/pallas_call | solution.py:815
  444.5 40.0 %shard_map.218 = (bf16[2,2,768,768]{3,2,1,0:T(8,128)(2,1)}, bf16[2,2,768,768]{3,2,1,0:T(8,128)(2,1)}, bf16[2,2,768,768]{3,2,1,0:T(8,128)(2,1)}, bf16[2,768,2048]{2,1,0:T(8,128)(2,1)}, bf16[2,768,2048]{2,1,0:T(8,128)(2,1)}) custom-call(bf16[2,2,768,2048]{3,2,1,0:T(8,128)(2,1)} %bitcast.150, bf16[2,2,768,2048]{3,2,1,0:T(8,128)(2,1)} %bitcast.154, ...), custom_call_target="tpu_custom_call" | custom-call | flops 28991029248 | bytes 50000000 | tf_op jit(solution)/shard_map/pallas_call | solution.py:838
  484.5 12.7 %shard_map.219 = (bf16[1536,2048]{1,0:T(8,128)(2,1)}, bf16[1536,2048]{1,0:T(8,128)(2,1)}) custom-call(bf16[8,192,2176]{2,1,0:T(8,128)(2,1)} %all-gather.11.cloned.1.call-done.tok_ref.routing_ref, bf16[2,8,96,2048]{3,2,1,0:T(8,128)(2,1)} %bitcast.163, bf16[2,8,96,2048]{3,2,1,0:T(8,128)(2,1)} %bitcast.164), custom_call_target="tpu_custom_call" | custom-call | flops 2415919104 | bytes 25000000 | tf_op jit(solution)/shard_map/pallas_call | solution.py:860
  499.2 14.4 %shard_map.220 = (bf16[2,2,8,96,2048]{4,3,2,1,0:T(8,128)(2,1)}, bf16[2,2,8,96,2048]{4,3,2,1,0:T(8,128)(2,1)}) custom-call(bf16[8,192,2176]{2,1,0:T(8,128)(2,1)} %all-gather.9.cloned.1.call-done.tok_ref.routing_ref, bf16[8,1,192,2048]{3,2,1,0:T(8,128)(2,1)} %bitcast.158, ...), custom_call_target="tpu_custom_call", output_to_operand_aliasing={{0}: (2, {}), {1}: (3, {})} | custom-call | flops 2415919104 | bytes 25000000 | tf_op jit(solution)/shard_map/pallas_call | solution.py:815
  513.6 40.0 %shard_map.221 = (bf16[2,2,768,768]{3,2,1,0:T(8,128)(2,1)}, bf16[2,2,768,768]{3,2,1,0:T(8,128)(2,1)}, bf16[2,2,768,768]{3,2,1,0:T(8,128)(2,1)}, bf16[2,768,2048]{2,1,0:T(8,128)(2,1)}, bf16[2,768,2048]{2,1,0:T(8,128)(2,1)}) custom-call(bf16[2,2,768,2048]{3,2,1,0:T(8,128)(2,1)} %bitcast.151, ...), custom_call_target="tpu_custom_call", output_to_operand_aliasing={{0}: (17, {}), {1}: (18, {}), {2}: (19, {})} | custom-call | flops 28991029248 | bytes 50000000 | tf_op jit(solution)/shard_map/pallas_call | solution.py:838
  553.6 12.7 %shard_map.222 = (bf16[1536,2048]{1,0:T(8,128)(2,1)}, bf16[1536,2048]{1,0:T(8,128)(2,1)}) custom-call(bf16[8,192,2176]{2,1,0:T(8,128)(2,1)} %all-gather.9.cloned.1.call-done.tok_ref.routing_ref, bf16[2,8,96,2048]{3,2,1,0:T(8,128)(2,1)} %bitcast.161, bf16[2,8,96,2048]{3,2,1,0:T(8,128)(2,1)} %bitcast.162), custom_call_target="tpu_custom_call" | custom-call | flops 2415919104 | bytes 25000000 | tf_op jit(solution)/shard_map/pallas_call | solution.py:860
  569.5 15.2 %convolution_convert_fusion.3 = bf16[2,2048,768]{2,1,0:T(8,128)(2,1)S(1)} fusion(bf16[2,1536,2048]{2,1,0:T(8,128)(2,1)} %bitcast.152, bf16[2,1536,768]{2,1,0:T(8,128)(2,1)} %bitcast.200), kind=kOutput, calls=%fused_computation.5 | convolution fusion | flops 9666822144 | bytes 23592960 | tf_op jit(solution)/shard_map/era,erb->eab/dot_general | solution.py:1270
  591.3 15.3 %convolution_convert_fusion.4 = bf16[2,2048,768]{2,1,0:T(8,128)(2,1)S(1)} fusion(bf16[2,1536,2048]{2,1,0:T(8,128)(2,1)} %bitcast.153, bf16[2,1536,768]{2,1,0:T(8,128)(2,1)} %bitcast.201), kind=kOutput, calls=%fused_computation.6 | convolution fusion | flops 9666822144 | bytes 23592960 | tf_op jit(solution)/shard_map/era,erb->eab/dot_general | solution.py:1270
  616.9 13.7 %collective-permute-done.12 = bf16[1,512,768]{2,1,0:T(8,128)(2,1)} collective-permute-done((bf16[1,512,768]{2,1,0:T(8,128)(2,1)S(1)}, bf16[1,512,768]{2,1,0:T(8,128)(2,1)}, u32[]{:S(2)}, u32[]{:S(2)}) %collective-permute-start.12) | collective-permute-done | bytes 786464 | tf_op jit(solution)/shard_map/ppermute | solution.py:894
  639.9 14.5 %convolution_convert_fusion.2 = bf16[2,768,2048]{2,1,0:T(8,128)(2,1)S(1)} fusion(bf16[2,1536,768]{2,1,0:T(8,128)(2,1)} %bitcast.199, bf16[2,1536,2048]{2,1,0:T(8,128)(2,1)} %bitcast.156), kind=kOutput, calls=%fused_computation.4 | convolution fusion | flops 9666822144 | bytes 23592960 | tf_op jit(solution)/shard_map/era,erb->eab/dot_general | solution.py:1270
  699.5 18.4 %shard_map.223 = (bf16[384,4096]{1,0:T(8,128)(2,1)}, f32[384,2048]{1,0:T(8,128)}, bf16[384,2048]{1,0:T(8,128)(2,1)}, f32[1,2048]{1,0:T(1,128)}) custom-call(bf16[192,2048]{1,0:T(8,128)(2,1)} %reduce-scatter.8.cloned.1.call-done.r0_ref, bf16[192,2048]{1,0:T(8,128)(2,1)} %reduce-scatter.10.cloned.1.call-done.r1_ref, f32[2,192,2048]{2,1,0:T(8,128)} %bitcast.149, ...), custom_call_target="tpu_custom_call" | custom-call | flops 6442450944 | bytes 35000000 | tf_op jit(solution)/shard_map/pallas_call | solution.py:318
  736.9 35.5 %shard_map.224 = (bf16[2,192,4096]{2,1,0:T(8,128)(2,1)}, bf16[8,1,192,1024]{3,2,1,0:T(8,128)(2,1)}, f32[1,128]{1,0:T(1,128)}) custom-call(bf16[2,192,4096]{2,1,0:T(8,128)(2,1)} %bitcast.204, bf16[8,1,192,1024]{3,2,1,0:T(8,128)(2,1)} %bitcast.196, f32[2,1536,384]{2,1,0:T(8,128)} %copy.80.refs_2_, bf16[2,192,4096]{2,1,0:T(8,128)(2,1)} %get-tuple-element.213.refs_3_, ...), custom_call_target="tpu_custom_call" | custom-call | flops 12079595520 | bytes 30000000 | tf_op jit(solution)/shard_map/pallas_call | solution.py:271
  805.6 35.6 %shard_map.225 = (bf16[2,192,4096]{2,1,0:T(8,128)(2,1)}, bf16[8,1,192,1024]{3,2,1,0:T(8,128)(2,1)}, f32[1,128]{1,0:T(1,128)}) custom-call(bf16[2,192,4096]{2,1,0:T(8,128)(2,1)} %bitcast.205, bf16[8,1,192,1024]{3,2,1,0:T(8,128)(2,1)} %bitcast.194, f32[2,1536,384]{2,1,0:T(8,128)} %copy.80.refs_2_, ...), custom_call_target="tpu_custom_call", output_to_operand_aliasing={{0}: (10, {})} | custom-call | flops 12079595520 | bytes 30000000 | tf_op jit(solution)/shard_map/pallas_call | solution.py:271
  851.1 20.4 %collective-permute-done.35 = bf16[1,256,2048]{2,1,0:T(8,128)(2,1)S(1)} collective-permute-done((bf16[1,256,2048]{2,1,0:T(8,128)(2,1)S(1)}, bf16[1,256,2048]{2,1,0:T(8,128)(2,1)S(1)}, u32[]{:S(2)}, u32[]{:S(2)}) %collective-permute-start.35) | collective-permute-done | bytes 1048608 | tf_op jit(solution)/shard_map/ppermute | solution.py:894
  874.7 19.3 %collective-permute-done.33 = bf16[1,256,2048]{2,1,0:T(8,128)(2,1)S(1)} collective-permute-done((bf16[1,256,2048]{2,1,0:T(8,128)(2,1)S(1)}, bf16[1,256,2048]{2,1,0:T(8,128)(2,1)S(1)}, u32[]{:S(2)}, u32[]{:S(2)}) %collective-permute-start.33) | collective-permute-done | bytes 1048608 | tf_op jit(solution)/shard_map/ppermute | solution.py:894
  932.1 140.3 %shard_map.227 = (f32[160,2048]{1,0:T(8,128)}, f32[1,256]{1,0:T(1,128)}) custom-call(bf16[384,4096]{1,0:T(8,128)(2,1)} %bitcast.208, bf16[1024,384]{1,0:T(8,128)(2,1)} %get-tuple-element.347.extra_ref, bf16[384,2048]{1,0:T(8,128)(2,1)} %fusion.2.x_ref.b_ref, f32[64,256]{1,0:T(8,128)} %bitcast.180), custom_call_target="tpu_custom_call" | custom-call | flops 8053063680 | bytes 10000000 | tf_op jit(solution)/shard_map/pallas_call | solution.py:687
  (341 shorter events, 300.1 us)
Async XLA Ops:
  7.2 237.4 %all-gather.15.cloned.1.call-start = ((), (), s32[]{:S(2)}) async-start(), calls=%async_computation.17 | async-start | bytes 3538944 | tf_op jit(solution)/shard_map/all_gather | solution.py:1230
  201.8 82.7 %all-gather.13.cloned.1.call-start = ((), (), s32[]{:S(2)}) async-start(), calls=%async_computation.16 | async-start | bytes 3538944 | tf_op jit(solution)/shard_map/all_gather | solution.py:1229
  202.5 161.9 %all-gather.17.cloned.1.call-start = ((), (), s32[]{:S(2)}) async-start(), calls=%async_computation.18 | async-start | bytes 7077888 | tf_op jit(solution)/shard_map/all_gather | solution.py:1233
  244.6 185.9 %all-gather.11.cloned.1.call-start = ((), (), s32[]{:S(2)}) async-start(), calls=%async_computation.8 | async-start | bytes 7520256 | tf_op jit(solution)/shard_map/all_gather | solution.py:1258
  247.8 83.0 %collective-permute-start.2 = (bf16[2,512,768]{2,1,0:T(8,128)(2,1)}, bf16[2,512,768]{2,1,0:T(8,128)(2,1)}, u32[]{:S(2)}, u32[]{:S(2)}) collective-permute-start(bf16[2,512,768]{2,1,0:T(8,128)(2,1)} %refs_7_.1), channel_id=1, source_target_pairs={{0,8},{8,0},{16,24},{24,16},{1,9},{9,1},{17,25},{25,17},{2,10},{10... | collective-permute-start | bytes 4718600 | tf_op jit(solution)/shard_map/ppermute | solution.py:894
  248.4 82.5 %collective-permute-start.3 = (bf16[2,512,768]{2,1,0:T(8,128)(2,1)}, bf16[2,512,768]{2,1,0:T(8,128)(2,1)}, u32[]{:S(2)}, u32[]{:S(2)}) collective-permute-start(bf16[2,512,768]{2,1,0:T(8,128)(2,1)} %refs_7_.1), channel_id=1, source_target_pairs={{0,16},{8,24},{16,0},{24,8},{1,17},{9,25},{17,1},{25,9},{2,18},{10... | collective-permute-start | bytes 4718600 | tf_op jit(solution)/shard_map/ppermute | solution.py:894
  249.0 100.2 %collective-permute-start.4 = (bf16[2,768,512]{2,1,0:T(8,128)(2,1)}, bf16[2,768,512]{2,1,0:T(8,128)(2,1)}, u32[]{:S(2)}, u32[]{:S(2)}) collective-permute-start(bf16[2,768,512]{2,1,0:T(8,128)(2,1)} %refs_12_.1), channel_id=1, source_target_pairs={{0,8},{8,0},{16,24},{24,16},{1,9},{9,1},{17,25},{25,17},{2,10},{10... | collective-permute-start | bytes 4718600 | tf_op jit(solution)/shard_map/ppermute | solution.py:894
  282.4 67.9 %collective-permute-start.5 = (bf16[2,768,512]{2,1,0:T(8,128)(2,1)}, bf16[2,768,512]{2,1,0:T(8,128)(2,1)}, u32[]{:S(2)}, u32[]{:S(2)}) collective-permute-start(bf16[2,768,512]{2,1,0:T(8,128)(2,1)} %refs_12_.1), channel_id=1, source_target_pairs={{0,16},{8,24},{16,0},{24,8},{1,17},{9,25},{17,1},{25,9},{2,18},{10... | collective-permute-start | bytes 4718600 | tf_op jit(solution)/shard_map/ppermute | solution.py:894
  365.8 133.4 %all-gather.9.cloned.1.call-start = ((), (), s32[]{:S(2)}) async-start(), calls=%async_computation.7 | async-start | bytes 7520256 | tf_op jit(solution)/shard_map/all_gather | solution.py:1258
  366.4 203.0 %reduce-scatter.8.cloned.1.call-start = ((), (), s32[]{:S(2)}) async-start(), calls=%async_computation.9 | async-start | bytes 7077888 | tf_op jit(solution)/shard_map/reduce_scatter | solution.py:1263
  497.3 142.6 %reduce-scatter.10.cloned.1.call-start = ((), (), s32[]{:S(2)}) async-start(), calls=%async_computation.10 | async-start | bytes 7077888 | tf_op jit(solution)/shard_map/reduce_scatter | solution.py:1263
  569.4 273.6 %reduce-scatter.12.cloned.1.call-start = ((), (), s32[]{:S(2)}) async-start(), calls=%async_computation.11 | async-start | bytes 7077888 | tf_op jit(solution)/shard_map/reduce_scatter | solution.py:1295
  639.9 256.7 %reduce-scatter.14.cloned.1.call-start = ((), (), s32[]{:S(2)}) async-start(), calls=%async_computation.12 | async-start | bytes 3538944 | tf_op jit(solution)/shard_map/reduce_scatter | solution.py:1306
  665.1 52.8 %collective-permute-start.21 = (bf16[1,768,512]{2,1,0:T(8,128)(2,1)}, bf16[1,768,512]{2,1,0:T(8,128)(2,1)}, u32[]{:S(2)}, u32[]{:S(2)}) collective-permute-start(bf16[1,768,512]{2,1,0:T(8,128)(2,1)} %get-tuple-element.426), channel_id=1, source_target_pairs={{0,16},{8,24},{16,0},{24,8},{1,17},{9,25},{17,1},{25,9},{2,18},{10... | collective-permute-start | bytes 2359304 | tf_op jit(solution)/shard_map/ppermute | solution.py:894
  669.0 48.9 %collective-permute-start.19 = (bf16[1,512,768]{2,1,0:T(8,128)(2,1)}, bf16[1,512,768]{2,1,0:T(8,128)(2,1)}, u32[]{:S(2)}, u32[]{:S(2)}) collective-permute-start(bf16[1,512,768]{2,1,0:T(8,128)(2,1)} %add_convert_fusion.8), channel_id=1, source_target_pairs={{0,8},{8,0},{16,24},{24,16},{1,9},{9,1},{17,25},{25,17},{2,10},{10... | collective-permute-start | bytes 2359304 | tf_op jit(solution)/shard_map/ppermute | solution.py:894
  672.1 45.8 %collective-permute-start.18 = (bf16[1,512,768]{2,1,0:T(8,128)(2,1)}, bf16[1,512,768]{2,1,0:T(8,128)(2,1)}, u32[]{:S(2)}, u32[]{:S(2)}) collective-permute-start(bf16[1,512,768]{2,1,0:T(8,128)(2,1)} %add_convert_fusion.9), channel_id=1, source_target_pairs={{0,16},{8,24},{16,0},{24,8},{1,17},{9,25},{17,1},{25,9},{2,18},{10... | collective-permute-start | bytes 2359304 | tf_op jit(solution)/shard_map/ppermute | solution.py:894
  672.5 45.4 %collective-permute-start.16 = (bf16[1,512,768]{2,1,0:T(8,128)(2,1)}, bf16[1,512,768]{2,1,0:T(8,128)(2,1)}, u32[]{:S(2)}, u32[]{:S(2)}) collective-permute-start(bf16[1,512,768]{2,1,0:T(8,128)(2,1)} %get-tuple-element.291), channel_id=1, source_target_pairs={{0,8},{8,0},{16,24},{24,16},{1,9},{9,1},{17,25},{25,17},{2,10},{10... | collective-permute-start | bytes 2359304 | tf_op jit(solution)/shard_map/ppermute | solution.py:894
  727.7 45.7 %collective-permute-start.22 = (bf16[2048,2048]{1,0:T(8,128)(2,1)}, bf16[2048,2048]{1,0:T(8,128)(2,1)}, u32[]{:S(2)}, u32[]{:S(2)}) collective-permute-start(bf16[2048,2048]{1,0:T(8,128)(2,1)} %convolution_convert_fusion.1), channel_id=1, source_target_pairs={{0,1},{1,0},{2,3},{3,2},{4,5},{5,4},{6,7},{7,6},{8,9},{9,8},{10,11... | collective-permute-start | bytes 25165832 | tf_op jit(solution)/shard_map/ppermute | solution.py:1294
  773.7 122.9 %reduce-scatter.16.cloned.1.call-start = ((), (), s32[]{:S(2)}) async-start(), calls=%async_computation.13 | async-start | bytes 3538944 | tf_op jit(solution)/shard_map/reduce_scatter | solution.py:1314
  785.0 56.3 %collective-permute-start.31 = (bf16[1,768,512]{2,1,0:T(8,128)(2,1)S(1)}, bf16[1,768,512]{2,1,0:T(8,128)(2,1)}, u32[]{:S(2)}, u32[]{:S(2)}) collective-permute-start(bf16[1,768,512]{2,1,0:T(8,128)(2,1)S(1)} %add_convert_fusion.5), channel_id=1, source_target_pairs={{0,16},{8,24},{16,0},{24,8},{1,17},{9,25},{17,1},{25,9},{2,18},{10... | collective-permute-start | bytes 2359304 | tf_op jit(solution)/shard_map/ppermute | solution.py:894
  791.3 50.0 %collective-permute-start.29 = (bf16[1,768,512]{2,1,0:T(8,128)(2,1)S(1)}, bf16[1,768,512]{2,1,0:T(8,128)(2,1)}, u32[]{:S(2)}, u32[]{:S(2)}) collective-permute-start(bf16[1,768,512]{2,1,0:T(8,128)(2,1)S(1)} %copy-done.17), channel_id=1, source_target_pairs={{0,8},{8,0},{16,24},{24,16},{1,9},{9,1},{17,25},{25,17},{2,10},{10... | collective-permute-start | bytes 2359304 | tf_op jit(solution)/shard_map/ppermute | solution.py:894
  792.8 48.4 %collective-permute-start.30 = (bf16[1,768,512]{2,1,0:T(8,128)(2,1)S(1)}, bf16[1,768,512]{2,1,0:T(8,128)(2,1)}, u32[]{:S(2)}, u32[]{:S(2)}) collective-permute-start(bf16[1,768,512]{2,1,0:T(8,128)(2,1)S(1)} %copy-done.16), channel_id=1, source_target_pairs={{0,16},{8,24},{16,0},{24,8},{1,17},{9,25},{17,1},{25,9},{2,18},{10... | collective-permute-start | bytes 2359304 | tf_op jit(solution)/shard_map/ppermute | solution.py:894
  843.0 239.1 %reduce-scatter.20.cloned.1.call-start = ((), (), s32[]{:S(2)}) async-start(), calls=%async_computation.15 | async-start | bytes 2621440 | tf_op jit(solution)/shard_map/reduce_scatter | solution.py:1325
  902.3 182.0 %reduce-scatter.18.cloned.1.call-start = ((), (), s32[]{:S(2)}) async-start(), calls=%async_computation.14 | async-start | bytes 7077888 | tf_op jit(solution)/shard_map/reduce_scatter | solution.py:1320
  (85 other events, 1986.2 us)
Sparse Core Ops, SparseCore 0:
  201.9 42.6 all-gather.14
  246.8 37.1 all-gather.12
  286.2 62.3 all-gather.16
  365.9 64.5 all-gather.10
  432.6 66.6 all-gather.8
  501.4 67.9 reduce-scatter.7
  571.7 68.1 reduce-scatter.9
  642.2 68.1 reduce-scatter.11
  773.8 34.8 reduce-scatter.13
  843.1 35.7 reduce-scatter.15
  902.4 40.5 reduce-scatter.19
  945.2 113.4 reduce-scatter.17

commit v8 on v7

--- a/solution.py
+++ b/solution.py
@@ -152,7 +152,7 @@
     )(dkv, key_raw, cosine, sine, gain)
 
 
-def attend_forward(step_heads, chunk, q_ref, kv_ref, bias_ref, o_ref, log_ref):
+def attend_forward(step_heads, chunk, q_ref, kv_ref, bias_ref, o_ref, log_ref, o2_ref=None):
     group_len = bias_ref.shape[1]
     keys = kv_ref[:, 0, :, :HD].reshape(group_len, HD)
     values_t = kv_ref[:, 0, :, HD:].reshape(group_len, HD).T
@@ -168,7 +168,11 @@
             mixed += mm(values_t[:, at : at + chunk], prob.astype(bf16))
         out = (mixed / row_sum).T.astype(bf16)
         for i, h in enumerate(heads):
-            o_ref[0, :, h * HD : (h + 1) * HD] = out[i * rows : (i + 1) * rows]
+            part = out[i * rows : (i + 1) * rows]
+            o_ref[0, :, h * HD : (h + 1) * HD] = part
+            if o2_ref is not None:
+                lane = (h // 2) % 2 * HD
+                o2_ref[h % 2, h // 4, 0, :, lane : lane + HD] = part
         log_ref[0, 0, step : step + 1, :] = jnp.log2(row_sum)
 
 
@@ -230,7 +234,7 @@
     return q_spec, kv_spec, bias_spec, log_spec
 
 
-def run_forward(query, kv_all, bias, step_heads, chunk, at, earlier):
+def run_forward(query, kv_all, bias, step_heads, chunk, at, earlier, again=False):
     micro, rows, _ = query.shape
     blocks = kv_all.shape[0]
     group_len = bias.shape[1]
@@ -244,11 +248,13 @@
         kernel,
         grid=(KVH,),
         in_specs=[q_spec, kv_spec, bias_spec] + [pl.BlockSpec(memory_space=pl.ANY)] * len(earlier),
-        out_specs=[q_spec, log_spec],
+        out_specs=[q_spec, log_spec]
+        + again * [pl.BlockSpec((2, 2, 1, rows, 2 * HD), lambda g: (0, 0, at, 0, g))],
         out_shape=[
             jax.ShapeDtypeStruct(query.shape, bf16),
             jax.ShapeDtypeStruct((micro, KVH, PER_KV // step_heads, step_heads * rows), f32),
-        ],
+        ]
+        + again * [jax.ShapeDtypeStruct((2, 2, micro, rows, KVH * 2 * HD), bf16)],
         input_output_aliases={3 + i: i for i in range(len(earlier))},
         compiler_params=pltpu.CompilerParams(vmem_limit_bytes=VMEM_LIMIT),
         cost_estimate=pl.CostEstimate(
@@ -726,9 +732,10 @@
     return jnp.where(hit, 1.0, 0.0).astype(bf16), weighted.astype(bf16)
 
 
-def pick_kernel(capacity, local_experts, n_alias, tok_ref, cot_ref, *refs):
+def pick_kernel(capacity, local_experts, n_alias, tok_ref, cot_a, cot_b, *refs):
     x_ref, dy_ref = refs[n_alias:]
-    width = cot_ref.shape[3]
+    width = cot_a.shape[3]
+    cot = jnp.concatenate([cot_a[0, 0], cot_b[0, 0]], axis=0)
     first = lax.axis_index("expert") * local_experts
     routing = tok_ref[0, :, width:]
     hit, _ = picks_of(routing.astype(f32), first, local_experts, capacity)
@@ -738,7 +745,7 @@
     owner = lax.broadcasted_iota(jnp.int32, rows.shape, 0) // capacity
     at = lanes - first - owner
     weight = jnp.sum(jnp.where((at == 32) | (at == 64), rows, 0.0), axis=1, keepdims=True)
-    dy = (mm(hit, cot_ref[0, 0], TN) * weight).astype(bf16)
+    dy = (mm(hit, cot, TN) * weight).astype(bf16)
     for e in range(local_experts):
         x_ref[e, 0, 0] = x[e * capacity : (e + 1) * capacity]
         dy_ref[e, 0, 0] = dy[e * capacity : (e + 1) * capacity]
@@ -804,7 +811,8 @@
 
 
 def run_experts(tokens, cot, parts, capacity, batch_at, micro, earlier):
-    blocks, _, rows, width = cot.shape
+    blocks, rows, _ = tokens.shape
+    width = cot[0][0].shape[3]
     local_experts, _, hidden = parts[0][0].shape
     flat = [p for group in parts for p in group]
     any_spec = pl.BlockSpec(memory_space=pl.ANY)
@@ -817,17 +825,17 @@
         grid=(blocks,),
         in_specs=[
             pl.BlockSpec((1, rows, tokens.shape[2]), lambda b: (b, 0, 0)),
-            pl.BlockSpec((1, 1, rows, width), lambda b: (b, 0, 0, 0)),
         ]
+        + [pl.BlockSpec((1, 1, rows // 2, width), lambda b, i=i: (b, i, 0, 0)) for _, i in cot]
         + [any_spec] * len(earlier[:2]),
         out_specs=[picked_spec] * 2,
         out_shape=[picked] * 2,
-        input_output_aliases={2 + i: i for i in range(len(earlier[:2]))},
+        input_output_aliases={3 + i: i for i in range(len(earlier[:2]))},
         compiler_params=params,
         cost_estimate=pl.CostEstimate(
             flops=4 * slots * local_experts * rows * width, bytes_accessed=25_000_000, transcendentals=0
         ),
-    )(tokens, cot, *[a.reshape(picked.shape) for a in earlier[:2]])
+    )(tokens, cot[0][0], cot[1][0], *[a.reshape(picked.shape) for a in earlier[:2]])
     x, dy = (a.reshape(local_experts, micro, slots, width) for a in (x, dy))
     chunk = slots // 2
     row_spec = pl.BlockSpec((1, 1, chunk, width), lambda e, i: (e, batch_at, i, 0))
@@ -894,38 +902,31 @@
     return lax.ppermute(values, "dp", [(i, i ^ bit) for i in range(lax.axis_size("dp"))])
 
 
+def dp_part(total, axis, bits, expert, count=1):
+    size = total.shape[axis] // 4
+    start, sizes = [expert, 0, 0], list(total.shape)
+    start[axis] = (lax.axis_index("dp") ^ bits) * size
+    sizes[0], sizes[axis] = count, size
+    return lax.dynamic_slice(total, start, sizes)
+
+
 def scatter_far(total, axis):
-    at = lax.axis_index("dp")
-    size = total.shape[axis] // 4
-
-    def part(bits, expert):
-        start, sizes = [expert, 0, 0], list(total.shape)
-        start[axis] = (at ^ bits) * size
-        sizes[0], sizes[axis] = 1, size
-        return lax.dynamic_slice(total, start, sizes)
-
-    return [
-        swap(part(3, 0), 1),
-        swap(part(3, 1), 2),
-        part(1, 0),
-        part(2, 1),
-        part(2, 0),
-        part(1, 1),
-        lax.dynamic_slice_in_dim(total, at * size, size, axis=axis),
-    ]
-
-
-def scatter_near(for_y, for_x, by_x, by_y, near_y, near_x, own):
-    by_x, by_y = swap(by_x, 1), swap(by_y, 2)
-    near_y = swap((near_y.astype(f32) + for_y.astype(f32)).astype(bf16), 2)
-    near_x = swap((near_x.astype(f32) + for_x.astype(f32)).astype(bf16), 1)
-    return (by_x, by_y, near_y, near_x, own)
-
-
-def scatter_sum(by_x, by_y, near_y, near_x, own):
+    return swap(dp_part(total, axis, 3, 0), 1), swap(dp_part(total, axis, 3, 1), 2), total
+
+
+def scatter_near(pieces, axis):
+    for_y, for_x, total = pieces
+    by_x, by_y = swap(dp_part(total, axis, 1, 0), 1), swap(dp_part(total, axis, 2, 1), 2)
+    near_y = dp_part(total, axis, 2, 0).astype(f32) + for_y.astype(f32)
+    near_x = dp_part(total, axis, 1, 1).astype(f32) + for_x.astype(f32)
+    return by_x, by_y, swap(near_y.astype(bf16), 2), swap(near_x.astype(bf16), 1), total
+
+
+def scatter_sum(pieces, axis):
+    by_x, by_y, near_y, near_x, total = pieces
     by_x = jnp.concatenate([by_x, near_x], axis=0).astype(f32)
     by_y = jnp.concatenate([near_y, by_y], axis=0).astype(f32)
-    return own.astype(f32) + by_x + by_y
+    return dp_part(total, axis, 0, 0, total.shape[0]).astype(f32) + by_x + by_y
 
 
 def body_plain(
@@ -1188,17 +1189,19 @@
     gain_len = norm_gains.shape[0]
     gain_shard = jnp.zeros((2048,), bf16).at[:gain_len].set(norm_gains).reshape(16, 128)
     kv_w = jnp.concatenate([w_key.T, w_value.T], axis=0)
-    q_w, kv_w, out_w, gain_full, cot_0 = gather_rows(
-        [w_query.T, kv_w, w_output, gain_shard, cotangent[0, 0]], [(3, 0, 1, 2)], 1, (4,)
+    halves = cotangent.reshape(2 * micro, rows // 2, width)
+    cot_first = halves[:3].reshape(-1, width)
+    q_w, kv_w, out_w, gain_full, cot_first = gather_rows(
+        [w_query.T, kv_w, w_output, gain_shard, cot_first], [(3, 0, 1, 2)], 1, (4,)
     )
-    cot_0 = cot_0.reshape(blocks, 1, rows, width)
-    q_w, w_gate, w_up, w_down = tie((q_w, w_gate, w_up, w_down))
+    cot_first = cot_first.reshape(blocks, 3, rows // 2, width)
+    q_w, w_gate = tie((q_w, w_gate))
     gains = gain_full.reshape(shards, 2048)[:, :gain_len].reshape(-1).astype(f32)
     gain_in = gains[:width]
     gain_mid = gains[width : 2 * width]
     gain_q = gains[2 * width : 2 * width + HD]
     gain_k = gains[2 * width + HD :]
-    gate_near, up_near, down_near = ((swap(w, 1), swap(w, 2)) for w in (w_gate, w_up, w_down))
+    gate_near = (swap(w_gate, 1), swap(w_gate, 2))
 
     key_index = jnp.arange(group_len, dtype=jnp.int32)
     start_row = member * rows
@@ -1226,18 +1229,20 @@
     )
     q_low, q_raw = (a.reshape(micro, rows, H * HD) for a in (q_low, q_raw))
     kv_own = kv_own.reshape(micro, rows, KVH * 2 * HD)
+    kv_own, gate_near, w_up = tie((kv_own, gate_near, w_up))
+    up_near = (swap(w_up, 1), swap(w_up, 2))
     kv_0 = lax.all_gather(kv_own[0], "expert", axis=0, tiled=False)
     kv_1 = lax.all_gather(kv_own[1], "expert", axis=0, tiled=False)
-    kv_0, gate_near = tie((kv_0, gate_near))
-    kv_1, cot_1 = tie((kv_1, cotangent[1, 0]))
-    cot_1 = lax.all_gather(cot_1, "expert", axis=0, tiled=False)
+    kv_0, up_near, w_down = tie((kv_0, up_near, w_down))
+    down_near = (swap(w_down, 1), swap(w_down, 2))
+    kv_1, cot_last = tie((kv_1, halves[3]))
+    cot_last = lax.all_gather(cot_last, "expert", axis=0, tiled=False)[:, None]
     kv_all = [kv_0[:, None], kv_1[:, None]]
-    cots = [cot_0, cot_1[:, None]]
     chunk = 256
-    mixed = run_forward(q_low, kv_all[0], bias, step_heads, chunk, 0, [])
+    mixed = run_forward(q_low, kv_all[0], bias, step_heads, chunk, 0, [], True)
     mixed, kv_all = tie((mixed, kv_all))
-    mixed, logs = run_forward(q_low, kv_all[1], bias, step_heads, chunk, 1, mixed)
-    mixed, up_near, down_near = tie((mixed, up_near, down_near))
+    mixed, logs, shares = run_forward(q_low, kv_all[1], bias, step_heads, chunk, 1, mixed, True)
+    mixed, down_near = tie((mixed, down_near))
     parts = [
         (own, near[0], near[1], swap(near[0][:1], 2), swap(near[1][1:], 1))
         for own, near in ((w_gate, gate_near), (w_up, up_near), (w_down, down_near))
@@ -1248,7 +1253,8 @@
     scale_mid = rms_scale(middle)
     routed = (middle * scale_mid * gain_mid).astype(bf16).reshape(micro, rows, width)
     routed = jnp.concatenate([routed, routing], axis=-1)
-    routed, cots[1] = tie((routed, cots[1]))
+    routed, cot_last = tie((routed, cot_last))
+    cots = [((cot_first, 0), (cot_first, 1)), ((cot_first, 2), (cot_last, 0))]
     middle = middle.reshape(micro, rows, width)
     scale_mid = scale_mid.reshape(micro, rows, 1)
 
@@ -1272,26 +1278,28 @@
     first = scatter_far(weight_grad(picked, d_gate), 1)
     second = scatter_far(weight_grad(picked, d_up), 1)
     first, hidden_low = tie((first, hidden_low))
-    first = scatter_near(*first)
-    third = scatter_far(weight_grad(hidden_low, d_result), 2)
-    d_routeds[-1], second, mix_parts[0] = tie((d_routeds[-1], second, mix_parts[0]))
-    second = scatter_near(*second)
+    first = scatter_near(first, 1)
+    third = weight_grad(hidden_low, d_result)
+    d_routeds[-1], first, second, third, mix_parts[0] = tie(
+        (d_routeds[-1], first, second, third, mix_parts[0])
+    )
+    second = scatter_near(second, 1)
+    third = scatter_far(third, 2)
     d_mixed, d_middle, d_branch, grad_mid = run_middle_back(
         d_routeds, middle, cotangent[:, 0], gain_mid[None, :], out_w
     )
-    d_mixed, d_branch, first, third = tie((d_mixed, d_branch, first, third))
-    third = scatter_near(*third)
+    d_mixed, d_branch, third = tie((d_mixed, d_branch, third))
+    third = scatter_near(third, 2)
     d_mixed = d_mixed.reshape(micro, rows, H * HD)
     cos_rows, sine_rows = (a.reshape(micro, rows, HD) for a in (cosine, sine))
-    heads = mixed.reshape(total, 4, 2, 2, 2, HD)
-
     def share(core):
-        part = lax.dynamic_index_in_dim(heads, core, axis=4, keepdims=False)
-        return part.transpose(0, 2, 1, 3, 4).reshape(total, -1)
+        part = lax.dynamic_index_in_dim(shares, core, axis=0, keepdims=False)
+        part = part.reshape(2, total, -1)
+        return jnp.einsum("zta,td->zad", part, d_branch, preferred_element_type=f32).astype(bf16)
 
     core = member % 2
     pairs = [(i, i ^ 1) for i in range(blocks)]
-    got = lax.ppermute(mm(share(1 - core), d_branch, TN).astype(bf16), "expert", pairs)
+    got = lax.ppermute(share(1 - core), "expert", pairs)
     mixes = [lax.psum_scatter(mix_parts[0], "expert", scatter_dimension=0, tiled=True)]
 
     def backward(at, earlier):
@@ -1304,15 +1312,15 @@
     d_query, dkv_0, gain_0 = backward(0, [])
     d_query, dkv_0, got, second = tie((d_query, dkv_0, got, second))
     dkv_0 = lax.psum_scatter(dkv_0, "expert", scatter_dimension=0, tiled=False)
-    out_grad = tie(mm(share(core), d_branch, TN).astype(bf16))
+    out_grad = tie(share(core))
     out_grad = (out_grad.astype(f32) + got.astype(f32)).astype(bf16)
     d_query, out_grad = tie((d_query, out_grad))
-    out_grad = scatter_far(out_grad.reshape(2, -1, width), 1)
+    out_grad = scatter_far(out_grad, 1)
     d_query, dkv_1, gain_1 = backward(1, [d_query])
     grad_qn = gain_0 + gain_1
     d_query, dkv_1, out_grad, mixes, third = tie((d_query, dkv_1, out_grad, mixes, third))
     dkv_1 = lax.psum_scatter(dkv_1, "expert", scatter_dimension=0, tiled=False)
-    out_grad = scatter_sum(*scatter_near(*out_grad)).astype(bf16).reshape(-1, width)
+    out_grad = scatter_sum(scatter_near(out_grad, 1), 1).astype(bf16).reshape(-1, width)
     d_query = d_query.reshape(total, H * HD)
     dkv = jnp.concatenate([dkv_0, dkv_1], axis=0)
     dkv = dkv.reshape(total, KVH * 2 * HD)
@@ -1333,7 +1341,7 @@
     input_grad = d_middle + d_in_norm
     gain_grads = jnp.concatenate([grad_in, grad_mid[0], grad_qn[0], grad_kn[0]]).reshape(shards, gain_len)
     grad_qkv, grad_gains = reduce_rows(d_query, dkv_t, normed, 3, gain_grads)
-    expert_grads = [scatter_sum(*pieces) for pieces in (first, second, third)]
+    expert_grads = [scatter_sum(first, 1), scatter_sum(second, 1), scatter_sum(third, 2)]
     return (
         jnp.stack(outputs)[:, None],
         input_grad.reshape(micro, 1, rows, width),

time: 1100 us -> 1070 us (0.973)
  local copies, waits for them, and re-layouts: 89.5 us -> 68.1 us
  waiting for transfers between devices: 211 us -> 190 us
    all_gather x1, waiting for transfers between devices: 0.02 us -> 34.6 us  [body_fast(): kv_0 = lax.all_gather(kv_own[0], 'expert', axis=0, tiled=False)]
    ppermute x36, waiting for transfers between devices: 145 us -> 111 us  [swap(): lax.ppermute(values, 'dp', [(i, i ^ bit) for i in range(lax.axis_size('dp...]
    dot_general x0 -> x2, matrix products: none -> 13.3 us  [share(): jnp.einsum('zta,td->zad', part, d_branch, preferred_element_type=f32)]
    dot_general x5 -> x3, matrix products: 38.2 us -> 25 us  [mm(): return lax.dot_general(a, b, dims, preferred_element_type=f32)]
    transpose x2 -> x0, local copies, waits for them, and re-layouts: 13.1 us -> none  [share(): return part.transpose(0, 2, 1, 3, 4).reshape(total, -1)]
    all_gather x1, waiting for transfers between devices: 42 us -> 29.3 us  [body_fast(): kv_1 = lax.all_gather(kv_own[1], 'expert', axis=0, tiled=False)]
  transfers between devices with their start and end apart: 49 -> 49, of which waited for: 23 -> 20; matrix products, arithmetic and copies ran while one was open for 18% -> 18% of each run, Pallas kernels for 37% -> 40%
where the time goes in v8:
time: 1070 us; the launch traced here: 1060 us
  Pallas kernels  602 us (56%)
  waiting for transfers between devices  190 us (18%)
  matrix products  86.2 us (8%)
  local copies, waits for them, and re-layouts  68.1 us (6%)
  other arithmetic  64.6 us (6%)
  starting transfers between devices  38.2 us (4%)
  between operations  15.7 us (1%)
    pallas_call x1, Pallas kernels, gather_rows(): pl.pallas_call(functools.partial(gather_kernel, phases, len(arrays), late...  172 us
    pallas_call x1, Pallas kernels, reduce_rows(): pl.pallas_call(functools.partial(reduce_kernel, rows, 4), out_shape=[jax....  139 us
    ppermute x36, waiting for transfers between devices, swap(): lax.ppermute(values, 'dp', [(i, i ^ bit) for i in range(lax.axis_size('dp...  111 us
    pallas_call x2, Pallas kernels, run_experts(): pl.pallas_call(functools.partial(expert_kernel, len(earlier[2:])), grid=(...  80 us
    pallas_call x2, Pallas kernels, run_backward(): pl.pallas_call(kernel, grid=(KVH,), in_specs=[q_spec, kv_spec, bias_spec,...  71.3 us
    dot_general x3, matrix products, weight_grad(): jnp.einsum('era,erb->eab', rows_in, rows_out, preferred_element_type=f32)  47.9 us
    pallas_call x2, Pallas kernels, run_forward(): pl.pallas_call(kernel, grid=(KVH,), in_specs=[q_spec, kv_spec, bias_spec]...  46.8 us
    ppermute x36, starting transfers between devices, swap(): lax.ppermute(values, 'dp', [(i, i ^ bit) for i in range(lax.axis_size('dp...  37.2 us
  transfers between devices with their start and end apart: 49, of which 20 were waited for; matrix products, arithmetic and copies ran while one was open for 18% of the time, Pallas kernels for 40%

profile of v8, /device:TPU:8, one launch (start us, length us, event | category | flops | bytes accessed | tf_op | source)
XLA Modules:
  0.0 1064.5 jit_solution(9247196804746800742)
XLA Ops:
  13.1 171.9 %shard_map.213 = (bf16[4096,2048]{1,0:T(8,128)(2,1)}, bf16[1024,2048]{1,0:T(8,128)(2,1)}, bf16[4096,2048]{1,0:T(8,128)(2,1)}, bf16[512,128]{1,0:T(8,128)(2,1)}, bf16[2304,2048]{1,0:T(8,128)(2,1)}) custom-call(bf16[128,2048]{1,0:T(8,128)(2,1)} %bitcast.162, bf16[32,2048]{1,0:T(8,128)(2,1)} %pad_maximum_fusion.5.refs_1_, bf16[128,2048]{1,0:T(8,128)(2,1)} %refs_2_.1, ...), custom_call_target="tpu_custom_call" | custom-call | bytes 400000000 | tf_op jit(solution)/shard_map/pallas_call | solution.py:499
  201.3 16.4 %shard_map.214 = (bf16[384,4096]{1,0:T(8,128)(2,1)}, f32[384,4096]{1,0:T(8,128)}, bf16[384,1024]{1,0:T(8,128)(2,1)}, f32[384,512]{1,0:T(8,128)}, bf16[1024,2048]{1,0:T(8,128)(2,1)}) custom-call(bf16[384,2048]{1,0:T(8,128)(2,1)} %fusion.2.x_ref.b_ref, bf16[4096,2048]{1,0:T(8,128)(2,1)} %get-tuple-element.187.wq_ref, ...), custom_call_target="tpu_custom_call" | custom-call | flops 8053063680 | bytes 40000000 | tf_op jit(solution)/shard_map/pallas_call | solution.py:96
  239.3 29.3 %all-gather.9.cloned.1.call-done = bf16[8,192,1024]{2,1,0:T(8,128)(2,1)} async-done(((bf16[1,192,1024]{2,1,0:T(8,128)(2,1)}), bf16[8,192,1024]{2,1,0:T(8,128)(2,1)}) %all-gather.9.cloned.1.call-update) | async-done | bytes 3145744 | tf_op jit(solution)/shard_map/all_gather | solution.py:1235
  273.4 34.6 %all-gather.7.cloned.1.call-done = bf16[8,192,1024]{2,1,0:T(8,128)(2,1)} async-done(((bf16[1,192,1024]{2,1,0:T(8,128)(2,1)}), bf16[8,192,1024]{2,1,0:T(8,128)(2,1)}) %all-gather.7.cloned.1.call-update) | async-done | bytes 3145744 | tf_op jit(solution)/shard_map/all_gather | solution.py:1234
  311.4 23.4 %shard_map.215 = (bf16[2,192,4096]{2,1,0:T(8,128)(2,1)}, f32[2,4,4,384]{3,2,1,0:T(4,128)}, bf16[2,2,2,192,1024]{4,3,2,1,0:T(8,128)(2,1)}) custom-call(bf16[2,192,4096]{2,1,0:T(8,128)(2,1)} %bitcast.198, bf16[8,1,192,1024]{3,2,1,0:T(8,128)(2,1)} %bitcast.191, f32[2,1536,384]{2,1,0:T(8,128)} %copy.81.refs_2_), custom_call_target="tpu_custom_call" | custom-call | flops 4831838208 | bytes 20000000 | tf_op jit(solution)/shard_map/pallas_call | solution.py:247
  334.8 23.4 %shard_map.216 = (bf16[2,192,4096]{2,1,0:T(8,128)(2,1)}, f32[2,4,4,384]{3,2,1,0:T(4,128)}, bf16[2,2,2,192,1024]{4,3,2,1,0:T(8,128)(2,1)}) custom-call(bf16[2,192,4096]{2,1,0:T(8,128)(2,1)} %bitcast.199, bf16[8,1,192,1024]{3,2,1,0:T(8,128)(2,1)} %bitcast.189, ...), custom_call_target="tpu_custom_call", output_to_operand_aliasing={{0}: (3, {}), {1}: (4, {}), {2}: (5, {})} | custom-call | flops 4831838208 | bytes 20000000 | tf_op jit(solution)/shard_map/pallas_call | solution.py:247
  397.0 15.1 %collective-permute-done.8.refs_10_ = bf16[1,512,768]{2,1,0:T(8,128)(2,1)S(1)} collective-permute-done((bf16[1,512,768]{2,1,0:T(8,128)(2,1)S(1)}, bf16[1,512,768]{2,1,0:T(8,128)(2,1)S(1)}, u32[]{:S(2)}, u32[]{:S(2)}) %collective-permute-start.8) | collective-permute-done | bytes 786464 | tf_op jit(solution)/shard_map/ppermute | solution.py:902
  413.8 13.7 %collective-permute-done.10.refs_15_ = bf16[1,768,512]{2,1,0:T(8,128)(2,1)S(1)} collective-permute-done((bf16[1,768,512]{2,1,0:T(8,128)(2,1)S(1)}, bf16[1,768,512]{2,1,0:T(8,128)(2,1)S(1)}, u32[]{:S(2)}, u32[]{:S(2)}) %collective-permute-start.10) | collective-permute-done | bytes 786464 | tf_op jit(solution)/shard_map/ppermute | solution.py:902
  437.8 14.0 %shard_map.217 = (bf16[2,2,8,96,2048]{4,3,2,1,0:T(8,128)(2,1)}, bf16[2,2,8,96,2048]{4,3,2,1,0:T(8,128)(2,1)}) custom-call(bf16[8,192,2176]{2,1,0:T(8,128)(2,1)} %all-gather.13.cloned.1.call-done.tok_ref.routing_ref, bf16[8,3,96,2048]{3,2,1,0:T(8,128)(2,1)} %bitcast.137, bf16[8,3,96,2048]{3,2,1,0:T(8,128)(2,1)} %bitcast.138), custom_call_target="tpu_custom_call" | custom-call | flops 2415919104 | bytes 25000000 | tf_op jit(solution)/shard_map/pallas_call | solution.py:823
  451.8 40.0 %shard_map.218 = (bf16[2,2,768,768]{3,2,1,0:T(8,128)(2,1)}, bf16[2,2,768,768]{3,2,1,0:T(8,128)(2,1)}, bf16[2,2,768,768]{3,2,1,0:T(8,128)(2,1)}, bf16[2,768,2048]{2,1,0:T(8,128)(2,1)}, bf16[2,768,2048]{2,1,0:T(8,128)(2,1)}) custom-call(bf16[2,2,768,2048]{3,2,1,0:T(8,128)(2,1)} %bitcast.142, bf16[2,2,768,2048]{3,2,1,0:T(8,128)(2,1)} %bitcast.146, ...), custom_call_target="tpu_custom_call" | custom-call | flops 28991029248 | bytes 50000000 | tf_op jit(solution)/shard_map/pallas_call | solution.py:846
  491.8 12.7 %shard_map.219 = (bf16[1536,2048]{1,0:T(8,128)(2,1)}, bf16[1536,2048]{1,0:T(8,128)(2,1)}) custom-call(bf16[8,192,2176]{2,1,0:T(8,128)(2,1)} %all-gather.13.cloned.1.call-done.tok_ref.routing_ref, bf16[2,8,96,2048]{3,2,1,0:T(8,128)(2,1)} %bitcast.155, bf16[2,8,96,2048]{3,2,1,0:T(8,128)(2,1)} %bitcast.156), custom_call_target="tpu_custom_call" | custom-call | flops 2415919104 | bytes 25000000 | tf_op jit(solution)/shard_map/pallas_call | solution.py:868
  506.5 14.1 %shard_map.220 = (bf16[2,2,8,96,2048]{4,3,2,1,0:T(8,128)(2,1)}, bf16[2,2,8,96,2048]{4,3,2,1,0:T(8,128)(2,1)}) custom-call(bf16[8,192,2176]{2,1,0:T(8,128)(2,1)} %all-gather.11.cloned.1.call-done.tok_ref.routing_ref, bf16[8,3,96,2048]{3,2,1,0:T(8,128)(2,1)} %bitcast.139, ...), custom_call_target="tpu_custom_call", output_to_operand_aliasing={{0}: (3, {}), {1}: (4, {})} | custom-call | flops 2415919104 | bytes 25000000 | tf_op jit(solution)/shard_map/pallas_call | solution.py:823
  520.6 40.0 %shard_map.221 = (bf16[2,2,768,768]{3,2,1,0:T(8,128)(2,1)}, bf16[2,2,768,768]{3,2,1,0:T(8,128)(2,1)}, bf16[2,2,768,768]{3,2,1,0:T(8,128)(2,1)}, bf16[2,768,2048]{2,1,0:T(8,128)(2,1)}, bf16[2,768,2048]{2,1,0:T(8,128)(2,1)}) custom-call(bf16[2,2,768,2048]{3,2,1,0:T(8,128)(2,1)} %bitcast.143, ...), custom_call_target="tpu_custom_call", output_to_operand_aliasing={{0}: (17, {}), {1}: (18, {}), {2}: (19, {})} | custom-call | flops 28991029248 | bytes 50000000 | tf_op jit(solution)/shard_map/pallas_call | solution.py:846
  560.6 12.7 %shard_map.222 = (bf16[1536,2048]{1,0:T(8,128)(2,1)}, bf16[1536,2048]{1,0:T(8,128)(2,1)}) custom-call(bf16[8,192,2176]{2,1,0:T(8,128)(2,1)} %all-gather.11.cloned.1.call-done.tok_ref.routing_ref, bf16[2,8,96,2048]{3,2,1,0:T(8,128)(2,1)} %bitcast.153, bf16[2,8,96,2048]{3,2,1,0:T(8,128)(2,1)} %bitcast.154), custom_call_target="tpu_custom_call" | custom-call | flops 2415919104 | bytes 25000000 | tf_op jit(solution)/shard_map/pallas_call | solution.py:868
  576.8 15.2 %convolution_convert_fusion.4 = bf16[2,2048,768]{2,1,0:T(8,128)(2,1)S(1)} fusion(bf16[2,1536,2048]{2,1,0:T(8,128)(2,1)} %bitcast.144, bf16[2,1536,768]{2,1,0:T(8,128)(2,1)} %bitcast.196), kind=kOutput, calls=%fused_computation.6 | convolution fusion | flops 9666822144 | bytes 23592960 | tf_op jit(solution)/shard_map/era,erb->eab/dot_general | solution.py:1276
  596.4 15.4 %convolution_convert_fusion.3 = bf16[2,2048,768]{2,1,0:T(8,128)(2,1)S(1)} fusion(bf16[2,1536,2048]{2,1,0:T(8,128)(2,1)} %bitcast.145, bf16[2,1536,768]{2,1,0:T(8,128)(2,1)} %bitcast.197), kind=kOutput, calls=%fused_computation.5 | convolution fusion | flops 9666822144 | bytes 23592960 | tf_op jit(solution)/shard_map/era,erb->eab/dot_general | solution.py:1276
  636.1 17.3 %convolution_convert_fusion.2 = bf16[2,768,2048]{2,1,0:T(8,128)(2,1)} fusion(bf16[2,1536,768]{2,1,0:T(8,128)(2,1)} %bitcast.195, bf16[2,1536,2048]{2,1,0:T(8,128)(2,1)} %bitcast.148), kind=kOutput, calls=%fused_computation.4 | convolution fusion | flops 9666822144 | bytes 23592960 | tf_op jit(solution)/shard_map/era,erb->eab/dot_general | solution.py:1276
  654.4 14.6 %collective-permute-done.14 = bf16[1,512,768]{2,1,0:T(8,128)(2,1)S(1)} collective-permute-done((bf16[1,512,768]{2,1,0:T(8,128)(2,1)S(1)}, bf16[1,512,768]{2,1,0:T(8,128)(2,1)S(1)}, u32[]{:S(2)}, u32[]{:S(2)}) %collective-permute-start.14) | collective-permute-done | bytes 786464 | tf_op jit(solution)/shard_map/ppermute | solution.py:902
  676.4 19.5 %shard_map.223 = (bf16[384,4096]{1,0:T(8,128)(2,1)}, f32[384,2048]{1,0:T(8,128)}, bf16[384,2048]{1,0:T(8,128)(2,1)}, f32[1,2048]{1,0:T(1,128)}) custom-call(bf16[192,2048]{1,0:T(8,128)(2,1)} %reduce-scatter.8.cloned.1.call-done.r0_ref, bf16[192,2048]{1,0:T(8,128)(2,1)} %reduce-scatter.10.cloned.1.call-done.r1_ref, f32[2,192,2048]{2,1,0:T(8,128)} %bitcast.141, ...), custom_call_target="tpu_custom_call" | custom-call | flops 6442450944 | bytes 35000000 | tf_op jit(solution)/shard_map/pallas_call | solution.py:324
  712.5 35.8 %shard_map.224 = (bf16[2,192,4096]{2,1,0:T(8,128)(2,1)}, bf16[8,1,192,1024]{3,2,1,0:T(8,128)(2,1)}, f32[1,128]{1,0:T(1,128)}) custom-call(bf16[2,192,4096]{2,1,0:T(8,128)(2,1)} %bitcast.200, bf16[8,1,192,1024]{3,2,1,0:T(8,128)(2,1)} %bitcast.192, f32[2,1536,384]{2,1,0:T(8,128)} %copy.81.refs_2_, bf16[2,192,4096]{2,1,0:T(8,128)(2,1)} %get-tuple-element.205.refs_3_, ...), custom_call_target="tpu_custom_call" | custom-call | flops 12079595520 | bytes 30000000 | tf_op jit(solution)/shard_map/pallas_call | solution.py:277
  774.3 35.6 %shard_map.225 = (bf16[2,192,4096]{2,1,0:T(8,128)(2,1)}, bf16[8,1,192,1024]{3,2,1,0:T(8,128)(2,1)}, f32[1,128]{1,0:T(1,128)}) custom-call(bf16[2,192,4096]{2,1,0:T(8,128)(2,1)} %bitcast.201, bf16[8,1,192,1024]{3,2,1,0:T(8,128)(2,1)} %bitcast.190, f32[2,1536,384]{2,1,0:T(8,128)} %copy.81.refs_2_, ...), custom_call_target="tpu_custom_call", output_to_operand_aliasing={{0}: (10, {})} | custom-call | flops 12079595520 | bytes 30000000 | tf_op jit(solution)/shard_map/pallas_call | solution.py:277
  821.2 19.1 %collective-permute-done.34 = bf16[1,256,2048]{2,1,0:T(8,128)(2,1)S(1)} collective-permute-done((bf16[1,256,2048]{2,1,0:T(8,128)(2,1)}, bf16[1,256,2048]{2,1,0:T(8,128)(2,1)S(1)}, u32[]{:S(2)}, u32[]{:S(2)}) %collective-permute-start.34) | collective-permute-done | bytes 1048608 | tf_op jit(solution)/shard_map/ppermute | solution.py:902
  841.3 18.5 %collective-permute-done.33 = bf16[1,256,2048]{2,1,0:T(8,128)(2,1)S(1)} collective-permute-done((bf16[1,256,2048]{2,1,0:T(8,128)(2,1)}, bf16[1,256,2048]{2,1,0:T(8,128)(2,1)S(1)}, u32[]{:S(2)}, u32[]{:S(2)}) %collective-permute-start.33) | collective-permute-done | bytes 1048608 | tf_op jit(solution)/shard_map/ppermute | solution.py:902
  902.3 138.6 %shard_map.227 = (f32[160,2048]{1,0:T(8,128)}, f32[1,256]{1,0:T(1,128)}) custom-call(bf16[384,4096]{1,0:T(8,128)(2,1)} %bitcast.204, bf16[1024,384]{1,0:T(8,128)(2,1)} %get-tuple-element.325.extra_ref, bf16[384,2048]{1,0:T(8,128)(2,1)} %fusion.2.x_ref.b_ref, f32[64,256]{1,0:T(8,128)} %bitcast.176), custom_call_target="tpu_custom_call" | custom-call | flops 8053063680 | bytes 10000000 | tf_op jit(solution)/shard_map/pallas_call | solution.py:693
  (344 shorter events, 258.0 us)
Async XLA Ops:
  7.2 261.4 %all-gather.9.cloned.1.call-start = ((), (), s32[]{:S(2)}) async-start(), calls=%async_computation.8 | async-start | bytes 3538944 | tf_op jit(solution)/shard_map/all_gather | solution.py:1235
  221.7 86.4 %all-gather.7.cloned.1.call-start = ((), (), s32[]{:S(2)}) async-start(), calls=%async_computation.7 | async-start | bytes 3538944 | tf_op jit(solution)/shard_map/all_gather | solution.py:1234
  222.4 150.2 %all-gather.15.cloned.1.call-start = ((), (), s32[]{:S(2)}) async-start(), calls=%async_computation.18 | async-start | bytes 3538944 | tf_op jit(solution)/shard_map/all_gather | solution.py:1239
  224.8 48.6 %collective-permute-start.2 = (bf16[2,512,768]{2,1,0:T(8,128)(2,1)}, bf16[2,512,768]{2,1,0:T(8,128)(2,1)}, u32[]{:S(2)}, u32[]{:S(2)}) collective-permute-start(bf16[2,512,768]{2,1,0:T(8,128)(2,1)} %refs_7_.1), channel_id=1, source_target_pairs={{0,8},{8,0},{16,24},{24,16},{1,9},{9,1},{17,25},{25,17},{2,10},{10... | collective-permute-start | bytes 4718600 | tf_op jit(solution)/shard_map/ppermute | solution.py:902
  225.5 47.9 %collective-permute-start.3 = (bf16[2,512,768]{2,1,0:T(8,128)(2,1)}, bf16[2,512,768]{2,1,0:T(8,128)(2,1)}, u32[]{:S(2)}, u32[]{:S(2)}) collective-permute-start(bf16[2,512,768]{2,1,0:T(8,128)(2,1)} %refs_7_.1), channel_id=1, source_target_pairs={{0,16},{8,24},{16,0},{24,8},{1,17},{9,25},{17,1},{25,9},{2,18},{10... | collective-permute-start | bytes 4718600 | tf_op jit(solution)/shard_map/ppermute | solution.py:902
  268.6 169.2 %all-gather.13.cloned.1.call-start = ((), (), s32[]{:S(2)}) async-start(), calls=%async_computation.10 | async-start | bytes 7520256 | tf_op jit(solution)/shard_map/all_gather | solution.py:1264
  308.0 50.2 %collective-permute-start.4 = (bf16[2,768,512]{2,1,0:T(8,128)(2,1)}, bf16[2,768,512]{2,1,0:T(8,128)(2,1)}, u32[]{:S(2)}, u32[]{:S(2)}) collective-permute-start(bf16[2,768,512]{2,1,0:T(8,128)(2,1)} %refs_12_.1), channel_id=1, source_target_pairs={{0,8},{8,0},{16,24},{24,16},{1,9},{9,1},{17,25},{25,17},{2,10},{10... | collective-permute-start | bytes 4718600 | tf_op jit(solution)/shard_map/ppermute | solution.py:902
  309.5 48.8 %collective-permute-start.5 = (bf16[2,768,512]{2,1,0:T(8,128)(2,1)}, bf16[2,768,512]{2,1,0:T(8,128)(2,1)}, u32[]{:S(2)}, u32[]{:S(2)}) collective-permute-start(bf16[2,768,512]{2,1,0:T(8,128)(2,1)} %refs_12_.1), channel_id=1, source_target_pairs={{0,16},{8,24},{16,0},{24,8},{1,17},{9,25},{17,1},{25,9},{2,18},{10... | collective-permute-start | bytes 4718600 | tf_op jit(solution)/shard_map/ppermute | solution.py:902
  374.0 132.6 %all-gather.11.cloned.1.call-start = ((), (), s32[]{:S(2)}) async-start(), calls=%async_computation.9 | async-start | bytes 7520256 | tf_op jit(solution)/shard_map/all_gather | solution.py:1264
  374.6 202.1 %reduce-scatter.8.cloned.1.call-start = ((), (), s32[]{:S(2)}) async-start(), calls=%async_computation.11 | async-start | bytes 7077888 | tf_op jit(solution)/shard_map/reduce_scatter | solution.py:1269
  383.8 43.8 %collective-permute-start.10 = (bf16[1,768,512]{2,1,0:T(8,128)(2,1)S(1)}, bf16[1,768,512]{2,1,0:T(8,128)(2,1)S(1)}, u32[]{:S(2)}, u32[]{:S(2)}) collective-permute-start(bf16[1,768,512]{2,1,0:T(8,128)(2,1)S(1)} %slice.98), channel_id=1, source_target_pairs={{0,16},{8,24},{16,0},{24,8},{1,17},{9,25},{17,1},{25,9},{2,18},{10... | collective-permute-start | bytes 2359304 | tf_op jit(solution)/shard_map/ppermute | solution.py:902
  504.5 165.3 %reduce-scatter.10.cloned.1.call-start = ((), (), s32[]{:S(2)}) async-start(), calls=%async_computation.12 | async-start | bytes 7077888 | tf_op jit(solution)/shard_map/reduce_scatter | solution.py:1269
  576.7 233.5 %reduce-scatter.12.cloned.1.call-start = ((), (), s32[]{:S(2)}) async-start(), calls=%async_computation.13 | async-start | bytes 7077888 | tf_op jit(solution)/shard_map/reduce_scatter | solution.py:1303
  622.8 46.1 %collective-permute-start.14 = (bf16[1,512,768]{2,1,0:T(8,128)(2,1)S(1)}, bf16[1,512,768]{2,1,0:T(8,128)(2,1)S(1)}, u32[]{:S(2)}, u32[]{:S(2)}) collective-permute-start(bf16[1,512,768]{2,1,0:T(8,128)(2,1)S(1)} %get-tuple-element.415), channel_id=1, source_target_pairs={{0,8},{8,0},{16,24},{24,16},{1,9},{9,1},{17,25},{25,17},{2,10},{10... | collective-permute-start | bytes 2359304 | tf_op jit(solution)/shard_map/ppermute | solution.py:902
  669.9 195.4 %reduce-scatter.14.cloned.1.call-start = ((), (), s32[]{:S(2)}) async-start(), calls=%async_computation.14 | async-start | bytes 3538944 | tf_op jit(solution)/shard_map/reduce_scatter | solution.py:1314
  704.3 44.0 %collective-permute-start.22 = (bf16[2,1024,2048]{2,1,0:T(8,128)(2,1)}, bf16[2,1024,2048]{2,1,0:T(8,128)(2,1)}, u32[]{:S(2)}, u32[]{:S(2)}) collective-permute-start(bf16[2,1024,2048]{2,1,0:T(8,128)(2,1)} %convolution_convert_fusion.1), channel_id=1, source_target_pairs={{0,1},{1,0},{2,3},{3,2},{4,5},{5,4},{6,7},{7,6},{8,9},{9,8},{10,11... | collective-permute-start | bytes 25165832 | tf_op jit(solution)/shard_map/ppermute | solution.py:1302
  707.1 41.1 %collective-permute-start.25 = (bf16[1,512,768]{2,1,0:T(8,128)(2,1)S(1)}, bf16[1,512,768]{2,1,0:T(8,128)(2,1)}, u32[]{:S(2)}, u32[]{:S(2)}) collective-permute-start(bf16[1,512,768]{2,1,0:T(8,128)(2,1)S(1)} %get-tuple-element.405), channel_id=1, source_target_pairs={{0,16},{8,24},{16,0},{24,8},{1,17},{9,25},{17,1},{25,9},{2,18},{10... | collective-permute-start | bytes 2359304 | tf_op jit(solution)/shard_map/ppermute | solution.py:902
  748.3 116.9 %reduce-scatter.16.cloned.1.call-start = ((), (), s32[]{:S(2)}) async-start(), calls=%async_computation.15 | async-start | bytes 3538944 | tf_op jit(solution)/shard_map/reduce_scatter | solution.py:1322
  752.3 57.5 %collective-permute-start.32 = (bf16[1,768,512]{2,1,0:T(8,128)(2,1)S(1)}, bf16[1,768,512]{2,1,0:T(8,128)(2,1)}, u32[]{:S(2)}, u32[]{:S(2)}) collective-permute-start(bf16[1,768,512]{2,1,0:T(8,128)(2,1)S(1)} %get-tuple-element.400), channel_id=1, source_target_pairs={{0,8},{8,0},{16,24},{24,16},{1,9},{9,1},{17,25},{25,17},{2,10},{10... | collective-permute-start | bytes 2359304 | tf_op jit(solution)/shard_map/ppermute | solution.py:902
  759.8 50.0 %collective-permute-start.29 = (bf16[1,768,512]{2,1,0:T(8,128)(2,1)S(1)}, bf16[1,768,512]{2,1,0:T(8,128)(2,1)}, u32[]{:S(2)}, u32[]{:S(2)}) collective-permute-start(bf16[1,768,512]{2,1,0:T(8,128)(2,1)S(1)} %get-tuple-element.403), channel_id=1, source_target_pairs={{0,8},{8,0},{16,24},{24,16},{1,9},{9,1},{17,25},{25,17},{2,10},{10... | collective-permute-start | bytes 2359304 | tf_op jit(solution)/shard_map/ppermute | solution.py:902
  760.9 49.0 %collective-permute-start.30 = (bf16[1,768,512]{2,1,0:T(8,128)(2,1)S(1)}, bf16[1,768,512]{2,1,0:T(8,128)(2,1)}, u32[]{:S(2)}, u32[]{:S(2)}) collective-permute-start(bf16[1,768,512]{2,1,0:T(8,128)(2,1)S(1)} %get-tuple-element.402), channel_id=1, source_target_pairs={{0,16},{8,24},{16,0},{24,8},{1,17},{9,25},{17,1},{25,9},{2,18},{10... | collective-permute-start | bytes 2359304 | tf_op jit(solution)/shard_map/ppermute | solution.py:902
  810.2 240.4 %reduce-scatter.20.cloned.1.call-start = ((), (), s32[]{:S(2)}) async-start(), calls=%async_computation.17 | async-start | bytes 2621440 | tf_op jit(solution)/shard_map/reduce_scatter | solution.py:1333
  819.8 41.1 %collective-permute-start.36 = (bf16[1,256,2048]{2,1,0:T(8,128)(2,1)}, bf16[1,256,2048]{2,1,0:T(8,128)(2,1)}, u32[]{:S(2)}, u32[]{:S(2)}) collective-permute-start(bf16[1,256,2048]{2,1,0:T(8,128)(2,1)} %get-tuple-element.396), channel_id=1, source_target_pairs={{0,16},{8,24},{16,0},{24,8},{1,17},{9,25},{17,1},{25,9},{2,18},{10... | collective-permute-start | bytes 3145736 | tf_op jit(solution)/shard_map/ppermute | solution.py:902
  871.0 181.8 %reduce-scatter.18.cloned.1.call-start = ((), (), s32[]{:S(2)}) async-start(), calls=%async_computation.16 | async-start | bytes 7077888 | tf_op jit(solution)/shard_map/reduce_scatter | solution.py:1328
  (89 other events, 1863.1 us)
Sparse Core Ops, SparseCore 0:
  221.8 46.7 all-gather.8
  270.8 37.1 all-gather.6
  310.2 37.1 all-gather.14
  374.1 63.6 all-gather.12
  439.9 66.6 all-gather.10
  508.7 67.9 reduce-scatter.7
  579.0 68.1 reduce-scatter.9
  670.0 66.8 reduce-scatter.11
  748.4 35.2 reduce-scatter.13
  810.3 34.6 reduce-scatter.15
  871.0 40.3 reduce-scatter.19
  913.7 113.6 reduce-scatter.17

commit v9 on v8

--- a/solution.py
+++ b/solution.py
@@ -914,19 +914,21 @@
     return swap(dp_part(total, axis, 3, 0), 1), swap(dp_part(total, axis, 3, 1), 2), total
 
 
+def scatter_add(pieces, axis):
+    for_y, for_x, total = pieces
+    near_x = dp_part(total, axis, 1, 0, 2).astype(f32) + jnp.pad(for_x.astype(f32), ((1, 0), (0, 0), (0, 0)))
+    near_y = dp_part(total, axis, 2, 0, 2).astype(f32) + jnp.pad(for_y.astype(f32), ((0, 1), (0, 0), (0, 0)))
+    return near_x.astype(bf16), near_y.astype(bf16), total
+
+
 def scatter_near(pieces, axis):
-    for_y, for_x, total = pieces
-    by_x, by_y = swap(dp_part(total, axis, 1, 0), 1), swap(dp_part(total, axis, 2, 1), 2)
-    near_y = dp_part(total, axis, 2, 0).astype(f32) + for_y.astype(f32)
-    near_x = dp_part(total, axis, 1, 1).astype(f32) + for_x.astype(f32)
-    return by_x, by_y, swap(near_y.astype(bf16), 2), swap(near_x.astype(bf16), 1), total
+    near_x, near_y, total = scatter_add(pieces, axis)
+    return swap(near_x, 1), swap(near_y, 2), total
 
 
 def scatter_sum(pieces, axis):
-    by_x, by_y, near_y, near_x, total = pieces
-    by_x = jnp.concatenate([by_x, near_x], axis=0).astype(f32)
-    by_y = jnp.concatenate([near_y, by_y], axis=0).astype(f32)
-    return dp_part(total, axis, 0, 0, total.shape[0]).astype(f32) + by_x + by_y
+    by_x, by_y, total = pieces
+    return dp_part(total, axis, 0, 0, total.shape[0]).astype(f32) + by_x.astype(f32) + by_y.astype(f32)
 
 
 def body_plain(
@@ -1187,7 +1189,7 @@
     )
 
     gain_len = norm_gains.shape[0]
-    gain_shard = jnp.zeros((2048,), bf16).at[:gain_len].set(norm_gains).reshape(16, 128)
+    gain_shard = jnp.pad(norm_gains[None], ((0, 15), (0, 256 - gain_len)))
     kv_w = jnp.concatenate([w_key.T, w_value.T], axis=0)
     halves = cotangent.reshape(2 * micro, rows // 2, width)
     cot_first = halves[:3].reshape(-1, width)
@@ -1196,7 +1198,7 @@
     )
     cot_first = cot_first.reshape(blocks, 3, rows // 2, width)
     q_w, w_gate = tie((q_w, w_gate))
-    gains = gain_full.reshape(shards, 2048)[:, :gain_len].reshape(-1).astype(f32)
+    gains = gain_full.reshape(shards, 16, 256)[:, 0, :gain_len].reshape(-1).astype(f32)
     gain_in = gains[:width]
     gain_mid = gains[width : 2 * width]
     gain_q = gains[2 * width : 2 * width + HD]
@@ -1235,12 +1237,11 @@
     kv_1 = lax.all_gather(kv_own[1], "expert", axis=0, tiled=False)
     kv_0, up_near, w_down = tie((kv_0, up_near, w_down))
     down_near = (swap(w_down, 1), swap(w_down, 2))
-    kv_1, cot_last = tie((kv_1, halves[3]))
+    chunk = 256
+    mixed = run_forward(q_low, kv_0[:, None], bias, step_heads, chunk, 0, [], True)
+    mixed, kv_1, cot_last = tie((mixed, kv_1, halves[3]))
     cot_last = lax.all_gather(cot_last, "expert", axis=0, tiled=False)[:, None]
     kv_all = [kv_0[:, None], kv_1[:, None]]
-    chunk = 256
-    mixed = run_forward(q_low, kv_all[0], bias, step_heads, chunk, 0, [], True)
-    mixed, kv_all = tie((mixed, kv_all))
     mixed, logs, shares = run_forward(q_low, kv_all[1], bias, step_heads, chunk, 1, mixed, True)
     mixed, down_near = tie((mixed, down_near))
     parts = [
@@ -1320,16 +1321,21 @@
     grad_qn = gain_0 + gain_1
     d_query, dkv_1, out_grad, mixes, third = tie((d_query, dkv_1, out_grad, mixes, third))
     dkv_1 = lax.psum_scatter(dkv_1, "expert", scatter_dimension=0, tiled=False)
-    out_grad = scatter_sum(scatter_near(out_grad, 1), 1).astype(bf16).reshape(-1, width)
+    out_grad = scatter_add(out_grad, 1)
+    out_grad, first, second, third, d_query = tie((out_grad, first, second, third, d_query))
+    out_grad = (swap(out_grad[0], 1), swap(out_grad[1], 2), out_grad[2])
+    out_grad = scatter_sum(out_grad, 1).astype(bf16).reshape(-1, width)
     d_query = d_query.reshape(total, H * HD)
     dkv = jnp.concatenate([dkv_0, dkv_1], axis=0)
     dkv = dkv.reshape(total, KVH * 2 * HD)
     mix_part, dkv = tie((mix_parts[1], dkv))
     mixes.append(lax.psum_scatter(mix_part, "expert", scatter_dimension=0, tiled=True))
     outputs = [(middle[at] + mixes[at].astype(f32)).astype(bf16) for at in range(micro)]
+    expert_grads = [scatter_sum(first, 1), scatter_sum(second, 1), scatter_sum(third, 2)]
+    d_normed = mm(d_query, q_w)
+    dkv, out_grad, expert_grads, d_normed = tie((dkv, out_grad, expert_grads, d_normed))
     dkv, dkv_t, grad_kn = run_key_back(dkv, k_raw, cosine, sine, gain_k)
-    dkv, out_grad = tie((dkv, out_grad))
-    d_normed = mm(d_query, q_w) + mm(dkv, kv_w)
+    d_normed = d_normed + mm(dkv, kv_w)
     grad_output = lax.psum_scatter(
         out_grad,
         "expert",
@@ -1341,7 +1347,6 @@
     input_grad = d_middle + d_in_norm
     gain_grads = jnp.concatenate([grad_in, grad_mid[0], grad_qn[0], grad_kn[0]]).reshape(shards, gain_len)
     grad_qkv, grad_gains = reduce_rows(d_query, dkv_t, normed, 3, gain_grads)
-    expert_grads = [scatter_sum(first, 1), scatter_sum(second, 1), scatter_sum(third, 2)]
     return (
         jnp.stack(outputs)[:, None],
         input_grad.reshape(micro, 1, rows, width),

time: 1070 us -> 1070 us (level)
    ppermute x36 -> x28, waiting for transfers between devices: 111 us -> 140 us  [swap(): lax.ppermute(values, 'dp', [(i, i ^ bit) for i in range(lax.axis_size('dp...]
    all_gather x1, waiting for transfers between devices: 34.6 us -> 12.4 us  [body_fast(): kv_0 = lax.all_gather(kv_own[0], 'expert', axis=0, tiled=False)]
    all_gather x1, waiting for transfers between devices: 29.3 us -> 16 us  [body_fast(): kv_1 = lax.all_gather(kv_own[1], 'expert', axis=0, tiled=False)]
    ppermute x36 -> x28, starting transfers between devices: 37.2 us -> 30.4 us  [swap(): lax.ppermute(values, 'dp', [(i, i ^ bit) for i in range(lax.axis_size('dp...]
  transfers between devices with their start and end apart: 49 -> 41, of which waited for: 20 -> 23; matrix products, arithmetic and copies ran while one was open for 18% -> 18% of each run, Pallas kernels for 40% -> 41%
where the time goes in v9:
time: 1070 us; the launch traced here: 1060 us
  Pallas kernels  612 us (57%)
  waiting for transfers between devices  184 us (17%)
  matrix products  94 us (9%)
  other arithmetic  65.6 us (6%)
  local copies, waits for them, and re-layouts  57.5 us (5%)
  starting transfers between devices  32.4 us (3%)
  between operations  15.4 us (1%)
    pallas_call x1, Pallas kernels, gather_rows(): pl.pallas_call(functools.partial(gather_kernel, phases, len(arrays), late...  172 us
    pallas_call x1, Pallas kernels, reduce_rows(): pl.pallas_call(functools.partial(reduce_kernel, rows, 4), out_shape=[jax....  149 us
    ppermute x28, waiting for transfers between devices, swap(): lax.ppermute(values, 'dp', [(i, i ^ bit) for i in range(lax.axis_size('dp...  140 us
    pallas_call x2, Pallas kernels, run_experts(): pl.pallas_call(functools.partial(expert_kernel, len(earlier[2:])), grid=(...  79.9 us
    pallas_call x2, Pallas kernels, run_backward(): pl.pallas_call(kernel, grid=(KVH,), in_specs=[q_spec, kv_spec, bias_spec,...  71.4 us
    dot_general x3, matrix products, weight_grad(): jnp.einsum('era,erb->eab', rows_in, rows_out, preferred_element_type=f32)  47.6 us
    pallas_call x2, Pallas kernels, run_forward(): pl.pallas_call(kernel, grid=(KVH,), in_specs=[q_spec, kv_spec, bias_spec]...  47 us
    dot_general x3, matrix products, mm(): return lax.dot_general(a, b, dims, preferred_element_type=f32)  31.4 us
  transfers between devices with their start and end apart: 41, of which 23 were waited for; matrix products, arithmetic and copies ran while one was open for 18% of the time, Pallas kernels for 41%

profile of v9, /device:TPU:8, one launch (start us, length us, event | category | flops | bytes accessed | tf_op | source)
XLA Modules:
  0.0 1060.9 jit_solution(3932637112704409900)
XLA Ops:
  13.1 172.4 %shard_map.213 = (bf16[4096,2048]{1,0:T(8,128)(2,1)}, bf16[1024,2048]{1,0:T(8,128)(2,1)}, bf16[4096,2048]{1,0:T(8,128)(2,1)}, bf16[512,256]{1,0:T(8,128)(2,1)}, bf16[2304,2048]{1,0:T(8,128)(2,1)}) custom-call(bf16[128,2048]{1,0:T(8,128)(2,1)} %bitcast.165, bf16[32,2048]{1,0:T(8,128)(2,1)} %pad_maximum_fusion.5.refs_1_, bf16[128,2048]{1,0:T(8,128)(2,1)} %refs_2_.1, ...), custom_call_target="tpu_custom_call" | custom-call | bytes 400000000 | tf_op jit(solution)/shard_map/pallas_call | solution.py:499
  200.4 16.4 %shard_map.214 = (bf16[384,4096]{1,0:T(8,128)(2,1)}, f32[384,4096]{1,0:T(8,128)}, bf16[384,1024]{1,0:T(8,128)(2,1)}, f32[384,512]{1,0:T(8,128)}, bf16[1024,2048]{1,0:T(8,128)(2,1)}) custom-call(bf16[384,2048]{1,0:T(8,128)(2,1)} %fusion.2.x_ref.b_ref, bf16[4096,2048]{1,0:T(8,128)(2,1)} %get-tuple-element.184.wq_ref, ...), custom_call_target="tpu_custom_call" | custom-call | flops 8053063680 | bytes 40000000 | tf_op jit(solution)/shard_map/pallas_call | solution.py:96
  237.1 18.7 %collective-permute-done.2.refs_8_ = bf16[2,512,768]{2,1,0:T(8,128)(2,1)} collective-permute-done((bf16[2,512,768]{2,1,0:T(8,128)(2,1)}, bf16[2,512,768]{2,1,0:T(8,128)(2,1)}, u32[]{:S(2)}, u32[]{:S(2)}) %collective-permute-start.2) | collective-permute-done | bytes 1572896 | tf_op jit(solution)/shard_map/ppermute | solution.py:902
  256.7 12.4 %all-gather.7.cloned.1.call-done = bf16[8,192,1024]{2,1,0:T(8,128)(2,1)} async-done(((bf16[1,192,1024]{2,1,0:T(8,128)(2,1)}), bf16[8,192,1024]{2,1,0:T(8,128)(2,1)}) %all-gather.7.cloned.1.call-update) | async-done | bytes 3145744 | tf_op jit(solution)/shard_map/all_gather | solution.py:1236
  269.1 23.4 %shard_map.215 = (bf16[2,192,4096]{2,1,0:T(8,128)(2,1)}, f32[2,4,4,384]{3,2,1,0:T(4,128)}, bf16[2,2,2,192,1024]{4,3,2,1,0:T(8,128)(2,1)}) custom-call(bf16[2,192,4096]{2,1,0:T(8,128)(2,1)} %bitcast.200, bf16[8,1,192,1024]{3,2,1,0:T(8,128)(2,1)} %bitcast.193, f32[2,1536,384]{2,1,0:T(8,128)} %copy.81.refs_2_), custom_call_target="tpu_custom_call" | custom-call | flops 4831838208 | bytes 20000000 | tf_op jit(solution)/shard_map/pallas_call | solution.py:247
  292.6 16.0 %all-gather.9.cloned.1.call-done = bf16[8,192,1024]{2,1,0:T(8,128)(2,1)} async-done(((bf16[1,192,1024]{2,1,0:T(8,128)(2,1)}), bf16[8,192,1024]{2,1,0:T(8,128)(2,1)}) %all-gather.9.cloned.1.call-update) | async-done | bytes 3145744 | tf_op jit(solution)/shard_map/all_gather | solution.py:1237
  317.0 23.6 %shard_map.216 = (bf16[2,192,4096]{2,1,0:T(8,128)(2,1)}, f32[2,4,4,384]{3,2,1,0:T(4,128)}, bf16[2,2,2,192,1024]{4,3,2,1,0:T(8,128)(2,1)}) custom-call(bf16[2,192,4096]{2,1,0:T(8,128)(2,1)} %bitcast.201, bf16[8,1,192,1024]{3,2,1,0:T(8,128)(2,1)} %bitcast.191, ...), custom_call_target="tpu_custom_call", output_to_operand_aliasing={{0}: (3, {}), {1}: (4, {}), {2}: (5, {})} | custom-call | flops 4831838208 | bytes 20000000 | tf_op jit(solution)/shard_map/pallas_call | solution.py:247
  390.7 14.1 %collective-permute-done.8.refs_10_ = bf16[1,512,768]{2,1,0:T(8,128)(2,1)S(1)} collective-permute-done((bf16[1,512,768]{2,1,0:T(8,128)(2,1)S(1)}, bf16[1,512,768]{2,1,0:T(8,128)(2,1)S(1)}, u32[]{:S(2)}, u32[]{:S(2)}) %collective-permute-start.8) | collective-permute-done | bytes 786464 | tf_op jit(solution)/shard_map/ppermute | solution.py:902
  431.2 14.0 %shard_map.217 = (bf16[2,2,8,96,2048]{4,3,2,1,0:T(8,128)(2,1)}, bf16[2,2,8,96,2048]{4,3,2,1,0:T(8,128)(2,1)}) custom-call(bf16[8,192,2176]{2,1,0:T(8,128)(2,1)} %all-gather.13.cloned.1.call-done.tok_ref.routing_ref, bf16[8,3,96,2048]{3,2,1,0:T(8,128)(2,1)} %bitcast.136, bf16[8,3,96,2048]{3,2,1,0:T(8,128)(2,1)} %bitcast.137), custom_call_target="tpu_custom_call" | custom-call | flops 2415919104 | bytes 25000000 | tf_op jit(solution)/shard_map/pallas_call | solution.py:823
  445.2 40.0 %shard_map.218 = (bf16[2,2,768,768]{3,2,1,0:T(8,128)(2,1)}, bf16[2,2,768,768]{3,2,1,0:T(8,128)(2,1)}, bf16[2,2,768,768]{3,2,1,0:T(8,128)(2,1)}, bf16[2,768,2048]{2,1,0:T(8,128)(2,1)}, bf16[2,768,2048]{2,1,0:T(8,128)(2,1)}) custom-call(bf16[2,2,768,2048]{3,2,1,0:T(8,128)(2,1)} %bitcast.141, bf16[2,2,768,2048]{3,2,1,0:T(8,128)(2,1)} %bitcast.145, ...), custom_call_target="tpu_custom_call" | custom-call | flops 28991029248 | bytes 50000000 | tf_op jit(solution)/shard_map/pallas_call | solution.py:846
  485.2 12.7 %shard_map.219 = (bf16[1536,2048]{1,0:T(8,128)(2,1)}, bf16[1536,2048]{1,0:T(8,128)(2,1)}) custom-call(bf16[8,192,2176]{2,1,0:T(8,128)(2,1)} %all-gather.13.cloned.1.call-done.tok_ref.routing_ref, bf16[2,8,96,2048]{3,2,1,0:T(8,128)(2,1)} %bitcast.154, bf16[2,8,96,2048]{3,2,1,0:T(8,128)(2,1)} %bitcast.155), custom_call_target="tpu_custom_call" | custom-call | flops 2415919104 | bytes 25000000 | tf_op jit(solution)/shard_map/pallas_call | solution.py:868
  500.0 14.0 %shard_map.220 = (bf16[2,2,8,96,2048]{4,3,2,1,0:T(8,128)(2,1)}, bf16[2,2,8,96,2048]{4,3,2,1,0:T(8,128)(2,1)}) custom-call(bf16[8,192,2176]{2,1,0:T(8,128)(2,1)} %all-gather.11.cloned.1.call-done.tok_ref.routing_ref, bf16[8,3,96,2048]{3,2,1,0:T(8,128)(2,1)} %bitcast.138, ...), custom_call_target="tpu_custom_call", output_to_operand_aliasing={{0}: (3, {}), {1}: (4, {})} | custom-call | flops 2415919104 | bytes 25000000 | tf_op jit(solution)/shard_map/pallas_call | solution.py:823
  513.9 40.0 %shard_map.221 = (bf16[2,2,768,768]{3,2,1,0:T(8,128)(2,1)}, bf16[2,2,768,768]{3,2,1,0:T(8,128)(2,1)}, bf16[2,2,768,768]{3,2,1,0:T(8,128)(2,1)}, bf16[2,768,2048]{2,1,0:T(8,128)(2,1)}, bf16[2,768,2048]{2,1,0:T(8,128)(2,1)}) custom-call(bf16[2,2,768,2048]{3,2,1,0:T(8,128)(2,1)} %bitcast.142, ...), custom_call_target="tpu_custom_call", output_to_operand_aliasing={{0}: (17, {}), {1}: (18, {}), {2}: (19, {})} | custom-call | flops 28991029248 | bytes 50000000 | tf_op jit(solution)/shard_map/pallas_call | solution.py:846
  553.9 12.7 %shard_map.222 = (bf16[1536,2048]{1,0:T(8,128)(2,1)}, bf16[1536,2048]{1,0:T(8,128)(2,1)}) custom-call(bf16[8,192,2176]{2,1,0:T(8,128)(2,1)} %all-gather.11.cloned.1.call-done.tok_ref.routing_ref, bf16[2,8,96,2048]{3,2,1,0:T(8,128)(2,1)} %bitcast.152, bf16[2,8,96,2048]{3,2,1,0:T(8,128)(2,1)} %bitcast.153), custom_call_target="tpu_custom_call" | custom-call | flops 2415919104 | bytes 25000000 | tf_op jit(solution)/shard_map/pallas_call | solution.py:868
  570.4 16.9 %convolution_convert_fusion.4 = bf16[2,2048,768]{2,1,0:T(8,128)(2,1)} fusion(bf16[2,1536,2048]{2,1,0:T(8,128)(2,1)} %bitcast.143, bf16[2,1536,768]{2,1,0:T(8,128)(2,1)} %bitcast.198), kind=kOutput, calls=%fused_computation.6 | convolution fusion | flops 9666822144 | bytes 23592960 | tf_op jit(solution)/shard_map/era,erb->eab/dot_general | solution.py:1277
  593.0 17.2 %convolution_convert_fusion.3 = bf16[2,2048,768]{2,1,0:T(8,128)(2,1)} fusion(bf16[2,1536,2048]{2,1,0:T(8,128)(2,1)} %bitcast.144, bf16[2,1536,768]{2,1,0:T(8,128)(2,1)} %bitcast.199), kind=kOutput, calls=%fused_computation.5 | convolution fusion | flops 9666822144 | bytes 23592960 | tf_op jit(solution)/shard_map/era,erb->eab/dot_general | solution.py:1277
  619.8 13.5 %convolution_convert_fusion.2 = bf16[2,768,2048]{2,1,0:T(8,128)(2,1)} fusion(bf16[2,1536,768]{2,1,0:T(8,128)(2,1)} %bitcast.197, bf16[2,1536,2048]{2,1,0:T(8,128)(2,1)S(1)} %bitcast.149), kind=kOutput, calls=%fused_computation.4 | convolution fusion | flops 9666822144 | bytes 23592960 | tf_op jit(solution)/shard_map/era,erb->eab/dot_general | solution.py:1277
  633.9 32.8 %collective-permute-done.14 = bf16[2,512,768]{2,1,0:T(8,128)(2,1)S(1)} collective-permute-done((bf16[2,512,768]{2,1,0:T(8,128)(2,1)S(1)}, bf16[2,512,768]{2,1,0:T(8,128)(2,1)S(1)}, u32[]{:S(2)}, u32[]{:S(2)}) %collective-permute-start.14) | collective-permute-done | bytes 1572896 | tf_op jit(solution)/shard_map/ppermute | solution.py:902
  674.2 19.4 %shard_map.223 = (bf16[384,4096]{1,0:T(8,128)(2,1)}, f32[384,2048]{1,0:T(8,128)}, bf16[384,2048]{1,0:T(8,128)(2,1)}, f32[1,2048]{1,0:T(1,128)}) custom-call(bf16[192,2048]{1,0:T(8,128)(2,1)} %reduce-scatter.8.cloned.1.call-done.r0_ref, bf16[192,2048]{1,0:T(8,128)(2,1)} %reduce-scatter.10.cloned.1.call-done.r1_ref, f32[2,192,2048]{2,1,0:T(8,128)} %bitcast.140, ...), custom_call_target="tpu_custom_call" | custom-call | flops 6442450944 | bytes 35000000 | tf_op jit(solution)/shard_map/pallas_call | solution.py:324
  708.8 35.8 %shard_map.224 = (bf16[2,192,4096]{2,1,0:T(8,128)(2,1)}, bf16[8,1,192,1024]{3,2,1,0:T(8,128)(2,1)}, f32[1,128]{1,0:T(1,128)}) custom-call(bf16[2,192,4096]{2,1,0:T(8,128)(2,1)} %bitcast.202, bf16[8,1,192,1024]{3,2,1,0:T(8,128)(2,1)} %bitcast.194, f32[2,1536,384]{2,1,0:T(8,128)} %copy.81.refs_2_, bf16[2,192,4096]{2,1,0:T(8,128)(2,1)} %get-tuple-element.201.refs_3_, ...), custom_call_target="tpu_custom_call" | custom-call | flops 12079595520 | bytes 30000000 | tf_op jit(solution)/shard_map/pallas_call | solution.py:277
  771.2 35.6 %shard_map.225 = (bf16[2,192,4096]{2,1,0:T(8,128)(2,1)}, bf16[8,1,192,1024]{3,2,1,0:T(8,128)(2,1)}, f32[1,128]{1,0:T(1,128)}) custom-call(bf16[2,192,4096]{2,1,0:T(8,128)(2,1)} %bitcast.203, bf16[8,1,192,1024]{3,2,1,0:T(8,128)(2,1)} %bitcast.192, f32[2,1536,384]{2,1,0:T(8,128)} %copy.81.refs_2_, ...), custom_call_target="tpu_custom_call", output_to_operand_aliasing={{0}: (10, {})} | custom-call | flops 12079595520 | bytes 30000000 | tf_op jit(solution)/shard_map/pallas_call | solution.py:277
  834.8 12.4 %fusion.23 = f32[384,2048]{1,0:T(8,128)} fusion(bf16[384,4096]{1,0:T(8,128)(2,1)S(1)} %bitcast.207, bf16[4096,2048]{1,0:T(8,128)(2,1)} %get-tuple-element.184.wq_ref), kind=kOutput, calls=%fused_computation.109 | convolution fusion | flops 6442450944 | bytes 23068672 | tf_op jit(solution)/shard_map/dot_general | solution.py:35
  847.2 21.0 %collective-permute-done.27 = bf16[2,256,2048]{2,1,0:T(8,128)(2,1)S(1)} collective-permute-done((bf16[2,256,2048]{2,1,0:T(8,128)(2,1)S(1)}, bf16[2,256,2048]{2,1,0:T(8,128)(2,1)S(1)}, u32[]{:S(2)}, u32[]{:S(2)}) %collective-permute-start.27) | collective-permute-done | bytes 2097184 | tf_op jit(solution)/shard_map/ppermute | solution.py:902
  887.8 148.8 %shard_map.227 = (f32[160,2048]{1,0:T(8,128)}, f32[1,256]{1,0:T(1,128)}) custom-call(bf16[384,4096]{1,0:T(8,128)(2,1)} %bitcast.206, bf16[1024,384]{1,0:T(8,128)(2,1)} %get-tuple-element.343.extra_ref, bf16[384,2048]{1,0:T(8,128)(2,1)} %fusion.2.x_ref.b_ref, f32[64,256]{1,0:T(8,128)} %bitcast.179), custom_call_target="tpu_custom_call" | custom-call | flops 8053063680 | bytes 10000000 | tf_op jit(solution)/shard_map/pallas_call | solution.py:693
  (313 shorter events, 262.1 us)
Async XLA Ops:
  7.2 261.9 %all-gather.7.cloned.1.call-start = ((), (), s32[]{:S(2)}) async-start(), calls=%async_computation.7 | async-start | bytes 3538944 | tf_op jit(solution)/shard_map/all_gather | solution.py:1236
  222.3 86.3 %all-gather.9.cloned.1.call-start = ((), (), s32[]{:S(2)}) async-start(), calls=%async_computation.8 | async-start | bytes 3538944 | tf_op jit(solution)/shard_map/all_gather | solution.py:1237
  223.0 142.2 %all-gather.15.cloned.1.call-start = ((), (), s32[]{:S(2)}) async-start(), calls=%async_computation.18 | async-start | bytes 3538944 | tf_op jit(solution)/shard_map/all_gather | solution.py:1243
  308.6 122.7 %all-gather.13.cloned.1.call-start = ((), (), s32[]{:S(2)}) async-start(), calls=%async_computation.10 | async-start | bytes 7520256 | tf_op jit(solution)/shard_map/all_gather | solution.py:1265
  366.5 133.5 %all-gather.11.cloned.1.call-start = ((), (), s32[]{:S(2)}) async-start(), calls=%async_computation.9 | async-start | bytes 7520256 | tf_op jit(solution)/shard_map/all_gather | solution.py:1265
  367.1 203.0 %reduce-scatter.8.cloned.1.call-start = ((), (), s32[]{:S(2)}) async-start(), calls=%async_computation.11 | async-start | bytes 7077888 | tf_op jit(solution)/shard_map/reduce_scatter | solution.py:1270
  376.6 43.2 %collective-permute-start.10 = (bf16[1,768,512]{2,1,0:T(8,128)(2,1)S(1)}, bf16[1,768,512]{2,1,0:T(8,128)(2,1)S(1)}, u32[]{:S(2)}, u32[]{:S(2)}) collective-permute-start(bf16[1,768,512]{2,1,0:T(8,128)(2,1)S(1)} %slice.87), channel_id=1, source_target_pairs={{0,16},{8,24},{16,0},{24,8},{1,17},{9,25},{17,1},{25,9},{2,18},{10... | collective-permute-start | bytes 2359304 | tf_op jit(solution)/shard_map/ppermute | solution.py:902
  497.9 170.0 %reduce-scatter.10.cloned.1.call-start = ((), (), s32[]{:S(2)}) async-start(), calls=%async_computation.12 | async-start | bytes 7077888 | tf_op jit(solution)/shard_map/reduce_scatter | solution.py:1270
  570.1 247.3 %reduce-scatter.12.cloned.1.call-start = ((), (), s32[]{:S(2)}) async-start(), calls=%async_computation.13 | async-start | bytes 7077888 | tf_op jit(solution)/shard_map/reduce_scatter | solution.py:1304
  616.7 49.9 %collective-permute-start.14 = (bf16[2,512,768]{2,1,0:T(8,128)(2,1)S(1)}, bf16[2,512,768]{2,1,0:T(8,128)(2,1)S(1)}, u32[]{:S(2)}, u32[]{:S(2)}) collective-permute-start(bf16[2,512,768]{2,1,0:T(8,128)(2,1)S(1)} %get-tuple-element.413), channel_id=1, source_target_pairs={{0,8},{8,0},{16,24},{24,16},{1,9},{9,1},{17,25},{25,17},{2,10},{10... | collective-permute-start | bytes 4718600 | tf_op jit(solution)/shard_map/ppermute | solution.py:902
  618.2 49.7 %collective-permute-start.15 = (bf16[2,512,768]{2,1,0:T(8,128)(2,1)S(1)}, bf16[2,512,768]{2,1,0:T(8,128)(2,1)}, u32[]{:S(2)}, u32[]{:S(2)}) collective-permute-start(bf16[2,512,768]{2,1,0:T(8,128)(2,1)S(1)} %get-tuple-element.412), channel_id=1, source_target_pairs={{0,16},{8,24},{16,0},{24,8},{1,17},{9,25},{17,1},{25,9},{2,18},{10... | collective-permute-start | bytes 4718600 | tf_op jit(solution)/shard_map/ppermute | solution.py:902
  668.0 204.8 %reduce-scatter.14.cloned.1.call-start = ((), (), s32[]{:S(2)}) async-start(), calls=%async_computation.14 | async-start | bytes 3538944 | tf_op jit(solution)/shard_map/reduce_scatter | solution.py:1315
  702.0 43.8 %collective-permute-start.20 = (bf16[2,1024,2048]{2,1,0:T(8,128)(2,1)}, bf16[2,1024,2048]{2,1,0:T(8,128)(2,1)}, u32[]{:S(2)}, u32[]{:S(2)}) collective-permute-start(bf16[2,1024,2048]{2,1,0:T(8,128)(2,1)} %convolution_convert_fusion.1), channel_id=1, source_target_pairs={{0,1},{1,0},{2,3},{3,2},{4,5},{5,4},{6,7},{7,6},{8,9},{9,8},{10,11... | collective-permute-start | bytes 25165832 | tf_op jit(solution)/shard_map/ppermute | solution.py:1303
  703.7 41.0 %collective-permute-start.21 = (bf16[2,512,768]{2,1,0:T(8,128)(2,1)}, bf16[2,512,768]{2,1,0:T(8,128)(2,1)S(1)}, u32[]{:S(2)}, u32[]{:S(2)}) collective-permute-start(bf16[2,512,768]{2,1,0:T(8,128)(2,1)} %get-tuple-element.407), channel_id=1, source_target_pairs={{0,8},{8,0},{16,24},{24,16},{1,9},{9,1},{17,25},{25,17},{2,10},{10... | collective-permute-start | bytes 4718600 | tf_op jit(solution)/shard_map/ppermute | solution.py:902
  705.1 39.6 %collective-permute-start.22 = (bf16[2,512,768]{2,1,0:T(8,128)(2,1)S(1)}, bf16[2,512,768]{2,1,0:T(8,128)(2,1)S(1)}, u32[]{:S(2)}, u32[]{:S(2)}) collective-permute-start(bf16[2,512,768]{2,1,0:T(8,128)(2,1)S(1)} %get-tuple-element.406), channel_id=1, source_target_pairs={{0,16},{8,24},{16,0},{24,8},{1,17},{9,25},{17,1},{25,9},{2,18},{10... | collective-permute-start | bytes 4718600 | tf_op jit(solution)/shard_map/ppermute | solution.py:902
  747.0 125.8 %reduce-scatter.16.cloned.1.call-start = ((), (), s32[]{:S(2)}) async-start(), calls=%async_computation.15 | async-start | bytes 3538944 | tf_op jit(solution)/shard_map/reduce_scatter | solution.py:1323
  757.6 49.2 %collective-permute-start.25 = (bf16[2,768,512]{2,1,0:T(8,128)(2,1)}, bf16[2,768,512]{2,1,0:T(8,128)(2,1)S(1)}, u32[]{:S(2)}, u32[]{:S(2)}) collective-permute-start(bf16[2,768,512]{2,1,0:T(8,128)(2,1)} %get-tuple-element.405), channel_id=1, source_target_pairs={{0,8},{8,0},{16,24},{24,16},{1,9},{9,1},{17,25},{25,17},{2,10},{10... | collective-permute-start | bytes 4718600 | tf_op jit(solution)/shard_map/ppermute | solution.py:902
  758.2 48.7 %collective-permute-start.26 = (bf16[2,768,512]{2,1,0:T(8,128)(2,1)}, bf16[2,768,512]{2,1,0:T(8,128)(2,1)S(1)}, u32[]{:S(2)}, u32[]{:S(2)}) collective-permute-start(bf16[2,768,512]{2,1,0:T(8,128)(2,1)} %get-tuple-element.404), channel_id=1, source_target_pairs={{0,16},{8,24},{16,0},{24,8},{1,17},{9,25},{17,1},{25,9},{2,18},{10... | collective-permute-start | bytes 4718600 | tf_op jit(solution)/shard_map/ppermute | solution.py:902
  768.3 48.1 %collective-permute-start.23 = (bf16[1,256,2048]{2,1,0:T(8,128)(2,1)S(1)}, bf16[1,256,2048]{2,1,0:T(8,128)(2,1)S(1)}, u32[]{:S(2)}, u32[]{:S(2)}) collective-permute-start(bf16[1,256,2048]{2,1,0:T(8,128)(2,1)S(1)} %get-tuple-element.403), channel_id=1, source_target_pairs={{0,8},{8,0},{16,24},{24,16},{1,9},{9,1},{17,25},{25,17},{2,10},{10... | collective-permute-start | bytes 3145736 | tf_op jit(solution)/shard_map/ppermute | solution.py:902
  769.8 47.6 %collective-permute-start.24 = (bf16[1,256,2048]{2,1,0:T(8,128)(2,1)S(1)}, bf16[1,256,2048]{2,1,0:T(8,128)(2,1)}, u32[]{:S(2)}, u32[]{:S(2)}) collective-permute-start(bf16[1,256,2048]{2,1,0:T(8,128)(2,1)S(1)} %get-tuple-element.402), channel_id=1, source_target_pairs={{0,16},{8,24},{16,0},{24,8},{1,17},{9,25},{17,1},{25,9},{2,18},{10... | collective-permute-start | bytes 3145736 | tf_op jit(solution)/shard_map/ppermute | solution.py:902
  817.4 229.8 %reduce-scatter.20.cloned.1.call-start = ((), (), s32[]{:S(2)}) async-start(), calls=%async_computation.17 | async-start | bytes 2621440 | tf_op jit(solution)/shard_map/reduce_scatter | solution.py:1339
  821.4 46.7 %collective-permute-start.27 = (bf16[2,256,2048]{2,1,0:T(8,128)(2,1)S(1)}, bf16[2,256,2048]{2,1,0:T(8,128)(2,1)S(1)}, u32[]{:S(2)}, u32[]{:S(2)}) collective-permute-start(bf16[2,256,2048]{2,1,0:T(8,128)(2,1)S(1)} %get-tuple-element.326), channel_id=1, source_target_pairs={{0,8},{8,0},{16,24},{24,16},{1,9},{9,1},{17,25},{25,17},{2,10},{10... | collective-permute-start | bytes 6291464 | tf_op jit(solution)/shard_map/ppermute | solution.py:902
  822.3 46.3 %collective-permute-start.28 = (bf16[2,256,2048]{2,1,0:T(8,128)(2,1)S(1)}, bf16[2,256,2048]{2,1,0:T(8,128)(2,1)S(1)}, u32[]{:S(2)}, u32[]{:S(2)}) collective-permute-start(bf16[2,256,2048]{2,1,0:T(8,128)(2,1)S(1)} %get-tuple-element.327), channel_id=1, source_target_pairs={{0,16},{8,24},{16,0},{24,8},{1,17},{9,25},{17,1},{25,9},{2,18},{10... | collective-permute-start | bytes 6291464 | tf_op jit(solution)/shard_map/ppermute | solution.py:902
  874.9 174.5 %reduce-scatter.18.cloned.1.call-start = ((), (), s32[]{:S(2)}) async-start(), calls=%async_computation.16 | async-start | bytes 7077888 | tf_op jit(solution)/shard_map/reduce_scatter | solution.py:1332
  (75 other events, 1703.5 us)
Sparse Core Ops, SparseCore 0:
  222.4 46.7 all-gather.6
  271.3 37.1 all-gather.8
  310.8 37.1 all-gather.14
  366.6 64.5 all-gather.12
  433.3 66.6 all-gather.10
  502.1 67.9 reduce-scatter.7
  572.4 68.1 reduce-scatter.9
  668.1 66.2 reduce-scatter.11
  747.1 34.0 reduce-scatter.13
  817.6 34.5 reduce-scatter.15
  875.0 40.5 reduce-scatter.19
  917.8 123.1 reduce-scatter.17

commit v10 on v9

--- a/solution.py
+++ b/solution.py
@@ -1238,26 +1238,30 @@
     kv_0, up_near, w_down = tie((kv_0, up_near, w_down))
     down_near = (swap(w_down, 1), swap(w_down, 2))
     chunk = 256
-    mixed = run_forward(q_low, kv_0[:, None], bias, step_heads, chunk, 0, [], True)
-    mixed, kv_1, cot_last = tie((mixed, kv_1, halves[3]))
+
+    def middle_of(mixed, at):
+        part = hidden[at * rows : (at + 1) * rows]
+        middle = part + mm(mixed[at], out_w)
+        routed = (middle * rms_scale(middle) * gain_mid).astype(bf16)
+        return middle, jnp.concatenate([routed, routing[at]], axis=-1)
+
+    mixed, logs, shares = run_forward(q_low, kv_0[:, None], bias, step_heads, chunk, 0, [], True)
+    middle_0, routed_0 = middle_of(mixed, 0)
+    mixed, kv_1, routed_0 = tie((mixed, kv_1, routed_0))
+    kv_all = [kv_0[:, None], kv_1[:, None]]
+    mixed, logs, shares = run_forward(
+        q_low, kv_all[1], bias, step_heads, chunk, 1, [mixed, logs, shares], True
+    )
+    middle_1, routed_1 = middle_of(mixed, 1)
+    routed_1, down_near, cot_last = tie((routed_1, down_near, halves[3]))
     cot_last = lax.all_gather(cot_last, "expert", axis=0, tiled=False)[:, None]
-    kv_all = [kv_0[:, None], kv_1[:, None]]
-    mixed, logs, shares = run_forward(q_low, kv_all[1], bias, step_heads, chunk, 1, mixed, True)
-    mixed, down_near = tie((mixed, down_near))
     parts = [
         (own, near[0], near[1], swap(near[0][:1], 2), swap(near[1][1:], 1))
         for own, near in ((w_gate, gate_near), (w_up, up_near), (w_down, down_near))
     ]
-
-    branch = mm(mixed.reshape(total, H * HD), out_w)
-    middle = hidden + branch
-    scale_mid = rms_scale(middle)
-    routed = (middle * scale_mid * gain_mid).astype(bf16).reshape(micro, rows, width)
-    routed = jnp.concatenate([routed, routing], axis=-1)
-    routed, cot_last = tie((routed, cot_last))
     cots = [((cot_first, 0), (cot_first, 1)), ((cot_first, 2), (cot_last, 0))]
-    middle = middle.reshape(micro, rows, width)
-    scale_mid = scale_mid.reshape(micro, rows, 1)
+    routed = [routed_0, routed_1]
+    middle = jnp.stack([middle_0, middle_1])
 
     mix_parts, d_routeds = [], []
     kept = []

time: 1070 us -> 1050 us (0.981)
  waiting for transfers between devices: 184 us -> 154 us
    ppermute x28, waiting for transfers between devices: 140 us -> 125 us  [swap(): lax.ppermute(values, 'dp', [(i, i ^ bit) for i in range(lax.axis_size('dp...]
    all_gather x1, waiting for transfers between devices: 0.02 us -> 13.8 us  [body_fast(): cot_last = lax.all_gather(cot_last, 'expert', axis=0, tiled=False)[:, None]]
    all_gather x1, waiting for transfers between devices: 16 us -> 4.68 us  [body_fast(): kv_1 = lax.all_gather(kv_own[1], 'expert', axis=0, tiled=False)]
    dot_general x3 -> x4, matrix products: 31.4 us -> 35.1 us  [mm(): return lax.dot_general(a, b, dims, preferred_element_type=f32)]
  transfers between devices with their start and end apart: 41 -> 41, of which waited for: 23 -> 22; matrix products, arithmetic and copies ran while one was open for 18% -> 20% of each run, Pallas kernels for 41% -> 42%
where the time goes in v10:
time: 1050 us; the launch traced here: 1040 us
  Pallas kernels  611 us (58%)
  waiting for transfers between devices  154 us (15%)
  matrix products  98.1 us (9%)
  other arithmetic  74.7 us (7%)
  local copies, waits for them, and re-layouts  58.5 us (6%)
  starting transfers between devices  33.2 us (3%)
  between operations  15.5 us (1%)
    pallas_call x1, Pallas kernels, gather_rows(): pl.pallas_call(functools.partial(gather_kernel, phases, len(arrays), late...  172 us
    pallas_call x1, Pallas kernels, reduce_rows(): pl.pallas_call(functools.partial(reduce_kernel, rows, 4), out_shape=[jax....  148 us
    ppermute x28, waiting for transfers between devices, swap(): lax.ppermute(values, 'dp', [(i, i ^ bit) for i in range(lax.axis_size('dp...  125 us
    pallas_call x2, Pallas kernels, run_experts(): pl.pallas_call(functools.partial(expert_kernel, len(earlier[2:])), grid=(...  80 us
    pallas_call x2, Pallas kernels, run_backward(): pl.pallas_call(kernel, grid=(KVH,), in_specs=[q_spec, kv_spec, bias_spec,...  71.5 us
    dot_general x3, matrix products, weight_grad(): jnp.einsum('era,erb->eab', rows_in, rows_out, preferred_element_type=f32)  47.6 us
    pallas_call x2, Pallas kernels, run_forward(): pl.pallas_call(kernel, grid=(KVH,), in_specs=[q_spec, kv_spec, bias_spec]...  46.9 us
    dot_general x4, matrix products, mm(): return lax.dot_general(a, b, dims, preferred_element_type=f32)  35.1 us
  transfers between devices with their start and end apart: 41, of which 22 were waited for; matrix products, arithmetic and copies ran while one was open for 20% of the time, Pallas kernels for 42%

profile of v10, /device:TPU:8, one launch (start us, length us, event | category | flops | bytes accessed | tf_op | source)
XLA Modules:
  0.0 1044.1 jit_solution(10871818679512569322)
XLA Ops:
  13.1 172.4 %shard_map.213 = (bf16[4096,2048]{1,0:T(8,128)(2,1)}, bf16[1024,2048]{1,0:T(8,128)(2,1)}, bf16[4096,2048]{1,0:T(8,128)(2,1)}, bf16[512,256]{1,0:T(8,128)(2,1)}, bf16[2304,2048]{1,0:T(8,128)(2,1)}) custom-call(bf16[128,2048]{1,0:T(8,128)(2,1)} %bitcast.187, bf16[32,2048]{1,0:T(8,128)(2,1)} %pad_maximum_fusion.8.refs_1_, bf16[128,2048]{1,0:T(8,128)(2,1)} %refs_2_.1, ...), custom_call_target="tpu_custom_call" | custom-call | bytes 400000000 | tf_op jit(solution)/shard_map/pallas_call | solution.py:499
  200.4 16.4 %shard_map.214 = (bf16[384,4096]{1,0:T(8,128)(2,1)}, f32[384,4096]{1,0:T(8,128)}, bf16[384,1024]{1,0:T(8,128)(2,1)}, f32[384,512]{1,0:T(8,128)}, bf16[1024,2048]{1,0:T(8,128)(2,1)}) custom-call(bf16[384,2048]{1,0:T(8,128)(2,1)} %fusion.2.x_ref.b_ref, bf16[4096,2048]{1,0:T(8,128)(2,1)} %get-tuple-element.181.wq_ref, ...), custom_call_target="tpu_custom_call" | custom-call | flops 8053063680 | bytes 40000000 | tf_op jit(solution)/shard_map/pallas_call | solution.py:96
  245.7 16.2 %collective-permute-done.2.refs_8_ = bf16[2,512,768]{2,1,0:T(8,128)(2,1)} collective-permute-done((bf16[2,512,768]{2,1,0:T(8,128)(2,1)}, bf16[2,512,768]{2,1,0:T(8,128)(2,1)}, u32[]{:S(2)}, u32[]{:S(2)}) %collective-permute-start.2) | collective-permute-done | bytes 1572896 | tf_op jit(solution)/shard_map/ppermute | solution.py:902
  269.1 23.5 %shard_map.215 = (bf16[2,192,4096]{2,1,0:T(8,128)(2,1)}, f32[2,4,4,384]{3,2,1,0:T(4,128)}, bf16[2,2,2,192,1024]{4,3,2,1,0:T(8,128)(2,1)}) custom-call(bf16[2,192,4096]{2,1,0:T(8,128)(2,1)} %bitcast.222, bf16[8,1,192,1024]{3,2,1,0:T(8,128)(2,1)} %bitcast.215, f32[2,1536,384]{2,1,0:T(8,128)} %copy.102.refs_2_), custom_call_target="tpu_custom_call" | custom-call | flops 4831838208 | bytes 20000000 | tf_op jit(solution)/shard_map/pallas_call | solution.py:247
  312.9 23.4 %shard_map.216 = (bf16[2,192,4096]{2,1,0:T(8,128)(2,1)}, f32[2,4,4,384]{3,2,1,0:T(4,128)}, bf16[2,2,2,192,1024]{4,3,2,1,0:T(8,128)(2,1)}) custom-call(bf16[2,192,4096]{2,1,0:T(8,128)(2,1)} %bitcast.223, bf16[8,1,192,1024]{3,2,1,0:T(8,128)(2,1)} %bitcast.213, ...), custom_call_target="tpu_custom_call", output_to_operand_aliasing={{0}: (3, {}), {1}: (4, {}), {2}: (5, {})} | custom-call | flops 4831838208 | bytes 20000000 | tf_op jit(solution)/shard_map/pallas_call | solution.py:247
  372.3 14.1 %collective-permute-done.8.refs_10_ = bf16[1,512,768]{2,1,0:T(8,128)(2,1)S(1)} collective-permute-done((bf16[1,512,768]{2,1,0:T(8,128)(2,1)S(1)}, bf16[1,512,768]{2,1,0:T(8,128)(2,1)S(1)}, u32[]{:S(2)}, u32[]{:S(2)}) %collective-permute-start.8) | collective-permute-done | bytes 786464 | tf_op jit(solution)/shard_map/ppermute | solution.py:902
  389.1 12.2 %collective-permute-done.10.refs_15_ = bf16[1,768,512]{2,1,0:T(8,128)(2,1)S(1)} collective-permute-done((bf16[1,768,512]{2,1,0:T(8,128)(2,1)S(1)}, bf16[1,768,512]{2,1,0:T(8,128)(2,1)S(1)}, u32[]{:S(2)}, u32[]{:S(2)}) %collective-permute-start.10) | collective-permute-done | bytes 786464 | tf_op jit(solution)/shard_map/ppermute | solution.py:902
  403.9 13.9 %shard_map.217 = (bf16[2,2,8,96,2048]{4,3,2,1,0:T(8,128)(2,1)}, bf16[2,2,8,96,2048]{4,3,2,1,0:T(8,128)(2,1)}) custom-call(bf16[8,192,2176]{2,1,0:T(8,128)(2,1)} %bitcast.161, bf16[8,3,96,2048]{3,2,1,0:T(8,128)(2,1)} %bitcast.158, bf16[8,3,96,2048]{3,2,1,0:T(8,128)(2,1)} %bitcast.159), custom_call_target="tpu_custom_call" | custom-call | flops 2415919104 | bytes 25000000 | tf_op jit(solution)/shard_map/pallas_call | solution.py:823
  417.8 40.0 %shard_map.218 = (bf16[2,2,768,768]{3,2,1,0:T(8,128)(2,1)}, bf16[2,2,768,768]{3,2,1,0:T(8,128)(2,1)}, bf16[2,2,768,768]{3,2,1,0:T(8,128)(2,1)}, bf16[2,768,2048]{2,1,0:T(8,128)(2,1)}, bf16[2,768,2048]{2,1,0:T(8,128)(2,1)}) custom-call(bf16[2,2,768,2048]{3,2,1,0:T(8,128)(2,1)} %bitcast.168, bf16[2,2,768,2048]{3,2,1,0:T(8,128)(2,1)} %bitcast.172, ...), custom_call_target="tpu_custom_call" | custom-call | flops 28991029248 | bytes 50000000 | tf_op jit(solution)/shard_map/pallas_call | solution.py:846
  457.8 12.7 %shard_map.219 = (bf16[1536,2048]{1,0:T(8,128)(2,1)}, bf16[1536,2048]{1,0:T(8,128)(2,1)}) custom-call(bf16[8,192,2176]{2,1,0:T(8,128)(2,1)} %bitcast.162, bf16[2,8,96,2048]{3,2,1,0:T(8,128)(2,1)} %bitcast.180, bf16[2,8,96,2048]{3,2,1,0:T(8,128)(2,1)} %bitcast.181), custom_call_target="tpu_custom_call" | custom-call | flops 2415919104 | bytes 25000000 | tf_op jit(solution)/shard_map/pallas_call | solution.py:868
  470.9 13.8 %all-gather.17.cloned.1.call-done = bf16[768,2048]{1,0:T(8,128)(2,1)} async-done(((bf16[96,2048]{1,0:T(8,128)(2,1)}), bf16[768,2048]{1,0:T(8,128)(2,1)}) %all-gather.17.cloned.1.call-update) | async-done | bytes 3145744 | tf_op jit(solution)/shard_map/all_gather | solution.py:1257
  484.7 13.9 %shard_map.220 = (bf16[2,2,8,96,2048]{4,3,2,1,0:T(8,128)(2,1)}, bf16[2,2,8,96,2048]{4,3,2,1,0:T(8,128)(2,1)}) custom-call(bf16[8,192,2176]{2,1,0:T(8,128)(2,1)} %bitcast.163, bf16[8,3,96,2048]{3,2,1,0:T(8,128)(2,1)} %bitcast.160, bf16[8,1,96,2048]{3,2,1,0:T(8,128)(2,1)} %bitcast.186, ...), custom_call_target="tpu_custom_call", output_to_operand_aliasing={{0}: (3, {}), {1}: (4, {})} | custom-call | flops 2415919104 | bytes 25000000 | tf_op jit(solution)/shard_map/pallas_call | solution.py:823
  498.5 40.0 %shard_map.221 = (bf16[2,2,768,768]{3,2,1,0:T(8,128)(2,1)}, bf16[2,2,768,768]{3,2,1,0:T(8,128)(2,1)}, bf16[2,2,768,768]{3,2,1,0:T(8,128)(2,1)}, bf16[2,768,2048]{2,1,0:T(8,128)(2,1)}, bf16[2,768,2048]{2,1,0:T(8,128)(2,1)}) custom-call(bf16[2,2,768,2048]{3,2,1,0:T(8,128)(2,1)} %bitcast.169, ...), custom_call_target="tpu_custom_call", output_to_operand_aliasing={{0}: (17, {}), {1}: (18, {}), {2}: (19, {})} | custom-call | flops 28991029248 | bytes 50000000 | tf_op jit(solution)/shard_map/pallas_call | solution.py:846
  538.5 12.7 %shard_map.222 = (bf16[1536,2048]{1,0:T(8,128)(2,1)}, bf16[1536,2048]{1,0:T(8,128)(2,1)}) custom-call(bf16[8,192,2176]{2,1,0:T(8,128)(2,1)} %bitcast.164, bf16[2,8,96,2048]{3,2,1,0:T(8,128)(2,1)} %bitcast.178, bf16[2,8,96,2048]{3,2,1,0:T(8,128)(2,1)} %bitcast.179), custom_call_target="tpu_custom_call" | custom-call | flops 2415919104 | bytes 25000000 | tf_op jit(solution)/shard_map/pallas_call | solution.py:868
  554.2 16.9 %convolution_convert_fusion.4 = bf16[2,2048,768]{2,1,0:T(8,128)(2,1)} fusion(bf16[2,1536,2048]{2,1,0:T(8,128)(2,1)} %bitcast.170, bf16[2,1536,768]{2,1,0:T(8,128)(2,1)} %bitcast.220), kind=kOutput, calls=%fused_computation.6 | convolution fusion | flops 9666822144 | bytes 23592960 | tf_op jit(solution)/shard_map/era,erb->eab/dot_general | solution.py:1281
  576.8 17.1 %convolution_convert_fusion.3 = bf16[2,2048,768]{2,1,0:T(8,128)(2,1)} fusion(bf16[2,1536,2048]{2,1,0:T(8,128)(2,1)} %bitcast.171, bf16[2,1536,768]{2,1,0:T(8,128)(2,1)} %bitcast.221), kind=kOutput, calls=%fused_computation.5 | convolution fusion | flops 9666822144 | bytes 23592960 | tf_op jit(solution)/shard_map/era,erb->eab/dot_general | solution.py:1281
  603.5 13.5 %convolution_convert_fusion.2 = bf16[2,768,2048]{2,1,0:T(8,128)(2,1)} fusion(bf16[2,1536,768]{2,1,0:T(8,128)(2,1)} %bitcast.219, bf16[2,1536,2048]{2,1,0:T(8,128)(2,1)S(1)} %bitcast.176), kind=kOutput, calls=%fused_computation.4 | convolution fusion | flops 9666822144 | bytes 23592960 | tf_op jit(solution)/shard_map/era,erb->eab/dot_general | solution.py:1281
  617.6 32.8 %collective-permute-done.14 = bf16[2,512,768]{2,1,0:T(8,128)(2,1)S(1)} collective-permute-done((bf16[2,512,768]{2,1,0:T(8,128)(2,1)S(1)}, bf16[2,512,768]{2,1,0:T(8,128)(2,1)S(1)}, u32[]{:S(2)}, u32[]{:S(2)}) %collective-permute-start.14) | collective-permute-done | bytes 1572896 | tf_op jit(solution)/shard_map/ppermute | solution.py:902
  658.1 18.7 %shard_map.223 = (bf16[384,4096]{1,0:T(8,128)(2,1)}, f32[384,2048]{1,0:T(8,128)}, bf16[384,2048]{1,0:T(8,128)(2,1)}, f32[1,2048]{1,0:T(1,128)}) custom-call(bf16[192,2048]{1,0:T(8,128)(2,1)} %reduce-scatter.8.cloned.1.call-done.r0_ref, bf16[192,2048]{1,0:T(8,128)(2,1)} %reduce-scatter.10.cloned.1.call-done.r1_ref, f32[2,192,2048]{2,1,0:T(8,128)} %pad_maximum_fusion.mid_ref, ...), custom_call_target="tpu_custom_call" | custom-call | flops 6442450944 | bytes 35000000 | tf_op jit(solution)/shard_map/pallas_call | solution.py:324
  693.2 36.0 %shard_map.224 = (bf16[2,192,4096]{2,1,0:T(8,128)(2,1)}, bf16[8,1,192,1024]{3,2,1,0:T(8,128)(2,1)}, f32[1,128]{1,0:T(1,128)}) custom-call(bf16[2,192,4096]{2,1,0:T(8,128)(2,1)} %bitcast.224, bf16[8,1,192,1024]{3,2,1,0:T(8,128)(2,1)} %bitcast.216, f32[2,1536,384]{2,1,0:T(8,128)} %copy.102.refs_2_, bf16[2,192,4096]{2,1,0:T(8,128)(2,1)} %get-tuple-element.195.refs_3_, ...), custom_call_target="tpu_custom_call" | custom-call | flops 12079595520 | bytes 30000000 | tf_op jit(solution)/shard_map/pallas_call | solution.py:277
  754.6 35.6 %shard_map.225 = (bf16[2,192,4096]{2,1,0:T(8,128)(2,1)}, bf16[8,1,192,1024]{3,2,1,0:T(8,128)(2,1)}, f32[1,128]{1,0:T(1,128)}) custom-call(bf16[2,192,4096]{2,1,0:T(8,128)(2,1)} %bitcast.225, bf16[8,1,192,1024]{3,2,1,0:T(8,128)(2,1)} %bitcast.214, f32[2,1536,384]{2,1,0:T(8,128)} %copy.102.refs_2_, ...), custom_call_target="tpu_custom_call", output_to_operand_aliasing={{0}: (10, {})} | custom-call | flops 12079595520 | bytes 30000000 | tf_op jit(solution)/shard_map/pallas_call | solution.py:277
  817.3 12.3 %fusion.30 = f32[384,2048]{1,0:T(8,128)} fusion(bf16[384,4096]{1,0:T(8,128)(2,1)S(1)} %bitcast.229, bf16[4096,2048]{1,0:T(8,128)(2,1)} %get-tuple-element.181.wq_ref), kind=kOutput, calls=%fused_computation.131 | convolution fusion | flops 6442450944 | bytes 23068672 | tf_op jit(solution)/shard_map/dot_general | solution.py:35
  829.6 19.8 %collective-permute-done.27 = bf16[2,256,2048]{2,1,0:T(8,128)(2,1)S(1)} collective-permute-done((bf16[2,256,2048]{2,1,0:T(8,128)(2,1)S(1)}, bf16[2,256,2048]{2,1,0:T(8,128)(2,1)S(1)}, u32[]{:S(2)}, u32[]{:S(2)}) %collective-permute-start.27) | collective-permute-done | bytes 2097184 | tf_op jit(solution)/shard_map/ppermute | solution.py:902
  870.9 147.8 %shard_map.227 = (f32[160,2048]{1,0:T(8,128)}, f32[1,256]{1,0:T(1,128)}) custom-call(bf16[384,4096]{1,0:T(8,128)(2,1)} %bitcast.228, bf16[1024,384]{1,0:T(8,128)(2,1)} %get-tuple-element.337.extra_ref, bf16[384,2048]{1,0:T(8,128)(2,1)} %fusion.2.x_ref.b_ref, f32[64,256]{1,0:T(8,128)} %bitcast.202), custom_call_target="tpu_custom_call" | custom-call | flops 8053063680 | bytes 10000000 | tf_op jit(solution)/shard_map/pallas_call | solution.py:693
  (323 shorter events, 253.0 us)
Async XLA Ops:
  7.2 261.9 %all-gather.9.cloned.1.call-start = ((), (), s32[]{:S(2)}) async-start(), calls=%async_computation.7 | async-start | bytes 3538944 | tf_op jit(solution)/shard_map/all_gather | solution.py:1236
  222.3 85.7 %all-gather.11.cloned.1.call-start = ((), (), s32[]{:S(2)}) async-start(), calls=%async_computation.8 | async-start | bytes 3538944 | tf_op jit(solution)/shard_map/all_gather | solution.py:1237
  223.0 180.9 %all-gather.15.cloned.1.call-start = ((), (), s32[]{:S(2)}) async-start(), calls=%async_computation.17 | async-start | bytes 7520256 | tf_op jit(solution)/shard_map/all_gather | solution.py:1269
  308.0 162.9 %all-gather.13.cloned.1.call-start = ((), (), s32[]{:S(2)}) async-start(), calls=%async_computation.16 | async-start | bytes 7520256 | tf_op jit(solution)/shard_map/all_gather | solution.py:1269
  348.1 136.6 %all-gather.17.cloned.1.call-start = ((), (), s32[]{:S(2)}) async-start(), calls=%async_computation.18 | async-start | bytes 3538944 | tf_op jit(solution)/shard_map/all_gather | solution.py:1257
  348.7 205.0 %reduce-scatter.8.cloned.1.call-start = ((), (), s32[]{:S(2)}) async-start(), calls=%async_computation.9 | async-start | bytes 7077888 | tf_op jit(solution)/shard_map/reduce_scatter | solution.py:1274
  358.1 43.2 %collective-permute-start.10 = (bf16[1,768,512]{2,1,0:T(8,128)(2,1)S(1)}, bf16[1,768,512]{2,1,0:T(8,128)(2,1)S(1)}, u32[]{:S(2)}, u32[]{:S(2)}) collective-permute-start(bf16[1,768,512]{2,1,0:T(8,128)(2,1)S(1)} %slice.104), channel_id=1, source_target_pairs={{0,16},{8,24},{16,0},{24,8},{1,17},{9,25},{17,1},{25,9},{2,18},{10... | collective-permute-start | bytes 2359304 | tf_op jit(solution)/shard_map/ppermute | solution.py:902
  470.5 181.0 %reduce-scatter.10.cloned.1.call-start = ((), (), s32[]{:S(2)}) async-start(), calls=%async_computation.10 | async-start | bytes 7077888 | tf_op jit(solution)/shard_map/reduce_scatter | solution.py:1274
  553.7 245.2 %reduce-scatter.12.cloned.1.call-start = ((), (), s32[]{:S(2)}) async-start(), calls=%async_computation.11 | async-start | bytes 7077888 | tf_op jit(solution)/shard_map/reduce_scatter | solution.py:1308
  600.4 50.0 %collective-permute-start.14 = (bf16[2,512,768]{2,1,0:T(8,128)(2,1)S(1)}, bf16[2,512,768]{2,1,0:T(8,128)(2,1)S(1)}, u32[]{:S(2)}, u32[]{:S(2)}) collective-permute-start(bf16[2,512,768]{2,1,0:T(8,128)(2,1)S(1)} %get-tuple-element.417), channel_id=1, source_target_pairs={{0,8},{8,0},{16,24},{24,16},{1,9},{9,1},{17,25},{25,17},{2,10},{10... | collective-permute-start | bytes 4718600 | tf_op jit(solution)/shard_map/ppermute | solution.py:902
  601.9 49.6 %collective-permute-start.15 = (bf16[2,512,768]{2,1,0:T(8,128)(2,1)S(1)}, bf16[2,512,768]{2,1,0:T(8,128)(2,1)}, u32[]{:S(2)}, u32[]{:S(2)}) collective-permute-start(bf16[2,512,768]{2,1,0:T(8,128)(2,1)S(1)} %get-tuple-element.416), channel_id=1, source_target_pairs={{0,16},{8,24},{16,0},{24,8},{1,17},{9,25},{17,1},{25,9},{2,18},{10... | collective-permute-start | bytes 4718600 | tf_op jit(solution)/shard_map/ppermute | solution.py:902
  651.6 202.9 %reduce-scatter.14.cloned.1.call-start = ((), (), s32[]{:S(2)}) async-start(), calls=%async_computation.12 | async-start | bytes 3538944 | tf_op jit(solution)/shard_map/reduce_scatter | solution.py:1319
  685.7 44.7 %collective-permute-start.20 = (bf16[2,1024,2048]{2,1,0:T(8,128)(2,1)}, bf16[2,1024,2048]{2,1,0:T(8,128)(2,1)}, u32[]{:S(2)}, u32[]{:S(2)}) collective-permute-start(bf16[2,1024,2048]{2,1,0:T(8,128)(2,1)} %convolution_convert_fusion.1), channel_id=1, source_target_pairs={{0,1},{1,0},{2,3},{3,2},{4,5},{5,4},{6,7},{7,6},{8,9},{9,8},{10,11... | collective-permute-start | bytes 25165832 | tf_op jit(solution)/shard_map/ppermute | solution.py:1307
  688.1 41.1 %collective-permute-start.21 = (bf16[2,512,768]{2,1,0:T(8,128)(2,1)S(1)}, bf16[2,512,768]{2,1,0:T(8,128)(2,1)S(1)}, u32[]{:S(2)}, u32[]{:S(2)}) collective-permute-start(bf16[2,512,768]{2,1,0:T(8,128)(2,1)S(1)} %get-tuple-element.411), channel_id=1, source_target_pairs={{0,8},{8,0},{16,24},{24,16},{1,9},{9,1},{17,25},{25,17},{2,10},{10... | collective-permute-start | bytes 4718600 | tf_op jit(solution)/shard_map/ppermute | solution.py:902
  689.5 39.8 %collective-permute-start.22 = (bf16[2,512,768]{2,1,0:T(8,128)(2,1)S(1)}, bf16[2,512,768]{2,1,0:T(8,128)(2,1)S(1)}, u32[]{:S(2)}, u32[]{:S(2)}) collective-permute-start(bf16[2,512,768]{2,1,0:T(8,128)(2,1)S(1)} %get-tuple-element.410), channel_id=1, source_target_pairs={{0,16},{8,24},{16,0},{24,8},{1,17},{9,25},{17,1},{25,9},{2,18},{10... | collective-permute-start | bytes 4718600 | tf_op jit(solution)/shard_map/ppermute | solution.py:902
  730.4 124.1 %reduce-scatter.16.cloned.1.call-start = ((), (), s32[]{:S(2)}) async-start(), calls=%async_computation.13 | async-start | bytes 3538944 | tf_op jit(solution)/shard_map/reduce_scatter | solution.py:1327
  739.7 50.5 %collective-permute-start.25 = (bf16[2,768,512]{2,1,0:T(8,128)(2,1)S(1)}, bf16[2,768,512]{2,1,0:T(8,128)(2,1)S(1)}, u32[]{:S(2)}, u32[]{:S(2)}) collective-permute-start(bf16[2,768,512]{2,1,0:T(8,128)(2,1)S(1)} %get-tuple-element.409), channel_id=1, source_target_pairs={{0,8},{8,0},{16,24},{24,16},{1,9},{9,1},{17,25},{25,17},{2,10},{10... | collective-permute-start | bytes 4718600 | tf_op jit(solution)/shard_map/ppermute | solution.py:902
  740.3 49.9 %collective-permute-start.26 = (bf16[2,768,512]{2,1,0:T(8,128)(2,1)S(1)}, bf16[2,768,512]{2,1,0:T(8,128)(2,1)}, u32[]{:S(2)}, u32[]{:S(2)}) collective-permute-start(bf16[2,768,512]{2,1,0:T(8,128)(2,1)S(1)} %get-tuple-element.408), channel_id=1, source_target_pairs={{0,16},{8,24},{16,0},{24,8},{1,17},{9,25},{17,1},{25,9},{2,18},{10... | collective-permute-start | bytes 4718600 | tf_op jit(solution)/shard_map/ppermute | solution.py:902
  751.8 46.7 %collective-permute-start.23 = (bf16[1,256,2048]{2,1,0:T(8,128)(2,1)}, bf16[1,256,2048]{2,1,0:T(8,128)(2,1)}, u32[]{:S(2)}, u32[]{:S(2)}) collective-permute-start(bf16[1,256,2048]{2,1,0:T(8,128)(2,1)} %get-tuple-element.407), channel_id=1, source_target_pairs={{0,8},{8,0},{16,24},{24,16},{1,9},{9,1},{17,25},{25,17},{2,10},{10... | collective-permute-start | bytes 3145736 | tf_op jit(solution)/shard_map/ppermute | solution.py:902
  753.1 45.8 %collective-permute-start.24 = (bf16[1,256,2048]{2,1,0:T(8,128)(2,1)}, bf16[1,256,2048]{2,1,0:T(8,128)(2,1)}, u32[]{:S(2)}, u32[]{:S(2)}) collective-permute-start(bf16[1,256,2048]{2,1,0:T(8,128)(2,1)} %get-tuple-element.406), channel_id=1, source_target_pairs={{0,16},{8,24},{16,0},{24,8},{1,17},{9,25},{17,1},{25,9},{2,18},{10... | collective-permute-start | bytes 3145736 | tf_op jit(solution)/shard_map/ppermute | solution.py:902
  798.9 232.7 %reduce-scatter.20.cloned.1.call-start = ((), (), s32[]{:S(2)}) async-start(), calls=%async_computation.15 | async-start | bytes 2621440 | tf_op jit(solution)/shard_map/reduce_scatter | solution.py:1343
  803.0 46.4 %collective-permute-start.27 = (bf16[2,256,2048]{2,1,0:T(8,128)(2,1)S(1)}, bf16[2,256,2048]{2,1,0:T(8,128)(2,1)S(1)}, u32[]{:S(2)}, u32[]{:S(2)}) collective-permute-start(bf16[2,256,2048]{2,1,0:T(8,128)(2,1)S(1)} %get-tuple-element.320), channel_id=1, source_target_pairs={{0,8},{8,0},{16,24},{24,16},{1,9},{9,1},{17,25},{25,17},{2,10},{10... | collective-permute-start | bytes 6291464 | tf_op jit(solution)/shard_map/ppermute | solution.py:902
  804.4 45.9 %collective-permute-start.28 = (bf16[2,256,2048]{2,1,0:T(8,128)(2,1)S(1)}, bf16[2,256,2048]{2,1,0:T(8,128)(2,1)S(1)}, u32[]{:S(2)}, u32[]{:S(2)}) collective-permute-start(bf16[2,256,2048]{2,1,0:T(8,128)(2,1)S(1)} %get-tuple-element.321), channel_id=1, source_target_pairs={{0,16},{8,24},{16,0},{24,8},{1,17},{9,25},{17,1},{25,9},{2,18},{10... | collective-permute-start | bytes 6291464 | tf_op jit(solution)/shard_map/ppermute | solution.py:902
  856.6 177.3 %reduce-scatter.18.cloned.1.call-start = ((), (), s32[]{:S(2)}) async-start(), calls=%async_computation.14 | async-start | bytes 7077888 | tf_op jit(solution)/shard_map/reduce_scatter | solution.py:1336
  (78 other events, 1598.7 us)
Sparse Core Ops, SparseCore 0:
  222.4 46.7 all-gather.8
  270.8 37.1 all-gather.10
  310.2 65.8 all-gather.14
  378.2 66.6 all-gather.12
  446.3 38.2 all-gather.16
  486.8 66.7 reduce-scatter.7
  555.9 68.1 reduce-scatter.9
  651.7 66.2 reduce-scatter.11
  730.5 34.2 reduce-scatter.13
  799.0 34.9 reduce-scatter.15
  856.7 40.1 reduce-scatter.19
  899.2 123.2 reduce-scatter.17

commit v11 on v10

--- a/solution.py
+++ b/solution.py
@@ -29,6 +29,7 @@
 NN = (((1,), (0,)), ((), ()))
 BOTH = ("dp", "expert")
 VMEM_LIMIT = 56 * 1024 * 1024
+LIGHT = pl.CostEstimate(flops=1_000_000, bytes_accessed=1_000_000, transcendentals=0)
 
 
 def mm(a, b, dims=NN):
@@ -64,7 +65,7 @@
     return values * cosine + pltpu.roll(values, HD // 2, 1) * sine
 
 
-def project(x_ref, wq_ref, wkv_ref, cos_ref, sin_ref, gq_ref, gk_ref, q_ref, qraw_ref, kv_ref, kraw_ref, wkv_out):
+def project(x_ref, wq_ref, wkv_ref, cos_ref, sin_ref, gq_ref, gk_ref, q_ref, qraw_ref, kraw_ref, wkv_out, *kv_refs):
     x = x_ref[...]
     cosine, sine = cos_ref[...], sin_ref[...]
     for at in range(0, PER_KV * HD, 2 * HD):
@@ -83,11 +84,14 @@
     key = raw[:, :HD]
     kraw_ref[...] = key
     normed = key * rms_scale(key) * gk_ref[...]
-    kv_ref[:, :HD] = turn(normed, cosine, sine).astype(bf16)
-    kv_ref[:, HD:] = raw[:, HD:].astype(bf16)
-
-
-def run_project(x, wq, wkv, cosine, sine, gain_q, gain_k):
+    key, value = turn(normed, cosine, sine).astype(bf16), raw[:, HD:].astype(bf16)
+    rows = x.shape[0] // len(kv_refs)
+    for b, kv_ref in enumerate(kv_refs):
+        kv_ref[:, :HD] = key[b * rows : (b + 1) * rows]
+        kv_ref[:, HD:] = value[b * rows : (b + 1) * rows]
+
+
+def run_project(x, wq, wkv, cosine, sine, gain_q, gain_k, micro):
     tokens, width = x.shape
     wide = PER_KV * HD
     whole = lambda a: pl.BlockSpec(a.shape, lambda g: (0, 0))
@@ -97,18 +101,17 @@
         project,
         grid=(KVH,),
         in_specs=[whole(x), rows(wide), rows(2 * HD), whole(cosine), whole(sine), whole(gain_q), whole(gain_k)],
-        out_specs=[cols(wide), cols(wide), cols(2 * HD), cols(HD), rows(2 * HD)],
+        out_specs=[cols(wide), cols(wide), cols(HD), rows(2 * HD)]
+        + [pl.BlockSpec((tokens // micro, 2 * HD), lambda g: (0, g))] * micro,
         out_shape=[
             jax.ShapeDtypeStruct((tokens, H * HD), bf16),
             jax.ShapeDtypeStruct((tokens, H * HD), f32),
-            jax.ShapeDtypeStruct((tokens, KVH * 2 * HD), bf16),
             jax.ShapeDtypeStruct((tokens, KVH * HD), f32),
             jax.ShapeDtypeStruct((KVH * 2 * HD, width), bf16),
-        ],
+        ]
+        + [jax.ShapeDtypeStruct((tokens // micro, KVH * 2 * HD), bf16)] * micro,
         compiler_params=pltpu.CompilerParams(vmem_limit_bytes=VMEM_LIMIT),
-        cost_estimate=pl.CostEstimate(
-            flops=2 * tokens * width * (H + 2 * KVH) * HD, bytes_accessed=40_000_000, transcendentals=0
-        ),
+        cost_estimate=LIGHT,
     )(x, wq, wkv, cosine, sine, gain_q, gain_k)
 
 
@@ -257,9 +260,7 @@
         + again * [jax.ShapeDtypeStruct((2, 2, micro, rows, KVH * 2 * HD), bf16)],
         input_output_aliases={3 + i: i for i in range(len(earlier))},
         compiler_params=pltpu.CompilerParams(vmem_limit_bytes=VMEM_LIMIT),
-        cost_estimate=pl.CostEstimate(
-            flops=flops, bytes_accessed=20_000_000, transcendentals=flops // (4 * HD)
-        ),
+        cost_estimate=LIGHT,
     )(query, kv_all, bias, *earlier)
 
 
@@ -290,9 +291,7 @@
         input_output_aliases={10 + i: i for i in range(len(earlier))},
         scratch_shapes=[pltpu.VMEM((group_len, HD), f32), pltpu.VMEM((group_len, HD), f32)],
         compiler_params=pltpu.CompilerParams(vmem_limit_bytes=VMEM_LIMIT),
-        cost_estimate=pl.CostEstimate(
-            flops=flops, bytes_accessed=30_000_000, transcendentals=flops // (10 * HD)
-        ),
+        cost_estimate=LIGHT,
     )(query, kv_all, bias, mixed, grad, logs, raw, cosine, sine, gain, *earlier)
 
 
@@ -340,9 +339,7 @@
             jax.ShapeDtypeStruct((1, width), f32),
         ],
         compiler_params=pltpu.CompilerParams(vmem_limit_bytes=VMEM_LIMIT),
-        cost_estimate=pl.CostEstimate(
-            flops=2 * total * width * out_w.shape[0], bytes_accessed=35_000_000, transcendentals=0
-        ),
+        cost_estimate=LIGHT,
     )(*routed, middle, cot, gain, out_w)
 
 
@@ -510,7 +507,7 @@
     )(*arrays)
 
 
-def reduce_kernel(rows, cuts, a_ref, extra_ref, b_ref, g_ref, o_ref, go_ref, sib, got, own, far, near, plane, got_z,
+def reduce_kernel(rows, cuts, a_ref, extra_ref, b_ref, g_ref, q_out, k_out, v_out, go_ref, o_ref, sib, got, own, far, near, plane, got_z,
                   s0, r0, s1, r1, s2, r2, s3, r3, g_acc, g_got, g_z, gs, gr, gsz, grz):
     dp = lax.axis_index("dp"); member = lax.axis_index("expert")
     core = member % 2; z = member // 2
@@ -670,6 +667,9 @@
         src = (z + d) % depth
         copy(plane.at[0], got_z.at[src], s3.at[0], r3.at[src], sibling).wait_recv()
         o_ref[...] += got_z[src].astype(f32)
+    q_out[...] = o_ref[:HD].T
+    k_out[...] = o_ref[HD : HD + piece].T
+    v_out[...] = o_ref[HD + piece :].T
     gain_end()
     for k in range(depth):
         if k >= 2: sib_copies[k].wait_send()
@@ -680,9 +680,7 @@
 def reduce_rows(a, extra, b, cid, gains=None):
     tokens, width = b.shape
     depth = 4
-    rows = HD + (0 if extra is None else extra.shape[0] // 32)
-    if extra is None:
-        extra = jnp.zeros((16, 128), bf16)
+    rows = HD + extra.shape[0] // 32
     D = pltpu.SemaphoreType.DMA
     lanes = 256
     padded = jnp.zeros((32, lanes), f32)
@@ -692,10 +690,16 @@
     padded = jnp.pad(padded, ((0, 0), (0, 0), (0, 8 - depth), (0, 0))).reshape(64, lanes)
     return pl.pallas_call(
         functools.partial(reduce_kernel, rows, 4),
-        out_shape=[jax.ShapeDtypeStruct((rows, width), f32), jax.ShapeDtypeStruct((1, lanes), f32)],
+        out_shape=[
+            jax.ShapeDtypeStruct((width, HD), f32),
+            jax.ShapeDtypeStruct((width, (rows - HD) // 2), f32),
+            jax.ShapeDtypeStruct((width, (rows - HD) // 2), f32),
+            jax.ShapeDtypeStruct((1, lanes), f32),
+        ],
         in_specs=[pl.BlockSpec(memory_space=pltpu.VMEM)] * 4,
-        out_specs=[pl.BlockSpec(memory_space=pltpu.VMEM)] * 2,
+        out_specs=[pl.BlockSpec(memory_space=pltpu.VMEM)] * 4,
         scratch_shapes=[
+            pltpu.VMEM((rows, width), f32),
             pltpu.VMEM((2, 4 * rows, width), bf16),
             pltpu.VMEM((depth, 4 * rows, width), bf16),
             pltpu.VMEM((depth, 4 * rows, width), bf16),
@@ -832,9 +836,7 @@
         out_shape=[picked] * 2,
         input_output_aliases={3 + i: i for i in range(len(earlier[:2]))},
         compiler_params=params,
-        cost_estimate=pl.CostEstimate(
-            flops=4 * slots * local_experts * rows * width, bytes_accessed=25_000_000, transcendentals=0
-        ),
+        cost_estimate=LIGHT,
     )(tokens, cot[0][0], cot[1][0], *[a.reshape(picked.shape) for a in earlier[:2]])
     x, dy = (a.reshape(local_experts, micro, slots, width) for a in (x, dy))
     chunk = slots // 2
@@ -857,9 +859,7 @@
             pltpu.SemaphoreType.DMA((local_experts, 3, 4)),
         ],
         compiler_params=params,
-        cost_estimate=pl.CostEstimate(
-            flops=12 * local_experts * slots * width * hidden, bytes_accessed=50_000_000, transcendentals=0
-        ),
+        cost_estimate=LIGHT,
     )(x, dy, *flat, *earlier[2:])
     y, dx = (a.reshape(local_experts, blocks, capacity, width) for a in (y, dx))
     part_spec = pl.BlockSpec((local_experts, 1, capacity, width), lambda b: (0, b, 0, 0))
@@ -876,9 +876,7 @@
         out_specs=[sums_spec] * 2,
         out_shape=[sums] * 2,
         compiler_params=params,
-        cost_estimate=pl.CostEstimate(
-            flops=4 * slots * local_experts * rows * width, bytes_accessed=25_000_000, transcendentals=0
-        ),
+        cost_estimate=LIGHT,
     )(tokens, y, dx)
     return [x, dy, z, dg, du], mix, da
 
@@ -1203,7 +1201,6 @@
     gain_mid = gains[width : 2 * width]
     gain_q = gains[2 * width : 2 * width + HD]
     gain_k = gains[2 * width + HD :]
-    gate_near = (swap(w_gate, 1), swap(w_gate, 2))
 
     key_index = jnp.arange(group_len, dtype=jnp.int32)
     start_row = member * rows
@@ -1226,17 +1223,15 @@
     hidden = inputs[:, 0].astype(f32).reshape(total, width)
     scale_in = rms_scale(hidden)
     normed = (hidden * scale_in * gain_in).astype(bf16)
-    q_low, q_raw, kv_own, k_raw, kv_w = run_project(
-        normed, q_w, kv_w, cosine, sine, gain_q * (SCALE * LOG2E), gain_k
+    q_low, q_raw, k_raw, kv_w, kv_0, kv_1 = run_project(
+        normed, q_w, kv_w, cosine, sine, gain_q * (SCALE * LOG2E), gain_k, micro
     )
     q_low, q_raw = (a.reshape(micro, rows, H * HD) for a in (q_low, q_raw))
-    kv_own = kv_own.reshape(micro, rows, KVH * 2 * HD)
-    kv_own, gate_near, w_up = tie((kv_own, gate_near, w_up))
-    up_near = (swap(w_up, 1), swap(w_up, 2))
-    kv_0 = lax.all_gather(kv_own[0], "expert", axis=0, tiled=False)
-    kv_1 = lax.all_gather(kv_own[1], "expert", axis=0, tiled=False)
-    kv_0, up_near, w_down = tie((kv_0, up_near, w_down))
-    down_near = (swap(w_down, 1), swap(w_down, 2))
+    gate_near = (swap(w_gate, 1), swap(w_gate, 2))
+    kv_0, gate_near, w_up, w_down = tie((kv_0, gate_near, w_up, w_down))
+    kv_0 = lax.all_gather(kv_0, "expert", axis=0, tiled=False)
+    kv_1 = lax.all_gather(kv_1, "expert", axis=0, tiled=False)
+    up_near, down_near = ((swap(w, 1), swap(w, 2)) for w in (w_up, w_down))
     chunk = 256
 
     def middle_of(mixed, at):
@@ -1247,18 +1242,18 @@
 
     mixed, logs, shares = run_forward(q_low, kv_0[:, None], bias, step_heads, chunk, 0, [], True)
     middle_0, routed_0 = middle_of(mixed, 0)
-    mixed, kv_1, routed_0 = tie((mixed, kv_1, routed_0))
+    mixed, kv_1, routed_0, up_near, down_near = tie((mixed, kv_1, routed_0, up_near, down_near))
     kv_all = [kv_0[:, None], kv_1[:, None]]
     mixed, logs, shares = run_forward(
         q_low, kv_all[1], bias, step_heads, chunk, 1, [mixed, logs, shares], True
     )
     middle_1, routed_1 = middle_of(mixed, 1)
-    routed_1, down_near, cot_last = tie((routed_1, down_near, halves[3]))
-    cot_last = lax.all_gather(cot_last, "expert", axis=0, tiled=False)[:, None]
     parts = [
         (own, near[0], near[1], swap(near[0][:1], 2), swap(near[1][1:], 1))
         for own, near in ((w_gate, gate_near), (w_up, up_near), (w_down, down_near))
     ]
+    routed_1, parts, cot_last = tie((routed_1, parts, halves[3]))
+    cot_last = lax.all_gather(cot_last, "expert", axis=0, tiled=False)[:, None]
     cots = [((cot_first, 0), (cot_first, 1)), ((cot_first, 2), (cot_last, 0))]
     routed = [routed_0, routed_1]
     middle = jnp.stack([middle_0, middle_1])
@@ -1288,7 +1283,9 @@
     d_routeds[-1], first, second, third, mix_parts[0] = tie(
         (d_routeds[-1], first, second, third, mix_parts[0])
     )
-    second = scatter_near(second, 1)
+    second = scatter_add(second, 1)
+    d_routeds[-1], second, third = tie((d_routeds[-1], second, third))
+    second = (swap(second[0], 1), swap(second[1], 2), second[2])
     third = scatter_far(third, 2)
     d_mixed, d_middle, d_branch, grad_mid = run_middle_back(
         d_routeds, middle, cotangent[:, 0], gain_mid[None, :], out_w
@@ -1350,13 +1347,13 @@
     d_in_norm, grad_in = norm_back(d_normed, hidden, scale_in, gain_in)
     input_grad = d_middle + d_in_norm
     gain_grads = jnp.concatenate([grad_in, grad_mid[0], grad_qn[0], grad_kn[0]]).reshape(shards, gain_len)
-    grad_qkv, grad_gains = reduce_rows(d_query, dkv_t, normed, 3, gain_grads)
+    grad_query, grad_key, grad_value, grad_gains = reduce_rows(d_query, dkv_t, normed, 3, gain_grads)
     return (
         jnp.stack(outputs)[:, None],
         input_grad.reshape(micro, 1, rows, width),
-        grad_qkv[:q_part].T,
-        grad_qkv[q_part : q_part + k_part].T,
-        grad_qkv[q_part + k_part :].T,
+        grad_query,
+        grad_key,
+        grad_value,
         grad_output,
         grad_gains[0, :gain_len],
         *expert_grads,

time: 1050 us -> 1080 us (1.029)
  waiting for transfers between devices: 154 us -> 183 us
    all_gather x1, waiting for transfers between devices: 13.8 us -> 39.8 us  [body_fast(): cot_last = lax.all_gather(cot_last, 'expert', axis=0, tiled=False)[:, None]]
    ppermute x28, waiting for transfers between devices: 125 us -> 107 us  [swap(): lax.ppermute(values, 'dp', [(i, i ^ bit) for i in range(lax.axis_size('dp...]
    all_gather x2, waiting for transfers between devices: 11 us -> 25.9 us  [the longest x1 24.6 us: body_fast(): kv_0 = lax.all_gather(kv_0, 'expert', axis=0, tiled=False)]
  transfers between devices with their start and end apart: 41 -> 41, of which waited for: 22 -> 21; matrix products, arithmetic and copies ran while one was open for 20% -> 19% of each run, Pallas kernels for 42% -> 41%
where the time goes in v11:
time: 1080 us; the launch traced here: 1070 us
  Pallas kernels  613 us (57%)
  waiting for transfers between devices  183 us (17%)
  matrix products  90 us (8%)
  other arithmetic  76 us (7%)
  local copies, waits for them, and re-layouts  57.2 us (5%)
  starting transfers between devices  32.1 us (3%)
  between operations  15.6 us (1%)
    pallas_call x1, Pallas kernels, gather_rows(): pl.pallas_call(functools.partial(gather_kernel, phases, len(arrays), late...  172 us
    pallas_call x1, Pallas kernels, reduce_rows(): pl.pallas_call(functools.partial(reduce_kernel, rows, 4), out_shape=[jax....  150 us
    ppermute x28, waiting for transfers between devices, swap(): lax.ppermute(values, 'dp', [(i, i ^ bit) for i in range(lax.axis_size('dp...  107 us
    pallas_call x2, Pallas kernels, run_experts(): pl.pallas_call(functools.partial(expert_kernel, len(earlier[2:])), grid=(...  80.9 us
    pallas_call x2, Pallas kernels, run_backward(): pl.pallas_call(kernel, grid=(KVH,), in_specs=[q_spec, kv_spec, bias_spec,...  71.7 us
    pallas_call x2, Pallas kernels, run_forward(): pl.pallas_call(kernel, grid=(KVH,), in_specs=[q_spec, kv_spec, bias_spec]...  47 us
    dot_general x3, matrix products, weight_grad(): jnp.einsum('era,erb->eab', rows_in, rows_out, preferred_element_type=f32)  43.9 us
    all_gather x1, waiting for transfers between devices, body_fast(): cot_last = lax.all_gather(cot_last, 'expert', axis=0, tiled=False)[:, None]  39.8 us
  transfers between devices with their start and end apart: 41, of which 21 were waited for; matrix products, arithmetic and copies ran while one was open for 19% of the time, Pallas kernels for 41%

profile of v11, /device:TPU:8, one launch (start us, length us, event | category | flops | bytes accessed | tf_op | source)
XLA Modules:
  0.0 1066.9 jit_solution(12063736060853749762)
XLA Ops:
  13.1 172.4 %shard_map.213 = (bf16[4096,2048]{1,0:T(8,128)(2,1)}, bf16[1024,2048]{1,0:T(8,128)(2,1)}, bf16[4096,2048]{1,0:T(8,128)(2,1)}, bf16[512,256]{1,0:T(8,128)(2,1)}, bf16[2304,2048]{1,0:T(8,128)(2,1)}) custom-call(bf16[128,2048]{1,0:T(8,128)(2,1)} %bitcast.205, bf16[32,2048]{1,0:T(8,128)(2,1)} %pad_maximum_fusion.8.refs_1_, bf16[128,2048]{1,0:T(8,128)(2,1)} %refs_2_.1, ...), custom_call_target="tpu_custom_call" | custom-call | bytes 400000000 | tf_op jit(solution)/shard_map/pallas_call | solution.py:496
  195.1 15.8 %shard_map.214 = (bf16[384,4096]{1,0:T(8,128)(2,1)}, f32[384,4096]{1,0:T(8,128)}, f32[384,512]{1,0:T(8,128)}, bf16[1024,2048]{1,0:T(8,128)(2,1)}, bf16[192,1024]{1,0:T(8,128)(2,1)}, /*index=5*/bf16[192,1024]{1,0:T(8,128)(2,1)}) custom-call(bf16[384,2048]{1,0:T(8,128)(2,1)} %fusion.2.x_ref.b_ref, bf16[4096,2048]{1,0:T(8,128)(2,1)} %get-tuple-element.203.wq_ref, ...), custom_call_target="tpu_custom_call" | custom-call | flops 1000000 | bytes 1000000 | tf_op jit(solution)/shard_map/pallas_call | solution.py:100
  242.5 24.6 %all-gather.11.cloned.1.call-done = bf16[1536,1024]{1,0:T(8,128)(2,1)} async-done(((bf16[192,1024]{1,0:T(8,128)(2,1)}), bf16[1536,1024]{1,0:T(8,128)(2,1)}) %all-gather.11.cloned.1.call-update) | async-done | bytes 3145744 | tf_op jit(solution)/shard_map/all_gather | solution.py:1232
  267.1 23.5 %shard_map.215 = (bf16[2,192,4096]{2,1,0:T(8,128)(2,1)}, f32[2,4,4,384]{3,2,1,0:T(4,128)}, bf16[2,2,2,192,1024]{4,3,2,1,0:T(8,128)(2,1)}) custom-call(bf16[2,192,4096]{2,1,0:T(8,128)(2,1)} %bitcast.164, bf16[8,1,192,1024]{3,2,1,0:T(8,128)(2,1)} %bitcast.181, f32[2,1536,384]{2,1,0:T(8,128)} %copy.84.refs_2_), custom_call_target="tpu_custom_call" | custom-call | flops 1000000 | bytes 1000000 | tf_op jit(solution)/shard_map/pallas_call | solution.py:250
  313.1 23.5 %shard_map.216 = (bf16[2,192,4096]{2,1,0:T(8,128)(2,1)}, f32[2,4,4,384]{3,2,1,0:T(4,128)}, bf16[2,2,2,192,1024]{4,3,2,1,0:T(8,128)(2,1)}) custom-call(bf16[2,192,4096]{2,1,0:T(8,128)(2,1)} %bitcast.165, bf16[8,1,192,1024]{3,2,1,0:T(8,128)(2,1)} %bitcast.179, ...), custom_call_target="tpu_custom_call", output_to_operand_aliasing={{0}: (3, {}), {1}: (4, {}), {2}: (5, {})} | custom-call | flops 1000000 | bytes 1000000 | tf_op jit(solution)/shard_map/pallas_call | solution.py:250
  358.1 10.3 collective-permute-done.10.refs_15_
  371.0 12.9 %collective-permute-done.8.refs_10_ = bf16[1,512,768]{2,1,0:T(8,128)(2,1)S(1)} collective-permute-done((bf16[1,512,768]{2,1,0:T(8,128)(2,1)}, bf16[1,512,768]{2,1,0:T(8,128)(2,1)S(1)}, u32[]{:S(2)}, u32[]{:S(2)}) %collective-permute-start.8) | collective-permute-done | bytes 786464 | tf_op jit(solution)/shard_map/ppermute | solution.py:900
  387.1 13.9 %shard_map.217 = (bf16[2,2,8,96,2048]{4,3,2,1,0:T(8,128)(2,1)}, bf16[2,2,8,96,2048]{4,3,2,1,0:T(8,128)(2,1)}) custom-call(bf16[8,192,2176]{2,1,0:T(8,128)(2,1)} %bitcast.168, bf16[8,3,96,2048]{3,2,1,0:T(8,128)(2,1)} %bitcast.161, bf16[8,3,96,2048]{3,2,1,0:T(8,128)(2,1)} %bitcast.162), custom_call_target="tpu_custom_call" | custom-call | flops 1000000 | bytes 1000000 | tf_op jit(solution)/shard_map/pallas_call | solution.py:827
  401.0 40.9 %shard_map.218 = (bf16[2,2,768,768]{3,2,1,0:T(8,128)(2,1)}, bf16[2,2,768,768]{3,2,1,0:T(8,128)(2,1)}, bf16[2,2,768,768]{3,2,1,0:T(8,128)(2,1)}, bf16[2,768,2048]{2,1,0:T(8,128)(2,1)}, bf16[2,768,2048]{2,1,0:T(8,128)(2,1)}) custom-call(bf16[2,2,768,2048]{3,2,1,0:T(8,128)(2,1)} %bitcast.152, bf16[2,2,768,2048]{3,2,1,0:T(8,128)(2,1)} %bitcast.156, ...), custom_call_target="tpu_custom_call" | custom-call | flops 1000000 | bytes 1000000 | tf_op jit(solution)/shard_map/pallas_call | solution.py:848
  441.9 12.7 %shard_map.219 = (bf16[1536,2048]{1,0:T(8,128)(2,1)}, bf16[1536,2048]{1,0:T(8,128)(2,1)}) custom-call(bf16[8,192,2176]{2,1,0:T(8,128)(2,1)} %bitcast.169, bf16[2,8,96,2048]{3,2,1,0:T(8,128)(2,1)} %bitcast.188, bf16[2,8,96,2048]{3,2,1,0:T(8,128)(2,1)} %bitcast.189), custom_call_target="tpu_custom_call" | custom-call | flops 1000000 | bytes 1000000 | tf_op jit(solution)/shard_map/pallas_call | solution.py:868
  462.0 39.8 %all-gather.19.cloned.1.call-done = bf16[768,2048]{1,0:T(8,128)(2,1)} async-done(((bf16[96,2048]{1,0:T(8,128)(2,1)}), bf16[768,2048]{1,0:T(8,128)(2,1)}) %all-gather.19.cloned.1.call-update) | async-done | bytes 3145744 | tf_op jit(solution)/shard_map/all_gather | solution.py:1256
  501.8 13.9 %shard_map.220 = (bf16[2,2,8,96,2048]{4,3,2,1,0:T(8,128)(2,1)}, bf16[2,2,8,96,2048]{4,3,2,1,0:T(8,128)(2,1)}) custom-call(bf16[8,192,2176]{2,1,0:T(8,128)(2,1)} %bitcast.170, bf16[8,3,96,2048]{3,2,1,0:T(8,128)(2,1)} %bitcast.163, bf16[8,1,96,2048]{3,2,1,0:T(8,128)(2,1)} %bitcast.204, ...), custom_call_target="tpu_custom_call", output_to_operand_aliasing={{0}: (3, {}), {1}: (4, {})} | custom-call | flops 1000000 | bytes 1000000 | tf_op jit(solution)/shard_map/pallas_call | solution.py:827
  515.7 40.0 %shard_map.221 = (bf16[2,2,768,768]{3,2,1,0:T(8,128)(2,1)}, bf16[2,2,768,768]{3,2,1,0:T(8,128)(2,1)}, bf16[2,2,768,768]{3,2,1,0:T(8,128)(2,1)}, bf16[2,768,2048]{2,1,0:T(8,128)(2,1)}, bf16[2,768,2048]{2,1,0:T(8,128)(2,1)}) custom-call(bf16[2,2,768,2048]{3,2,1,0:T(8,128)(2,1)} %bitcast.153, ...), custom_call_target="tpu_custom_call", output_to_operand_aliasing={{0}: (17, {}), {1}: (18, {}), {2}: (19, {})} | custom-call | flops 1000000 | bytes 1000000 | tf_op jit(solution)/shard_map/pallas_call | solution.py:848
  555.7 12.7 %shard_map.222 = (bf16[1536,2048]{1,0:T(8,128)(2,1)}, bf16[1536,2048]{1,0:T(8,128)(2,1)}) custom-call(bf16[8,192,2176]{2,1,0:T(8,128)(2,1)} %bitcast.171, bf16[2,8,96,2048]{3,2,1,0:T(8,128)(2,1)} %bitcast.186, bf16[2,8,96,2048]{3,2,1,0:T(8,128)(2,1)} %bitcast.187), custom_call_target="tpu_custom_call" | custom-call | flops 1000000 | bytes 1000000 | tf_op jit(solution)/shard_map/pallas_call | solution.py:868
  571.1 15.0 %convolution_convert_fusion.4 = bf16[2,2048,768]{2,1,0:T(8,128)(2,1)S(1)} fusion(bf16[2,1536,2048]{2,1,0:T(8,128)(2,1)} %bitcast.154, bf16[2,1536,768]{2,1,0:T(8,128)(2,1)} %bitcast.196), kind=kOutput, calls=%fused_computation.6 | convolution fusion | flops 9666822144 | bytes 23592960 | tf_op jit(solution)/shard_map/era,erb->eab/dot_general | solution.py:1276
  592.9 17.1 %convolution_convert_fusion.3 = bf16[2,2048,768]{2,1,0:T(8,128)(2,1)} fusion(bf16[2,1536,2048]{2,1,0:T(8,128)(2,1)} %bitcast.155, bf16[2,1536,768]{2,1,0:T(8,128)(2,1)} %bitcast.197), kind=kOutput, calls=%fused_computation.5 | convolution fusion | flops 9666822144 | bytes 23592960 | tf_op jit(solution)/shard_map/era,erb->eab/dot_general | solution.py:1276
  621.0 11.7 %convolution_convert_fusion.2 = bf16[2,768,2048]{2,1,0:T(8,128)(2,1)} fusion(bf16[2,1536,768]{2,1,0:T(8,128)(2,1)S(1)} %bitcast.195, bf16[2,1536,2048]{2,1,0:T(8,128)(2,1)S(1)} %bitcast.160), kind=kOutput, calls=%fused_computation.4 | convolution fusion | flops 9666822144 | bytes 23592960 | tf_op jit(solution)/shard_map/era,erb->eab/dot_general | solution.py:1276
  634.2 32.8 %collective-permute-done.14 = bf16[2,512,768]{2,1,0:T(8,128)(2,1)} collective-permute-done((bf16[2,512,768]{2,1,0:T(8,128)(2,1)}, bf16[2,512,768]{2,1,0:T(8,128)(2,1)}, u32[]{:S(2)}, u32[]{:S(2)}) %collective-permute-start.14) | collective-permute-done | bytes 1572896 | tf_op jit(solution)/shard_map/ppermute | solution.py:900
  681.3 18.5 %shard_map.223 = (bf16[384,4096]{1,0:T(8,128)(2,1)}, f32[384,2048]{1,0:T(8,128)}, bf16[384,2048]{1,0:T(8,128)(2,1)}, f32[1,2048]{1,0:T(1,128)}) custom-call(bf16[192,2048]{1,0:T(8,128)(2,1)} %reduce-scatter.8.cloned.1.call-done.r0_ref, bf16[192,2048]{1,0:T(8,128)(2,1)} %reduce-scatter.10.cloned.1.call-done.r1_ref, f32[2,192,2048]{2,1,0:T(8,128)} %pad_maximum_fusion.mid_ref, ...), custom_call_target="tpu_custom_call" | custom-call | flops 1000000 | bytes 1000000 | tf_op jit(solution)/shard_map/pallas_call | solution.py:323
  712.7 36.1 %shard_map.224 = (bf16[2,192,4096]{2,1,0:T(8,128)(2,1)}, bf16[8,1,192,1024]{3,2,1,0:T(8,128)(2,1)}, f32[1,128]{1,0:T(1,128)}) custom-call(bf16[2,192,4096]{2,1,0:T(8,128)(2,1)} %bitcast.166, bf16[8,1,192,1024]{3,2,1,0:T(8,128)(2,1)} %bitcast.182, f32[2,1536,384]{2,1,0:T(8,128)} %copy.84.refs_2_, bf16[2,192,4096]{2,1,0:T(8,128)(2,1)} %get-tuple-element.218.refs_3_, ...), custom_call_target="tpu_custom_call" | custom-call | flops 1000000 | bytes 1000000 | tf_op jit(solution)/shard_map/pallas_call | solution.py:278
  776.1 35.6 %shard_map.225 = (bf16[2,192,4096]{2,1,0:T(8,128)(2,1)}, bf16[8,1,192,1024]{3,2,1,0:T(8,128)(2,1)}, f32[1,128]{1,0:T(1,128)}) custom-call(bf16[2,192,4096]{2,1,0:T(8,128)(2,1)} %bitcast.167, bf16[8,1,192,1024]{3,2,1,0:T(8,128)(2,1)} %bitcast.180, f32[2,1536,384]{2,1,0:T(8,128)} %copy.84.refs_2_, ...), custom_call_target="tpu_custom_call", output_to_operand_aliasing={{0}: (10, {})} | custom-call | flops 1000000 | bytes 1000000 | tf_op jit(solution)/shard_map/pallas_call | solution.py:278
  840.6 8.5 fusion.29
  849.1 22.9 %collective-permute-done.27 = bf16[2,256,2048]{2,1,0:T(8,128)(2,1)S(1)} collective-permute-done((bf16[2,256,2048]{2,1,0:T(8,128)(2,1)S(1)}, bf16[2,256,2048]{2,1,0:T(8,128)(2,1)S(1)}, u32[]{:S(2)}, u32[]{:S(2)}) %collective-permute-start.27) | collective-permute-done | bytes 2097184 | tf_op jit(solution)/shard_map/ppermute | solution.py:900
  892.9 149.6 %shard_map.227 = (f32[2048,128]{1,0:T(8,128)}, f32[2048,16]{1,0:T(8,128)}, f32[2048,16]{1,0:T(8,128)}, f32[1,256]{1,0:T(1,128)}) custom-call(bf16[384,4096]{1,0:T(8,128)(2,1)} %bitcast.201, bf16[1024,384]{1,0:T(8,128)(2,1)} %get-tuple-element.379.extra_ref, bf16[384,2048]{1,0:T(8,128)(2,1)} %fusion.2.x_ref.b_ref, f32[64,256]{1,0:T(8,128)} %bitcast.216), custom_call_target="tpu_custom_call" | custom-call | flops 8053063680 | bytes 10000000 | tf_op jit(solution)/shard_map/pallas_call | solution.py:691
  (318 shorter events, 246.7 us)
Async XLA Ops:
  7.2 259.9 %all-gather.11.cloned.1.call-start = ((), (), s32[]{:S(2)}) async-start(), calls=%async_computation.14 | async-start | bytes 3538944 | tf_op jit(solution)/shard_map/all_gather | solution.py:1232
  220.2 85.7 %all-gather.13.cloned.1.call-start = ((), (), s32[]{:S(2)}) async-start(), calls=%async_computation.15 | async-start | bytes 3538944 | tf_op jit(solution)/shard_map/all_gather | solution.py:1233
  221.0 166.1 %all-gather.17.cloned.1.call-start = ((), (), s32[]{:S(2)}) async-start(), calls=%async_computation.17 | async-start | bytes 7520256 | tf_op jit(solution)/shard_map/all_gather | solution.py:1264
  238.4 62.9 %collective-permute-start.2 = (bf16[2,512,768]{2,1,0:T(8,128)(2,1)}, bf16[2,512,768]{2,1,0:T(8,128)(2,1)S(1)}, u32[]{:S(2)}, u32[]{:S(2)}) collective-permute-start(bf16[2,512,768]{2,1,0:T(8,128)(2,1)} %refs_7_.1), channel_id=1, source_target_pairs={{0,8},{8,0},{16,24},{24,16},{1,9},{9,1},{17,25},{25,17},{2,10},{10... | collective-permute-start | bytes 4718600 | tf_op jit(solution)/shard_map/ppermute | solution.py:900
  239.0 62.3 %collective-permute-start.3 = (bf16[2,512,768]{2,1,0:T(8,128)(2,1)}, bf16[2,512,768]{2,1,0:T(8,128)(2,1)}, u32[]{:S(2)}, u32[]{:S(2)}) collective-permute-start(bf16[2,512,768]{2,1,0:T(8,128)(2,1)} %refs_7_.1), channel_id=1, source_target_pairs={{0,16},{8,24},{16,0},{24,8},{1,17},{9,25},{17,1},{25,9},{2,18},{10... | collective-permute-start | bytes 4718600 | tf_op jit(solution)/shard_map/ppermute | solution.py:900
  240.4 63.9 %collective-permute-start.4 = (bf16[2,768,512]{2,1,0:T(8,128)(2,1)}, bf16[2,768,512]{2,1,0:T(8,128)(2,1)}, u32[]{:S(2)}, u32[]{:S(2)}) collective-permute-start(bf16[2,768,512]{2,1,0:T(8,128)(2,1)} %refs_12_.1), channel_id=1, source_target_pairs={{0,8},{8,0},{16,24},{24,16},{1,9},{9,1},{17,25},{25,17},{2,10},{10... | collective-permute-start | bytes 4718600 | tf_op jit(solution)/shard_map/ppermute | solution.py:900
  241.0 63.7 %collective-permute-start.5 = (bf16[2,768,512]{2,1,0:T(8,128)(2,1)}, bf16[2,768,512]{2,1,0:T(8,128)(2,1)}, u32[]{:S(2)}, u32[]{:S(2)}) collective-permute-start(bf16[2,768,512]{2,1,0:T(8,128)(2,1)} %refs_12_.1), channel_id=1, source_target_pairs={{0,16},{8,24},{16,0},{24,8},{1,17},{9,25},{17,1},{25,9},{2,18},{10... | collective-permute-start | bytes 4718600 | tf_op jit(solution)/shard_map/ppermute | solution.py:900
  305.9 156.1 %all-gather.15.cloned.1.call-start = ((), (), s32[]{:S(2)}) async-start(), calls=%async_computation.16 | async-start | bytes 7520256 | tf_op jit(solution)/shard_map/all_gather | solution.py:1264
  308.0 47.3 %collective-permute-start.6 = (bf16[1,512,768]{2,1,0:T(8,128)(2,1)S(1)}, bf16[1,512,768]{2,1,0:T(8,128)(2,1)S(1)}, u32[]{:S(2)}, u32[]{:S(2)}) collective-permute-start(bf16[1,512,768]{2,1,0:T(8,128)(2,1)S(1)} %slice.82), channel_id=1, source_target_pairs={{0,16},{8,24},{16,0},{24,8},{1,17},{9,25},{17,1},{25,9},{2,18},{10... | collective-permute-start | bytes 2359304 | tf_op jit(solution)/shard_map/ppermute | solution.py:900
  311.7 46.5 %collective-permute-start.7 = (bf16[1,512,768]{2,1,0:T(8,128)(2,1)}, bf16[1,512,768]{2,1,0:T(8,128)(2,1)S(1)}, u32[]{:S(2)}, u32[]{:S(2)}) collective-permute-start(bf16[1,512,768]{2,1,0:T(8,128)(2,1)} %slice.83), channel_id=1, source_target_pairs={{0,8},{8,0},{16,24},{24,16},{1,9},{9,1},{17,25},{25,17},{2,10},{10... | collective-permute-start | bytes 2359304 | tf_op jit(solution)/shard_map/ppermute | solution.py:900
  386.2 115.6 %all-gather.19.cloned.1.call-start = ((), (), s32[]{:S(2)}) async-start(), calls=%async_computation.18 | async-start | bytes 3538944 | tf_op jit(solution)/shard_map/all_gather | solution.py:1256
  386.8 184.0 %reduce-scatter.8.cloned.1.call-start = ((), (), s32[]{:S(2)}) async-start(), calls=%async_computation.7 | async-start | bytes 7077888 | tf_op jit(solution)/shard_map/reduce_scatter | solution.py:1269
  454.6 212.6 %reduce-scatter.10.cloned.1.call-start = ((), (), s32[]{:S(2)}) async-start(), calls=%async_computation.8 | async-start | bytes 7077888 | tf_op jit(solution)/shard_map/reduce_scatter | solution.py:1269
  570.8 250.5 %reduce-scatter.12.cloned.1.call-start = ((), (), s32[]{:S(2)}) async-start(), calls=%async_computation.9 | async-start | bytes 7077888 | tf_op jit(solution)/shard_map/reduce_scatter | solution.py:1305
  617.9 49.1 %collective-permute-start.14 = (bf16[2,512,768]{2,1,0:T(8,128)(2,1)}, bf16[2,512,768]{2,1,0:T(8,128)(2,1)}, u32[]{:S(2)}, u32[]{:S(2)}) collective-permute-start(bf16[2,512,768]{2,1,0:T(8,128)(2,1)} %get-tuple-element.451), channel_id=1, source_target_pairs={{0,8},{8,0},{16,24},{24,16},{1,9},{9,1},{17,25},{25,17},{2,10},{10... | collective-permute-start | bytes 4718600 | tf_op jit(solution)/shard_map/ppermute | solution.py:900
  619.5 47.7 %collective-permute-start.15 = (bf16[2,512,768]{2,1,0:T(8,128)(2,1)S(1)}, bf16[2,512,768]{2,1,0:T(8,128)(2,1)}, u32[]{:S(2)}, u32[]{:S(2)}) collective-permute-start(bf16[2,512,768]{2,1,0:T(8,128)(2,1)S(1)} %get-tuple-element.450), channel_id=1, source_target_pairs={{0,16},{8,24},{16,0},{24,8},{1,17},{9,25},{17,1},{25,9},{2,18},{10... | collective-permute-start | bytes 4718600 | tf_op jit(solution)/shard_map/ppermute | solution.py:900
  667.3 209.2 %reduce-scatter.14.cloned.1.call-start = ((), (), s32[]{:S(2)}) async-start(), calls=%async_computation.10 | async-start | bytes 3538944 | tf_op jit(solution)/shard_map/reduce_scatter | solution.py:1316
  751.1 125.4 %reduce-scatter.16.cloned.1.call-start = ((), (), s32[]{:S(2)}) async-start(), calls=%async_computation.11 | async-start | bytes 3538944 | tf_op jit(solution)/shard_map/reduce_scatter | solution.py:1324
  761.3 50.4 %collective-permute-start.25 = (bf16[2,768,512]{2,1,0:T(8,128)(2,1)S(1)}, bf16[2,768,512]{2,1,0:T(8,128)(2,1)S(1)}, u32[]{:S(2)}, u32[]{:S(2)}) collective-permute-start(bf16[2,768,512]{2,1,0:T(8,128)(2,1)S(1)} %get-tuple-element.443), channel_id=1, source_target_pairs={{0,8},{8,0},{16,24},{24,16},{1,9},{9,1},{17,25},{25,17},{2,10},{10... | collective-permute-start | bytes 4718600 | tf_op jit(solution)/shard_map/ppermute | solution.py:900
  762.8 48.9 %collective-permute-start.26 = (bf16[2,768,512]{2,1,0:T(8,128)(2,1)S(1)}, bf16[2,768,512]{2,1,0:T(8,128)(2,1)S(1)}, u32[]{:S(2)}, u32[]{:S(2)}) collective-permute-start(bf16[2,768,512]{2,1,0:T(8,128)(2,1)S(1)} %get-tuple-element.442), channel_id=1, source_target_pairs={{0,16},{8,24},{16,0},{24,8},{1,17},{9,25},{17,1},{25,9},{2,18},{10... | collective-permute-start | bytes 4718600 | tf_op jit(solution)/shard_map/ppermute | solution.py:900
  774.6 46.7 %collective-permute-start.24 = (bf16[1,256,2048]{2,1,0:T(8,128)(2,1)}, bf16[1,256,2048]{2,1,0:T(8,128)(2,1)}, u32[]{:S(2)}, u32[]{:S(2)}) collective-permute-start(bf16[1,256,2048]{2,1,0:T(8,128)(2,1)} %get-tuple-element.440), channel_id=1, source_target_pairs={{0,16},{8,24},{16,0},{24,8},{1,17},{9,25},{17,1},{25,9},{2,18},{10... | collective-permute-start | bytes 3145736 | tf_op jit(solution)/shard_map/ppermute | solution.py:900
  821.3 231.9 %reduce-scatter.20.cloned.1.call-start = ((), (), s32[]{:S(2)}) async-start(), calls=%async_computation.13 | async-start | bytes 2621440 | tf_op jit(solution)/shard_map/reduce_scatter | solution.py:1340
  825.7 46.3 %collective-permute-start.27 = (bf16[2,256,2048]{2,1,0:T(8,128)(2,1)S(1)}, bf16[2,256,2048]{2,1,0:T(8,128)(2,1)S(1)}, u32[]{:S(2)}, u32[]{:S(2)}) collective-permute-start(bf16[2,256,2048]{2,1,0:T(8,128)(2,1)S(1)} %get-tuple-element.362), channel_id=1, source_target_pairs={{0,8},{8,0},{16,24},{24,16},{1,9},{9,1},{17,25},{25,17},{2,10},{10... | collective-permute-start | bytes 6291464 | tf_op jit(solution)/shard_map/ppermute | solution.py:900
  878.6 176.8 %reduce-scatter.18.cloned.1.call-start = ((), (), s32[]{:S(2)}) async-start(), calls=%async_computation.12 | async-start | bytes 7077888 | tf_op jit(solution)/shard_map/reduce_scatter | solution.py:1333
  (75 other events, 1736.4 us)
Sparse Core Ops, SparseCore 0:
  220.3 46.7 all-gather.10
  268.7 37.1 all-gather.12
  308.1 75.6 all-gather.16
  386.3 75.6 all-gather.14
  463.5 38.2 all-gather.18
  504.0 66.7 reduce-scatter.7
  573.1 68.1 reduce-scatter.9
  667.4 65.9 reduce-scatter.11
  751.2 34.8 reduce-scatter.13
  821.5 33.9 reduce-scatter.15
  878.7 40.6 reduce-scatter.19
  921.6 123.1 reduce-scatter.17

commit v12 on v11

--- a/solution.py
+++ b/solution.py
@@ -1189,12 +1189,10 @@
     gain_len = norm_gains.shape[0]
     gain_shard = jnp.pad(norm_gains[None], ((0, 15), (0, 256 - gain_len)))
     kv_w = jnp.concatenate([w_key.T, w_value.T], axis=0)
-    halves = cotangent.reshape(2 * micro, rows // 2, width)
-    cot_first = halves[:3].reshape(-1, width)
-    q_w, kv_w, out_w, gain_full, cot_first = gather_rows(
-        [w_query.T, kv_w, w_output, gain_shard, cot_first], [(3, 0, 1, 2)], 1, (4,)
-    )
-    cot_first = cot_first.reshape(blocks, 3, rows // 2, width)
+    q_w, kv_w, out_w, gain_full, cot_all = gather_rows(
+        [w_query.T, kv_w, w_output, gain_shard, cotangent.reshape(total, width)], [(3, 0, 1, 2)], 1, (4,)
+    )
+    cot_all = cot_all.reshape(blocks, 2 * micro, rows // 2, width)
     q_w, w_gate = tie((q_w, w_gate))
     gains = gain_full.reshape(shards, 16, 256)[:, 0, :gain_len].reshape(-1).astype(f32)
     gain_in = gains[:width]
@@ -1231,7 +1229,8 @@
     kv_0, gate_near, w_up, w_down = tie((kv_0, gate_near, w_up, w_down))
     kv_0 = lax.all_gather(kv_0, "expert", axis=0, tiled=False)
     kv_1 = lax.all_gather(kv_1, "expert", axis=0, tiled=False)
-    up_near, down_near = ((swap(w, 1), swap(w, 2)) for w in (w_up, w_down))
+    gate_far = (swap(gate_near[0][:1], 2), swap(gate_near[1][1:], 1))
+    up_near = (swap(w_up, 1), swap(w_up, 2))
     chunk = 256
 
     def middle_of(mixed, at):
@@ -1241,20 +1240,25 @@
         return middle, jnp.concatenate([routed, routing[at]], axis=-1)
 
     mixed, logs, shares = run_forward(q_low, kv_0[:, None], bias, step_heads, chunk, 0, [], True)
+    mixed, up_near, gate_far = tie((mixed, up_near, gate_far))
+    up_far = (swap(up_near[0][:1], 2), swap(up_near[1][1:], 1))
     middle_0, routed_0 = middle_of(mixed, 0)
-    mixed, kv_1, routed_0, up_near, down_near = tie((mixed, kv_1, routed_0, up_near, down_near))
+    mixed, routed_0 = tie((mixed, routed_0))
+    mixed, kv_1, up_far, w_down = tie((mixed, kv_1, up_far, w_down))
+    down_near = (swap(w_down, 1), swap(w_down, 2))
     kv_all = [kv_0[:, None], kv_1[:, None]]
     mixed, logs, shares = run_forward(
         q_low, kv_all[1], bias, step_heads, chunk, 1, [mixed, logs, shares], True
     )
+    mixed, down_near = tie((mixed, down_near))
+    down_far = (swap(down_near[0][:1], 2), swap(down_near[1][1:], 1))
     middle_1, routed_1 = middle_of(mixed, 1)
     parts = [
-        (own, near[0], near[1], swap(near[0][:1], 2), swap(near[1][1:], 1))
-        for own, near in ((w_gate, gate_near), (w_up, up_near), (w_down, down_near))
+        (w_gate, *gate_near, *gate_far),
+        (w_up, *up_near, *up_far),
+        (w_down, *down_near, *down_far),
     ]
-    routed_1, parts, cot_last = tie((routed_1, parts, halves[3]))
-    cot_last = lax.all_gather(cot_last, "expert", axis=0, tiled=False)[:, None]
-    cots = [((cot_first, 0), (cot_first, 1)), ((cot_first, 2), (cot_last, 0))]
+    cots = [[(cot_all, 2 * b), (cot_all, 2 * b + 1)] for b in range(micro)]
     routed = [routed_0, routed_1]
     middle = jnp.stack([middle_0, middle_1])
 
@@ -1283,9 +1287,7 @@
     d_routeds[-1], first, second, third, mix_parts[0] = tie(
         (d_routeds[-1], first, second, third, mix_parts[0])
     )
-    second = scatter_add(second, 1)
-    d_routeds[-1], second, third = tie((d_routeds[-1], second, third))
-    second = (swap(second[0], 1), swap(second[1], 2), second[2])
+    second = scatter_near(second, 1)
     third = scatter_far(third, 2)
     d_mixed, d_middle, d_branch, grad_mid = run_middle_back(
         d_routeds, middle, cotangent[:, 0], gain_mid[None, :], out_w

time: 1080 us -> 1050 us (0.972)
  waiting for transfers between devices: 183 us -> 138 us
  Pallas kernels: 613 us -> 629 us
    all_gather x1 -> x0, waiting for transfers between devices: 39.8 us -> none  [body_fast(): cot_last = lax.all_gather(cot_last, 'expert', axis=0, tiled=False)[:, None]]
    pallas_call x1, Pallas kernels: 172 us -> 189 us  [gather_rows(): pl.pallas_call(functools.partial(gather_kernel, phases, len(arrays), late...]
    ppermute x28, waiting for transfers between devices: 107 us -> 120 us  [swap(): lax.ppermute(values, 'dp', [(i, i ^ bit) for i in range(lax.axis_size('dp...]
  transfers between devices with their start and end apart: 41 -> 40, of which waited for: 21 -> 17; matrix products, arithmetic and copies ran while one was open for 19% -> 20% of each run, Pallas kernels for 41% -> 42%
where the time goes in v12:
time: 1050 us; the launch traced here: 1040 us
  Pallas kernels  629 us (60%)
  waiting for transfers between devices  138 us (13%)
  matrix products  92.5 us (9%)
  other arithmetic  79.5 us (8%)
  local copies, waits for them, and re-layouts  53.9 us (5%)
  starting transfers between devices  31.2 us (3%)
  between operations  15.3 us (1%)
    pallas_call x1, Pallas kernels, gather_rows(): pl.pallas_call(functools.partial(gather_kernel, phases, len(arrays), late...  189 us
    pallas_call x1, Pallas kernels, reduce_rows(): pl.pallas_call(functools.partial(reduce_kernel, rows, 4), out_shape=[jax....  150 us
    ppermute x28, waiting for transfers between devices, swap(): lax.ppermute(values, 'dp', [(i, i ^ bit) for i in range(lax.axis_size('dp...  120 us
    pallas_call x2, Pallas kernels, run_experts(): pl.pallas_call(functools.partial(expert_kernel, len(earlier[2:])), grid=(...  80 us
    pallas_call x2, Pallas kernels, run_backward(): pl.pallas_call(kernel, grid=(KVH,), in_specs=[q_spec, kv_spec, bias_spec,...  71.5 us
    pallas_call x2, Pallas kernels, run_forward(): pl.pallas_call(kernel, grid=(KVH,), in_specs=[q_spec, kv_spec, bias_spec]...  47 us
    dot_general x3, matrix products, weight_grad(): jnp.einsum('era,erb->eab', rows_in, rows_out, preferred_element_type=f32)  43.9 us
    dot_general x4, matrix products, mm(): return lax.dot_general(a, b, dims, preferred_element_type=f32)  32.4 us
  transfers between devices with their start and end apart: 40, of which 17 were waited for; matrix products, arithmetic and copies ran while one was open for 20% of the time, Pallas kernels for 42%

profile of v12, /device:TPU:8, one launch (start us, length us, event | category | flops | bytes accessed | tf_op | source)
XLA Modules:
  0.0 1039.4 jit_solution(8277988613730013328)
XLA Ops:
  12.2 189.0 %shard_map.213 = (bf16[4096,2048]{1,0:T(8,128)(2,1)}, bf16[1024,2048]{1,0:T(8,128)(2,1)}, bf16[4096,2048]{1,0:T(8,128)(2,1)}, bf16[512,256]{1,0:T(8,128)(2,1)}, bf16[3072,2048]{1,0:T(8,128)(2,1)}) custom-call(bf16[128,2048]{1,0:T(8,128)(2,1)} %bitcast.201, bf16[32,2048]{1,0:T(8,128)(2,1)} %pad_maximum_fusion.8.refs_1_, bf16[128,2048]{1,0:T(8,128)(2,1)} %refs_2_.1, ...), custom_call_target="tpu_custom_call" | custom-call | bytes 400000000 | tf_op jit(solution)/shard_map/pallas_call | solution.py:496
  211.3 15.8 %shard_map.214 = (bf16[384,4096]{1,0:T(8,128)(2,1)}, f32[384,4096]{1,0:T(8,128)}, f32[384,512]{1,0:T(8,128)}, bf16[1024,2048]{1,0:T(8,128)(2,1)}, bf16[192,1024]{1,0:T(8,128)(2,1)}, /*index=5*/bf16[192,1024]{1,0:T(8,128)(2,1)}) custom-call(bf16[384,2048]{1,0:T(8,128)(2,1)} %fusion.2.x_ref.b_ref, bf16[4096,2048]{1,0:T(8,128)(2,1)} %get-tuple-element.189.wq_ref, ...), custom_call_target="tpu_custom_call" | custom-call | flops 1000000 | bytes 1000000 | tf_op jit(solution)/shard_map/pallas_call | solution.py:100
  266.8 16.6 %all-gather.9.cloned.1.call-done = bf16[1536,1024]{1,0:T(8,128)(2,1)} async-done(((bf16[192,1024]{1,0:T(8,128)(2,1)}), bf16[1536,1024]{1,0:T(8,128)(2,1)}) %all-gather.9.cloned.1.call-update) | async-done | bytes 3145744 | tf_op jit(solution)/shard_map/all_gather | solution.py:1230
  283.4 23.5 %shard_map.215 = (bf16[2,192,4096]{2,1,0:T(8,128)(2,1)}, f32[2,4,4,384]{3,2,1,0:T(4,128)}, bf16[2,2,2,192,1024]{4,3,2,1,0:T(8,128)(2,1)}) custom-call(bf16[2,192,4096]{2,1,0:T(8,128)(2,1)} %bitcast.161, bf16[8,1,192,1024]{3,2,1,0:T(8,128)(2,1)} %bitcast.178, f32[2,1536,384]{2,1,0:T(8,128)} %copy.84.refs_2_), custom_call_target="tpu_custom_call" | custom-call | flops 1000000 | bytes 1000000 | tf_op jit(solution)/shard_map/pallas_call | solution.py:250
  323.9 15.5 %collective-permute-done.6.refs_10_ = bf16[1,512,768]{2,1,0:T(8,128)(2,1)S(1)} collective-permute-done((bf16[1,512,768]{2,1,0:T(8,128)(2,1)S(1)}, bf16[1,512,768]{2,1,0:T(8,128)(2,1)S(1)}, u32[]{:S(2)}, u32[]{:S(2)}) %collective-permute-start.6) | collective-permute-done | bytes 786464 | tf_op jit(solution)/shard_map/ppermute | solution.py:900
  344.8 23.5 %shard_map.216 = (bf16[2,192,4096]{2,1,0:T(8,128)(2,1)}, f32[2,4,4,384]{3,2,1,0:T(4,128)}, bf16[2,2,2,192,1024]{4,3,2,1,0:T(8,128)(2,1)}) custom-call(bf16[2,192,4096]{2,1,0:T(8,128)(2,1)} %bitcast.162, bf16[8,1,192,1024]{3,2,1,0:T(8,128)(2,1)} %bitcast.176, ...), custom_call_target="tpu_custom_call", output_to_operand_aliasing={{0}: (3, {}), {1}: (4, {}), {2}: (5, {})} | custom-call | flops 1000000 | bytes 1000000 | tf_op jit(solution)/shard_map/pallas_call | solution.py:250
  368.3 10.2 collective-permute-done.8.refs_13_
  392.7 16.2 %collective-permute-done.10.refs_15_ = bf16[1,768,512]{2,1,0:T(8,128)(2,1)S(1)} collective-permute-done((bf16[1,768,512]{2,1,0:T(8,128)(2,1)S(1)}, bf16[1,768,512]{2,1,0:T(8,128)(2,1)S(1)}, u32[]{:S(2)}, u32[]{:S(2)}) %collective-permute-start.10) | collective-permute-done | bytes 786464 | tf_op jit(solution)/shard_map/ppermute | solution.py:900
  409.0 14.3 %shard_map.217 = (bf16[2,2,8,96,2048]{4,3,2,1,0:T(8,128)(2,1)}, bf16[2,2,8,96,2048]{4,3,2,1,0:T(8,128)(2,1)}) custom-call(bf16[8,192,2176]{2,1,0:T(8,128)(2,1)} %bitcast.167, bf16[8,4,96,2048]{3,2,1,0:T(8,128)(2,1)} %bitcast.148, bf16[8,4,96,2048]{3,2,1,0:T(8,128)(2,1)} %bitcast.149), custom_call_target="tpu_custom_call" | custom-call | flops 1000000 | bytes 1000000 | tf_op jit(solution)/shard_map/pallas_call | solution.py:827
  423.4 40.0 %shard_map.218 = (bf16[2,2,768,768]{3,2,1,0:T(8,128)(2,1)}, bf16[2,2,768,768]{3,2,1,0:T(8,128)(2,1)}, bf16[2,2,768,768]{3,2,1,0:T(8,128)(2,1)}, bf16[2,768,2048]{2,1,0:T(8,128)(2,1)}, bf16[2,768,2048]{2,1,0:T(8,128)(2,1)}) custom-call(bf16[2,2,768,2048]{3,2,1,0:T(8,128)(2,1)} %bitcast.152, bf16[2,2,768,2048]{3,2,1,0:T(8,128)(2,1)} %bitcast.156, ...), custom_call_target="tpu_custom_call" | custom-call | flops 1000000 | bytes 1000000 | tf_op jit(solution)/shard_map/pallas_call | solution.py:848
  463.4 12.7 %shard_map.219 = (bf16[1536,2048]{1,0:T(8,128)(2,1)}, bf16[1536,2048]{1,0:T(8,128)(2,1)}) custom-call(bf16[8,192,2176]{2,1,0:T(8,128)(2,1)} %bitcast.168, bf16[2,8,96,2048]{3,2,1,0:T(8,128)(2,1)} %bitcast.185, bf16[2,8,96,2048]{3,2,1,0:T(8,128)(2,1)} %bitcast.186), custom_call_target="tpu_custom_call" | custom-call | flops 1000000 | bytes 1000000 | tf_op jit(solution)/shard_map/pallas_call | solution.py:868
  476.6 14.0 %shard_map.220 = (bf16[2,2,8,96,2048]{4,3,2,1,0:T(8,128)(2,1)}, bf16[2,2,8,96,2048]{4,3,2,1,0:T(8,128)(2,1)}) custom-call(bf16[8,192,2176]{2,1,0:T(8,128)(2,1)} %bitcast.165, bf16[8,4,96,2048]{3,2,1,0:T(8,128)(2,1)} %bitcast.150, bf16[8,4,96,2048]{3,2,1,0:T(8,128)(2,1)} %bitcast.151, ...), custom_call_target="tpu_custom_call", output_to_operand_aliasing={{0}: (3, {}), {1}: (4, {})} | custom-call | flops 1000000 | bytes 1000000 | tf_op jit(solution)/shard_map/pallas_call | solution.py:827
  490.7 40.0 %shard_map.221 = (bf16[2,2,768,768]{3,2,1,0:T(8,128)(2,1)}, bf16[2,2,768,768]{3,2,1,0:T(8,128)(2,1)}, bf16[2,2,768,768]{3,2,1,0:T(8,128)(2,1)}, bf16[2,768,2048]{2,1,0:T(8,128)(2,1)}, bf16[2,768,2048]{2,1,0:T(8,128)(2,1)}) custom-call(bf16[2,2,768,2048]{3,2,1,0:T(8,128)(2,1)} %bitcast.153, ...), custom_call_target="tpu_custom_call", output_to_operand_aliasing={{0}: (17, {}), {1}: (18, {}), {2}: (19, {})} | custom-call | flops 1000000 | bytes 1000000 | tf_op jit(solution)/shard_map/pallas_call | solution.py:848
  530.6 12.7 %shard_map.222 = (bf16[1536,2048]{1,0:T(8,128)(2,1)}, bf16[1536,2048]{1,0:T(8,128)(2,1)}) custom-call(bf16[8,192,2176]{2,1,0:T(8,128)(2,1)} %bitcast.166, bf16[2,8,96,2048]{3,2,1,0:T(8,128)(2,1)} %bitcast.183, bf16[2,8,96,2048]{3,2,1,0:T(8,128)(2,1)} %bitcast.184), custom_call_target="tpu_custom_call" | custom-call | flops 1000000 | bytes 1000000 | tf_op jit(solution)/shard_map/pallas_call | solution.py:868
  543.6 15.0 %convolution_convert_fusion.4 = bf16[2,2048,768]{2,1,0:T(8,128)(2,1)S(1)} fusion(bf16[2,1536,2048]{2,1,0:T(8,128)(2,1)} %bitcast.154, bf16[2,1536,768]{2,1,0:T(8,128)(2,1)} %bitcast.194), kind=kOutput, calls=%fused_computation.6 | convolution fusion | flops 9666822144 | bytes 23592960 | tf_op jit(solution)/shard_map/era,erb->eab/dot_general | solution.py:1280
  565.1 17.1 %convolution_convert_fusion.3 = bf16[2,2048,768]{2,1,0:T(8,128)(2,1)} fusion(bf16[2,1536,2048]{2,1,0:T(8,128)(2,1)} %bitcast.155, bf16[2,1536,768]{2,1,0:T(8,128)(2,1)} %bitcast.195), kind=kOutput, calls=%fused_computation.5 | convolution fusion | flops 9666822144 | bytes 23592960 | tf_op jit(solution)/shard_map/era,erb->eab/dot_general | solution.py:1280
  593.2 11.8 %convolution_convert_fusion.2 = bf16[2,768,2048]{2,1,0:T(8,128)(2,1)} fusion(bf16[2,1536,768]{2,1,0:T(8,128)(2,1)S(1)} %bitcast.193, bf16[2,1536,2048]{2,1,0:T(8,128)(2,1)S(1)} %bitcast.160), kind=kOutput, calls=%fused_computation.4 | convolution fusion | flops 9666822144 | bytes 23592960 | tf_op jit(solution)/shard_map/era,erb->eab/dot_general | solution.py:1280
  606.8 32.2 %collective-permute-done.14 = bf16[2,512,768]{2,1,0:T(8,128)(2,1)} collective-permute-done((bf16[2,512,768]{2,1,0:T(8,128)(2,1)}, bf16[2,512,768]{2,1,0:T(8,128)(2,1)}, u32[]{:S(2)}, u32[]{:S(2)}) %collective-permute-start.14) | collective-permute-done | bytes 1572896 | tf_op jit(solution)/shard_map/ppermute | solution.py:900
  650.3 19.0 %shard_map.223 = (bf16[384,4096]{1,0:T(8,128)(2,1)}, f32[384,2048]{1,0:T(8,128)}, bf16[384,2048]{1,0:T(8,128)(2,1)}, f32[1,2048]{1,0:T(1,128)}) custom-call(bf16[192,2048]{1,0:T(8,128)(2,1)} %reduce-scatter.8.cloned.1.call-done.r0_ref, bf16[192,2048]{1,0:T(8,128)(2,1)} %reduce-scatter.10.cloned.1.call-done.r1_ref, f32[2,192,2048]{2,1,0:T(8,128)} %pad_maximum_fusion.mid_ref, ...), custom_call_target="tpu_custom_call" | custom-call | flops 1000000 | bytes 1000000 | tf_op jit(solution)/shard_map/pallas_call | solution.py:323
  669.3 9.7 convolution_convert_fusion.1
  687.0 35.9 %shard_map.224 = (bf16[2,192,4096]{2,1,0:T(8,128)(2,1)}, bf16[8,1,192,1024]{3,2,1,0:T(8,128)(2,1)}, f32[1,128]{1,0:T(1,128)}) custom-call(bf16[2,192,4096]{2,1,0:T(8,128)(2,1)} %bitcast.163, bf16[8,1,192,1024]{3,2,1,0:T(8,128)(2,1)} %bitcast.179, f32[2,1536,384]{2,1,0:T(8,128)} %copy.84.refs_2_, bf16[2,192,4096]{2,1,0:T(8,128)(2,1)} %get-tuple-element.212.refs_3_, ...), custom_call_target="tpu_custom_call" | custom-call | flops 1000000 | bytes 1000000 | tf_op jit(solution)/shard_map/pallas_call | solution.py:278
  748.5 35.6 %shard_map.225 = (bf16[2,192,4096]{2,1,0:T(8,128)(2,1)}, bf16[8,1,192,1024]{3,2,1,0:T(8,128)(2,1)}, f32[1,128]{1,0:T(1,128)}) custom-call(bf16[2,192,4096]{2,1,0:T(8,128)(2,1)} %bitcast.164, bf16[8,1,192,1024]{3,2,1,0:T(8,128)(2,1)} %bitcast.177, f32[2,1536,384]{2,1,0:T(8,128)} %copy.84.refs_2_, ...), custom_call_target="tpu_custom_call", output_to_operand_aliasing={{0}: (10, {})} | custom-call | flops 1000000 | bytes 1000000 | tf_op jit(solution)/shard_map/pallas_call | solution.py:278
  822.3 22.1 %collective-permute-done.27 = bf16[2,256,2048]{2,1,0:T(8,128)(2,1)S(1)} collective-permute-done((bf16[2,256,2048]{2,1,0:T(8,128)(2,1)S(1)}, bf16[2,256,2048]{2,1,0:T(8,128)(2,1)S(1)}, u32[]{:S(2)}, u32[]{:S(2)}) %collective-permute-start.27) | collective-permute-done | bytes 2097184 | tf_op jit(solution)/shard_map/ppermute | solution.py:900
  865.5 149.7 %shard_map.227 = (f32[2048,128]{1,0:T(8,128)}, f32[2048,16]{1,0:T(8,128)}, f32[2048,16]{1,0:T(8,128)}, f32[1,256]{1,0:T(1,128)}) custom-call(bf16[384,4096]{1,0:T(8,128)(2,1)} %bitcast.198, bf16[1024,384]{1,0:T(8,128)(2,1)} %get-tuple-element.351.extra_ref, bf16[384,2048]{1,0:T(8,128)(2,1)} %fusion.2.x_ref.b_ref, f32[64,256]{1,0:T(8,128)} %bitcast.212), custom_call_target="tpu_custom_call" | custom-call | flops 8053063680 | bytes 10000000 | tf_op jit(solution)/shard_map/pallas_call | solution.py:691
  (312 shorter events, 231.8 us)
Async XLA Ops:
  7.2 276.2 %all-gather.9.cloned.1.call-start = ((), (), s32[]{:S(2)}) async-start(), calls=%async_computation.14 | async-start | bytes 3538944 | tf_op jit(solution)/shard_map/all_gather | solution.py:1230
  235.8 88.1 %all-gather.11.cloned.1.call-start = ((), (), s32[]{:S(2)}) async-start(), calls=%async_computation.15 | async-start | bytes 3538944 | tf_op jit(solution)/shard_map/all_gather | solution.py:1231
  236.5 172.5 %all-gather.15.cloned.1.call-start = ((), (), s32[]{:S(2)}) async-start(), calls=%async_computation.17 | async-start | bytes 7520256 | tf_op jit(solution)/shard_map/all_gather | solution.py:1268
  244.7 62.2 %collective-permute-start.2 = (bf16[2,512,768]{2,1,0:T(8,128)(2,1)}, bf16[2,512,768]{2,1,0:T(8,128)(2,1)}, u32[]{:S(2)}, u32[]{:S(2)}) collective-permute-start(bf16[2,512,768]{2,1,0:T(8,128)(2,1)} %refs_7_.1), channel_id=1, source_target_pairs={{0,8},{8,0},{16,24},{24,16},{1,9},{9,1},{17,25},{25,17},{2,10},{10... | collective-permute-start | bytes 4718600 | tf_op jit(solution)/shard_map/ppermute | solution.py:900
  245.3 61.6 %collective-permute-start.3 = (bf16[2,512,768]{2,1,0:T(8,128)(2,1)}, bf16[2,512,768]{2,1,0:T(8,128)(2,1)}, u32[]{:S(2)}, u32[]{:S(2)}) collective-permute-start(bf16[2,512,768]{2,1,0:T(8,128)(2,1)} %refs_7_.1), channel_id=1, source_target_pairs={{0,16},{8,24},{16,0},{24,8},{1,17},{9,25},{17,1},{25,9},{2,18},{10... | collective-permute-start | bytes 4718600 | tf_op jit(solution)/shard_map/ppermute | solution.py:900
  262.1 44.8 %collective-permute-start.4 = (bf16[1,512,768]{2,1,0:T(8,128)(2,1)}, bf16[1,512,768]{2,1,0:T(8,128)(2,1)S(1)}, u32[]{:S(2)}, u32[]{:S(2)}) collective-permute-start(bf16[1,512,768]{2,1,0:T(8,128)(2,1)} %slice.68), channel_id=1, source_target_pairs={{0,16},{8,24},{16,0},{24,8},{1,17},{9,25},{17,1},{25,9},{2,18},{10... | collective-permute-start | bytes 2359304 | tf_op jit(solution)/shard_map/ppermute | solution.py:900
  264.1 42.9 %collective-permute-start.5 = (bf16[1,512,768]{2,1,0:T(8,128)(2,1)S(1)}, bf16[1,512,768]{2,1,0:T(8,128)(2,1)S(1)}, u32[]{:S(2)}, u32[]{:S(2)}) collective-permute-start(bf16[1,512,768]{2,1,0:T(8,128)(2,1)S(1)} %slice.69), channel_id=1, source_target_pairs={{0,8},{8,0},{16,24},{24,16},{1,9},{9,1},{17,25},{25,17},{2,10},{10... | collective-permute-start | bytes 2359304 | tf_op jit(solution)/shard_map/ppermute | solution.py:900
  318.2 158.4 %all-gather.13.cloned.1.call-start = ((), (), s32[]{:S(2)}) async-start(), calls=%async_computation.16 | async-start | bytes 7520256 | tf_op jit(solution)/shard_map/all_gather | solution.py:1268
  390.9 152.5 %reduce-scatter.8.cloned.1.call-start = ((), (), s32[]{:S(2)}) async-start(), calls=%async_computation.7 | async-start | bytes 7077888 | tf_op jit(solution)/shard_map/reduce_scatter | solution.py:1273
  476.1 163.2 %reduce-scatter.10.cloned.1.call-start = ((), (), s32[]{:S(2)}) async-start(), calls=%async_computation.8 | async-start | bytes 7077888 | tf_op jit(solution)/shard_map/reduce_scatter | solution.py:1273
  543.4 250.4 %reduce-scatter.12.cloned.1.call-start = ((), (), s32[]{:S(2)}) async-start(), calls=%async_computation.9 | async-start | bytes 7077888 | tf_op jit(solution)/shard_map/reduce_scatter | solution.py:1307
  590.6 48.4 %collective-permute-start.14 = (bf16[2,512,768]{2,1,0:T(8,128)(2,1)}, bf16[2,512,768]{2,1,0:T(8,128)(2,1)}, u32[]{:S(2)}, u32[]{:S(2)}) collective-permute-start(bf16[2,512,768]{2,1,0:T(8,128)(2,1)} %get-tuple-element.423), channel_id=1, source_target_pairs={{0,8},{8,0},{16,24},{24,16},{1,9},{9,1},{17,25},{25,17},{2,10},{10... | collective-permute-start | bytes 4718600 | tf_op jit(solution)/shard_map/ppermute | solution.py:900
  591.6 47.7 %collective-permute-start.15 = (bf16[2,512,768]{2,1,0:T(8,128)(2,1)S(1)}, bf16[2,512,768]{2,1,0:T(8,128)(2,1)}, u32[]{:S(2)}, u32[]{:S(2)}) collective-permute-start(bf16[2,512,768]{2,1,0:T(8,128)(2,1)S(1)} %get-tuple-element.422), channel_id=1, source_target_pairs={{0,16},{8,24},{16,0},{24,8},{1,17},{9,25},{17,1},{25,9},{2,18},{10... | collective-permute-start | bytes 4718600 | tf_op jit(solution)/shard_map/ppermute | solution.py:900
  639.3 209.6 %reduce-scatter.14.cloned.1.call-start = ((), (), s32[]{:S(2)}) async-start(), calls=%async_computation.10 | async-start | bytes 3538944 | tf_op jit(solution)/shard_map/reduce_scatter | solution.py:1318
  679.1 43.9 %collective-permute-start.20 = (bf16[2,1024,2048]{2,1,0:T(8,128)(2,1)}, bf16[2,1024,2048]{2,1,0:T(8,128)(2,1)}, u32[]{:S(2)}, u32[]{:S(2)}) collective-permute-start(bf16[2,1024,2048]{2,1,0:T(8,128)(2,1)} %convolution_convert_fusion.1), channel_id=1, source_target_pairs={{0,1},{1,0},{2,3},{3,2},{4,5},{5,4},{6,7},{7,6},{8,9},{9,8},{10,11... | collective-permute-start | bytes 25165832 | tf_op jit(solution)/shard_map/ppermute | solution.py:1306
  722.9 126.0 %reduce-scatter.16.cloned.1.call-start = ((), (), s32[]{:S(2)}) async-start(), calls=%async_computation.11 | async-start | bytes 3538944 | tf_op jit(solution)/shard_map/reduce_scatter | solution.py:1326
  733.8 50.4 %collective-permute-start.25 = (bf16[2,768,512]{2,1,0:T(8,128)(2,1)S(1)}, bf16[2,768,512]{2,1,0:T(8,128)(2,1)S(1)}, u32[]{:S(2)}, u32[]{:S(2)}) collective-permute-start(bf16[2,768,512]{2,1,0:T(8,128)(2,1)S(1)} %get-tuple-element.415), channel_id=1, source_target_pairs={{0,8},{8,0},{16,24},{24,16},{1,9},{9,1},{17,25},{25,17},{2,10},{10... | collective-permute-start | bytes 4718600 | tf_op jit(solution)/shard_map/ppermute | solution.py:900
  735.3 48.8 %collective-permute-start.26 = (bf16[2,768,512]{2,1,0:T(8,128)(2,1)S(1)}, bf16[2,768,512]{2,1,0:T(8,128)(2,1)S(1)}, u32[]{:S(2)}, u32[]{:S(2)}) collective-permute-start(bf16[2,768,512]{2,1,0:T(8,128)(2,1)S(1)} %get-tuple-element.414), channel_id=1, source_target_pairs={{0,16},{8,24},{16,0},{24,8},{1,17},{9,25},{17,1},{25,9},{2,18},{10... | collective-permute-start | bytes 4718600 | tf_op jit(solution)/shard_map/ppermute | solution.py:900
  746.5 46.1 %collective-permute-start.23 = (bf16[1,256,2048]{2,1,0:T(8,128)(2,1)}, bf16[1,256,2048]{2,1,0:T(8,128)(2,1)}, u32[]{:S(2)}, u32[]{:S(2)}) collective-permute-start(bf16[1,256,2048]{2,1,0:T(8,128)(2,1)} %get-tuple-element.413), channel_id=1, source_target_pairs={{0,8},{8,0},{16,24},{24,16},{1,9},{9,1},{17,25},{25,17},{2,10},{10... | collective-permute-start | bytes 3145736 | tf_op jit(solution)/shard_map/ppermute | solution.py:900
  747.0 46.8 %collective-permute-start.24 = (bf16[1,256,2048]{2,1,0:T(8,128)(2,1)}, bf16[1,256,2048]{2,1,0:T(8,128)(2,1)}, u32[]{:S(2)}, u32[]{:S(2)}) collective-permute-start(bf16[1,256,2048]{2,1,0:T(8,128)(2,1)} %get-tuple-element.412), channel_id=1, source_target_pairs={{0,16},{8,24},{16,0},{24,8},{1,17},{9,25},{17,1},{25,9},{2,18},{10... | collective-permute-start | bytes 3145736 | tf_op jit(solution)/shard_map/ppermute | solution.py:900
  793.8 232.2 %reduce-scatter.20.cloned.1.call-start = ((), (), s32[]{:S(2)}) async-start(), calls=%async_computation.13 | async-start | bytes 2621440 | tf_op jit(solution)/shard_map/reduce_scatter | solution.py:1342
  798.1 46.3 %collective-permute-start.27 = (bf16[2,256,2048]{2,1,0:T(8,128)(2,1)S(1)}, bf16[2,256,2048]{2,1,0:T(8,128)(2,1)S(1)}, u32[]{:S(2)}, u32[]{:S(2)}) collective-permute-start(bf16[2,256,2048]{2,1,0:T(8,128)(2,1)S(1)} %get-tuple-element.334), channel_id=1, source_target_pairs={{0,8},{8,0},{16,24},{24,16},{1,9},{9,1},{17,25},{25,17},{2,10},{10... | collective-permute-start | bytes 6291464 | tf_op jit(solution)/shard_map/ppermute | solution.py:900
  798.8 46.0 %collective-permute-start.28 = (bf16[2,256,2048]{2,1,0:T(8,128)(2,1)S(1)}, bf16[2,256,2048]{2,1,0:T(8,128)(2,1)S(1)}, u32[]{:S(2)}, u32[]{:S(2)}) collective-permute-start(bf16[2,256,2048]{2,1,0:T(8,128)(2,1)S(1)} %get-tuple-element.335), channel_id=1, source_target_pairs={{0,16},{8,24},{16,0},{24,8},{1,17},{9,25},{17,1},{25,9},{2,18},{10... | collective-permute-start | bytes 6291464 | tf_op jit(solution)/shard_map/ppermute | solution.py:900
  851.0 177.1 %reduce-scatter.18.cloned.1.call-start = ((), (), s32[]{:S(2)}) async-start(), calls=%async_computation.12 | async-start | bytes 7077888 | tf_op jit(solution)/shard_map/reduce_scatter | solution.py:1335
  (73 other events, 1432.0 us)
Sparse Core Ops, SparseCore 0:
  235.9 47.4 all-gather.8
  285.0 37.1 all-gather.10
  324.4 65.4 all-gather.14
  392.0 66.6 all-gather.12
  476.2 66.5 reduce-scatter.7
  545.0 68.1 reduce-scatter.9
  639.4 67.6 reduce-scatter.11
  723.1 34.9 reduce-scatter.13
  793.9 34.1 reduce-scatter.15
  851.1 40.7 reduce-scatter.19
  894.3 123.1 reduce-scatter.17

commit v13 on v12

--- a/solution.py
+++ b/solution.py
@@ -1266,7 +1266,6 @@
     kept = []
     for at in range(micro):
         tokens = lax.all_gather(routed[at], "expert", axis=0, tiled=False)
-        tokens, parts = tie((tokens, parts))
         kept, mix, d_part = run_experts(tokens, cots[at], parts, capacity, at, micro, kept)
         kept, d_part, mix, d_routeds = tie((kept, d_part, mix, d_routeds))
         mix_parts.append(mix)

time: 1050 us -> 1040 us (level)
  waiting for transfers between devices: 138 us -> 124 us
    ppermute x28, waiting for transfers between devices: 120 us -> 106 us  [swap(): lax.ppermute(values, 'dp', [(i, i ^ bit) for i in range(lax.axis_size('dp...]
  transfers between devices with their start and end apart: 40 -> 40, of which waited for: 17 -> 17; matrix products, arithmetic and copies ran while one was open for 20% -> 20% of each run, Pallas kernels for 42% -> 43%
where the time goes in v13:
time: 1040 us; the launch traced here: 1030 us
  Pallas kernels  629 us (60%)
  waiting for transfers between devices  124 us (12%)
  matrix products  92.5 us (9%)
  other arithmetic  79.5 us (8%)
  local copies, waits for them, and re-layouts  56.6 us (5%)
  starting transfers between devices  31.2 us (3%)
  between operations  15.3 us (1%)
    pallas_call x1, Pallas kernels, gather_rows(): pl.pallas_call(functools.partial(gather_kernel, phases, len(arrays), late...  189 us
    pallas_call x1, Pallas kernels, reduce_rows(): pl.pallas_call(functools.partial(reduce_kernel, rows, 4), out_shape=[jax....  150 us
    ppermute x28, waiting for transfers between devices, swap(): lax.ppermute(values, 'dp', [(i, i ^ bit) for i in range(lax.axis_size('dp...  106 us
    pallas_call x2, Pallas kernels, run_experts(): pl.pallas_call(functools.partial(expert_kernel, len(earlier[2:])), grid=(...  79.9 us
    pallas_call x2, Pallas kernels, run_backward(): pl.pallas_call(kernel, grid=(KVH,), in_specs=[q_spec, kv_spec, bias_spec,...  71.5 us
    pallas_call x2, Pallas kernels, run_forward(): pl.pallas_call(kernel, grid=(KVH,), in_specs=[q_spec, kv_spec, bias_spec]...  47 us
    dot_general x3, matrix products, weight_grad(): jnp.einsum('era,erb->eab', rows_in, rows_out, preferred_element_type=f32)  43.9 us
    dot_general x4, matrix products, mm(): return lax.dot_general(a, b, dims, preferred_element_type=f32)  32.4 us
  transfers between devices with their start and end apart: 40, of which 17 were waited for; matrix products, arithmetic and copies ran while one was open for 20% of the time, Pallas kernels for 43%

profile of v13, /device:TPU:8, one launch (start us, length us, event | category | flops | bytes accessed | tf_op | source)
XLA Modules:
  0.0 1027.9 jit_solution(15794932859569203137)
XLA Ops:
  12.2 189.0 %shard_map.213 = (bf16[4096,2048]{1,0:T(8,128)(2,1)}, bf16[1024,2048]{1,0:T(8,128)(2,1)}, bf16[4096,2048]{1,0:T(8,128)(2,1)}, bf16[512,256]{1,0:T(8,128)(2,1)}, bf16[3072,2048]{1,0:T(8,128)(2,1)}) custom-call(bf16[128,2048]{1,0:T(8,128)(2,1)} %bitcast.201, bf16[32,2048]{1,0:T(8,128)(2,1)} %pad_maximum_fusion.8.refs_1_, bf16[128,2048]{1,0:T(8,128)(2,1)} %refs_2_.1, ...), custom_call_target="tpu_custom_call" | custom-call | bytes 400000000 | tf_op jit(solution)/shard_map/pallas_call | solution.py:496
  211.3 15.8 %shard_map.214 = (bf16[384,4096]{1,0:T(8,128)(2,1)}, f32[384,4096]{1,0:T(8,128)}, f32[384,512]{1,0:T(8,128)}, bf16[1024,2048]{1,0:T(8,128)(2,1)}, bf16[192,1024]{1,0:T(8,128)(2,1)}, /*index=5*/bf16[192,1024]{1,0:T(8,128)(2,1)}) custom-call(bf16[384,2048]{1,0:T(8,128)(2,1)} %fusion.2.x_ref.b_ref, bf16[4096,2048]{1,0:T(8,128)(2,1)} %get-tuple-element.157.wq_ref, ...), custom_call_target="tpu_custom_call" | custom-call | flops 1000000 | bytes 1000000 | tf_op jit(solution)/shard_map/pallas_call | solution.py:100
  266.8 16.6 %all-gather.9.cloned.1.call-done = bf16[1536,1024]{1,0:T(8,128)(2,1)} async-done(((bf16[192,1024]{1,0:T(8,128)(2,1)}), bf16[1536,1024]{1,0:T(8,128)(2,1)}) %all-gather.9.cloned.1.call-update) | async-done | bytes 3145744 | tf_op jit(solution)/shard_map/all_gather | solution.py:1230
  283.4 23.5 %shard_map.215 = (bf16[2,192,4096]{2,1,0:T(8,128)(2,1)}, f32[2,4,4,384]{3,2,1,0:T(4,128)}, bf16[2,2,2,192,1024]{4,3,2,1,0:T(8,128)(2,1)}) custom-call(bf16[2,192,4096]{2,1,0:T(8,128)(2,1)} %bitcast.161, bf16[8,1,192,1024]{3,2,1,0:T(8,128)(2,1)} %bitcast.178, f32[2,1536,384]{2,1,0:T(8,128)} %copy.84.refs_2_), custom_call_target="tpu_custom_call" | custom-call | flops 1000000 | bytes 1000000 | tf_op jit(solution)/shard_map/pallas_call | solution.py:250
  307.0 8.8 multiply_reduce_fusion.1
  323.9 15.5 %collective-permute-done.6.refs_10_ = bf16[1,512,768]{2,1,0:T(8,128)(2,1)S(1)} collective-permute-done((bf16[1,512,768]{2,1,0:T(8,128)(2,1)S(1)}, bf16[1,512,768]{2,1,0:T(8,128)(2,1)S(1)}, u32[]{:S(2)}, u32[]{:S(2)}) %collective-permute-start.6) | collective-permute-done | bytes 786464 | tf_op jit(solution)/shard_map/ppermute | solution.py:900
  344.8 23.5 %shard_map.216 = (bf16[2,192,4096]{2,1,0:T(8,128)(2,1)}, f32[2,4,4,384]{3,2,1,0:T(4,128)}, bf16[2,2,2,192,1024]{4,3,2,1,0:T(8,128)(2,1)}) custom-call(bf16[2,192,4096]{2,1,0:T(8,128)(2,1)} %bitcast.162, bf16[8,1,192,1024]{3,2,1,0:T(8,128)(2,1)} %bitcast.176, ...), custom_call_target="tpu_custom_call", output_to_operand_aliasing={{0}: (3, {}), {1}: (4, {}), {2}: (5, {})} | custom-call | flops 1000000 | bytes 1000000 | tf_op jit(solution)/shard_map/pallas_call | solution.py:250
  368.3 10.2 collective-permute-done.8.refs_13_
  394.3 14.0 %shard_map.217 = (bf16[2,2,8,96,2048]{4,3,2,1,0:T(8,128)(2,1)}, bf16[2,2,8,96,2048]{4,3,2,1,0:T(8,128)(2,1)}) custom-call(bf16[8,192,2176]{2,1,0:T(8,128)(2,1)} %bitcast.167, bf16[8,4,96,2048]{3,2,1,0:T(8,128)(2,1)} %bitcast.148, bf16[8,4,96,2048]{3,2,1,0:T(8,128)(2,1)} %bitcast.149), custom_call_target="tpu_custom_call" | custom-call | flops 1000000 | bytes 1000000 | tf_op jit(solution)/shard_map/pallas_call | solution.py:827
  411.7 40.0 %shard_map.218 = (bf16[2,2,768,768]{3,2,1,0:T(8,128)(2,1)}, bf16[2,2,768,768]{3,2,1,0:T(8,128)(2,1)}, bf16[2,2,768,768]{3,2,1,0:T(8,128)(2,1)}, bf16[2,768,2048]{2,1,0:T(8,128)(2,1)}, bf16[2,768,2048]{2,1,0:T(8,128)(2,1)}) custom-call(bf16[2,2,768,2048]{3,2,1,0:T(8,128)(2,1)} %bitcast.152, bf16[2,2,768,2048]{3,2,1,0:T(8,128)(2,1)} %bitcast.156, ...), custom_call_target="tpu_custom_call" | custom-call | flops 1000000 | bytes 1000000 | tf_op jit(solution)/shard_map/pallas_call | solution.py:848
  451.7 12.7 %shard_map.219 = (bf16[1536,2048]{1,0:T(8,128)(2,1)}, bf16[1536,2048]{1,0:T(8,128)(2,1)}) custom-call(bf16[8,192,2176]{2,1,0:T(8,128)(2,1)} %bitcast.168, bf16[2,8,96,2048]{3,2,1,0:T(8,128)(2,1)} %bitcast.185, bf16[2,8,96,2048]{3,2,1,0:T(8,128)(2,1)} %bitcast.186), custom_call_target="tpu_custom_call" | custom-call | flops 1000000 | bytes 1000000 | tf_op jit(solution)/shard_map/pallas_call | solution.py:868
  464.9 14.1 %shard_map.220 = (bf16[2,2,8,96,2048]{4,3,2,1,0:T(8,128)(2,1)}, bf16[2,2,8,96,2048]{4,3,2,1,0:T(8,128)(2,1)}) custom-call(bf16[8,192,2176]{2,1,0:T(8,128)(2,1)} %bitcast.165, bf16[8,4,96,2048]{3,2,1,0:T(8,128)(2,1)} %bitcast.150, bf16[8,4,96,2048]{3,2,1,0:T(8,128)(2,1)} %bitcast.151, ...), custom_call_target="tpu_custom_call", output_to_operand_aliasing={{0}: (3, {}), {1}: (4, {})} | custom-call | flops 1000000 | bytes 1000000 | tf_op jit(solution)/shard_map/pallas_call | solution.py:827
  479.0 40.0 %shard_map.221 = (bf16[2,2,768,768]{3,2,1,0:T(8,128)(2,1)}, bf16[2,2,768,768]{3,2,1,0:T(8,128)(2,1)}, bf16[2,2,768,768]{3,2,1,0:T(8,128)(2,1)}, bf16[2,768,2048]{2,1,0:T(8,128)(2,1)}, bf16[2,768,2048]{2,1,0:T(8,128)(2,1)}) custom-call(bf16[2,2,768,2048]{3,2,1,0:T(8,128)(2,1)} %bitcast.153, ...), custom_call_target="tpu_custom_call", output_to_operand_aliasing={{0}: (17, {}), {1}: (18, {}), {2}: (19, {})} | custom-call | flops 1000000 | bytes 1000000 | tf_op jit(solution)/shard_map/pallas_call | solution.py:848
  519.0 12.7 %shard_map.222 = (bf16[1536,2048]{1,0:T(8,128)(2,1)}, bf16[1536,2048]{1,0:T(8,128)(2,1)}) custom-call(bf16[8,192,2176]{2,1,0:T(8,128)(2,1)} %bitcast.166, bf16[2,8,96,2048]{3,2,1,0:T(8,128)(2,1)} %bitcast.183, bf16[2,8,96,2048]{3,2,1,0:T(8,128)(2,1)} %bitcast.184), custom_call_target="tpu_custom_call" | custom-call | flops 1000000 | bytes 1000000 | tf_op jit(solution)/shard_map/pallas_call | solution.py:868
  531.9 15.0 %convolution_convert_fusion.4 = bf16[2,2048,768]{2,1,0:T(8,128)(2,1)S(1)} fusion(bf16[2,1536,2048]{2,1,0:T(8,128)(2,1)} %bitcast.154, bf16[2,1536,768]{2,1,0:T(8,128)(2,1)} %bitcast.194), kind=kOutput, calls=%fused_computation.6 | convolution fusion | flops 9666822144 | bytes 23592960 | tf_op jit(solution)/shard_map/era,erb->eab/dot_general | solution.py:1279
  553.6 17.1 %convolution_convert_fusion.3 = bf16[2,2048,768]{2,1,0:T(8,128)(2,1)} fusion(bf16[2,1536,2048]{2,1,0:T(8,128)(2,1)} %bitcast.155, bf16[2,1536,768]{2,1,0:T(8,128)(2,1)} %bitcast.195), kind=kOutput, calls=%fused_computation.5 | convolution fusion | flops 9666822144 | bytes 23592960 | tf_op jit(solution)/shard_map/era,erb->eab/dot_general | solution.py:1279
  581.6 11.8 %convolution_convert_fusion.2 = bf16[2,768,2048]{2,1,0:T(8,128)(2,1)} fusion(bf16[2,1536,768]{2,1,0:T(8,128)(2,1)S(1)} %bitcast.193, bf16[2,1536,2048]{2,1,0:T(8,128)(2,1)S(1)} %bitcast.160), kind=kOutput, calls=%fused_computation.4 | convolution fusion | flops 9666822144 | bytes 23592960 | tf_op jit(solution)/shard_map/era,erb->eab/dot_general | solution.py:1279
  595.2 32.2 %collective-permute-done.14 = bf16[2,512,768]{2,1,0:T(8,128)(2,1)} collective-permute-done((bf16[2,512,768]{2,1,0:T(8,128)(2,1)}, bf16[2,512,768]{2,1,0:T(8,128)(2,1)}, u32[]{:S(2)}, u32[]{:S(2)}) %collective-permute-start.14) | collective-permute-done | bytes 1572896 | tf_op jit(solution)/shard_map/ppermute | solution.py:900
  638.8 19.0 %shard_map.223 = (bf16[384,4096]{1,0:T(8,128)(2,1)}, f32[384,2048]{1,0:T(8,128)}, bf16[384,2048]{1,0:T(8,128)(2,1)}, f32[1,2048]{1,0:T(1,128)}) custom-call(bf16[192,2048]{1,0:T(8,128)(2,1)} %reduce-scatter.8.cloned.1.call-done.r0_ref, bf16[192,2048]{1,0:T(8,128)(2,1)} %reduce-scatter.10.cloned.1.call-done.r1_ref, f32[2,192,2048]{2,1,0:T(8,128)} %pad_maximum_fusion.mid_ref, ...), custom_call_target="tpu_custom_call" | custom-call | flops 1000000 | bytes 1000000 | tf_op jit(solution)/shard_map/pallas_call | solution.py:323
  657.8 9.7 convolution_convert_fusion.1
  675.4 35.9 %shard_map.224 = (bf16[2,192,4096]{2,1,0:T(8,128)(2,1)}, bf16[8,1,192,1024]{3,2,1,0:T(8,128)(2,1)}, f32[1,128]{1,0:T(1,128)}) custom-call(bf16[2,192,4096]{2,1,0:T(8,128)(2,1)} %bitcast.163, bf16[8,1,192,1024]{3,2,1,0:T(8,128)(2,1)} %bitcast.179, f32[2,1536,384]{2,1,0:T(8,128)} %copy.84.refs_2_, bf16[2,192,4096]{2,1,0:T(8,128)(2,1)} %get-tuple-element.180.refs_3_, ...), custom_call_target="tpu_custom_call" | custom-call | flops 1000000 | bytes 1000000 | tf_op jit(solution)/shard_map/pallas_call | solution.py:278
  737.0 35.6 %shard_map.225 = (bf16[2,192,4096]{2,1,0:T(8,128)(2,1)}, bf16[8,1,192,1024]{3,2,1,0:T(8,128)(2,1)}, f32[1,128]{1,0:T(1,128)}) custom-call(bf16[2,192,4096]{2,1,0:T(8,128)(2,1)} %bitcast.164, bf16[8,1,192,1024]{3,2,1,0:T(8,128)(2,1)} %bitcast.177, f32[2,1536,384]{2,1,0:T(8,128)} %copy.84.refs_2_, ...), custom_call_target="tpu_custom_call", output_to_operand_aliasing={{0}: (10, {})} | custom-call | flops 1000000 | bytes 1000000 | tf_op jit(solution)/shard_map/pallas_call | solution.py:278
  810.8 22.1 %collective-permute-done.27 = bf16[2,256,2048]{2,1,0:T(8,128)(2,1)S(1)} collective-permute-done((bf16[2,256,2048]{2,1,0:T(8,128)(2,1)S(1)}, bf16[2,256,2048]{2,1,0:T(8,128)(2,1)S(1)}, u32[]{:S(2)}, u32[]{:S(2)}) %collective-permute-start.27) | collective-permute-done | bytes 2097184 | tf_op jit(solution)/shard_map/ppermute | solution.py:900
  854.0 149.7 %shard_map.227 = (f32[2048,128]{1,0:T(8,128)}, f32[2048,16]{1,0:T(8,128)}, f32[2048,16]{1,0:T(8,128)}, f32[1,256]{1,0:T(1,128)}) custom-call(bf16[384,4096]{1,0:T(8,128)(2,1)} %bitcast.198, bf16[1024,384]{1,0:T(8,128)(2,1)} %get-tuple-element.287.extra_ref, bf16[384,2048]{1,0:T(8,128)(2,1)} %fusion.2.x_ref.b_ref, f32[64,256]{1,0:T(8,128)} %bitcast.212), custom_call_target="tpu_custom_call" | custom-call | flops 8053063680 | bytes 10000000 | tf_op jit(solution)/shard_map/pallas_call | solution.py:691
  (312 shorter events, 228.1 us)
Async XLA Ops:
  7.2 276.2 %all-gather.9.cloned.1.call-start = ((), (), s32[]{:S(2)}) async-start(), calls=%async_computation.14 | async-start | bytes 3538944 | tf_op jit(solution)/shard_map/all_gather | solution.py:1230
  235.8 88.1 %all-gather.11.cloned.1.call-start = ((), (), s32[]{:S(2)}) async-start(), calls=%async_computation.15 | async-start | bytes 3538944 | tf_op jit(solution)/shard_map/all_gather | solution.py:1231
  236.5 157.8 %all-gather.15.cloned.1.call-start = ((), (), s32[]{:S(2)}) async-start(), calls=%async_computation.17 | async-start | bytes 7520256 | tf_op jit(solution)/shard_map/all_gather | solution.py:1268
  244.7 62.2 %collective-permute-start.2 = (bf16[2,512,768]{2,1,0:T(8,128)(2,1)}, bf16[2,512,768]{2,1,0:T(8,128)(2,1)}, u32[]{:S(2)}, u32[]{:S(2)}) collective-permute-start(bf16[2,512,768]{2,1,0:T(8,128)(2,1)} %refs_7_.1), channel_id=1, source_target_pairs={{0,8},{8,0},{16,24},{24,16},{1,9},{9,1},{17,25},{25,17},{2,10},{10... | collective-permute-start | bytes 4718600 | tf_op jit(solution)/shard_map/ppermute | solution.py:900
  245.3 61.6 %collective-permute-start.3 = (bf16[2,512,768]{2,1,0:T(8,128)(2,1)}, bf16[2,512,768]{2,1,0:T(8,128)(2,1)}, u32[]{:S(2)}, u32[]{:S(2)}) collective-permute-start(bf16[2,512,768]{2,1,0:T(8,128)(2,1)} %refs_7_.1), channel_id=1, source_target_pairs={{0,16},{8,24},{16,0},{24,8},{1,17},{9,25},{17,1},{25,9},{2,18},{10... | collective-permute-start | bytes 4718600 | tf_op jit(solution)/shard_map/ppermute | solution.py:900
  262.1 44.8 %collective-permute-start.4 = (bf16[1,512,768]{2,1,0:T(8,128)(2,1)}, bf16[1,512,768]{2,1,0:T(8,128)(2,1)S(1)}, u32[]{:S(2)}, u32[]{:S(2)}) collective-permute-start(bf16[1,512,768]{2,1,0:T(8,128)(2,1)} %slice.68), channel_id=1, source_target_pairs={{0,16},{8,24},{16,0},{24,8},{1,17},{9,25},{17,1},{25,9},{2,18},{10... | collective-permute-start | bytes 2359304 | tf_op jit(solution)/shard_map/ppermute | solution.py:900
  264.1 42.9 %collective-permute-start.5 = (bf16[1,512,768]{2,1,0:T(8,128)(2,1)S(1)}, bf16[1,512,768]{2,1,0:T(8,128)(2,1)S(1)}, u32[]{:S(2)}, u32[]{:S(2)}) collective-permute-start(bf16[1,512,768]{2,1,0:T(8,128)(2,1)S(1)} %slice.69), channel_id=1, source_target_pairs={{0,8},{8,0},{16,24},{24,16},{1,9},{9,1},{17,25},{25,17},{2,10},{10... | collective-permute-start | bytes 2359304 | tf_op jit(solution)/shard_map/ppermute | solution.py:900
  318.2 146.7 %all-gather.13.cloned.1.call-start = ((), (), s32[]{:S(2)}) async-start(), calls=%async_computation.16 | async-start | bytes 7520256 | tf_op jit(solution)/shard_map/all_gather | solution.py:1268
  390.9 140.8 %reduce-scatter.8.cloned.1.call-start = ((), (), s32[]{:S(2)}) async-start(), calls=%async_computation.7 | async-start | bytes 7077888 | tf_op jit(solution)/shard_map/reduce_scatter | solution.py:1272
  464.4 163.3 %reduce-scatter.10.cloned.1.call-start = ((), (), s32[]{:S(2)}) async-start(), calls=%async_computation.8 | async-start | bytes 7077888 | tf_op jit(solution)/shard_map/reduce_scatter | solution.py:1272
  531.7 250.5 %reduce-scatter.12.cloned.1.call-start = ((), (), s32[]{:S(2)}) async-start(), calls=%async_computation.9 | async-start | bytes 7077888 | tf_op jit(solution)/shard_map/reduce_scatter | solution.py:1306
  578.9 48.6 %collective-permute-start.14 = (bf16[2,512,768]{2,1,0:T(8,128)(2,1)}, bf16[2,512,768]{2,1,0:T(8,128)(2,1)}, u32[]{:S(2)}, u32[]{:S(2)}) collective-permute-start(bf16[2,512,768]{2,1,0:T(8,128)(2,1)} %get-tuple-element.359), channel_id=1, source_target_pairs={{0,8},{8,0},{16,24},{24,16},{1,9},{9,1},{17,25},{25,17},{2,10},{10... | collective-permute-start | bytes 4718600 | tf_op jit(solution)/shard_map/ppermute | solution.py:900
  580.0 47.7 %collective-permute-start.15 = (bf16[2,512,768]{2,1,0:T(8,128)(2,1)S(1)}, bf16[2,512,768]{2,1,0:T(8,128)(2,1)}, u32[]{:S(2)}, u32[]{:S(2)}) collective-permute-start(bf16[2,512,768]{2,1,0:T(8,128)(2,1)S(1)} %get-tuple-element.358), channel_id=1, source_target_pairs={{0,16},{8,24},{16,0},{24,8},{1,17},{9,25},{17,1},{25,9},{2,18},{10... | collective-permute-start | bytes 4718600 | tf_op jit(solution)/shard_map/ppermute | solution.py:900
  627.8 209.7 %reduce-scatter.14.cloned.1.call-start = ((), (), s32[]{:S(2)}) async-start(), calls=%async_computation.10 | async-start | bytes 3538944 | tf_op jit(solution)/shard_map/reduce_scatter | solution.py:1317
  667.5 43.9 %collective-permute-start.20 = (bf16[2,1024,2048]{2,1,0:T(8,128)(2,1)}, bf16[2,1024,2048]{2,1,0:T(8,128)(2,1)}, u32[]{:S(2)}, u32[]{:S(2)}) collective-permute-start(bf16[2,1024,2048]{2,1,0:T(8,128)(2,1)} %convolution_convert_fusion.1), channel_id=1, source_target_pairs={{0,1},{1,0},{2,3},{3,2},{4,5},{5,4},{6,7},{7,6},{8,9},{9,8},{10,11... | collective-permute-start | bytes 25165832 | tf_op jit(solution)/shard_map/ppermute | solution.py:1305
  711.5 126.0 %reduce-scatter.16.cloned.1.call-start = ((), (), s32[]{:S(2)}) async-start(), calls=%async_computation.11 | async-start | bytes 3538944 | tf_op jit(solution)/shard_map/reduce_scatter | solution.py:1325
  722.3 50.4 %collective-permute-start.25 = (bf16[2,768,512]{2,1,0:T(8,128)(2,1)S(1)}, bf16[2,768,512]{2,1,0:T(8,128)(2,1)S(1)}, u32[]{:S(2)}, u32[]{:S(2)}) collective-permute-start(bf16[2,768,512]{2,1,0:T(8,128)(2,1)S(1)} %get-tuple-element.351), channel_id=1, source_target_pairs={{0,8},{8,0},{16,24},{24,16},{1,9},{9,1},{17,25},{25,17},{2,10},{10... | collective-permute-start | bytes 4718600 | tf_op jit(solution)/shard_map/ppermute | solution.py:900
  723.8 48.9 %collective-permute-start.26 = (bf16[2,768,512]{2,1,0:T(8,128)(2,1)S(1)}, bf16[2,768,512]{2,1,0:T(8,128)(2,1)S(1)}, u32[]{:S(2)}, u32[]{:S(2)}) collective-permute-start(bf16[2,768,512]{2,1,0:T(8,128)(2,1)S(1)} %get-tuple-element.350), channel_id=1, source_target_pairs={{0,16},{8,24},{16,0},{24,8},{1,17},{9,25},{17,1},{25,9},{2,18},{10... | collective-permute-start | bytes 4718600 | tf_op jit(solution)/shard_map/ppermute | solution.py:900
  734.9 46.2 %collective-permute-start.23 = (bf16[1,256,2048]{2,1,0:T(8,128)(2,1)}, bf16[1,256,2048]{2,1,0:T(8,128)(2,1)}, u32[]{:S(2)}, u32[]{:S(2)}) collective-permute-start(bf16[1,256,2048]{2,1,0:T(8,128)(2,1)} %get-tuple-element.349), channel_id=1, source_target_pairs={{0,8},{8,0},{16,24},{24,16},{1,9},{9,1},{17,25},{25,17},{2,10},{10... | collective-permute-start | bytes 3145736 | tf_op jit(solution)/shard_map/ppermute | solution.py:900
  735.5 46.7 %collective-permute-start.24 = (bf16[1,256,2048]{2,1,0:T(8,128)(2,1)}, bf16[1,256,2048]{2,1,0:T(8,128)(2,1)}, u32[]{:S(2)}, u32[]{:S(2)}) collective-permute-start(bf16[1,256,2048]{2,1,0:T(8,128)(2,1)} %get-tuple-element.348), channel_id=1, source_target_pairs={{0,16},{8,24},{16,0},{24,8},{1,17},{9,25},{17,1},{25,9},{2,18},{10... | collective-permute-start | bytes 3145736 | tf_op jit(solution)/shard_map/ppermute | solution.py:900
  782.3 232.2 %reduce-scatter.20.cloned.1.call-start = ((), (), s32[]{:S(2)}) async-start(), calls=%async_computation.13 | async-start | bytes 2621440 | tf_op jit(solution)/shard_map/reduce_scatter | solution.py:1341
  786.6 46.3 %collective-permute-start.27 = (bf16[2,256,2048]{2,1,0:T(8,128)(2,1)S(1)}, bf16[2,256,2048]{2,1,0:T(8,128)(2,1)S(1)}, u32[]{:S(2)}, u32[]{:S(2)}) collective-permute-start(bf16[2,256,2048]{2,1,0:T(8,128)(2,1)S(1)} %get-tuple-element.270), channel_id=1, source_target_pairs={{0,8},{8,0},{16,24},{24,16},{1,9},{9,1},{17,25},{25,17},{2,10},{10... | collective-permute-start | bytes 6291464 | tf_op jit(solution)/shard_map/ppermute | solution.py:900
  787.3 46.0 %collective-permute-start.28 = (bf16[2,256,2048]{2,1,0:T(8,128)(2,1)S(1)}, bf16[2,256,2048]{2,1,0:T(8,128)(2,1)S(1)}, u32[]{:S(2)}, u32[]{:S(2)}) collective-permute-start(bf16[2,256,2048]{2,1,0:T(8,128)(2,1)S(1)} %get-tuple-element.271), channel_id=1, source_target_pairs={{0,16},{8,24},{16,0},{24,8},{1,17},{9,25},{17,1},{25,9},{2,18},{10... | collective-permute-start | bytes 6291464 | tf_op jit(solution)/shard_map/ppermute | solution.py:900
  839.5 177.1 %reduce-scatter.18.cloned.1.call-start = ((), (), s32[]{:S(2)}) async-start(), calls=%async_computation.12 | async-start | bytes 7077888 | tf_op jit(solution)/shard_map/reduce_scatter | solution.py:1334
  (73 other events, 1406.4 us)
Sparse Core Ops, SparseCore 0:
  235.9 47.4 all-gather.8
  285.0 37.1 all-gather.10
  324.4 65.4 all-gather.14
  392.0 66.6 all-gather.12
  464.5 66.7 reduce-scatter.7
  533.5 68.1 reduce-scatter.9
  627.9 67.5 reduce-scatter.11
  711.6 34.9 reduce-scatter.13
  782.4 34.1 reduce-scatter.15
  839.6 40.7 reduce-scatter.19
  882.8 123.1 reduce-scatter.17
